TPU v7x, 32 devices: a whole 2x2x4 slice. The times are simulated.
32 devices in a mesh: dp: 8 (over z, x), expert: 4 (over y, core).
Axes of the slice: x: 2, y: 2, z: 4, core: 2. Of those that a mesh axis runs over, the one named last changes fastest.
Arguments:
- tokens: bfloat16 [16384, 768], P(('dp', 'expert')), may hold values from -6 to 6
- qkv_weight: bfloat16 [3, 768, 768], P(None, 'dp'), may hold values from -0.21875 to 0.21875
- out_weight: bfloat16 [768, 768], P('dp'), may hold values from -1.75 to 1.75
- position_bias_table: float32 [12, 32], replicated, may hold values from -3 to 3
- gain_attn: float32 [768], replicated, may hold values from 0.5 to 1.5
- gain_moe: float32 [768], replicated, may hold values from 0.5 to 1.5
- router: bfloat16 [768, 8], replicated, may hold values from -0.15625 to 0.15625
- w_in: bfloat16 [8, 768, 3072], P('expert'), may hold values from -0.21875 to 0.21875
- w_out: bfloat16 [8, 3072, 768], P('expert'), may hold values from -0.109375 to 0.109375
- routes: int32 [16384, 2], P(('dp', 'expert')), may hold values from 0 to 7, all different within a row; in each aligned block of 512 rows (0 to 511, 512 to 1023, ...) at most 160 rows name the same one
- prefix: int32 [32], P(('dp', 'expert')), may hold values from 51 to 256
- valid_mask: int32 [16384], P(('dp', 'expert')), may hold values from 0 to 1, as said below
- teacher: bfloat16 [16384, 768], P(('dp', 'expert')), may hold values from -6 to 6
- cotangent: bfloat16 [16384, 768], P(('dp', 'expert')), may hold values from -6 to 6
Outputs:
- output: bfloat16 [16384, 768], P(('dp', 'expert'))
- distill_loss: float32 [], replicated
- grad_input: float32 [16384, 768], P(('dp', 'expert'))
- grad_qkv: float32 [3, 768, 768], P(None, 'dp')
- grad_out_weight: float32 [768, 768], P('dp')
- grad_w_in: float32 [8, 768, 3072], P('expert', 'dp')
- grad_w_out: float32 [8, 3072, 768], P('expert', 'dp')
- grad_router: float32 [768, 8], replicated
- grad_table: float32 [12, 32], replicated
- grad_gain_attn: float32 [768], replicated
- grad_gain_moe: float32 [768], replicated
Inputs may be any that keep to these rules, and one draw needn't show every extreme that they name: `routes`: each row names 2 different experts. Among the 512 rows of one device no expert is named more than 160 times, a bound that some block reaches. `valid_mask`: the first token of every sequence is valid.
All inputs are finite; a program needn't handle non-finite values.
Results may differ from a plain program's by a relative error of at most 0.015.
Values may be sent and summed in bfloat16 or wider, within the bound.
No kernel may reach another device: no remote copies, remote signals or barrier semaphores. Data moves between devices by JAX's collectives and lax.ppermute only.
A program may use at most 192 MiB of HBM per device.

v0:
```python
import math
import jax
import jax.numpy as jnp
from jax import lax
from jax.experimental import pallas as pl
from jax.experimental.pallas import tpu as pltpu
from jax.sharding import PartitionSpec as P

BLOCK = 128
THIRDS = 3
EPS = 1e-06
GELU_A = math.sqrt(2.0 / math.pi)
GELU_B = 0.044715
NT = (((1,), (1,)), ((), ()))
TN = (((0,), (0,)), ((), ()))
VMEM_BYTES = 56 * 1024 * 1024


def cost(micros):
    return pl.CostEstimate(flops=int(micros * 0.37e9), bytes_accessed=0, transcendentals=0)


def dot_f32(left, right, dims=(((1,), (0,)), ((), ()))):
    return lax.dot_general(left, right, dims, preferred_element_type=jnp.float32)


def assemble(rows, pieces):
    start = 0
    for piece in pieces:
        rows[pl.ds(start, piece.shape[0]), :] = piece[...]
        start += piece.shape[0]


def hand_out(total, outs):
    start = 0
    for out in outs:
        out[...] = total[pl.ds(start, out.shape[0]), :].astype(out.dtype)
        start += out.shape[0]


def whole(shape):
    return pl.BlockSpec(shape, lambda *step: (0,) * len(shape))


def expert_forward_kernel(pick, *refs, chunk, count):
    pieces, w_in, w_out = refs[:count], refs[count], refs[count + 1]
    hidden_t, slope, rows_t = refs[count + 2 : count + 5]
    outs, rows, total = refs[count + 5 : 2 * count + 5], refs[2 * count + 5], refs[2 * count + 6]
    step = pl.program_id(0)

    @pl.when(step == 0)
    def _():
        assemble(rows, pieces)
        total[...] = jnp.zeros_like(total)
        rows_t[...] = rows[...].T

    for start in range(0, rows.shape[0], chunk):
        part = pl.ds(start, chunk)
        pre = dot_f32(rows[part, :], w_in[0])
        square = pre * pre
        bend = jnp.tanh(pre * (GELU_A + (GELU_A * GELU_B) * square))
        half = 0.5 + 0.5 * bend
        act = (pre * half).astype(jnp.bfloat16)
        lift = pre * (0.5 * GELU_A + (1.5 * GELU_A * GELU_B) * square)
        slope[part, :] = (half + lift * (1.0 - bend * bend)).astype(jnp.bfloat16)
        hidden_t[:, part] = act.T
        total[part, :] += dot_f32(act, w_out[0])

    @pl.when(step == pl.num_programs(0) - 1)
    def _():
        hand_out(total, outs)


def expert_forward(pick, pieces, w_in, w_out, tile=512, chunk=128):
    many, width = sum(piece.shape[0] for piece in pieces), pieces[0].shape[1]
    inner = w_in.shape[2]
    bf16 = jnp.bfloat16
    return pl.pallas_call(
        lambda *refs: expert_forward_kernel(*refs, chunk=chunk, count=len(pieces)),
        grid_spec=pltpu.PrefetchScalarGridSpec(
            num_scalar_prefetch=1,
            grid=(inner // tile,),
            in_specs=[whole(piece.shape) for piece in pieces]
            + [
                pl.BlockSpec((1, width, tile), lambda f, pick: (pick[0], 0, f)),
                pl.BlockSpec((1, tile, width), lambda f, pick: (pick[0], f, 0)),
            ],
            out_specs=[
                pl.BlockSpec((tile, many), lambda f, pick: (f, 0)),
                pl.BlockSpec((many, tile), lambda f, pick: (0, f)),
                whole((width, many)),
            ]
            + [whole(piece.shape) for piece in pieces],
            scratch_shapes=[pltpu.VMEM((many, width), bf16), pltpu.VMEM((many, width), jnp.float32)],
        ),
        out_shape=[
            jax.ShapeDtypeStruct((inner, many), bf16),
            jax.ShapeDtypeStruct((many, inner), bf16),
            jax.ShapeDtypeStruct((width, many), bf16),
        ]
        + [jax.ShapeDtypeStruct(piece.shape, bf16) for piece in pieces],
        compiler_params=pltpu.CompilerParams(vmem_limit_bytes=VMEM_BYTES),
        cost_estimate=cost(13),
        name="expert_forward",
    )(pick, *pieces, w_in, w_out)


def expert_backward_kernel(pick, *refs, chunk, count):
    pieces, w_in, w_out, slope = refs[:count], refs[count], refs[count + 1], refs[count + 2]
    grad_pre, rows = refs[count + 3 : count + 5]
    outs, total = refs[count + 5 : 2 * count + 5], refs[2 * count + 5]
    step = pl.program_id(0)

    @pl.when(step == 0)
    def _():
        assemble(rows, pieces)
        total[...] = jnp.zeros_like(total)

    for start in range(0, rows.shape[0], chunk):
        part = pl.ds(start, chunk)
        back = dot_f32(rows[part, :], w_out[0], NT) * slope[part, :].astype(jnp.float32)
        back = back.astype(jnp.bfloat16)
        grad_pre[part, :] = back
        total[part, :] += dot_f32(back, w_in[0], NT)

    @pl.when(step == pl.num_programs(0) - 1)
    def _():
        hand_out(total, outs)


def expert_backward(pick, pieces, w_in, w_out, slope, tile=512, chunk=320):
    many, width = sum(piece.shape[0] for piece in pieces), pieces[0].shape[1]
    inner = w_in.shape[2]
    bf16 = jnp.bfloat16
    return pl.pallas_call(
        lambda *refs: expert_backward_kernel(*refs, chunk=chunk, count=len(pieces)),
        grid_spec=pltpu.PrefetchScalarGridSpec(
            num_scalar_prefetch=1,
            grid=(inner // tile,),
            in_specs=[whole(piece.shape) for piece in pieces]
            + [
                pl.BlockSpec((1, width, tile), lambda f, pick: (pick[0], 0, f)),
                pl.BlockSpec((1, tile, width), lambda f, pick: (pick[0], f, 0)),
                pl.BlockSpec((many, tile), lambda f, pick: (0, f)),
            ],
            out_specs=[pl.BlockSpec((many, tile), lambda f, pick: (0, f)), whole((many, width))]
            + [whole(piece.shape) for piece in pieces],
            scratch_shapes=[pltpu.VMEM((many, width), jnp.float32)],
        ),
        out_shape=[jax.ShapeDtypeStruct((many, inner), bf16), jax.ShapeDtypeStruct((many, width), bf16)]
        + [jax.ShapeDtypeStruct(piece.shape, bf16) for piece in pieces],
        compiler_params=pltpu.CompilerParams(vmem_limit_bytes=VMEM_BYTES),
        cost_estimate=cost(11),
        name="expert_backward",
    )(pick, *pieces, w_in, w_out, slope)


def seen_blocks(row_block, blocks):
    return max(row_block + 1, blocks // 2)


def attention_forward_kernel(far, prefix, queries, keys, values, offsets, attended, probs, *, heads, blocks):
    pair = pl.program_id(0)
    lane = lax.broadcasted_iota(jnp.int32, (BLOCK, 2 * heads), 1)
    row = lax.broadcasted_iota(jnp.int32, (BLOCK, BLOCK), 0)
    col = lax.broadcasted_iota(jnp.int32, (BLOCK, BLOCK), 1)
    turned = []
    for head in range(2):
        line = jnp.broadcast_to(offsets[head : head + 1, :], (BLOCK, 4 * BLOCK))
        turned.append(pltpu.roll(line, 0, 1, stride=1, stride_axis=0))
    for row_block in range(blocks):
        rows = pl.ds(row_block * BLOCK, BLOCK)
        span = seen_blocks(row_block, blocks)
        seen = pl.ds(0, span * BLOCK)
        outs = []
        for head in range(2):
            mine = (lane < heads) if head == 0 else (lane >= heads)
            query = jnp.where(mine, queries[rows, :] * 0.125, 0.0).astype(jnp.bfloat16)
            score = dot_f32(query, keys[seen, :], NT)
            far_bias = far[pair * 2 + head]
            pieces = []
            for key_block in range(span):
                piece = score[:, key_block * BLOCK : (key_block + 1) * BLOCK]
                shift = key_block - row_block
                if shift < -1:
                    piece = piece + far_bias
                elif shift < 2:
                    piece = piece + turned[head][:, (2 + shift) * BLOCK : (3 + shift) * BLOCK]
                else:
                    raise ValueError(shift)
                if shift >= 0:
                    shown = col + key_block * BLOCK < prefix[0]
                    piece = jnp.where((shown | (col <= row)) if shift == 0 else shown, piece, -1e30)
                pieces.append(piece)
            peak = pieces[0]
            for piece in pieces[1:]:
                peak = jnp.maximum(peak, piece)
            peak = jnp.max(peak, axis=1, keepdims=True)
            pieces = [jnp.exp(piece - peak) for piece in pieces]
            mass = pieces[0]
            for piece in pieces[1:]:
                mass = mass + piece
            scale = 1.0 / jnp.sum(mass, axis=1, keepdims=True)
            weights = jnp.concatenate([(piece * scale).astype(jnp.bfloat16) for piece in pieces], axis=1)
            probs[head, rows, seen] = weights
            outs.append(dot_f32(weights, values[seen, :]))
        attended[rows, :] = jnp.where(lane < heads, outs[0], outs[1]).astype(jnp.bfloat16)


def attention_forward(far, prefix, qkv_rows, offsets):
    length, width = qkv_rows.shape[1:]
    pairs = width // 128
    blocks = length // BLOCK
    return pl.pallas_call(
        lambda *refs: attention_forward_kernel(*refs, heads=64, blocks=blocks),
        grid_spec=pltpu.PrefetchScalarGridSpec(
            num_scalar_prefetch=2,
            grid=(pairs,),
            in_specs=[pl.BlockSpec((None, length, 128), lambda h, far, prefix, c=c: (c, 0, h)) for c in range(3)]
            + [pl.BlockSpec((None, 2, 4 * BLOCK), lambda h, far, prefix: (h, 0, 0))],
            out_specs=[
                pl.BlockSpec((length, 128), lambda h, far, prefix: (0, h)),
                pl.BlockSpec((2, length, length), lambda h, far, prefix: (h, 0, 0)),
            ],
        ),
        out_shape=[
            jax.ShapeDtypeStruct((length, width), jnp.bfloat16),
            jax.ShapeDtypeStruct((2 * pairs, length, length), jnp.bfloat16),
        ],
        compiler_params=pltpu.CompilerParams(vmem_limit_bytes=VMEM_BYTES),
        cost_estimate=cost(17),
        name="attention_forward",
    )(far, prefix, qkv_rows, qkv_rows, qkv_rows, offsets.reshape(pairs, 2, 4 * BLOCK))


def attention_backward_kernel(queries, keys, values, grads, probs, grad_rows, bands, flow, *, heads, blocks):
    lane = lax.broadcasted_iota(jnp.int32, (BLOCK, 2 * heads), 1)
    query_t = (queries[...] * 0.125).astype(jnp.bfloat16).T
    grad_t = grads[...].T
    half = blocks // 2
    dk, dv = [], []
    dq = [[], []]
    for head in range(2):
        mine = (lane < heads) if head == 0 else (lane >= heads)
        sums = [None] * 4
        for row_block in range(blocks):
            rows = pl.ds(row_block * BLOCK, BLOCK)
            span = seen_blocks(row_block, blocks)
            seen = pl.ds(0, span * BLOCK)
            grad = jnp.where(mine, grads[rows, :], 0.0).astype(jnp.bfloat16)
            soft = probs[head, rows, seen].astype(jnp.float32)
            back = dot_f32(grad, values[seen, :], NT)
            inner = jnp.sum(soft * back, axis=1, keepdims=True)
            score_grad = (soft * (back - inner)).astype(jnp.bfloat16)
            flow[rows, seen] = score_grad
            dq[head].append(dot_f32(score_grad, keys[seen, :]) * 0.125)
            for key_block in range(span):
                band = max(key_block - row_block, -2)
                if band > 1:
                    continue
                tile = score_grad[:, key_block * BLOCK : (key_block + 1) * BLOCK].astype(jnp.float32)
                sums[band + 2] = tile if sums[band + 2] is None else sums[band + 2] + tile
        for band in range(4):
            bands[head, band] = sums[band]
        part = slice(head * heads, (head + 1) * heads)
        key_pieces, value_pieces = [], []
        for key_block in range(blocks):
            first = 0 if key_block < half else key_block
            rows = pl.ds(first * BLOCK, (blocks - first) * BLOCK)
            cols = pl.ds(key_block * BLOCK, BLOCK)
            key_pieces.append(dot_f32(query_t[part, first * BLOCK :], flow[rows, cols]))
            value_pieces.append(dot_f32(grad_t[part, first * BLOCK :], probs[head, rows, cols]))
        dk.append(jnp.concatenate(key_pieces, axis=1))
        dv.append(jnp.concatenate(value_pieces, axis=1))
    for row_block in range(blocks):
        rows = pl.ds(row_block * BLOCK, BLOCK)
        grad_rows[0, rows, :] = jnp.where(lane < heads, dq[0][row_block], dq[1][row_block]).astype(jnp.bfloat16)
    grad_rows[1] = jnp.concatenate(dk, axis=0).T.astype(jnp.bfloat16)
    grad_rows[2] = jnp.concatenate(dv, axis=0).T.astype(jnp.bfloat16)


def attention_backward(qkv_rows, grads, probs):
    length, width = grads.shape
    pairs = width // 128
    blocks = length // BLOCK
    block = pl.BlockSpec((length, 128), lambda h: (0, h))
    of_three = [pl.BlockSpec((None, length, 128), lambda h, c=c: (c, 0, h)) for c in range(3)]
    return pl.pallas_call(
        lambda *refs: attention_backward_kernel(*refs, heads=64, blocks=blocks),
        grid=(pairs,),
        in_specs=[*of_three, block, pl.BlockSpec((2, length, length), lambda h: (h, 0, 0))],
        out_specs=[pl.BlockSpec((3, length, 128), lambda h: (0, 0, h)), pl.BlockSpec((2, 4, BLOCK, BLOCK), lambda h: (h, 0, 0, 0))],
        out_shape=[jax.ShapeDtypeStruct((3, length, width), jnp.bfloat16)]
        + [jax.ShapeDtypeStruct((2 * pairs, 4, BLOCK, BLOCK), jnp.float32)],
        scratch_shapes=[pltpu.VMEM((length, length), jnp.bfloat16)],
        compiler_params=pltpu.CompilerParams(vmem_limit_bytes=VMEM_BYTES),
        cost_estimate=cost(17),
        name="attention_backward",
    )(qkv_rows, qkv_rows, qkv_rows, grads, probs)


def pieces_left(lefts, plans, many):
    part = lefts[0][0].shape[0] // THIRDS
    return jnp.concatenate(
        [
            jnp.concatenate([ref[pl.ds(third * part, part), :] for ref in lefts[group * many + k]], axis=1)
            for plan in plans
            for group, third in plan
            for k in range(many)
        ]
    )


def put_pieces(result, outs):
    place = 0
    for out in outs:
        many, pieces, part = out.shape[:3]
        for piece in range(pieces):
            for k in range(many):
                out[k, piece] = result[place : place + part]
                place += part


def weight_part_kernel(picks, *refs, count, plans, many):
    lefts, rights, outs = refs[: 2 * count], refs[2 * count : 2 * count + 2], refs[2 * count + 2 :]
    left = pieces_left(list(zip(lefts[:count], lefts[count:])), plans, many)
    right = jnp.concatenate([ref[...] for ref in rights], axis=0)
    put_pieces(dot_f32(left, right).astype(jnp.bfloat16), outs)


def weight_part_plain(picks, lefts, rights, rows, plans, many):
    left, right = jnp.concatenate(lefts, axis=1), jnp.concatenate(rights, axis=0)
    depth, width = right.shape
    part = rows // THIRDS
    result = jnp.take(left.reshape(-1, rows, depth), picks, axis=0)
    result = jnp.einsum("srd,dw->srw", result, right, preferred_element_type=jnp.float32).astype(jnp.bfloat16)
    result = result.reshape(-1, many, THIRDS, part, width)
    return [jnp.stack([result[group, :, third] for group, third in plan], axis=1) for plan in plans]


def weight_part(picks, lefts, rights, rows, plans, many, tile):
    depth, width = rights[0].shape
    count, part = picks.shape[0], rows // THIRDS
    if part % 16:
        return weight_part_plain(picks, lefts, rights, rows, plans, many)
    return pl.pallas_call(
        lambda *refs: weight_part_kernel(*refs, count=count, plans=plans, many=many),
        grid_spec=pltpu.PrefetchScalarGridSpec(
            num_scalar_prefetch=1,
            grid=(width // tile,),
            in_specs=[pl.BlockSpec((rows, depth), lambda i, picks, k=k: (picks[k], 0)) for k in range(count)] * 2
            + [pl.BlockSpec((depth, tile), lambda i, picks: (0, i))] * 2,
            out_specs=[pl.BlockSpec((many, len(plan), part, tile), lambda i, picks: (0, 0, 0, i)) for plan in plans],
        ),
        out_shape=[jax.ShapeDtypeStruct((many, len(plan), part, width), jnp.bfloat16) for plan in plans],
        compiler_params=pltpu.CompilerParams(vmem_limit_bytes=VMEM_BYTES),
        cost_estimate=cost(4),
        name="weight_part",
    )(picks, *([lefts[0]] * count), *([lefts[1]] * count), *rights)


def hot_columns(slots, first, count):
    rows = first + lax.broadcasted_iota(jnp.int32, (count, slots.shape[1]), 0)
    return (rows == slots).astype(jnp.bfloat16)


def halves(core, mine, other):
    return jnp.where(core == 0, mine, other), jnp.where(core == 0, other, mine)


def join_kernel(places, *refs):
    pieces, out = refs[:-1], refs[-1]
    rows = pieces[0].shape[1]
    count = pieces[0].shape[0]
    for chunk in range(out.shape[0] // count):
        for step in range(len(pieces) * count // out.shape[0]):
            piece = pieces[chunk * (len(pieces) * count // out.shape[0]) + step]
            start = pl.multiple_of(places[step] * rows, rows)
            out[pl.ds(chunk * count, count), pl.ds(start, rows), :] = piece[...]


def join(places, chunks):
    count, rows, columns = chunks[0][0].shape
    steps = len(chunks[0])
    return pl.pallas_call(
        join_kernel,
        in_specs=[pl.BlockSpec(memory_space=pltpu.SMEM)] + [pl.BlockSpec(memory_space=pltpu.VMEM)] * (steps * len(chunks)),
        out_shape=jax.ShapeDtypeStruct((count * len(chunks), steps * rows, columns), jnp.bfloat16),
        compiler_params=pltpu.CompilerParams(vmem_limit_bytes=VMEM_BYTES),
        cost_estimate=cost(3),
        name="join",
    )(places, *[piece for chunk in chunks for piece in chunk])


def project_kernel(core, rows, mine, other, result):
    half = mine.shape[1]
    first, second = halves(core[0], mine[...], other[...])
    result[:, :half] = dot_f32(rows[...], first).astype(jnp.bfloat16)
    result[:, half:] = dot_f32(rows[...], second).astype(jnp.bfloat16)


def project(core, rows, mine, other, used):
    width, half = mine.shape[1:]
    length = rows.shape[0]
    return pl.pallas_call(
        project_kernel,
        grid_spec=pltpu.PrefetchScalarGridSpec(
            num_scalar_prefetch=1,
            grid=(used,),
            in_specs=[
                whole((length, width)),
                pl.BlockSpec((None, width, half), lambda i, core: (i, 0, 0)),
                pl.BlockSpec((None, width, half), lambda i, core: (i, 0, 0)),
            ],
            out_specs=pl.BlockSpec((None, length, 2 * half), lambda i, core: (i, 0, 0)),
        ),
        out_shape=jax.ShapeDtypeStruct((used, length, 2 * half), jnp.bfloat16),
        compiler_params=pltpu.CompilerParams(vmem_limit_bytes=VMEM_BYTES),
        cost_estimate=cost(4),
        name="project",
    )(core, rows, mine, other)


def route_kernel(core, attended, tokens, mine, other, gain, router, routes, slots, middle, normed, gates, *outs):
    f32 = jnp.float32
    first, second = halves(core[0], mine[...], other[...])
    rows = attended[...]
    moved = jnp.concatenate([dot_f32(rows, first), dot_f32(rows, second)], axis=1)
    value = tokens[...].astype(f32) + moved
    middle[...] = value
    low = (value * lax.rsqrt(jnp.mean(value * value, axis=1, keepdims=True) + EPS) * gain[...]).astype(jnp.bfloat16)
    normed[...] = low
    start = 0
    for first_out, second_out in zip(outs[::2], outs[1::2]):
        size = first_out.shape[0]
        hot = hot_columns(slots[0:1, :], start, 2 * size) + hot_columns(slots[1:2, :], start, 2 * size)
        part = dot_f32(hot, low).astype(jnp.bfloat16)
        first_out[...] = part[:size]
        second_out[...] = part[size:]
        start += 2 * size
    logits = dot_f32(low, router[...])
    soft = jnp.exp(logits - jnp.max(logits, axis=1, keepdims=True))
    soft = soft / jnp.sum(soft, axis=1, keepdims=True)
    expert = lax.broadcasted_iota(jnp.int32, soft.shape, 1)
    chosen = [jnp.sum(jnp.where(expert == routes[:, k : k + 1], soft, 0.0), axis=1, keepdims=True) for k in range(2)]
    for k in range(2):
        gates[:, k : k + 1] = chosen[k] / (chosen[0] + chosen[1])


def route(core, attended, tokens, mine, other, gain, router, routes, slots, pieces, count):
    length, width = tokens.shape
    last, half = mine.shape[0] - 1, mine.shape[2]
    f32, bf16 = jnp.float32, jnp.bfloat16
    weight = pl.BlockSpec((None, width, half), lambda i, core: (last, 0, 0))
    shapes = [((length, width), f32), ((length, width), bf16), ((length, 2), f32)] + [((count, width), bf16)] * pieces
    return pl.pallas_call(
        route_kernel,
        grid_spec=pltpu.PrefetchScalarGridSpec(
            num_scalar_prefetch=1,
            grid=(1,),
            in_specs=[whole((length, width)), whole((length, width)), weight, weight, whole((1, width)), whole(router.shape), whole(routes.shape), whole(slots.shape)],
            out_specs=[whole(shape) for shape, _ in shapes],
        ),
        out_shape=[jax.ShapeDtypeStruct(shape, kind) for shape, kind in shapes],
        compiler_params=pltpu.CompilerParams(vmem_limit_bytes=VMEM_BYTES),
        cost_estimate=cost(6),
        name="route",
    )(core, attended, tokens, mine, other, gain.reshape(1, -1), router, routes, slots)


def hot_route(slots, k, count):
    cols = lax.broadcasted_iota(jnp.int32, (slots.shape[0], count), 1)
    return cols == slots[:, k : k + 1]


def combine_kernel(*refs, count):
    slots, slots_t, scale = refs[:3]
    pieces = refs[3 : 3 + count]
    middle, teacher, cotangent, valid, gates, routes = refs[3 + count : 9 + count]
    output, grad_y, grad_logits, square = refs[9 + count : 13 + count]
    sends, rows = refs[13 + count : 13 + 2 * count], refs[13 + 2 * count]
    f32, bf16 = jnp.float32, jnp.bfloat16
    assemble(rows, pieces)
    table = rows[...]
    picked = [dot_f32(hot_route(slots, k, rows.shape[0]).astype(bf16), table) for k in range(2)]
    result = middle[...] + (gates[:, 0:1] * picked[0] + gates[:, 1:2] * picked[1])
    output[...] = result.astype(bf16)
    misfit = valid[...] * (result - teacher[...].astype(f32))
    square[...] = jnp.sum((misfit * misfit).reshape(-1, 8, misfit.shape[1]), axis=0)
    grad = cotangent[...].astype(f32) + misfit * scale[0, 0]
    grad_y[...] = grad
    steep = [jnp.sum(grad * picked[k], axis=1, keepdims=True) for k in range(2)]
    slack = gates[:, 0:1] * steep[0] + gates[:, 1:2] * steep[1]
    expert = lax.broadcasted_iota(jnp.int32, grad_logits.shape, 1)
    turn = [jnp.where(expert == routes[:, k : k + 1], gates[:, k : k + 1] * (steep[k] - slack), 0.0) for k in range(2)]
    grad_logits[...] = (turn[0] + turn[1]).astype(bf16)
    scaled = [(gates[:, k : k + 1] * grad).astype(bf16) for k in range(2)]
    start = 0
    for first, second in zip(sends[::2], sends[1::2]):
        size = first.shape[0]
        part = [dot_f32(hot_columns(slots_t[k : k + 1, :], start, 2 * size), scaled[k]) for k in range(2)]
        part = (part[0] + part[1]).astype(bf16)
        first[...] = part[:size]
        second[...] = part[size:]
        start += 2 * size


def combine(slots, slots_t, scale, pieces, middle, teacher, cotangent, valid, gates, routes, experts):
    length, width = middle.shape
    count = len(pieces)
    f32, bf16 = jnp.float32, jnp.bfloat16
    return pl.pallas_call(
        lambda *refs: combine_kernel(*refs, count=count),
        in_specs=[pl.BlockSpec(memory_space=pltpu.VMEM)] * 2
        + [pl.BlockSpec(memory_space=pltpu.SMEM)]
        + [pl.BlockSpec(memory_space=pltpu.VMEM)] * (6 + count),
        out_shape=[
            jax.ShapeDtypeStruct((length, width), bf16),
            jax.ShapeDtypeStruct((length, width), f32),
            jax.ShapeDtypeStruct((length, experts), bf16),
            jax.ShapeDtypeStruct((8, width), f32),
        ]
        + [jax.ShapeDtypeStruct(piece.shape, bf16) for piece in pieces],
        scratch_shapes=[pltpu.VMEM((sum(piece.shape[0] for piece in pieces), width), bf16)],
        compiler_params=pltpu.CompilerParams(vmem_limit_bytes=VMEM_BYTES),
        cost_estimate=cost(8),
        name="combine",
    )(slots, slots_t, scale, *pieces, middle, teacher, cotangent, valid, gates, routes)


def norm_back(value, gain, grad):
    root = lax.rsqrt(jnp.mean(value * value, axis=1, keepdims=True) + EPS)
    normed = value * root
    scaled = grad * gain
    inner = jnp.mean(scaled * normed, axis=1, keepdims=True)
    return root * (scaled - normed * inner), jnp.sum((grad * normed).reshape(-1, 8, value.shape[1]), axis=0)


def collect_kernel(core, *refs, count):
    slots, pieces = refs[0], refs[1 : 1 + count]
    middle, gain, grad_logits, router, grad_y, mine, other = refs[1 + count : 8 + count]
    grad_middle, rounded, grad_attended, grad_gain, rows = refs[8 + count :]
    assemble(rows, pieces)
    hot = (hot_route(slots, 0, rows.shape[0]) | hot_route(slots, 1, rows.shape[0])).astype(jnp.bfloat16)
    grad = dot_f32(grad_logits[...], router[...], NT) + dot_f32(hot, rows[...])
    turned, grad_gain[...] = norm_back(middle[...], gain[...], grad)
    result = grad_y[...] + turned
    grad_middle[...] = result
    low = result.astype(jnp.bfloat16)
    rounded[...] = low
    first, second = halves(core[0], mine[...], other[...])
    half = first.shape[1]
    grad_attended[...] = (dot_f32(low[:, :half], first, NT) + dot_f32(low[:, half:], second, NT)).astype(jnp.bfloat16)


def collect(core, slots, pieces, middle, gain, grad_logits, router, grad_y, mine, other):
    length, width = middle.shape
    last, half = mine.shape[0] - 1, mine.shape[2]
    f32, bf16 = jnp.float32, jnp.bfloat16
    weight = pl.BlockSpec((None, width, half), lambda i, core: (last, 0, 0))
    plain = [slots, *pieces, middle, gain.reshape(1, -1), grad_logits, router, grad_y]
    shapes = [((length, width), f32), ((length, width), bf16), ((length, width), bf16), ((8, width), f32)]
    return pl.pallas_call(
        lambda *refs: collect_kernel(*refs, count=len(pieces)),
        grid_spec=pltpu.PrefetchScalarGridSpec(
            num_scalar_prefetch=1,
            grid=(1,),
            in_specs=[whole(array.shape) for array in plain] + [weight, weight],
            out_specs=[whole(shape) for shape, _ in shapes],
            scratch_shapes=[pltpu.VMEM((sum(piece.shape[0] for piece in pieces), width), bf16)],
        ),
        out_shape=[jax.ShapeDtypeStruct(shape, kind) for shape, kind in shapes],
        compiler_params=pltpu.CompilerParams(vmem_limit_bytes=VMEM_BYTES),
        cost_estimate=cost(8),
        name="collect",
    )(core, *plain, mine, other)


def outer_halves_kernel(core, normed, attended, rights, last, away, stay, normed_t, attended_t, *, count):
    step = pl.program_id(0)
    half = away.shape[1]

    def put(result):
        result = result.astype(jnp.bfloat16)

        @pl.when(core[0] == 0)
        def _():
            stay[...] = result[:, :half]
            away[...] = result[:, half:]

        @pl.when(core[0] != 0)
        def _():
            away[...] = result[:, :half]
            stay[...] = result[:, half:]

    @pl.when(step == 0)
    def _():
        normed_t[...] = normed[...].T
        attended_t[...] = attended[...].T

    @pl.when(step < count)
    def _():
        put(dot_f32(normed_t[...], rights[...]))

    @pl.when(step == count)
    def _():
        put(dot_f32(attended_t[...], last[...]))


def outer_halves(core, normed, attended, rights, last):
    length, width = normed.shape
    count, half = rights.shape[0], width // 2
    shape = jax.ShapeDtypeStruct((count + 1, width, half), jnp.bfloat16)
    return pl.pallas_call(
        lambda *refs: outer_halves_kernel(*refs, count=count),
        grid_spec=pltpu.PrefetchScalarGridSpec(
            num_scalar_prefetch=1,
            grid=(count + 1,),
            in_specs=[
                whole((length, width)),
                whole((length, width)),
                pl.BlockSpec((None, length, width), lambda i, core: (jnp.minimum(i, count - 1), 0, 0)),
                whole((length, width)),
            ],
            out_specs=[pl.BlockSpec((None, width, half), lambda i, core: (i, 0, 0))] * 2,
            scratch_shapes=[pltpu.VMEM((width, length), jnp.bfloat16)] * 2,
        ),
        out_shape=[shape, shape],
        compiler_params=pltpu.CompilerParams(vmem_limit_bytes=VMEM_BYTES),
        cost_estimate=cost(6),
        name="outer_halves",
    )(core, normed, attended, rights, last)


def enter_kernel(core, grads, mine, other, tokens, gain, grad_middle, grad_input, grad_gain, total):
    step = pl.program_id(0)
    first, second = halves(core[0], mine[...], other[...])
    half = first.shape[1]
    rows = grads[...]
    part = dot_f32(rows[:, :half], first, NT) + dot_f32(rows[:, half:], second, NT)

    @pl.when(step == 0)
    def _():
        total[...] = part

    @pl.when(step > 0)
    def _():
        total[...] += part

    @pl.when(step == pl.num_programs(0) - 1)
    def _():
        turned, grad_gain[...] = norm_back(tokens[...].astype(jnp.float32), gain[...], total[...])
        grad_input[...] = grad_middle[...] + turned


def enter(core, grads, mine, other, tokens, gain, grad_middle):
    length, width = tokens.shape
    count, half = grads.shape[0], mine.shape[2]
    weight = pl.BlockSpec((None, width, half), lambda i, core: (i, 0, 0))
    return pl.pallas_call(
        enter_kernel,
        grid_spec=pltpu.PrefetchScalarGridSpec(
            num_scalar_prefetch=1,
            grid=(count,),
            in_specs=[pl.BlockSpec((None, length, width), lambda i, core: (i, 0, 0)), weight, weight, whole((length, width)), whole((1, width)), whole((length, width))],
            out_specs=[whole((length, width)), whole((8, width))],
            scratch_shapes=[pltpu.VMEM((length, width), jnp.float32)],
        ),
        out_shape=[jax.ShapeDtypeStruct((length, width), jnp.float32), jax.ShapeDtypeStruct((8, width), jnp.float32)],
        compiler_params=pltpu.CompilerParams(vmem_limit_bytes=VMEM_BYTES),
        cost_estimate=cost(6),
        name="enter",
    )(core, grads, mine, other, tokens, gain.reshape(1, -1), grad_middle)


BOUNDS = (12, 16, 23, 32, 46, 64, 91)
TOP_PRECISION = lax.Precision.HIGHEST
AXES = ("dp", "expert")
PAIR = 2


def after(value, *others):
    return lax.optimization_barrier((value, *others))[0] if others else value


def bucket_index(offset):
    distance = jnp.abs(offset)
    far_bucket = 8 + sum([(distance >= level).astype(jnp.int32) for level in BOUNDS])
    near_bucket = jnp.where(distance < 8, distance, far_bucket)
    return jnp.where(offset > 0, 16, 0) + near_bucket


def norm_apply(inputs, gain_vec):
    return inputs * lax.rsqrt(jnp.mean(inputs * inputs, axis=-1, keepdims=True) + EPS) * gain_vec


def tile_offsets(query_block, key_block):
    rows = query_block * BLOCK + lax.broadcasted_iota(jnp.int32, (BLOCK, BLOCK), 0)
    cols = key_block * BLOCK + lax.broadcasted_iota(jnp.int32, (BLOCK, BLOCK), 1)
    return rows, cols


def offset_bias(table):
    offsets = jnp.arange(4 * BLOCK, dtype=jnp.int32) - 2 * BLOCK
    hot = (bucket_index(offsets)[None] == jnp.arange(table.shape[1], dtype=jnp.int32)[:, None]).astype(jnp.float32)
    return jnp.dot(table, hot, precision=TOP_PRECISION)


def table_gradient(bands, buckets):
    rows, cols = tile_offsets(0, 0)
    ids = [jnp.full((BLOCK, BLOCK), bucket_far(), jnp.int32)]
    ids += [bucket_index(shift * BLOCK + cols - rows) for shift in (-1, 0, 1)]
    hot = (jnp.stack(ids)[..., None] == jnp.arange(buckets, dtype=jnp.int32)).astype(jnp.float32)
    return jnp.einsum("hdxy,dxyb->hb", bands, hot, precision=TOP_PRECISION)


def bucket_far():
    return 8 + len(BOUNDS)


def on_device(
    tokens,
    qkv_weight,
    out_weight,
    position_bias_table,
    gain_attn,
    gain_moe,
    router,
    w_in,
    w_out,
    routes,
    prefix,
    valid_mask,
    teacher,
    cotangent,
):
    length, width = tokens.shape
    bf16, f32 = jnp.bfloat16, jnp.float32
    expert_count = router.shape[1]
    top_count = routes.shape[1]
    groups = lax.axis_size("expert")
    copies = lax.axis_size("dp")
    inner = w_in.shape[2]
    capacity = 5 * length * top_count // (4 * expert_count)
    total_tokens = length * copies * groups
    sources = 2 * groups
    blocks = length // BLOCK
    here_dp, here_group = lax.axis_index("dp"), lax.axis_index("expert")
    half = (here_dp >> 1) & 1
    core = here_group & 1
    rest = copies // 4

    def swap(value, dp_mask, group_mask):
        pairs = [
            (i, ((i // groups) ^ dp_mask) * groups + ((i % groups) ^ group_mask))
            for i in range(copies * groups)
        ]
        return lax.ppermute(value, AXES, pairs)

    def bits(count):
        return [1 << place for place in range(count.bit_length() - 1)]

    def partial_sums(value):
        sums = []
        for masks in [(0, mask) for mask in bits(groups)] + [(mask, 0) for mask in bits(copies)]:
            value = value + swap(value, *masks)
            sums.append(value)
        return sums

    chips = groups

    def across(value, place):
        return swap(value, PAIR * (place // (groups // 2)), 2 * (place % (groups // 2)))

    def to_chips(pieces):
        return [pieces[0]] + [across(pieces[place], place) for place in range(1, chips)]

    def through(visit, sends):
        direct, relay = to_chips(sends[::2]), to_chips(sends[1::2])
        seen, direct = visit(direct)
        direct = to_chips(direct)
        relay = [after(part, seen) for part in relay]
        passed = visit(swap(jnp.concatenate(relay), 0, 1))
        passed = swap(after(passed, *direct), 0, 1)
        relay = [passed[place * capacity : (place + 1) * capacity] for place in range(chips)]
        return direct, relay

    def weave(direct, relay):
        return [part for pair in zip(direct, to_chips(relay)) for part in pair]

    ring = list(range(0, copies, 2)) + list(range(copies - 1, 0, -2))
    turns = [(1, step) for step in range(1, copies // 2 + 1)] + [(-1, step) for step in range(1, copies // 2)]

    def gather_ring(shard, due):
        got = [shard]
        for turn in (1, -1):
            held = shard
            pairs = [(ring[i], ring[(i + turn) % copies]) for i in range(copies)]
            for step in [step for way, step in turns if way == turn]:
                held = lax.ppermute(after(held, *due[step - 2 : step - 1]) if step > 1 else held, "dp", pairs)
                got.append(held)
        return got

    def ring_places():
        place = jnp.where(here_dp & 1 == 0, here_dp >> 1, copies - 1 - (here_dp >> 1))
        shift = jnp.array([0] + [turn * step for turn, step in turns], jnp.int32)
        place = (place - shift) & (copies - 1)
        return jnp.where(place < copies // 2, 2 * place, 2 * (copies - 1 - place) + 1).astype(jnp.int32)

    columns = width // 2
    core_index = core.reshape(1).astype(jnp.int32)
    valid_rows = valid_mask.astype(f32)[:, None]
    counts = partial_sums(jnp.broadcast_to(jnp.sum(valid_rows), (8, 128)))
    valid_count = counts[-1][0, 0]
    shards = [
        lax.dynamic_slice_in_dim(part, core * columns, columns, 2)
        for part in (qkv_weight[:2], jnp.concatenate([qkv_weight[2:], out_weight[None]]))
    ]
    if copies > 8:
        mine = lax.all_gather(jnp.concatenate(shards), "dp", axis=1, tiled=True)
    else:
        mine = join(ring_places(), [gather_ring(shards[0], counts), gather_ring(shards[1], ())])
    other = swap(mine, 0, 1)
    offsets = offset_bias(position_bias_table)

    flat_routes = routes.reshape(-1)
    pair_count = length * top_count
    slot_count = sources * capacity
    route_hits = (flat_routes[:, None] == jnp.arange(expert_count, dtype=jnp.int32)[None, :]).astype(bf16)
    lower_ones = (
        lax.broadcasted_iota(jnp.int32, (pair_count, pair_count), 0)
        >= lax.broadcasted_iota(jnp.int32, (pair_count, pair_count), 1)
    ).astype(bf16)
    running = jnp.dot(lower_ones, route_hits, preferred_element_type=f32)
    pair_rank = jnp.sum((running - 1.0) * route_hits.astype(f32), axis=1).astype(jnp.int32)
    away = (flat_routes >> 1) ^ here_group
    chip = ((flat_routes & 1) ^ half) * (groups // 2) + (away >> 1)
    slots = ((chip * 2 + (away & 1)) * capacity + pair_rank).reshape(length, top_count)
    slots_t = slots.T

    resid = tokens.astype(f32)
    normed1 = norm_apply(resid, gain_attn).astype(bf16)
    qkv_rows = project(core_index, normed1, mine, other, 3)
    offsets = after(offsets, valid_count)
    attended, probs = attention_forward(position_bias_table[:, bucket_far()], prefix, qkv_rows, offsets)
    middle, normed2, gates, *sends = route(
        core_index, attended, tokens, mine, other, gain_moe, router, routes, slots_t, 2 * chips, capacity
    )

    pick = half.reshape(1).astype(jnp.int32)
    hidden, slopes, rows_in = [], [], []

    def expert(pieces):
        one = not isinstance(pieces, list)
        hidden_t, slope, rows_t, *results = expert_forward(pick, [pieces] if one else pieces, w_in, w_out)
        for kept, value in zip((hidden, slopes, rows_in), (hidden_t, slope, rows_t)):
            kept.append(value)
        return results[0] if one else (hidden_t, results)

    back = weave(*through(expert, sends))
    scale = (total_tokens / valid_count).reshape(1, 1)
    output, grad_y, grad_logits, squares, *sends = combine(
        slots, slots_t, scale, back, middle, teacher, cotangent, valid_rows, gates, routes, expert_count
    )
    grad_router = jnp.einsum("td,te->de", normed2, grad_logits, preferred_element_type=f32)

    out_rows = inner // copies
    in_rows = width // copies
    far_bit = here_dp % 2
    slices = jnp.arange(rest, dtype=jnp.int32) * 4

    def picks(bit0):
        return jnp.concatenate([slices + ((half ^ other_half) * 2 + bit0) for other_half in (1, 0)]).astype(jnp.int32)

    sent, kept = picks(1 - far_bit), picks(far_bit)
    every = jnp.concatenate([sent, kept])

    def add(left, right):
        return (left.astype(f32) + right.astype(f32)).astype(bf16)

    def fold(unit, bit, axis=0):
        unit = unit.reshape(unit.shape[:axis] + (2, unit.shape[axis] // 2) + unit.shape[axis + 1 :])
        away_part = lax.dynamic_index_in_dim(unit, 1 - bit, axis, keepdims=False)
        return away_part, lax.dynamic_index_in_dim(unit, bit, axis, keepdims=False)

    far_masks = list(reversed(bits(copies)[2:]))

    def near_add(got, keep):
        away_part, stay_part = fold(add(got, keep), (here_dp // far_masks[0]) % 2)
        return away_part, stay_part

    def far_trade(away_part):
        return swap(away_part, far_masks[0], 0)

    def finish(got, stay):
        unit = add(got, stay)
        for mask in far_masks[1:]:
            away_part, stay_part = fold(unit, (here_dp // mask) % 2)
            unit = add(swap(away_part, mask, 0), stay_part)
        return unit[0]

    plan_a, plan_b, plan_c = ((0, 0),), ((0, 1), (0, 2)), ((1, 0), (1, 1), (1, 2))
    plan_d, plan_e, plan_f = ((0, 0), (0, 1)), ((0, 2), (1, 0), (1, 1)), ((1, 2),)
    out_plans, in_plans = (plan_a, plan_b, plan_c), (plan_d, plan_e, plan_f)

    def keep(plan):
        return tuple((group + 2, third) for group, third in plan)

    grad_rows, grad_pre, parts = [], [], []

    def expert_back(pieces):
        if isinstance(pieces, list):
            grad_pre_rows, grads, *results = expert_backward(pick, pieces, w_in, w_out, slopes[0])
            grad_rows.append(grads)
            grad_pre.append(grad_pre_rows)
            return grad_pre_rows, results
        grad_rows.append(pieces)
        parts.extend(weight_part(sent, hidden, grad_rows, out_rows, out_plans, rest, width))
        parts[0] = swap(parts[0], 1, 0)
        pieces = after(pieces, parts[1])
        grad_pre_rows, _, results = expert_backward(pick, [pieces], w_in, w_out, slopes[1])
        grad_pre.append(grad_pre_rows)
        return after(results, parts[0])

    direct, relay = through(expert_back, sends)
    got_a, send_b, send_c = parts
    got_b = swap(after(send_b, relay[0]), 1, 0)
    back = weave(direct, relay)
    grad_rows, grad_pre = lax.optimization_barrier((grad_rows, grad_pre, relay))[:2]
    keep_a, keep_b, keep_c = weight_part(kept, hidden, grad_rows, out_rows, out_plans, rest, width)
    away_a, stay_a = near_add(got_a, keep_a)
    far_a = far_trade(away_a)
    send_d, send_e, send_f, keep_d, keep_e, keep_f = weight_part(
        every, rows_in, after(grad_pre, away_a), in_rows, in_plans + tuple(keep(plan) for plan in in_plans), rest, inner // 2
    )
    back = [after(part, send_d) for part in back]
    got_c = swap(after(send_c, *back), 1, 0)
    grad_middle, grad_attn_proj, grad_attended, gain_moe_parts = collect(
        core_index, slots, back, middle, gain_moe, grad_logits, router, grad_y, mine, other
    )
    away_b, stay_b = near_add(after(got_b, grad_attended), keep_b)
    grad_attended, away_b, far_a = lax.optimization_barrier((grad_attended, away_b, far_a))
    far_b = far_trade(away_b)
    done_a = finish(far_a, stay_a)
    grad_qkv_rows, bands = attention_backward(qkv_rows, grad_attended, probs)
    grad_qkv_rows, got_c = lax.optimization_barrier((grad_qkv_rows, got_c))

    away_c, stay_c = near_add(got_c, keep_c)
    far_c = far_trade(away_c)
    got_d = swap(after(send_d, away_c), 1, 0)
    weights_away, weights_stay = outer_halves(
        core_index, normed1, attended, after(grad_qkv_rows, far_b, away_c), grad_attn_proj
    )
    done_b = finish(far_b, stay_b)
    weights_got = jnp.stack([swap(weights_away[place], 0, 1) for place in range(4)])
    grad_input, gain_attn_parts = enter(core_index, grad_qkv_rows, mine, other, tokens, gain_attn, grad_middle)
    away_d, stay_d = near_add(got_d, keep_d)
    far_d = far_trade(away_d)
    weights_total = add(after(weights_got, gain_attn_parts, away_d), weights_stay)
    got_e = swap(after(send_e, away_d), 1, 0)
    got_f = swap(after(send_f, away_d), 1, 0)

    group_masks = bits(groups)[1:]
    dp_masks = sorted(bits(copies), key=lambda mask: (mask != PAIR, mask))
    total = weights_total.reshape(4, copies, in_rows, columns)
    for mask in group_masks:
        away_part, stay_part = fold(total, (here_group // mask) % 2, 2)
        total = add(swap(away_part, 0, mask), stay_part)
    away_e, stay_e = near_add(after(got_e, total), keep_e)
    far_e = far_trade(away_e)
    away_f, stay_f = near_add(after(got_f, away_e), keep_f)
    far_f = far_trade(away_f)
    done_c = finish(after(far_c, total), stay_c)
    out_theirs = swap(after(jnp.concatenate([done_a, done_b]), total), PAIR, 0)

    grad_table = table_gradient(after(bands, weights_total), position_bias_table.shape[1])
    small = [
        jnp.sum(gain_moe_parts, axis=0),
        jnp.sum(gain_attn_parts, axis=0),
        grad_router,
        grad_table,
        jnp.sum(squares),
    ]
    sizes = [value.size for value in small]
    flat = jnp.concatenate([value.reshape(-1) for value in small])
    flat = after(jnp.pad(flat, (0, -sum(sizes) % 1024)).reshape(-1, 128), total)

    total = total.reshape((4,) + (2,) * len(dp_masks) + total.shape[2:])
    left_bits = sorted(dp_masks, reverse=True)
    for mask in dp_masks:
        axis = 1 + left_bits.index(mask)
        left_bits.remove(mask)
        bit = (here_dp // mask) % 2
        away_part = lax.dynamic_index_in_dim(total, 1 - bit, axis, keepdims=False)
        stay_part = lax.dynamic_index_in_dim(total, bit, axis, keepdims=False)
        got = swap(away_part, mask, 0)
        if mask == PAIR:
            total = add(after(got, done_c, away_f), stay_part)
            done_d = finish(after(far_d, total), stay_d)
        else:
            total = add(got, stay_part)
        flat = flat + swap(flat, mask, 0)
        total, flat = lax.optimization_barrier((total, flat))
    done_e = finish(after(far_e, total), stay_e)
    done_f = finish(after(far_f, total), stay_f)
    for mask in reversed(group_masks):
        bit = (here_group // mask) % 2
        other_part = swap(total, 0, mask)
        total = jnp.concatenate([jnp.where(bit == 0, total, other_part), jnp.where(bit == 0, other_part, total)], axis=1)
        flat = flat + swap(flat, 0, mask)
        total, flat = lax.optimization_barrier((total, flat))
    other_part = swap(total, 0, 1)
    flat = flat + swap(flat, 0, 1)
    total = jnp.concatenate([jnp.where(core == 0, total, other_part), jnp.where(core == 0, other_part, total)], axis=2)
    weights_done = total.astype(f32)
    grad_qkv, grad_out_weight = weights_done[:3], weights_done[3]
    flat = flat.reshape(-1)
    starts = [sum(sizes[:place]) for place in range(len(sizes))]
    grad_gain_moe, grad_gain_attn, grad_router, grad_table, square_total = [
        flat[start : start + value.size].reshape(value.shape) for start, value in zip(starts, small)
    ]

    in_theirs = jnp.concatenate([swap(done_d, PAIR, 0), swap(done_e[:1], PAIR, 0)])
    out_mine, in_mine = done_c, jnp.concatenate([done_e[1:], done_f])

    def both_experts(mine, theirs):
        mine, theirs = [part.reshape(-1, part.shape[-1]).astype(f32) for part in (mine, theirs)]
        return jnp.stack([jnp.where(half == 0, mine, theirs), jnp.where(half == 0, theirs, mine)])

    grad_w_out = both_experts(out_mine, out_theirs)
    grad_w_in = both_experts(in_mine, in_theirs)

    distill_loss = square_total / (width * valid_count)
    return (
        output.astype(bf16),
        distill_loss,
        grad_input,
        grad_qkv,
        grad_out_weight,
        grad_w_in,
        grad_w_out,
        grad_router,
        grad_table,
        grad_gain_attn,
        grad_gain_moe,
    )


def solution(mesh):
    rows = P(AXES, None)
    return jax.shard_map(
        on_device,
        mesh=mesh,
        in_specs=(
            rows,
            P(None, "dp", None),
            P("dp", None),
            P(),
            P(),
            P(),
            P(),
            P("expert", None, None),
            P("expert", None, None),
            rows,
            P(AXES),
            P(AXES),
            rows,
            rows,
        ),
        out_specs=(
            rows,
            P(),
            rows,
            P(None, "dp", None),
            P("dp", None),
            P("expert", "dp", None),
            P("expert", "dp", None),
            P(),
            P(),
            P(),
            P(),
        ),
        check_vma=False,
    )
```

profile of v0, /device:TPU:0, one launch (start us, length us, event | category | flops | bytes accessed | tf_op | source)
XLA Modules:
  0.0 456.5 jit_solution(12026183362982928243)
XLA Ops:
  27.0 3.4 collective-permute-done.2
  40.5 3.3 join.1.mine.refs_15_
  61.8 6.1 %project.1.refs_2_.refs_3_.refs_4_.refs_0_.refs_1_ = bf16[3,512,768]{2,1,0:T(8,128)(2,1)} custom-call(s32[1]{0:T(128)} %bitcast.4.core.refs_0_, bf16[512,768]{1,0:T(8,128)(2,1)} %fusion.7.rows.refs_1_, bf16[4,768,384]{2,1,0:T(8,128)(2,1)} %join.1.mine.refs_15_, bf16[4,768,384]{2,1,0:T(8,128)(2,1)} %copy-done), custom_call_target="tpu_custom_call" | custom-call | flops 1480000000 | tf_op jit(solution)/shard_map/project/pallas_call | solution.py:405
  67.9 16.7 %attention_forward.1 = (bf16[512,768]{1,0:T(8,128)(2,1)}, bf16[12,512,512]{2,1,0:T(8,128)(2,1)}) custom-call(f32[12]{0:T(128)} %slice_reduce_fusion.refs_0_, s32[1]{0:T(128)S(6)} %copy.98.refs_1_, bf16[3,512,768]{2,1,0:T(8,128)(2,1)} %project.1.refs_2_.refs_3_.refs_4_.refs_0_.refs_1_, bf16[3,512,768]{2,1,0:T(8,128)(2,1)} %project.1.refs_2_.refs_3_.refs_4_.refs_0_.refs_1_, ...), custom_call_target="tpu_custom_call" | custom-call | flops 6289999872 | tf_op jit(solution)/shard_map/attention_forward/pallas_call | solution.py:214
  84.6 5.9 %route.1 = (f32[512,768]{1,0:T(8,128)}, bf16[512,768]{1,0:T(8,128)(2,1)}, f32[512,2]{1,0:T(8,128)}, bf16[160,768]{1,0:T(8,128)(2,1)}, bf16[160,768]{1,0:T(8,128)...) custom-call(s32[1]{0:T(128)} %bitcast.4.core.refs_0_, ...), custom_call_target="tpu_custom_call" | custom-call | flops 2220000000 | tf_op jit(solution)/shard_map/route/pallas_call | solution.py:456
  97.2 6.2 %collective-permute-done.20.refs_2_ = bf16[160,768]{1,0:T(8,128)(2,1)S(1)} collective-permute-done((bf16[160,768]{1,0:T(8,128)(2,1)}, bf16[160,768]{1,0:T(8,128)(2,1)S(1)}, u32[]{:S(2)}, u32[]{:S(2)}) %collective-permute-start.20) | collective-permute-done | bytes 245792 | tf_op jit(solution)/shard_map/ppermute | solution.py:758
  107.1 16.3 %expert_forward.2 = (bf16[3072,640]{1,0:T(8,128)(2,1)}, bf16[640,3072]{1,0:T(8,128)(2,1)}, bf16[768,640]{1,0:T(8,128)(2,1)}, bf16[160,768]{1,0:T(8,128)(2,1)}, b...) custom-call(s32[1]{0:T(128)} %bitcast.3.refs_0_, ...), custom_call_target="tpu_custom_call" | custom-call | flops 4809999872 | tf_op jit(solution)/shard_map/expert_forward/pallas_call | solution.py:78
  128.8 16.5 %expert_forward.3 = (bf16[3072,640]{1,0:T(8,128)(2,1)}, bf16[640,3072]{1,0:T(8,128)(2,1)}, bf16[768,640]{1,0:T(8,128)(2,1)}, bf16[640,768]{1,0:T(8,128)(2,1)}) custom-call(s32[1]{0:T(128)} %bitcast.3.refs_0_, bf16[640,768]{1,0:T(8,128)(2,1)} %copy-done.13, bf16[2,768,3072]{2,1,0:T(8,128)(2,1)} %refs_2_.3, bf16[2,3072,768]{2,1,0:T(8,128)(2,1)} %refs_3_.3), custom_call_target="tpu_custom_call" | custom-call | flops 4809999872 | tf_op jit(solution)/shard_map/expert_forward/pallas_call | solution.py:78
  154.1 4.7 %collective-permute-done.33.refs_10_ = bf16[160,768]{1,0:T(8,128)(2,1)S(1)} collective-permute-done((bf16[160,768]{1,0:T(8,128)(2,1)S(1)}, bf16[160,768]{1,0:T(8,128)(2,1)S(1)}, u32[]{:S(2)}, u32[]{:S(2)}) %collective-permute-start.33) | collective-permute-done | bytes 245792 | tf_op jit(solution)/shard_map/ppermute | solution.py:758
  158.8 4.6 %collective-permute-done.32.refs_8_ = bf16[160,768]{1,0:T(8,128)(2,1)S(1)} collective-permute-done((bf16[160,768]{1,0:T(8,128)(2,1)S(1)}, bf16[160,768]{1,0:T(8,128)(2,1)S(1)}, u32[]{:S(2)}, u32[]{:S(2)}) %collective-permute-start.32) | collective-permute-done | bytes 245792 | tf_op jit(solution)/shard_map/ppermute | solution.py:758
  164.2 8.5 %combine.1 = (bf16[512,768]{1,0:T(8,128)(2,1)}, f32[512,768]{1,0:T(8,128)}, bf16[512,8]{1,0:T(8,128)(2,1)}, f32[8,768]{1,0:T(8,128)}, bf16[160,768]{1,0:T(8,128)...) custom-call(s32[512,2]{1,0:T(8,128)} %multiply_add_fusion.refs_0_.re, ...), custom_call_target="tpu_custom_call" | custom-call | flops 2960000000 | tf_op jit(solution)/shard_map/combine/pallas_call | solution.py:512
  179.2 4.2 collective-permute-done.34.refs_2_
  185.2 3.4 collective-permute-done.36.refs_4_
  189.3 13.4 %expert_backward.2 = (bf16[640,3072]{1,0:T(8,128)(2,1)}, bf16[640,768]{1,0:T(8,128)(2,1)}, bf16[160,768]{1,0:T(8,128)(2,1)}, bf16[160,768]{1,0:T(8,128)(2,1)}, b...) custom-call(s32[1]{0:T(128)} %bitcast.3.refs_0_, bf16[160,768]{1,0:T(8,128)(2,1)} %get-tuple-element.169.refs_1_, ...), custom_call_target="tpu_custom_call" | custom-call | flops 4070000128 | tf_op jit(solution)/shard_map/expert_backward/pallas_call | solution.py:135
  206.4 7.9 %weight_part.3 = (bf16[2,1,128,768]{3,2,1,0:T(8,128)(2,1)}, bf16[2,2,128,768]{3,2,1,0:T(8,128)(2,1)}, bf16[2,3,128,768]{3,2,1,0:T(8,128)(2,1)}) custom-call(s32[4]{0:T(128)} %pad_add_fusion.2.refs_0_, bf16[3072,640]{1,0:T(8,128)(2,1)} %get-tuple-element.153.refs_1_.refs_2_.refs_3_.refs_4_, ...), custom_call_target="tpu_custom_call" | custom-call | flops 1480000000 | tf_op jit(solution)/shard_map/weight_part/pallas_call | solution.py:346
  220.4 13.6 %expert_backward.3 = (bf16[640,3072]{1,0:T(8,128)(2,1)}, bf16[640,768]{1,0:T(8,128)(2,1)}, bf16[640,768]{1,0:T(8,128)(2,1)}) custom-call(s32[1]{0:T(128)} %bitcast.3.refs_0_, bf16[640,768]{1,0:T(8,128)(2,1)} %copy-done.1, bf16[2,768,3072]{2,1,0:T(8,128)(2,1)} %refs_2_.3, bf16[2,3072,768]{2,1,0:T(8,128)(2,1)} %refs_3_.3, ...), custom_call_target="tpu_custom_call" | custom-call | flops 4070000128 | tf_op jit(solution)/shard_map/expert_backward/pallas_call | solution.py:135
  241.3 7.7 %weight_part.4 = (bf16[2,1,128,768]{3,2,1,0:T(8,128)(2,1)}, bf16[2,2,128,768]{3,2,1,0:T(8,128)(2,1)}, bf16[2,3,128,768]{3,2,1,0:T(8,128)(2,1)}) custom-call(s32[4]{0:T(128)} %pad_add_fusion.3.refs_0_, bf16[3072,640]{1,0:T(8,128)(2,1)} %get-tuple-element.153.refs_1_.refs_2_.refs_3_.refs_4_, ...), custom_call_target="tpu_custom_call" | custom-call | flops 1480000000 | tf_op jit(solution)/shard_map/weight_part/pallas_call | solution.py:346
  250.9 11.5 %weight_part.5 = (bf16[2,2,32,3072]{3,2,1,0:T(8,128)(2,1)}, bf16[2,3,32,3072]{3,2,1,0:T(8,128)(2,1)}, bf16[2,1,32,3072]{3,2,1,0:T(8,128)(2,1)}, bf16[2,2,32,3072...) custom-call(s32[8]{0:T(128)} %pad_add_fusion.1.refs_0_, ...), custom_call_target="tpu_custom_call" | custom-call | flops 1480000000 | tf_op jit(solution)/shard_map/weight_part/pallas_call | solution.py:346
  265.7 8.5 %collect.1 = (f32[512,768]{1,0:T(8,128)}, bf16[512,768]{1,0:T(8,128)(2,1)}, bf16[512,768]{1,0:T(8,128)(2,1)}, f32[8,768]{1,0:T(8,128)}) custom-call(s32[1]{0:T(128)} %bitcast.4.core.refs_0_, s32[512,2]{1,0:T(8,128)} %multiply_add_fusion.refs_0_.refs_1_, bf16[160,768]{1,0:T(8,128)(2,1)} %get-tuple-element.207.refs_2_, ...), custom_call_target="tpu_custom_call" | custom-call | flops 2960000000 | tf_op jit(solution)/shard_map/collect/pallas_call | solution.py:563
  277.2 17.3 %attention_backward.1 = (bf16[3,512,768]{2,1,0:T(8,128)(2,1)}, f32[12,4,128,128]{3,2,1,0:T(8,128)}) custom-call(bf16[3,512,768]{2,1,0:T(8,128)(2,1)} %project.1.refs_2_.refs_3_.refs_4_.refs_0_.refs_1_, bf16[3,512,768]{2,1,0:T(8,128)(2,1)} %project.1.refs_2_.refs_3_.refs_4_.refs_0_.refs_1_, ...), custom_call_target="tpu_custom_call" | custom-call | flops 6289999872 | tf_op jit(solution)/shard_map/attention_backward/pallas_call | solution.py:288
  295.7 7.9 %outer_halves.1 = (bf16[4,768,384]{2,1,0:T(8,128)(2,1)}, bf16[4,768,384]{2,1,0:T(8,128)(2,1)}) custom-call(s32[1]{0:T(128)} %bitcast.4.core.refs_0_, bf16[512,768]{1,0:T(8,128)(2,1)} %fusion.7.rows.refs_1_, bf16[512,768]{1,0:T(8,128)(2,1)} %get-tuple-element.146.attended.refs_2_, bf16[3,512,768]{2,1,0:T(8,128)(2,1)} %get-tuple-element.230.refs_3_.grads, ...), custom_call_target="tpu_custom_call" | custom-call | flops 2220000000 | tf_op jit(solution)/shard_map/outer_halves/pallas_call | solution.py:614
  303.6 3.1 slice_bitcast_fusion.3
  313.8 8.3 %enter.1 = (f32[512,768]{1,0:T(8,128)}, f32[8,768]{1,0:T(8,128)}) custom-call(s32[1]{0:T(128)} %bitcast.4.core.refs_0_, bf16[3,512,768]{2,1,0:T(8,128)(2,1)} %get-tuple-element.230.refs_3_.grads, bf16[4,768,384]{2,1,0:T(8,128)(2,1)} %join.1.mine.refs_15_, bf16[4,768,384]{2,1,0:T(8,128)(2,1)} %copy-done, bf16[512,768]{1,0:T(8,128)(2,1)} %tokens.3, ...), custom_call_target="tpu_custom_call" | custom-call | flops 2220000000 | tf_op jit(solution)/shard_map/enter/pallas_call | solution.py:660
  324.1 5.5 %collective-permute-done.57 = bf16[2,2,32,3072]{3,2,1,0:T(8,128)(2,1)S(1)} collective-permute-done((bf16[2,2,32,3072]{3,2,1,0:T(8,128)(2,1)}, bf16[2,2,32,3072]{3,2,1,0:T(8,128)(2,1)S(1)}, u32[]{:S(2)}, u32[]{:S(2)}) %collective-permute-start.57) | collective-permute-done | bytes 786464 | tf_op jit(solution)/shard_map/ppermute | solution.py:758
  342.1 7.1 %fusion.12 = f32[12,32]{1,0:T(8,128)S(1)} fusion(s32[4,128,128]{2,1,0:T(8,128)} %pad_add_fusion, f32[12,4,128,128]{3,2,1,0:T(8,128)} %get-tuple-element.251), kind=kOutput, calls=%fused_computation.34 | convolution fusion | flops 304087040 | bytes 3409408 | tf_op jit(solution)/shard_map/hdxy,dxyb->hb/dot_general | solution.py:714
  354.5 5.5 %collective-permute-done.58 = bf16[4,8,48,384]{3,2,1,0:T(8,128)(2,1)} collective-permute-done((bf16[4,8,48,384]{3,2,1,0:T(8,128)(2,1)}, bf16[4,8,48,384]{3,2,1,0:T(8,128)(2,1)}, u32[]{:S(2)}, u32[]{:S(2)}) %collective-permute-start.58) | collective-permute-done | bytes 1179680 | tf_op jit(solution)/shard_map/ppermute | solution.py:758
  361.6 10.7 %collective-permute-done.76 = bf16[1,3,128,768]{3,2,1,0:T(8,128)(2,1)} collective-permute-done((bf16[1,3,128,768]{3,2,1,0:T(8,128)(2,1)}, bf16[1,3,128,768]{3,2,1,0:T(8,128)(2,1)}, u32[]{:S(2)}, u32[]{:S(2)}) %collective-permute-start.76) | collective-permute-done | bytes 589856 | tf_op jit(solution)/shard_map/ppermute | solution.py:758
  380.4 13.5 %collective-permute-done.62 = f32[64,128]{1,0:T(8,128)S(1)} collective-permute-done((f32[64,128]{1,0:T(8,128)S(1)}, f32[64,128]{1,0:T(8,128)S(1)}, u32[]{:S(2)}, u32[]{:S(2)}) %collective-permute-start.62) | collective-permute-done | bytes 32800 | tf_op jit(solution)/shard_map/ppermute | solution.py:758
  394.1 16.7 %collective-permute-done.59 = bf16[4,2,2,48,384]{4,3,2,1,0:T(8,128)(2,1)S(1)} collective-permute-done((bf16[4,2,2,48,384]{4,3,2,1,0:T(8,128)(2,1)S(1)}, bf16[4,2,2,48,384]{4,3,2,1,0:T(8,128)(2,1)S(1)}, u32[]{:S(2)}, u32[]{:S(2)}) %collective-permute-start.59) | collective-permute-done | bytes 589856 | tf_op jit(solution)/shard_map/ppermute | solution.py:758
  414.3 9.1 %collective-permute-done.77 = bf16[3,128,768]{2,1,0:T(8,128)(2,1)S(1)} collective-permute-done((bf16[3,128,768]{2,1,0:T(8,128)(2,1)S(1)}, bf16[3,128,768]{2,1,0:T(8,128)(2,1)S(1)}, u32[]{:S(2)}, u32[]{:S(2)}) %collective-permute-start.77) | collective-permute-done | bytes 589856 | tf_op jit(solution)/shard_map/ppermute | solution.py:758
  428.4 5.2 %collective-permute-done.66 = f32[64,128]{1,0:T(8,128)S(1)} collective-permute-done((f32[64,128]{1,0:T(8,128)S(1)}, f32[64,128]{1,0:T(8,128)S(1)}, u32[]{:S(2)}, u32[]{:S(2)}) %collective-permute-start.66) | collective-permute-done | bytes 32800 | tf_op jit(solution)/shard_map/ppermute | solution.py:758
  442.6 3.2 collective-permute-start.75
  (409 shorter events, 175.0 us)
Async XLA Ops:
  43.8 16.6 %collective-permute-start.19 = (bf16[4,768,384]{2,1,0:T(8,128)(2,1)}, bf16[4,768,384]{2,1,0:T(8,128)(2,1)S(1)}, u32[]{:S(2)}, u32[]{:S(2)}) collective-permute-start(bf16[4,768,384]{2,1,0:T(8,128)(2,1)} %join.1.mine.refs_15_), channel_id=1, source_target_pairs={{0,1},{1,0},{2,3},{3,2},{4,5},{5,4},{6,7},{7,6},{8,9},{9,8},{10,11... | collective-permute-start | bytes 7077896 | tf_op jit(solution)/shard_map/ppermute | solution.py:758
  94.0 29.4 %collective-permute-start.23 = (bf16[160,768]{1,0:T(8,128)(2,1)}, bf16[160,768]{1,0:T(8,128)(2,1)S(1)}, u32[]{:S(2)}, u32[]{:S(2)}) collective-permute-start(bf16[160,768]{1,0:T(8,128)(2,1)} %get-tuple-element.155), channel_id=1, source_target_pairs={{0,2},{1,3},{2,0},{3,1},{4,6},{5,7},{6,4},{7,5},{8,10},{9,11},{10,... | collective-permute-start | bytes 737288 | tf_op jit(solution)/shard_map/ppermute | solution.py:758
  95.6 27.8 %collective-permute-start.24 = (bf16[160,768]{1,0:T(8,128)(2,1)}, bf16[160,768]{1,0:T(8,128)(2,1)S(1)}, u32[]{:S(2)}, u32[]{:S(2)}) collective-permute-start(bf16[160,768]{1,0:T(8,128)(2,1)} %get-tuple-element.157), channel_id=1, source_target_pairs={{0,8},{1,9},{2,10},{3,11},{4,12},{5,13},{6,14},{7,15},{8,0},{9,1},... | collective-permute-start | bytes 737288 | tf_op jit(solution)/shard_map/ppermute | solution.py:758
  103.5 20.0 %collective-permute-start.25 = (bf16[160,768]{1,0:T(8,128)(2,1)}, bf16[160,768]{1,0:T(8,128)(2,1)S(1)}, u32[]{:S(2)}, u32[]{:S(2)}) collective-permute-start(bf16[160,768]{1,0:T(8,128)(2,1)} %get-tuple-element.159), channel_id=1, source_target_pairs={{0,10},{1,11},{2,8},{3,9},{4,14},{5,15},{6,12},{7,13},{8,2},{9,3},... | collective-permute-start | bytes 737288 | tf_op jit(solution)/shard_map/ppermute | solution.py:758
  124.3 21.0 %collective-permute-start.27 = (bf16[160,768]{1,0:T(8,128)(2,1)S(1)}, bf16[160,768]{1,0:T(8,128)(2,1)S(1)}, u32[]{:S(2)}, u32[]{:S(2)}) collective-permute-start(bf16[160,768]{1,0:T(8,128)(2,1)S(1)} %copy-done.72), channel_id=1, source_target_pairs={{0,2},{1,3},{2,0},{3,1},{4,6},{5,7},{6,4},{7,5},{8,10},{9,11},{10,... | collective-permute-start | bytes 737288 | tf_op jit(solution)/shard_map/ppermute | solution.py:758
  125.9 19.5 %collective-permute-start.28 = (bf16[160,768]{1,0:T(8,128)(2,1)S(1)}, bf16[160,768]{1,0:T(8,128)(2,1)S(1)}, u32[]{:S(2)}, u32[]{:S(2)}) collective-permute-start(bf16[160,768]{1,0:T(8,128)(2,1)S(1)} %copy-done.71), channel_id=1, source_target_pairs={{0,8},{1,9},{2,10},{3,11},{4,12},{5,13},{6,14},{7,15},{8,0},{9,1},... | collective-permute-start | bytes 737288 | tf_op jit(solution)/shard_map/ppermute | solution.py:758
  127.5 17.9 %collective-permute-start.29 = (bf16[160,768]{1,0:T(8,128)(2,1)S(1)}, bf16[160,768]{1,0:T(8,128)(2,1)S(1)}, u32[]{:S(2)}, u32[]{:S(2)}) collective-permute-start(bf16[160,768]{1,0:T(8,128)(2,1)S(1)} %copy-done.70), channel_id=1, source_target_pairs={{0,10},{1,11},{2,8},{3,9},{4,14},{5,15},{6,12},{7,13},{8,2},{9,3},... | collective-permute-start | bytes 737288 | tf_op jit(solution)/shard_map/ppermute | solution.py:758
  176.2 26.5 %collective-permute-start.37 = (bf16[160,768]{1,0:T(8,128)(2,1)}, bf16[160,768]{1,0:T(8,128)(2,1)S(1)}, u32[]{:S(2)}, u32[]{:S(2)}) collective-permute-start(bf16[160,768]{1,0:T(8,128)(2,1)} %get-tuple-element.181), channel_id=1, source_target_pairs={{0,2},{1,3},{2,0},{3,1},{4,6},{5,7},{6,4},{7,5},{8,10},{9,11},{10,... | collective-permute-start | bytes 737288 | tf_op jit(solution)/shard_map/ppermute | solution.py:758
  177.6 25.2 %collective-permute-start.38 = (bf16[160,768]{1,0:T(8,128)(2,1)}, bf16[160,768]{1,0:T(8,128)(2,1)S(1)}, u32[]{:S(2)}, u32[]{:S(2)}) collective-permute-start(bf16[160,768]{1,0:T(8,128)(2,1)} %get-tuple-element.183), channel_id=1, source_target_pairs={{0,8},{1,9},{2,10},{3,11},{4,12},{5,13},{6,14},{7,15},{8,0},{9,1},... | collective-permute-start | bytes 737288 | tf_op jit(solution)/shard_map/ppermute | solution.py:758
  183.4 19.4 %collective-permute-start.39 = (bf16[160,768]{1,0:T(8,128)(2,1)}, bf16[160,768]{1,0:T(8,128)(2,1)S(1)}, u32[]{:S(2)}, u32[]{:S(2)}) collective-permute-start(bf16[160,768]{1,0:T(8,128)(2,1)} %get-tuple-element.185), channel_id=1, source_target_pairs={{0,10},{1,11},{2,8},{3,9},{4,14},{5,15},{6,12},{7,13},{8,2},{9,3},... | collective-permute-start | bytes 737288 | tf_op jit(solution)/shard_map/ppermute | solution.py:758
  214.3 19.7 %collective-permute-start.41 = (bf16[2,1,128,768]{3,2,1,0:T(8,128)(2,1)}, bf16[2,1,128,768]{3,2,1,0:T(8,128)(2,1)S(1)}, u32[]{:S(2)}, u32[]{:S(2)}) collective-permute-start(bf16[2,1,128,768]{3,2,1,0:T(8,128)(2,1)} %get-tuple-element.193), channel_id=1, source_target_pairs={{0,4},{1,5},{2,6},{3,7},{4,0},{5,1},{6,2},{7,3},{8,12},{9,13},{10,... | collective-permute-start | bytes 1179656 | tf_op jit(solution)/shard_map/ppermute | solution.py:758
  216.9 17.1 %collective-permute-start.42 = (bf16[160,768]{1,0:T(8,128)(2,1)S(1)}, bf16[160,768]{1,0:T(8,128)(2,1)S(1)}, u32[]{:S(2)}, u32[]{:S(2)}) collective-permute-start(bf16[160,768]{1,0:T(8,128)(2,1)S(1)} %copy-done.60), channel_id=1, source_target_pairs={{0,2},{1,3},{2,0},{3,1},{4,6},{5,7},{6,4},{7,5},{8,10},{9,11},{10,... | collective-permute-start | bytes 737288 | tf_op jit(solution)/shard_map/ppermute | solution.py:758
  218.2 15.8 %collective-permute-start.43 = (bf16[160,768]{1,0:T(8,128)(2,1)S(1)}, bf16[160,768]{1,0:T(8,128)(2,1)S(1)}, u32[]{:S(2)}, u32[]{:S(2)}) collective-permute-start(bf16[160,768]{1,0:T(8,128)(2,1)S(1)} %copy-done.59), channel_id=1, source_target_pairs={{0,8},{1,9},{2,10},{3,11},{4,12},{5,13},{6,14},{7,15},{8,0},{9,1},... | collective-permute-start | bytes 737288 | tf_op jit(solution)/shard_map/ppermute | solution.py:758
  237.7 26.0 %collective-permute-start.48 = (bf16[160,768]{1,0:T(8,128)(2,1)S(1)}, bf16[160,768]{1,0:T(8,128)(2,1)S(1)}, u32[]{:S(2)}, u32[]{:S(2)}) collective-permute-start(bf16[160,768]{1,0:T(8,128)(2,1)S(1)} %get-tuple-element.299), channel_id=1, source_target_pairs={{0,10},{1,11},{2,8},{3,9},{4,14},{5,15},{6,12},{7,13},{8,2},{9,3},... | collective-permute-start | bytes 737288 | tf_op jit(solution)/shard_map/ppermute | solution.py:758
  239.0 24.7 %collective-permute-start.47 = (bf16[160,768]{1,0:T(8,128)(2,1)S(1)}, bf16[160,768]{1,0:T(8,128)(2,1)S(1)}, u32[]{:S(2)}, u32[]{:S(2)}) collective-permute-start(bf16[160,768]{1,0:T(8,128)(2,1)S(1)} %get-tuple-element.300), channel_id=1, source_target_pairs={{0,8},{1,9},{2,10},{3,11},{4,12},{5,13},{6,14},{7,15},{8,0},{9,1},... | collective-permute-start | bytes 737288 | tf_op jit(solution)/shard_map/ppermute | solution.py:758
  240.5 23.2 %collective-permute-start.46 = (bf16[160,768]{1,0:T(8,128)(2,1)S(1)}, bf16[160,768]{1,0:T(8,128)(2,1)S(1)}, u32[]{:S(2)}, u32[]{:S(2)}) collective-permute-start(bf16[160,768]{1,0:T(8,128)(2,1)S(1)} %get-tuple-element.301), channel_id=1, source_target_pairs={{0,2},{1,3},{2,0},{3,1},{4,6},{5,7},{6,4},{7,5},{8,10},{9,11},{10,... | collective-permute-start | bytes 737288 | tf_op jit(solution)/shard_map/ppermute | solution.py:758
  241.2 33.0 %collective-permute-start.49 = (bf16[2,2,128,768]{3,2,1,0:T(8,128)(2,1)S(1)}, bf16[2,2,128,768]{3,2,1,0:T(8,128)(2,1)S(1)}, u32[]{:S(2)}, u32[]{:S(2)}) collective-permute-start(bf16[2,2,128,768]{3,2,1,0:T(8,128)(2,1)S(1)} %copy-done.57), channel_id=1, source_target_pairs={{0,4},{1,5},{2,6},{3,7},{4,0},{5,1},{6,2},{7,3},{8,12},{9,13},{10,... | collective-permute-start | bytes 2359304 | tf_op jit(solution)/shard_map/ppermute | solution.py:758
  263.7 30.8 %collective-permute-start.51 = (bf16[2,3,128,768]{3,2,1,0:T(8,128)(2,1)S(1)}, bf16[2,3,128,768]{3,2,1,0:T(8,128)(2,1)S(1)}, u32[]{:S(2)}, u32[]{:S(2)}) collective-permute-start(bf16[2,3,128,768]{3,2,1,0:T(8,128)(2,1)S(1)} %copy-done.56), channel_id=1, source_target_pairs={{0,4},{1,5},{2,6},{3,7},{4,0},{5,1},{6,2},{7,3},{8,12},{9,13},{10,... | collective-permute-start | bytes 3538952 | tf_op jit(solution)/shard_map/ppermute | solution.py:758
  275.4 20.3 %collective-permute-start.52 = (bf16[1,2,128,768]{3,2,1,0:T(8,128)(2,1)S(1)}, bf16[1,2,128,768]{3,2,1,0:T(8,128)(2,1)S(1)}, u32[]{:S(2)}, u32[]{:S(2)}) collective-permute-start(bf16[1,2,128,768]{3,2,1,0:T(8,128)(2,1)S(1)} %constant_dynamic-slice_fusion.4), channel_id=1, source_target_pairs={{0,16},{1,17},{2,18},{3,19},{4,20},{5,21},{6,22},{7,23},{8,24},{9,... | collective-permute-start | bytes 1179656 | tf_op jit(solution)/shard_map/ppermute | solution.py:758
  306.8 15.3 %collective-permute-start.56 = (bf16[768,384]{1,0:T(8,128)(2,1)}, bf16[768,384]{1,0:T(8,128)(2,1)}, u32[]{:S(2)}, u32[]{:S(2)}) collective-permute-start(bf16[768,384]{1,0:T(8,128)(2,1)} %get-tuple-element.292), channel_id=1, source_target_pairs={{0,1},{1,0},{2,3},{3,2},{4,5},{5,4},{6,7},{7,6},{8,9},{9,8},{10,11... | collective-permute-start | bytes 1769480 | tf_op jit(solution)/shard_map/ppermute | solution.py:758
  309.8 19.8 %collective-permute-start.57 = (bf16[2,2,32,3072]{3,2,1,0:T(8,128)(2,1)}, bf16[2,2,32,3072]{3,2,1,0:T(8,128)(2,1)S(1)}, u32[]{:S(2)}, u32[]{:S(2)}) collective-permute-start(bf16[2,2,32,3072]{3,2,1,0:T(8,128)(2,1)} %get-tuple-element.235), channel_id=1, source_target_pairs={{0,4},{1,5},{2,6},{3,7},{4,0},{5,1},{6,2},{7,3},{8,12},{9,13},{10,... | collective-permute-start | bytes 2359304 | tf_op jit(solution)/shard_map/ppermute | solution.py:758
  332.6 27.4 %collective-permute-start.58 = (bf16[4,8,48,384]{3,2,1,0:T(8,128)(2,1)}, bf16[4,8,48,384]{3,2,1,0:T(8,128)(2,1)}, u32[]{:S(2)}, u32[]{:S(2)}) collective-permute-start(bf16[4,8,48,384]{3,2,1,0:T(8,128)(2,1)} %dynamic-slice_bitcast_fusion), channel_id=1, source_target_pairs={{0,2},{1,3},{2,0},{3,1},{4,6},{5,7},{6,4},{7,5},{8,10},{9,11},{10,... | collective-permute-start | bytes 3538952 | tf_op jit(solution)/shard_map/ppermute | solution.py:758
  335.7 36.6 %collective-permute-start.76 = (bf16[1,3,128,768]{3,2,1,0:T(8,128)(2,1)}, bf16[1,3,128,768]{3,2,1,0:T(8,128)(2,1)}, u32[]{:S(2)}, u32[]{:S(2)}) collective-permute-start(bf16[1,3,128,768]{3,2,1,0:T(8,128)(2,1)} %constant_dynamic-slice_fusion.3), channel_id=1, source_target_pairs={{0,16},{1,17},{2,18},{3,19},{4,20},{5,21},{6,22},{7,23},{8,24},{9,... | collective-permute-start | bytes 1769480 | tf_op jit(solution)/shard_map/ppermute | solution.py:758
  337.0 37.5 %collective-permute-start.61 = (bf16[2,3,32,3072]{3,2,1,0:T(8,128)(2,1)}, bf16[2,3,32,3072]{3,2,1,0:T(8,128)(2,1)}, u32[]{:S(2)}, u32[]{:S(2)}) collective-permute-start(bf16[2,3,32,3072]{3,2,1,0:T(8,128)(2,1)} %get-tuple-element.242), channel_id=1, source_target_pairs={{0,4},{1,5},{2,6},{3,7},{4,0},{5,1},{6,2},{7,3},{8,12},{9,13},{10,... | collective-permute-start | bytes 3538952 | tf_op jit(solution)/shard_map/ppermute | solution.py:758
  340.4 70.6 %collective-permute-start.73 = (bf16[1,2,32,3072]{3,2,1,0:T(8,128)(2,1)}, bf16[1,2,32,3072]{3,2,1,0:T(8,128)(2,1)}, u32[]{:S(2)}, u32[]{:S(2)}) collective-permute-start(bf16[1,2,32,3072]{3,2,1,0:T(8,128)(2,1)} %constant_dynamic-slice_fusion.2), channel_id=1, source_target_pairs={{0,16},{1,17},{2,18},{3,19},{4,20},{5,21},{6,22},{7,23},{8,24},{9,... | collective-permute-start | bytes 1179656 | tf_op jit(solution)/shard_map/ppermute | solution.py:758
  349.3 27.0 %collective-permute-start.60 = (bf16[2,1,32,3072]{3,2,1,0:T(8,128)(2,1)}, bf16[2,1,32,3072]{3,2,1,0:T(8,128)(2,1)S(1)}, u32[]{:S(2)}, u32[]{:S(2)}) collective-permute-start(bf16[2,1,32,3072]{3,2,1,0:T(8,128)(2,1)} %get-tuple-element.240), channel_id=1, source_target_pairs={{0,4},{1,5},{2,6},{3,7},{4,0},{5,1},{6,2},{7,3},{8,12},{9,13},{10,... | collective-permute-start | bytes 1179656 | tf_op jit(solution)/shard_map/ppermute | solution.py:758
  372.3 21.7 %collective-permute-start.62 = (f32[64,128]{1,0:T(8,128)S(1)}, f32[64,128]{1,0:T(8,128)S(1)}, u32[]{:S(2)}, u32[]{:S(2)}) collective-permute-start(f32[64,128]{1,0:T(8,128)S(1)} %pad_bitcast_fusion), channel_id=1, source_target_pairs={{0,8},{1,9},{2,10},{3,11},{4,12},{5,13},{6,14},{7,15},{8,0},{9,1},... | collective-permute-start | bytes 98312 | tf_op jit(solution)/shard_map/ppermute | solution.py:758
  372.4 38.4 %collective-permute-start.59 = (bf16[4,2,2,48,384]{4,3,2,1,0:T(8,128)(2,1)S(1)}, bf16[4,2,2,48,384]{4,3,2,1,0:T(8,128)(2,1)S(1)}, u32[]{:S(2)}, u32[]{:S(2)}) collective-permute-start(bf16[4,2,2,48,384]{4,3,2,1,0:T(8,128)(2,1)S(1)} %dynamic-slice_bitcast_fusion.1), channel_id=1, source_target_pairs={{0,8},{1,9},{2,10},{3,11},{4,12},{5,13},{6,14},{7,15},{8,0},{9,1},... | collective-permute-start | bytes 1769480 | tf_op jit(solution)/shard_map/ppermute | solution.py:758
  374.4 48.9 %collective-permute-start.77 = (bf16[3,128,768]{2,1,0:T(8,128)(2,1)S(1)}, bf16[3,128,768]{2,1,0:T(8,128)(2,1)S(1)}, u32[]{:S(2)}, u32[]{:S(2)}) collective-permute-start(bf16[3,128,768]{2,1,0:T(8,128)(2,1)S(1)} %copy-done.19), channel_id=1, source_target_pairs={{0,8},{1,9},{2,10},{3,11},{4,12},{5,13},{6,14},{7,15},{8,0},{9,1},... | collective-permute-start | bytes 1769480 | tf_op jit(solution)/shard_map/ppermute | solution.py:758
  376.3 61.9 %collective-permute-start.71 = (bf16[1,3,32,3072]{3,2,1,0:T(8,128)(2,1)S(1)}, bf16[1,3,32,3072]{3,2,1,0:T(8,128)(2,1)S(1)}, u32[]{:S(2)}, u32[]{:S(2)}) collective-permute-start(bf16[1,3,32,3072]{3,2,1,0:T(8,128)(2,1)S(1)} %constant_dynamic-slice_fusion.1), channel_id=1, source_target_pairs={{0,16},{1,17},{2,18},{3,19},{4,20},{5,21},{6,22},{7,23},{8,24},{9,... | collective-permute-start | bytes 1769480 | tf_op jit(solution)/shard_map/ppermute | solution.py:758
  394.0 44.5 %collective-permute-start.72 = (bf16[1,1,32,3072]{3,2,1,0:T(8,128)(2,1)S(1)}, bf16[1,1,32,3072]{3,2,1,0:T(8,128)(2,1)S(1)}, u32[]{:S(2)}, u32[]{:S(2)}) collective-permute-start(bf16[1,1,32,3072]{3,2,1,0:T(8,128)(2,1)S(1)} %constant_dynamic-slice_fusion), channel_id=1, source_target_pairs={{0,16},{1,17},{2,18},{3,19},{4,20},{5,21},{6,22},{7,23},{8,24},{9,... | collective-permute-start | bytes 589832 | tf_op jit(solution)/shard_map/ppermute | solution.py:758
  423.4 26.2 %collective-permute-start.74 = (bf16[2,32,3072]{2,1,0:T(8,128)(2,1)S(1)}, bf16[2,32,3072]{2,1,0:T(8,128)(2,1)S(1)}, u32[]{:S(2)}, u32[]{:S(2)}) collective-permute-start(bf16[2,32,3072]{2,1,0:T(8,128)(2,1)S(1)} %fusion.16), channel_id=1, source_target_pairs={{0,8},{1,9},{2,10},{3,11},{4,12},{5,13},{6,14},{7,15},{8,0},{9,1},... | collective-permute-start | bytes 1179656 | tf_op jit(solution)/shard_map/ppermute | solution.py:758
  (122 other events, 1081.5 us)
where the time goes:
time: 461 us; the launch traced here: 456 us
  Pallas kernels  169 us (37%)
  waiting for transfers between devices  119 us (26%)
  starting transfers between devices  85.2 us (18%)
  local copies, waits for them, and re-layouts  40.8 us (9%)
  other arithmetic  28.4 us (6%)
  matrix products  8.14 us (2%)
  between operations  5.93 us (1%)
    ppermute x64, waiting for transfers between devices, swap(): return lax.ppermute(value, AXES, pairs)  110 us
    ppermute x64, starting transfers between devices, swap(): return lax.ppermute(value, AXES, pairs)  68 us
    pallas_call x2, Pallas kernels, expert_forward(): pl.pallas_call(lambda *refs: expert_forward_kernel(*refs, chunk=chunk, co...  32.8 us
    pallas_call x3, Pallas kernels, weight_part(): pl.pallas_call(lambda *refs: weight_part_kernel(*refs, count=count, plans...  27.1 us
    pallas_call x2, Pallas kernels, expert_backward(): pl.pallas_call(lambda *refs: expert_backward_kernel(*refs, chunk=chunk, c...  27 us
    pallas_call x1, Pallas kernels, attention_backward(): pl.pallas_call(lambda *refs: attention_backward_kernel(*refs, heads=64, b...  17.3 us
    ppermute x14, starting transfers between devices, gather_ring(): lax.ppermute(after(held, *due[step - 2:step - 1]) if step > 1 else held,...  17.2 us
    pallas_call x1, Pallas kernels, attention_forward(): pl.pallas_call(lambda *refs: attention_forward_kernel(*refs, heads=64, bl...  16.7 us
  transfers between devices with their start and end apart: 78, of which 27 were waited for; matrix products, arithmetic and copies ran while one was open for 12% of the time, Pallas kernels for 25%

commit v1 on v0

--- a/solution.py
+++ b/solution.py
@@ -71,7 +71,7 @@
         hand_out(total, outs)
 
 
-def expert_forward(pick, pieces, w_in, w_out, tile=512, chunk=128):
+def expert_forward(pick, pieces, w_in, w_out, tile=768, chunk=320):
     many, width = sum(piece.shape[0] for piece in pieces), pieces[0].shape[1]
     inner = w_in.shape[2]
     bf16 = jnp.bfloat16
@@ -128,7 +128,7 @@
         hand_out(total, outs)
 
 
-def expert_backward(pick, pieces, w_in, w_out, slope, tile=512, chunk=320):
+def expert_backward(pick, pieces, w_in, w_out, slope, tile=768, chunk=640):
     many, width = sum(piece.shape[0] for piece in pieces), pieces[0].shape[1]
     inner = w_in.shape[2]
     bf16 = jnp.bfloat16
@@ -576,41 +576,40 @@
     )(core, *plain, mine, other)
 
 
-def outer_halves_kernel(core, normed, attended, rights, last, away, stay, normed_t, attended_t, *, count):
+def outer_halves_kernel(core, normed, attended, rights, last, *refs, count):
+    aways, stays, normed_t, attended_t = refs[:2], refs[2:4], refs[4], refs[5]
     step = pl.program_id(0)
-    half = away.shape[1]
-
-    def put(result):
-        result = result.astype(jnp.bfloat16)
-
-        @pl.when(core[0] == 0)
-        def _():
-            stay[...] = result[:, :half]
-            away[...] = result[:, half:]
-
-        @pl.when(core[0] != 0)
-        def _():
-            away[...] = result[:, :half]
-            stay[...] = result[:, half:]
 
     @pl.when(step == 0)
     def _():
         normed_t[...] = normed[...].T
         attended_t[...] = attended[...].T
 
-    @pl.when(step < count)
-    def _():
-        put(dot_f32(normed_t[...], rights[...]))
-
-    @pl.when(step == count)
-    def _():
-        put(dot_f32(attended_t[...], last[...]))
+    for place in range(count + 1):
+
+        @pl.when(step == place)
+        def _():
+            result = dot_f32(normed_t[...], rights[...]) if place < count else dot_f32(attended_t[...], last[...])
+            result = result.astype(jnp.bfloat16)
+            half = result.shape[1] // 2
+            away, stay = aways[place // 2], stays[place // 2]
+            slot = place % 2
+
+            @pl.when(core[0] == 0)
+            def _():
+                stay[slot] = result[:, :half]
+                away[slot] = result[:, half:]
+
+            @pl.when(core[0] != 0)
+            def _():
+                away[slot] = result[:, :half]
+                stay[slot] = result[:, half:]
 
 
 def outer_halves(core, normed, attended, rights, last):
     length, width = normed.shape
     count, half = rights.shape[0], width // 2
-    shape = jax.ShapeDtypeStruct((count + 1, width, half), jnp.bfloat16)
+    shape = jax.ShapeDtypeStruct((2, width, half), jnp.bfloat16)
     return pl.pallas_call(
         lambda *refs: outer_halves_kernel(*refs, count=count),
         grid_spec=pltpu.PrefetchScalarGridSpec(
@@ -622,10 +621,10 @@
                 pl.BlockSpec((None, length, width), lambda i, core: (jnp.minimum(i, count - 1), 0, 0)),
                 whole((length, width)),
             ],
-            out_specs=[pl.BlockSpec((None, width, half), lambda i, core: (i, 0, 0))] * 2,
+            out_specs=[whole(shape.shape)] * 4,
             scratch_shapes=[pltpu.VMEM((width, length), jnp.bfloat16)] * 2,
         ),
-        out_shape=[shape, shape],
+        out_shape=[shape] * 4,
         compiler_params=pltpu.CompilerParams(vmem_limit_bytes=VMEM_BYTES),
         cost_estimate=cost(6),
         name="outer_halves",
@@ -807,21 +806,6 @@
         place = (place - shift) & (copies - 1)
         return jnp.where(place < copies // 2, 2 * place, 2 * (copies - 1 - place) + 1).astype(jnp.int32)
 
-    columns = width // 2
-    core_index = core.reshape(1).astype(jnp.int32)
-    valid_rows = valid_mask.astype(f32)[:, None]
-    counts = partial_sums(jnp.broadcast_to(jnp.sum(valid_rows), (8, 128)))
-    valid_count = counts[-1][0, 0]
-    shards = [
-        lax.dynamic_slice_in_dim(part, core * columns, columns, 2)
-        for part in (qkv_weight[:2], jnp.concatenate([qkv_weight[2:], out_weight[None]]))
-    ]
-    if copies > 8:
-        mine = lax.all_gather(jnp.concatenate(shards), "dp", axis=1, tiled=True)
-    else:
-        mine = join(ring_places(), [gather_ring(shards[0], counts), gather_ring(shards[1], ())])
-    other = swap(mine, 0, 1)
-    offsets = offset_bias(position_bias_table)
 
     flat_routes = routes.reshape(-1)
     pair_count = length * top_count
@@ -840,8 +824,22 @@
 
     resid = tokens.astype(f32)
     normed1 = norm_apply(resid, gain_attn).astype(bf16)
+    columns = width // 2
+    core_index = core.reshape(1).astype(jnp.int32)
+    valid_rows = valid_mask.astype(f32)[:, None]
+    counts = partial_sums(jnp.broadcast_to(jnp.sum(valid_rows), (8, 128)))
+    valid_count = counts[-1][0, 0]
+    shards = [
+        lax.dynamic_slice_in_dim(part, core * columns, columns, 2)
+        for part in (qkv_weight[:2], jnp.concatenate([qkv_weight[2:], out_weight[None]]))
+    ]
+    if copies > 8:
+        mine = lax.all_gather(jnp.concatenate(shards), "dp", axis=1, tiled=True)
+    else:
+        mine = join(ring_places(), [gather_ring(shards[0], counts[:3]), gather_ring(shards[1], (slots_t, normed1, counts[3]))])
+    other = swap(mine, 0, 1)
     qkv_rows = project(core_index, normed1, mine, other, 3)
-    offsets = after(offsets, valid_count)
+    offsets = after(offset_bias(position_bias_table), valid_count)
     attended, probs = attention_forward(position_bias_table[:, bucket_far()], prefix, qkv_rows, offsets)
     middle, normed2, gates, *sends = route(
         core_index, attended, tokens, mine, other, gain_moe, router, routes, slots_t, 2 * chips, capacity
@@ -873,7 +871,6 @@
         return jnp.concatenate([slices + ((half ^ other_half) * 2 + bit0) for other_half in (1, 0)]).astype(jnp.int32)
 
     sent, kept = picks(1 - far_bit), picks(far_bit)
-    every = jnp.concatenate([sent, kept])
 
     def add(left, right):
         return (left.astype(f32) + right.astype(f32)).astype(bf16)
@@ -902,9 +899,6 @@
     plan_a, plan_b, plan_c = ((0, 0),), ((0, 1), (0, 2)), ((1, 0), (1, 1), (1, 2))
     plan_d, plan_e, plan_f = ((0, 0), (0, 1)), ((0, 2), (1, 0), (1, 1)), ((1, 2),)
     out_plans, in_plans = (plan_a, plan_b, plan_c), (plan_d, plan_e, plan_f)
-
-    def keep(plan):
-        return tuple((group + 2, third) for group, third in plan)
 
     grad_rows, grad_pre, parts = [], [], []
 
@@ -930,9 +924,8 @@
     keep_a, keep_b, keep_c = weight_part(kept, hidden, grad_rows, out_rows, out_plans, rest, width)
     away_a, stay_a = near_add(got_a, keep_a)
     far_a = far_trade(away_a)
-    send_d, send_e, send_f, keep_d, keep_e, keep_f = weight_part(
-        every, rows_in, after(grad_pre, away_a), in_rows, in_plans + tuple(keep(plan) for plan in in_plans), rest, inner // 2
-    )
+    grad_pre = after(grad_pre, away_a)
+    send_d, send_e, send_f = weight_part(sent, rows_in, grad_pre, in_rows, in_plans, rest, inner // 2)
     back = [after(part, send_d) for part in back]
     got_c = swap(after(send_c, *back), 1, 0)
     grad_middle, grad_attn_proj, grad_attended, gain_moe_parts = collect(
@@ -948,32 +941,56 @@
     away_c, stay_c = near_add(got_c, keep_c)
     far_c = far_trade(away_c)
     got_d = swap(after(send_d, away_c), 1, 0)
-    weights_away, weights_stay = outer_halves(
+    *weights_away, stay_1, stay_2 = outer_halves(
         core_index, normed1, attended, after(grad_qkv_rows, far_b, away_c), grad_attn_proj
     )
     done_b = finish(far_b, stay_b)
-    weights_got = jnp.stack([swap(weights_away[place], 0, 1) for place in range(4)])
-    grad_input, gain_attn_parts = enter(core_index, grad_qkv_rows, mine, other, tokens, gain_attn, grad_middle)
-    away_d, stay_d = near_add(got_d, keep_d)
-    far_d = far_trade(away_d)
-    weights_total = add(after(weights_got, gain_attn_parts, away_d), weights_stay)
-    got_e = swap(after(send_e, away_d), 1, 0)
-    got_f = swap(after(send_f, away_d), 1, 0)
-
+    keep_d, keep_e, keep_f = weight_part(
+        kept, rows_in, after(grad_pre, *weights_away), in_rows, in_plans, rest, inner // 2
+    )
     group_masks = bits(groups)[1:]
     dp_masks = sorted(bits(copies), key=lambda mask: (mask != PAIR, mask))
-    total = weights_total.reshape(4, copies, in_rows, columns)
-    for mask in group_masks:
-        away_part, stay_part = fold(total, (here_group // mask) % 2, 2)
-        total = add(swap(away_part, 0, mask), stay_part)
-    away_e, stay_e = near_add(after(got_e, total), keep_e)
+
+    def over_groups(got, stay, *due):
+        got = add(after(got, *due), stay).reshape(2, copies, in_rows, columns)
+        for mask in group_masks[:-1]:
+            away_part, stay_part = fold(got, (here_group // mask) % 2, 2)
+            got = add(swap(away_part, 0, mask), stay_part)
+        away_part, stay_part = fold(got, (here_group // group_masks[-1]) % 2, 2)
+        return swap(away_part, 0, group_masks[-1]), stay_part
+
+    def over_dp(total, mask, passed):
+        axis = 1 + sorted([other for other in dp_masks if other not in passed], reverse=True).index(mask)
+        bit = (here_dp // mask) % 2
+        away_part = lax.dynamic_index_in_dim(total, 1 - bit, axis, keepdims=False)
+        stay_part = lax.dynamic_index_in_dim(total, bit, axis, keepdims=False)
+        return swap(away_part, mask, 0), stay_part
+
+    weights_got = [swap(part, 0, 1) for part in weights_away]
+    first = over_groups(weights_got[0], stay_1, keep_d)
+    second = over_groups(weights_got[1], stay_2, first[1])
+    grad_input, gain_attn_parts = enter(
+        core_index, after(grad_qkv_rows, second[1]), mine, other, tokens, gain_attn, grad_middle
+    )
+    away_d, stay_d = near_add(after(got_d, second[1]), keep_d)
+    far_d = far_trade(away_d)
+    got_e = swap(after(send_e, away_c), 1, 0)
+    done_c = finish(after(far_c, away_d), stay_c)
+    grad_table = table_gradient(after(bands, second[1]), position_bias_table.shape[1])
+
+    chains = [add(after(first[0], away_d, gain_attn_parts), first[1]).reshape((2,) + (2,) * len(dp_masks) + (-1, columns)), None]
+    trades = [over_dp(chains[0], dp_masks[0], ()), None]
+    away_e, stay_e = near_add(after(got_e, trades[0][1]), keep_e)
     far_e = far_trade(away_e)
-    away_f, stay_f = near_add(after(got_f, away_e), keep_f)
-    far_f = far_trade(away_f)
-    done_c = finish(after(far_c, total), stay_c)
+    got_f = swap(after(send_f, away_e), 1, 0)
+    chains[1] = add(after(second[0], done_c, grad_table, away_e), second[1]).reshape(chains[0].shape)
+    trades[1] = over_dp(chains[1], dp_masks[0], ())
+    trades[0] = (after(trades[0][0], trades[1][1]), trades[0][1])
+    total = trades[1][1]
     out_theirs = swap(after(jnp.concatenate([done_a, done_b]), total), PAIR, 0)
-
-    grad_table = table_gradient(after(bands, weights_total), position_bias_table.shape[1])
+    away_f, stay_f = near_add(after(got_f, total), keep_f)
+    trades[1] = (after(trades[1][0], away_f), trades[1][1])
+
     small = [
         jnp.sum(gain_moe_parts, axis=0),
         jnp.sum(gain_attn_parts, axis=0),
@@ -985,24 +1002,24 @@
     flat = jnp.concatenate([value.reshape(-1) for value in small])
     flat = after(jnp.pad(flat, (0, -sum(sizes) % 1024)).reshape(-1, 128), total)
 
-    total = total.reshape((4,) + (2,) * len(dp_masks) + total.shape[2:])
-    left_bits = sorted(dp_masks, reverse=True)
-    for mask in dp_masks:
-        axis = 1 + left_bits.index(mask)
-        left_bits.remove(mask)
-        bit = (here_dp // mask) % 2
-        away_part = lax.dynamic_index_in_dim(total, 1 - bit, axis, keepdims=False)
-        stay_part = lax.dynamic_index_in_dim(total, bit, axis, keepdims=False)
-        got = swap(away_part, mask, 0)
+    for place, mask in enumerate(dp_masks):
+        flat_got = swap(flat, mask, 0)
+        chains = [add(*trades[0]), None]
+        if place + 1 < len(dp_masks):
+            trades_next = [over_dp(chains[0], dp_masks[place + 1], dp_masks[: place + 1]), None]
+        chains[1] = add(after(trades[1][0], chains[0]), trades[1][1])
+        flat = flat + flat_got
+        if place + 1 < len(dp_masks):
+            trades_next[1] = over_dp(chains[1], dp_masks[place + 1], dp_masks[: place + 1])
+            trades = trades_next
         if mask == PAIR:
-            total = add(after(got, done_c, away_f), stay_part)
-            done_d = finish(after(far_d, total), stay_d)
-        else:
-            total = add(got, stay_part)
-        flat = flat + swap(flat, mask, 0)
-        total, flat = lax.optimization_barrier((total, flat))
+            done_d = finish(after(far_d, chains[1]), stay_d)
+            in_first = swap(done_d, PAIR, 0)
+        flat = after(flat, chains[1])
+    total = jnp.concatenate(chains)
+    far_f = far_trade(after(away_f, total))
     done_e = finish(after(far_e, total), stay_e)
-    done_f = finish(after(far_f, total), stay_f)
+    in_theirs = jnp.concatenate([in_first, swap(done_e[:1], PAIR, 0)])
     for mask in reversed(group_masks):
         bit = (here_group // mask) % 2
         other_part = swap(total, 0, mask)
@@ -1014,13 +1031,13 @@
     total = jnp.concatenate([jnp.where(core == 0, total, other_part), jnp.where(core == 0, other_part, total)], axis=2)
     weights_done = total.astype(f32)
     grad_qkv, grad_out_weight = weights_done[:3], weights_done[3]
+    done_f = finish(far_f, stay_f)
     flat = flat.reshape(-1)
     starts = [sum(sizes[:place]) for place in range(len(sizes))]
     grad_gain_moe, grad_gain_attn, grad_router, grad_table, square_total = [
         flat[start : start + value.size].reshape(value.shape) for start, value in zip(starts, small)
     ]
 
-    in_theirs = jnp.concatenate([swap(done_d, PAIR, 0), swap(done_e[:1], PAIR, 0)])
     out_mine, in_mine = done_c, jnp.concatenate([done_e[1:], done_f])
 
     def both_experts(mine, theirs):

time: 461 us -> 429 us (0.931)
  waiting for transfers between devices: 119 us -> 103 us
  local copies, waits for them, and re-layouts: 40.8 us -> 34.9 us
    ppermute x64 -> x66, waiting for transfers between devices: 110 us -> 94.8 us  [swap(): return lax.ppermute(value, AXES, pairs)]
    pallas_call x2, Pallas kernels: 32.8 us -> 27.7 us  [expert_forward(): pl.pallas_call(lambda *refs: expert_forward_kernel(*refs, chunk=chunk, co...]
    pallas_call x3 -> x4, Pallas kernels: 27.1 us -> 30.6 us  [weight_part(): pl.pallas_call(lambda *refs: weight_part_kernel(*refs, count=count, plans...]
    ppermute x64 -> x66, starting transfers between devices: 68 us -> 64.6 us  [swap(): return lax.ppermute(value, AXES, pairs)]
    unnamed x159 -> x147, local copies, waits for them, and re-layouts: 16.3 us -> 15.1 us
  transfers between devices with their start and end apart: 78 -> 80, of which waited for: 27 -> 29; matrix products, arithmetic and copies ran while one was open for 12% -> 13% of each run, Pallas kernels for 25% -> 26%
where the time goes in v1:
time: 429 us; the launch traced here: 425 us
  Pallas kernels  167 us (39%)
  waiting for transfers between devices  103 us (24%)
  starting transfers between devices  82.1 us (19%)
  local copies, waits for them, and re-layouts  34.9 us (8%)
  other arithmetic  24.5 us (6%)
  matrix products  7.41 us (2%)
  between operations  6.2 us (1%)
    ppermute x66, waiting for transfers between devices, swap(): return lax.ppermute(value, AXES, pairs)  94.8 us
    ppermute x66, starting transfers between devices, swap(): return lax.ppermute(value, AXES, pairs)  64.6 us
    pallas_call x4, Pallas kernels, weight_part(): pl.pallas_call(lambda *refs: weight_part_kernel(*refs, count=count, plans...  30.6 us
    pallas_call x2, Pallas kernels, expert_forward(): pl.pallas_call(lambda *refs: expert_forward_kernel(*refs, chunk=chunk, co...  27.7 us
    pallas_call x2, Pallas kernels, expert_backward(): pl.pallas_call(lambda *refs: expert_backward_kernel(*refs, chunk=chunk, c...  25.4 us
    ppermute x14, starting transfers between devices, gather_ring(): lax.ppermute(after(held, *due[step - 2:step - 1]) if step > 1 else held,...  17.5 us
    pallas_call x1, Pallas kernels, attention_backward(): pl.pallas_call(lambda *refs: attention_backward_kernel(*refs, heads=64, b...  17.3 us
    pallas_call x1, Pallas kernels, attention_forward(): pl.pallas_call(lambda *refs: attention_forward_kernel(*refs, heads=64, bl...  16.8 us
  transfers between devices with their start and end apart: 80, of which 29 were waited for; matrix products, arithmetic and copies ran while one was open for 13% of the time, Pallas kernels for 26%

profile of v1, /device:TPU:0, one launch (start us, length us, event | category | flops | bytes accessed | tf_op | source)
XLA Modules:
  0.0 424.5 jit_solution(936036983243256396)
XLA Ops:
  21.3 3.4 collective-permute-done.6.refs_2_
  28.4 4.7 %collective-permute-done.2 = f32[8,128]{1,0:T(8,128)S(1)} collective-permute-done((f32[8,128]{1,0:T(8,128)S(1)}, f32[8,128]{1,0:T(8,128)S(1)}, u32[]{:S(2)}, u32[]{:S(2)}) %collective-permute-start.2) | collective-permute-done | bytes 4128 | tf_op jit(solution)/shard_map/ppermute | solution.py:757
  33.1 3.6 collective-permute-done.3
  46.5 3.3 join.1.mine.refs_15_
  57.4 6.4 %project.1.refs_2_.refs_3_.refs_4_.refs_0_.refs_1_ = bf16[3,512,768]{2,1,0:T(8,128)(2,1)} custom-call(s32[1]{0:T(128)} %bitcast.4.core.refs_0_, bf16[512,768]{1,0:T(8,128)(2,1)} %fusion.6.rows.refs_1_, bf16[4,768,384]{2,1,0:T(8,128)(2,1)} %join.1.mine.refs_15_, bf16[4,768,384]{2,1,0:T(8,128)(2,1)} %copy-done), custom_call_target="tpu_custom_call" | custom-call | flops 1480000000 | tf_op jit(solution)/shard_map/project/pallas_call | solution.py:405
  63.8 16.8 %attention_forward.1 = (bf16[512,768]{1,0:T(8,128)(2,1)}, bf16[12,512,512]{2,1,0:T(8,128)(2,1)}) custom-call(f32[12]{0:T(128)} %slice_reduce_fusion.refs_0_, s32[1]{0:T(128)S(6)} %copy.114.refs_1_, bf16[3,512,768]{2,1,0:T(8,128)(2,1)} %project.1.refs_2_.refs_3_.refs_4_.refs_0_.refs_1_, bf16[3,512,768]{2,1,0:T(8,128)(2,1)} %project.1.refs_2_.refs_3_.refs_4_.refs_0_.refs_1_, ...), custom_call_target="tpu_custom_call" | custom-call | flops 6289999872 | tf_op jit(solution)/shard_map/attention_forward/pallas_call | solution.py:214
  80.6 5.9 %route.1 = (f32[512,768]{1,0:T(8,128)}, bf16[512,768]{1,0:T(8,128)(2,1)}, f32[512,2]{1,0:T(8,128)}, bf16[160,768]{1,0:T(8,128)(2,1)}, bf16[160,768]{1,0:T(8,128)...) custom-call(s32[1]{0:T(128)} %bitcast.4.core.refs_0_, ...), custom_call_target="tpu_custom_call" | custom-call | flops 2220000000 | tf_op jit(solution)/shard_map/route/pallas_call | solution.py:456
  91.3 4.8 %collective-permute-done.20.refs_2_ = bf16[160,768]{1,0:T(8,128)(2,1)S(1)} collective-permute-done((bf16[160,768]{1,0:T(8,128)(2,1)}, bf16[160,768]{1,0:T(8,128)(2,1)S(1)}, u32[]{:S(2)}, u32[]{:S(2)}) %collective-permute-start.20) | collective-permute-done | bytes 245792 | tf_op jit(solution)/shard_map/ppermute | solution.py:757
  96.8 5.6 %collective-permute-done.22.refs_4_ = bf16[160,768]{1,0:T(8,128)(2,1)S(1)} collective-permute-done((bf16[160,768]{1,0:T(8,128)(2,1)}, bf16[160,768]{1,0:T(8,128)(2,1)S(1)}, u32[]{:S(2)}, u32[]{:S(2)}) %collective-permute-start.22) | collective-permute-done | bytes 245792 | tf_op jit(solution)/shard_map/ppermute | solution.py:757
  103.0 13.8 %expert_forward.2 = (bf16[3072,640]{1,0:T(8,128)(2,1)}, bf16[640,3072]{1,0:T(8,128)(2,1)}, bf16[768,640]{1,0:T(8,128)(2,1)}, bf16[160,768]{1,0:T(8,128)(2,1)}, b...) custom-call(s32[1]{0:T(128)} %bitcast.3.refs_0_, ...), custom_call_target="tpu_custom_call" | custom-call | flops 4809999872 | tf_op jit(solution)/shard_map/expert_forward/pallas_call | solution.py:78
  122.3 13.9 %expert_forward.3 = (bf16[3072,640]{1,0:T(8,128)(2,1)}, bf16[640,3072]{1,0:T(8,128)(2,1)}, bf16[768,640]{1,0:T(8,128)(2,1)}, bf16[640,768]{1,0:T(8,128)(2,1)}) custom-call(s32[1]{0:T(128)} %bitcast.3.refs_0_, bf16[640,768]{1,0:T(8,128)(2,1)} %copy-done.10, bf16[2,768,3072]{2,1,0:T(8,128)(2,1)} %refs_2_.3, bf16[2,3072,768]{2,1,0:T(8,128)(2,1)} %refs_3_.3), custom_call_target="tpu_custom_call" | custom-call | flops 4809999872 | tf_op jit(solution)/shard_map/expert_forward/pallas_call | solution.py:78
  144.8 4.7 %collective-permute-done.33.refs_10_ = bf16[160,768]{1,0:T(8,128)(2,1)S(1)} collective-permute-done((bf16[160,768]{1,0:T(8,128)(2,1)S(1)}, bf16[160,768]{1,0:T(8,128)(2,1)S(1)}, u32[]{:S(2)}, u32[]{:S(2)}) %collective-permute-start.33) | collective-permute-done | bytes 245792 | tf_op jit(solution)/shard_map/ppermute | solution.py:757
  149.5 3.5 collective-permute-done.32.refs_8_
  154.6 8.5 %combine.1 = (bf16[512,768]{1,0:T(8,128)(2,1)}, f32[512,768]{1,0:T(8,128)}, bf16[512,8]{1,0:T(8,128)(2,1)}, f32[8,768]{1,0:T(8,128)}, bf16[160,768]{1,0:T(8,128)...) custom-call(s32[512,2]{1,0:T(8,128)} %copy-done.9, ...), custom_call_target="tpu_custom_call" | custom-call | flops 2960000000 | tf_op jit(solution)/shard_map/combine/pallas_call | solution.py:512
  168.1 5.1 %collective-permute-done.34.refs_2_ = bf16[160,768]{1,0:T(8,128)(2,1)S(1)} collective-permute-done((bf16[160,768]{1,0:T(8,128)(2,1)}, bf16[160,768]{1,0:T(8,128)(2,1)S(1)}, u32[]{:S(2)}, u32[]{:S(2)}) %collective-permute-start.34) | collective-permute-done | bytes 245792 | tf_op jit(solution)/shard_map/ppermute | solution.py:757
  174.7 4.4 %collective-permute-done.36.refs_4_ = bf16[160,768]{1,0:T(8,128)(2,1)S(1)} collective-permute-done((bf16[160,768]{1,0:T(8,128)(2,1)}, bf16[160,768]{1,0:T(8,128)(2,1)S(1)}, u32[]{:S(2)}, u32[]{:S(2)}) %collective-permute-start.36) | collective-permute-done | bytes 245792 | tf_op jit(solution)/shard_map/ppermute | solution.py:757
  179.7 12.5 %expert_backward.2 = (bf16[640,3072]{1,0:T(8,128)(2,1)}, bf16[640,768]{1,0:T(8,128)(2,1)}, bf16[160,768]{1,0:T(8,128)(2,1)}, bf16[160,768]{1,0:T(8,128)(2,1)}, b...) custom-call(s32[1]{0:T(128)} %bitcast.3.refs_0_, bf16[160,768]{1,0:T(8,128)(2,1)} %get-tuple-element.189.refs_1_, ...), custom_call_target="tpu_custom_call" | custom-call | flops 4070000128 | tf_op jit(solution)/shard_map/expert_backward/pallas_call | solution.py:135
  195.9 7.8 %weight_part.4 = (bf16[2,1,128,768]{3,2,1,0:T(8,128)(2,1)}, bf16[2,2,128,768]{3,2,1,0:T(8,128)(2,1)}, bf16[2,3,128,768]{3,2,1,0:T(8,128)(2,1)}) custom-call(s32[4]{0:T(128)} %pad_add_fusion.1.refs_0_, bf16[3072,640]{1,0:T(8,128)(2,1)} %get-tuple-element.173.refs_1_.refs_2_.refs_3_.refs_4_, ...), custom_call_target="tpu_custom_call" | custom-call | flops 1480000000 | tf_op jit(solution)/shard_map/weight_part/pallas_call | solution.py:346
  209.8 12.9 %expert_backward.3 = (bf16[640,3072]{1,0:T(8,128)(2,1)}, bf16[640,768]{1,0:T(8,128)(2,1)}, bf16[640,768]{1,0:T(8,128)(2,1)}) custom-call(s32[1]{0:T(128)} %bitcast.3.refs_0_, bf16[640,768]{1,0:T(8,128)(2,1)} %copy-done.1, bf16[2,768,3072]{2,1,0:T(8,128)(2,1)} %refs_2_.3, bf16[2,3072,768]{2,1,0:T(8,128)(2,1)} %refs_3_.3, ...), custom_call_target="tpu_custom_call" | custom-call | flops 4070000128 | tf_op jit(solution)/shard_map/expert_backward/pallas_call | solution.py:135
  229.9 7.7 %weight_part.5 = (bf16[2,1,128,768]{3,2,1,0:T(8,128)(2,1)}, bf16[2,2,128,768]{3,2,1,0:T(8,128)(2,1)}, bf16[2,3,128,768]{3,2,1,0:T(8,128)(2,1)}) custom-call(s32[4]{0:T(128)} %pad_add_fusion.2.refs_0_, bf16[3072,640]{1,0:T(8,128)(2,1)} %get-tuple-element.173.refs_1_.refs_2_.refs_3_.refs_4_, ...), custom_call_target="tpu_custom_call" | custom-call | flops 1480000000 | tf_op jit(solution)/shard_map/weight_part/pallas_call | solution.py:346
  239.9 7.7 %weight_part.6 = (bf16[2,2,32,3072]{3,2,1,0:T(8,128)(2,1)}, bf16[2,3,32,3072]{3,2,1,0:T(8,128)(2,1)}, bf16[2,1,32,3072]{3,2,1,0:T(8,128)(2,1)}) custom-call(s32[4]{0:T(128)} %pad_add_fusion.1.refs_0_, bf16[768,640]{1,0:T(8,128)(2,1)} %get-tuple-element.195.refs_1_.refs_2_.refs_3_.refs_4_, ...), custom_call_target="tpu_custom_call" | custom-call | flops 1480000000 | tf_op jit(solution)/shard_map/weight_part/pallas_call | solution.py:346
  249.7 8.5 %collect.1 = (f32[512,768]{1,0:T(8,128)}, bf16[512,768]{1,0:T(8,128)(2,1)}, bf16[512,768]{1,0:T(8,128)(2,1)}, f32[8,768]{1,0:T(8,128)}) custom-call(s32[1]{0:T(128)} %bitcast.4.core.refs_0_, s32[512,2]{1,0:T(8,128)} %copy-done.9, bf16[160,768]{1,0:T(8,128)(2,1)} %get-tuple-element.227.refs_2_, bf16[160,768]{1,0:T(8,128)(2,1)} %get-tuple-element.228.refs_3_, ...), custom_call_target="tpu_custom_call" | custom-call | flops 2960000000 | tf_op jit(solution)/shard_map/collect/pallas_call | solution.py:563
  260.4 17.3 %attention_backward.1 = (bf16[3,512,768]{2,1,0:T(8,128)(2,1)}, f32[12,4,128,128]{3,2,1,0:T(8,128)}) custom-call(bf16[3,512,768]{2,1,0:T(8,128)(2,1)} %project.1.refs_2_.refs_3_.refs_4_.refs_0_.refs_1_, bf16[3,512,768]{2,1,0:T(8,128)(2,1)} %project.1.refs_2_.refs_3_.refs_4_.refs_0_.refs_1_, ...), custom_call_target="tpu_custom_call" | custom-call | flops 6289999872 | tf_op jit(solution)/shard_map/attention_backward/pallas_call | solution.py:288
  278.9 8.2 %outer_halves.1 = (bf16[2,768,384]{2,1,0:T(8,128)(2,1)}, bf16[2,768,384]{2,1,0:T(8,128)(2,1)}, bf16[2,768,384]{2,1,0:T(8,128)(2,1)}, bf16[2,768,384]{2,1,0:T(8,128)(2,1)}) custom-call(s32[1]{0:T(128)} %bitcast.4.core.refs_0_, bf16[512,768]{1,0:T(8,128)(2,1)} %fusion.6.rows.refs_1_, bf16[512,768]{1,0:T(8,128)(2,1)} %get-tuple-element.166.attended.refs_2_, ...), custom_call_target="tpu_custom_call" | custom-call | flops 2220000000 | tf_op jit(solution)/shard_map/outer_halves/pallas_call | solution.py:613
  299.9 7.5 %weight_part.7 = (bf16[2,2,32,3072]{3,2,1,0:T(8,128)(2,1)}, bf16[2,3,32,3072]{3,2,1,0:T(8,128)(2,1)}, bf16[2,1,32,3072]{3,2,1,0:T(8,128)(2,1)}) custom-call(s32[4]{0:T(128)} %pad_add_fusion.2.refs_0_, bf16[768,640]{1,0:T(8,128)(2,1)} %get-tuple-element.195.refs_1_.refs_2_.refs_3_.refs_4_, ...), custom_call_target="tpu_custom_call" | custom-call | flops 1480000000 | tf_op jit(solution)/shard_map/weight_part/pallas_call | solution.py:346
  312.0 6.3 %collective-permute-done.55 = bf16[2,2,32,3072]{3,2,1,0:T(8,128)(2,1)S(1)} collective-permute-done((bf16[2,2,32,3072]{3,2,1,0:T(8,128)(2,1)S(1)}, bf16[2,2,32,3072]{3,2,1,0:T(8,128)(2,1)S(1)}, u32[]{:S(2)}, u32[]{:S(2)}) %collective-permute-start.55) | collective-permute-done | bytes 786464 | tf_op jit(solution)/shard_map/ppermute | solution.py:757
  320.4 5.3 %fusion.10 = f32[12,32]{1,0:T(8,128)S(1)} fusion(s32[4,128,128]{2,1,0:T(8,128)S(1)} %pad_add_fusion, f32[12,4,128,128]{3,2,1,0:T(8,128)S(1)} %copy-done.3), kind=kOutput, calls=%fused_computation.31 | convolution fusion | flops 304087040 | bytes 3409408 | tf_op jit(solution)/shard_map/hdxy,dxyb->hb/dot_general | solution.py:713
  325.7 8.3 %enter.1 = (f32[512,768]{1,0:T(8,128)}, f32[8,768]{1,0:T(8,128)}) custom-call(s32[1]{0:T(128)} %bitcast.4.core.refs_0_, bf16[3,512,768]{2,1,0:T(8,128)(2,1)} %get-tuple-element.263.refs_3_.grads, bf16[4,768,384]{2,1,0:T(8,128)(2,1)} %join.1.mine.refs_15_, bf16[4,768,384]{2,1,0:T(8,128)(2,1)} %copy-done, bf16[512,768]{1,0:T(8,128)(2,1)} %tokens.3, ...), custom_call_target="tpu_custom_call" | custom-call | flops 2220000000 | tf_op jit(solution)/shard_map/enter/pallas_call | solution.py:659
  354.2 5.5 %collective-permute-done.67 = f32[64,128]{1,0:T(8,128)S(1)} collective-permute-done((f32[64,128]{1,0:T(8,128)S(1)}, f32[64,128]{1,0:T(8,128)S(1)}, u32[]{:S(2)}, u32[]{:S(2)}) %collective-permute-start.67) | collective-permute-done | bytes 32800 | tf_op jit(solution)/shard_map/ppermute | solution.py:757
  362.9 18.8 %collective-permute-done.62 = bf16[2,2,2,48,384]{4,3,0,1,2:T(8,128)(2,1)S(1)} collective-permute-done((bf16[2,2,2,48,384]{4,3,0,1,2:T(8,128)(2,1)S(1)}, bf16[2,2,2,48,384]{4,3,0,1,2:T(8,128)(2,1)S(1)}, u32[]{:S(2)}, u32[]{:S(2)}) %collective-permute-start.62) | collective-permute-done | bytes 294944 | tf_op jit(solution)/shard_map/ppermute | solution.py:757
  391.7 3.9 collective-permute-done.69
  412.9 6.4 %collective-permute-done.74 = bf16[1,1,32,3072]{3,2,1,0:T(8,128)(2,1)S(1)} collective-permute-done((bf16[1,1,32,3072]{3,2,1,0:T(8,128)(2,1)S(1)}, bf16[1,1,32,3072]{3,2,1,0:T(8,128)(2,1)S(1)}, u32[]{:S(2)}, u32[]{:S(2)}) %collective-permute-start.74) | collective-permute-done | bytes 196640 | tf_op jit(solution)/shard_map/ppermute | solution.py:757
  (410 shorter events, 165.4 us)
Async XLA Ops:
  2.6 17.4 %collective-permute-start.16 = (bf16[2,96,384]{2,1,0:T(8,128)(2,1)S(1)}, bf16[2,96,384]{2,1,0:T(8,128)(2,1)S(1)}, u32[]{:S(2)}, u32[]{:S(2)}) collective-permute-start(bf16[2,96,384]{2,1,0:T(8,128)(2,1)S(1)} %fusion.19.refs_8_), channel_id=1, source_target_pairs={{0,4},{8,0},{16,8},{24,16},{28,24},{20,28},{12,20},{4,12},{1,5},{9... | collective-permute-start | bytes 442376 | tf_op jit(solution)/shard_map/ppermute | solution.py:799
  19.5 17.3 %collective-permute-start.10 = (bf16[2,96,384]{2,1,0:T(8,128)(2,1)S(1)}, bf16[2,96,384]{2,1,0:T(8,128)(2,1)S(1)}, u32[]{:S(2)}, u32[]{:S(2)}) collective-permute-start(bf16[2,96,384]{2,1,0:T(8,128)(2,1)S(1)} %collective-permute-done.9.refs_5_), channel_id=1, source_target_pairs={{0,4},{8,0},{16,8},{24,16},{28,24},{20,28},{12,20},{4,12},{1,5},{9... | collective-permute-start | bytes 442376 | tf_op jit(solution)/shard_map/ppermute | solution.py:799
  20.0 16.9 %collective-permute-start.17 = (bf16[2,96,384]{2,1,0:T(8,128)(2,1)S(1)}, bf16[2,96,384]{2,1,0:T(8,128)(2,1)S(1)}, u32[]{:S(2)}, u32[]{:S(2)}) collective-permute-start(bf16[2,96,384]{2,1,0:T(8,128)(2,1)S(1)} %collective-permute-done.16.refs_13_), channel_id=1, source_target_pairs={{0,4},{8,0},{16,8},{24,16},{28,24},{20,28},{12,20},{4,12},{1,5},{9... | collective-permute-start | bytes 442376 | tf_op jit(solution)/shard_map/ppermute | solution.py:799
  90.0 26.9 %collective-permute-start.23 = (bf16[160,768]{1,0:T(8,128)(2,1)}, bf16[160,768]{1,0:T(8,128)(2,1)S(1)}, u32[]{:S(2)}, u32[]{:S(2)}) collective-permute-start(bf16[160,768]{1,0:T(8,128)(2,1)} %get-tuple-element.175), channel_id=1, source_target_pairs={{0,2},{1,3},{2,0},{3,1},{4,6},{5,7},{6,4},{7,5},{8,10},{9,11},{10,... | collective-permute-start | bytes 737288 | tf_op jit(solution)/shard_map/ppermute | solution.py:757
  90.5 26.4 %collective-permute-start.24 = (bf16[160,768]{1,0:T(8,128)(2,1)}, bf16[160,768]{1,0:T(8,128)(2,1)S(1)}, u32[]{:S(2)}, u32[]{:S(2)}) collective-permute-start(bf16[160,768]{1,0:T(8,128)(2,1)} %get-tuple-element.177), channel_id=1, source_target_pairs={{0,8},{1,9},{2,10},{3,11},{4,12},{5,13},{6,14},{7,15},{8,0},{9,1},... | collective-permute-start | bytes 737288 | tf_op jit(solution)/shard_map/ppermute | solution.py:757
  96.1 20.8 %collective-permute-start.25 = (bf16[160,768]{1,0:T(8,128)(2,1)}, bf16[160,768]{1,0:T(8,128)(2,1)S(1)}, u32[]{:S(2)}, u32[]{:S(2)}) collective-permute-start(bf16[160,768]{1,0:T(8,128)(2,1)} %get-tuple-element.179), channel_id=1, source_target_pairs={{0,10},{1,11},{2,8},{3,9},{4,14},{5,15},{6,12},{7,13},{8,2},{9,3},... | collective-permute-start | bytes 737288 | tf_op jit(solution)/shard_map/ppermute | solution.py:757
  117.8 18.3 %collective-permute-start.27 = (bf16[160,768]{1,0:T(8,128)(2,1)S(1)}, bf16[160,768]{1,0:T(8,128)(2,1)S(1)}, u32[]{:S(2)}, u32[]{:S(2)}) collective-permute-start(bf16[160,768]{1,0:T(8,128)(2,1)S(1)} %copy-done.65), channel_id=1, source_target_pairs={{0,2},{1,3},{2,0},{3,1},{4,6},{5,7},{6,4},{7,5},{8,10},{9,11},{10,... | collective-permute-start | bytes 737288 | tf_op jit(solution)/shard_map/ppermute | solution.py:757
  118.3 17.9 %collective-permute-start.28 = (bf16[160,768]{1,0:T(8,128)(2,1)S(1)}, bf16[160,768]{1,0:T(8,128)(2,1)S(1)}, u32[]{:S(2)}, u32[]{:S(2)}) collective-permute-start(bf16[160,768]{1,0:T(8,128)(2,1)S(1)} %copy-done.64), channel_id=1, source_target_pairs={{0,8},{1,9},{2,10},{3,11},{4,12},{5,13},{6,14},{7,15},{8,0},{9,1},... | collective-permute-start | bytes 737288 | tf_op jit(solution)/shard_map/ppermute | solution.py:757
  119.1 17.1 %collective-permute-start.29 = (bf16[160,768]{1,0:T(8,128)(2,1)S(1)}, bf16[160,768]{1,0:T(8,128)(2,1)S(1)}, u32[]{:S(2)}, u32[]{:S(2)}) collective-permute-start(bf16[160,768]{1,0:T(8,128)(2,1)S(1)} %copy-done.63), channel_id=1, source_target_pairs={{0,10},{1,11},{2,8},{3,9},{4,14},{5,15},{6,12},{7,13},{8,2},{9,3},... | collective-permute-start | bytes 737288 | tf_op jit(solution)/shard_map/ppermute | solution.py:757
  166.7 25.6 %collective-permute-start.37 = (bf16[160,768]{1,0:T(8,128)(2,1)}, bf16[160,768]{1,0:T(8,128)(2,1)S(1)}, u32[]{:S(2)}, u32[]{:S(2)}) collective-permute-start(bf16[160,768]{1,0:T(8,128)(2,1)} %get-tuple-element.201), channel_id=1, source_target_pairs={{0,2},{1,3},{2,0},{3,1},{4,6},{5,7},{6,4},{7,5},{8,10},{9,11},{10,... | collective-permute-start | bytes 737288 | tf_op jit(solution)/shard_map/ppermute | solution.py:757
  167.4 24.8 %collective-permute-start.38 = (bf16[160,768]{1,0:T(8,128)(2,1)}, bf16[160,768]{1,0:T(8,128)(2,1)S(1)}, u32[]{:S(2)}, u32[]{:S(2)}) collective-permute-start(bf16[160,768]{1,0:T(8,128)(2,1)} %get-tuple-element.203), channel_id=1, source_target_pairs={{0,8},{1,9},{2,10},{3,11},{4,12},{5,13},{6,14},{7,15},{8,0},{9,1},... | collective-permute-start | bytes 737288 | tf_op jit(solution)/shard_map/ppermute | solution.py:757
  173.3 19.0 %collective-permute-start.39 = (bf16[160,768]{1,0:T(8,128)(2,1)}, bf16[160,768]{1,0:T(8,128)(2,1)S(1)}, u32[]{:S(2)}, u32[]{:S(2)}) collective-permute-start(bf16[160,768]{1,0:T(8,128)(2,1)} %get-tuple-element.205), channel_id=1, source_target_pairs={{0,10},{1,11},{2,8},{3,9},{4,14},{5,15},{6,12},{7,13},{8,2},{9,3},... | collective-permute-start | bytes 737288 | tf_op jit(solution)/shard_map/ppermute | solution.py:757
  203.7 19.0 %collective-permute-start.41 = (bf16[2,1,128,768]{3,2,1,0:T(8,128)(2,1)}, bf16[2,1,128,768]{3,2,1,0:T(8,128)(2,1)S(1)}, u32[]{:S(2)}, u32[]{:S(2)}) collective-permute-start(bf16[2,1,128,768]{3,2,1,0:T(8,128)(2,1)} %get-tuple-element.213), channel_id=1, source_target_pairs={{0,4},{1,5},{2,6},{3,7},{4,0},{5,1},{6,2},{7,3},{8,12},{9,13},{10,... | collective-permute-start | bytes 1179656 | tf_op jit(solution)/shard_map/ppermute | solution.py:757
  206.3 16.4 %collective-permute-start.42 = (bf16[160,768]{1,0:T(8,128)(2,1)S(1)}, bf16[160,768]{1,0:T(8,128)(2,1)S(1)}, u32[]{:S(2)}, u32[]{:S(2)}) collective-permute-start(bf16[160,768]{1,0:T(8,128)(2,1)S(1)} %copy-done.56), channel_id=1, source_target_pairs={{0,2},{1,3},{2,0},{3,1},{4,6},{5,7},{6,4},{7,5},{8,10},{9,11},{10,... | collective-permute-start | bytes 737288 | tf_op jit(solution)/shard_map/ppermute | solution.py:757
  226.4 21.2 %collective-permute-start.48 = (bf16[160,768]{1,0:T(8,128)(2,1)S(1)}, bf16[160,768]{1,0:T(8,128)(2,1)S(1)}, u32[]{:S(2)}, u32[]{:S(2)}) collective-permute-start(bf16[160,768]{1,0:T(8,128)(2,1)S(1)} %get-tuple-element.340), channel_id=1, source_target_pairs={{0,10},{1,11},{2,8},{3,9},{4,14},{5,15},{6,12},{7,13},{8,2},{9,3},... | collective-permute-start | bytes 737288 | tf_op jit(solution)/shard_map/ppermute | solution.py:757
  227.8 19.9 %collective-permute-start.47 = (bf16[160,768]{1,0:T(8,128)(2,1)S(1)}, bf16[160,768]{1,0:T(8,128)(2,1)S(1)}, u32[]{:S(2)}, u32[]{:S(2)}) collective-permute-start(bf16[160,768]{1,0:T(8,128)(2,1)S(1)} %get-tuple-element.341), channel_id=1, source_target_pairs={{0,8},{1,9},{2,10},{3,11},{4,12},{5,13},{6,14},{7,15},{8,0},{9,1},... | collective-permute-start | bytes 737288 | tf_op jit(solution)/shard_map/ppermute | solution.py:757
  228.6 19.1 %collective-permute-start.46 = (bf16[160,768]{1,0:T(8,128)(2,1)S(1)}, bf16[160,768]{1,0:T(8,128)(2,1)S(1)}, u32[]{:S(2)}, u32[]{:S(2)}) collective-permute-start(bf16[160,768]{1,0:T(8,128)(2,1)S(1)} %get-tuple-element.342), channel_id=1, source_target_pairs={{0,2},{1,3},{2,0},{3,1},{4,6},{5,7},{6,4},{7,5},{8,10},{9,11},{10,... | collective-permute-start | bytes 737288 | tf_op jit(solution)/shard_map/ppermute | solution.py:757
  229.9 28.4 %collective-permute-start.49 = (bf16[2,2,128,768]{3,2,1,0:T(8,128)(2,1)S(1)}, bf16[2,2,128,768]{3,2,1,0:T(8,128)(2,1)S(1)}, u32[]{:S(2)}, u32[]{:S(2)}) collective-permute-start(bf16[2,2,128,768]{3,2,1,0:T(8,128)(2,1)S(1)} %copy-done.49), channel_id=1, source_target_pairs={{0,4},{1,5},{2,6},{3,7},{4,0},{5,1},{6,2},{7,3},{8,12},{9,13},{10,... | collective-permute-start | bytes 2359304 | tf_op jit(solution)/shard_map/ppermute | solution.py:757
  238.8 19.7 %collective-permute-start.50 = (bf16[1,1,128,768]{3,2,1,0:T(8,128)(2,1)S(1)}, bf16[1,1,128,768]{3,2,1,0:T(8,128)(2,1)}, u32[]{:S(2)}, u32[]{:S(2)}) collective-permute-start(bf16[1,1,128,768]{3,2,1,0:T(8,128)(2,1)S(1)} %constant_dynamic-slice_fusion.5), channel_id=1, source_target_pairs={{0,16},{1,17},{2,18},{3,19},{4,20},{5,21},{6,22},{7,23},{8,24},{9,... | collective-permute-start | bytes 589832 | tf_op jit(solution)/shard_map/ppermute | solution.py:757
  247.7 30.0 %collective-permute-start.51 = (bf16[2,3,128,768]{3,2,1,0:T(8,128)(2,1)S(1)}, bf16[2,3,128,768]{3,2,1,0:T(8,128)(2,1)S(1)}, u32[]{:S(2)}, u32[]{:S(2)}) collective-permute-start(bf16[2,3,128,768]{3,2,1,0:T(8,128)(2,1)S(1)} %copy-done.47), channel_id=1, source_target_pairs={{0,4},{1,5},{2,6},{3,7},{4,0},{5,1},{6,2},{7,3},{8,12},{9,13},{10,... | collective-permute-start | bytes 3538952 | tf_op jit(solution)/shard_map/ppermute | solution.py:757
  258.5 20.4 %collective-permute-start.52 = (bf16[1,2,128,768]{3,2,1,0:T(8,128)(2,1)S(1)}, bf16[1,2,128,768]{3,2,1,0:T(8,128)(2,1)S(1)}, u32[]{:S(2)}, u32[]{:S(2)}) collective-permute-start(bf16[1,2,128,768]{3,2,1,0:T(8,128)(2,1)S(1)} %constant_dynamic-slice_fusion.4), channel_id=1, source_target_pairs={{0,16},{1,17},{2,18},{3,19},{4,20},{5,21},{6,22},{7,23},{8,24},{9,... | collective-permute-start | bytes 1179656 | tf_op jit(solution)/shard_map/ppermute | solution.py:757
  287.1 20.3 %collective-permute-start.53 = (bf16[2,768,384]{2,1,0:T(8,128)(2,1)}, bf16[2,768,384]{2,1,0:T(8,128)(2,1)}, u32[]{:S(2)}, u32[]{:S(2)}) collective-permute-start(bf16[2,768,384]{2,1,0:T(8,128)(2,1)} %get-tuple-element.252), channel_id=1, source_target_pairs={{0,1},{1,0},{2,3},{3,2},{4,5},{5,4},{6,7},{7,6},{8,9},{9,8},{10,11... | collective-permute-start | bytes 3538952 | tf_op jit(solution)/shard_map/ppermute | solution.py:757
  296.8 40.0 %collective-permute-start.78 = (bf16[1,3,128,768]{3,2,1,0:T(8,128)(2,1)}, bf16[1,3,128,768]{3,2,1,0:T(8,128)(2,1)}, u32[]{:S(2)}, u32[]{:S(2)}) collective-permute-start(bf16[1,3,128,768]{3,2,1,0:T(8,128)(2,1)} %constant_dynamic-slice_fusion.3), channel_id=1, source_target_pairs={{0,16},{1,17},{2,18},{3,19},{4,20},{5,21},{6,22},{7,23},{8,24},{9,... | collective-permute-start | bytes 1769480 | tf_op jit(solution)/shard_map/ppermute | solution.py:757
  297.9 20.4 %collective-permute-start.55 = (bf16[2,2,32,3072]{3,2,1,0:T(8,128)(2,1)S(1)}, bf16[2,2,32,3072]{3,2,1,0:T(8,128)(2,1)S(1)}, u32[]{:S(2)}, u32[]{:S(2)}) collective-permute-start(bf16[2,2,32,3072]{3,2,1,0:T(8,128)(2,1)S(1)} %copy-done.48), channel_id=1, source_target_pairs={{0,4},{1,5},{2,6},{3,7},{4,0},{5,1},{6,2},{7,3},{8,12},{9,13},{10,... | collective-permute-start | bytes 2359304 | tf_op jit(solution)/shard_map/ppermute | solution.py:757
  298.6 46.8 %collective-permute-start.59 = (bf16[2,3,32,3072]{3,2,1,0:T(8,128)(2,1)}, bf16[2,3,32,3072]{3,2,1,0:T(8,128)(2,1)}, u32[]{:S(2)}, u32[]{:S(2)}) collective-permute-start(bf16[2,3,32,3072]{3,2,1,0:T(8,128)(2,1)} %get-tuple-element.270), channel_id=1, source_target_pairs={{0,4},{1,5},{2,6},{3,7},{4,0},{5,1},{6,2},{7,3},{8,12},{9,13},{10,... | collective-permute-start | bytes 3538952 | tf_op jit(solution)/shard_map/ppermute | solution.py:757
  309.9 34.2 %collective-permute-start.54 = (bf16[2,8,48,384]{3,2,1,0:T(8,128)(2,1)}, bf16[2,8,48,384]{3,2,1,0:T(8,128)(2,1)}, u32[]{:S(2)}, u32[]{:S(2)}) collective-permute-start(bf16[2,8,48,384]{3,2,1,0:T(8,128)(2,1)} %get-tuple-element.336), channel_id=1, source_target_pairs={{0,2},{1,3},{2,0},{3,1},{4,6},{5,7},{6,4},{7,5},{8,10},{9,11},{10,... | collective-permute-start | bytes 1769480 | tf_op jit(solution)/shard_map/ppermute | solution.py:757
  334.8 47.0 %collective-permute-start.75 = (bf16[1,2,32,3072]{3,2,1,0:T(8,128)(2,1)S(1)}, bf16[1,2,32,3072]{3,2,1,0:T(8,128)(2,1)S(1)}, u32[]{:S(2)}, u32[]{:S(2)}) collective-permute-start(bf16[1,2,32,3072]{3,2,1,0:T(8,128)(2,1)S(1)} %copy-done.17), channel_id=1, source_target_pairs={{0,16},{1,17},{2,18},{3,19},{4,20},{5,21},{6,22},{7,23},{8,24},{9,... | collective-permute-start | bytes 1179656 | tf_op jit(solution)/shard_map/ppermute | solution.py:757
  352.3 49.9 %collective-permute-start.73 = (bf16[1,3,32,3072]{3,2,1,0:T(8,128)(2,1)S(1)}, bf16[1,3,32,3072]{3,2,1,0:T(8,128)(2,1)S(1)}, u32[]{:S(2)}, u32[]{:S(2)}) collective-permute-start(bf16[1,3,32,3072]{3,2,1,0:T(8,128)(2,1)S(1)} %constant_dynamic-slice_fusion.1), channel_id=1, source_target_pairs={{0,16},{1,17},{2,18},{3,19},{4,20},{5,21},{6,22},{7,23},{8,24},{9,... | collective-permute-start | bytes 1769480 | tf_op jit(solution)/shard_map/ppermute | solution.py:757
  359.7 22.0 %collective-permute-start.62 = (bf16[2,2,2,48,384]{4,3,0,1,2:T(8,128)(2,1)S(1)}, bf16[2,2,2,48,384]{4,3,0,1,2:T(8,128)(2,1)S(1)}, u32[]{:S(2)}, u32[]{:S(2)}) collective-permute-start(bf16[2,2,2,48,384]{4,3,0,1,2:T(8,128)(2,1)S(1)} %copy.80), channel_id=1, source_target_pairs={{0,8},{1,9},{2,10},{3,11},{4,12},{5,13},{6,14},{7,15},{8,0},{9,1},... | collective-permute-start | bytes 884744 | tf_op jit(solution)/shard_map/ppermute | solution.py:757
  359.7 38.5 %collective-permute-start.79 = (bf16[3,128,768]{2,1,0:T(8,128)(2,1)S(1)}, bf16[3,128,768]{2,1,0:T(8,128)(2,1)S(1)}, u32[]{:S(2)}, u32[]{:S(2)}) collective-permute-start(bf16[3,128,768]{2,1,0:T(8,128)(2,1)S(1)} %copy-done.15), channel_id=1, source_target_pairs={{0,8},{1,9},{2,10},{3,11},{4,12},{5,13},{6,14},{7,15},{8,0},{9,1},... | collective-permute-start | bytes 1769480 | tf_op jit(solution)/shard_map/ppermute | solution.py:757
  361.9 20.8 %collective-permute-start.60 = (bf16[2,2,48,384]{3,2,1,0:T(8,128)(2,1)S(1)}, bf16[2,2,48,384]{3,2,1,0:T(8,128)(2,1)S(1)}, u32[]{:S(2)}, u32[]{:S(2)}) collective-permute-start(bf16[2,2,48,384]{3,2,1,0:T(8,128)(2,1)S(1)} %dynamic-slice_bitcast_fusion.9), channel_id=1, source_target_pairs={{0,4},{1,5},{2,6},{3,7},{4,0},{5,1},{6,2},{7,3},{8,12},{9,13},{10,... | collective-permute-start | bytes 442376 | tf_op jit(solution)/shard_map/ppermute | solution.py:757
  386.3 33.2 %collective-permute-start.76 = (bf16[2,32,3072]{2,1,0:T(8,128)(2,1)S(1)}, bf16[2,32,3072]{2,1,0:T(8,128)(2,1)S(1)}, u32[]{:S(2)}, u32[]{:S(2)}) collective-permute-start(bf16[2,32,3072]{2,1,0:T(8,128)(2,1)S(1)} %fusion.13), channel_id=1, source_target_pairs={{0,8},{1,9},{2,10},{3,11},{4,12},{5,13},{6,14},{7,15},{8,0},{9,1},... | collective-permute-start | bytes 1179656 | tf_op jit(solution)/shard_map/ppermute | solution.py:757
  (118 other events, 1079.9 us)

commit v2 on v1

--- a/solution.py
+++ b/solution.py
@@ -161,31 +161,28 @@
 
 def attention_forward_kernel(far, prefix, queries, keys, values, offsets, attended, probs, *, heads, blocks):
     pair = pl.program_id(0)
-    lane = lax.broadcasted_iota(jnp.int32, (BLOCK, 2 * heads), 1)
+    lane = lax.broadcasted_iota(jnp.int32, queries.shape, 1)
     row = lax.broadcasted_iota(jnp.int32, (BLOCK, BLOCK), 0)
     col = lax.broadcasted_iota(jnp.int32, (BLOCK, BLOCK), 1)
-    turned = []
+    outs = []
     for head in range(2):
         line = jnp.broadcast_to(offsets[head : head + 1, :], (BLOCK, 4 * BLOCK))
-        turned.append(pltpu.roll(line, 0, 1, stride=1, stride_axis=0))
-    for row_block in range(blocks):
-        rows = pl.ds(row_block * BLOCK, BLOCK)
-        span = seen_blocks(row_block, blocks)
-        seen = pl.ds(0, span * BLOCK)
-        outs = []
-        for head in range(2):
-            mine = (lane < heads) if head == 0 else (lane >= heads)
-            query = jnp.where(mine, queries[rows, :] * 0.125, 0.0).astype(jnp.bfloat16)
-            score = dot_f32(query, keys[seen, :], NT)
-            far_bias = far[pair * 2 + head]
+        turned = pltpu.roll(line, 0, 1, stride=1, stride_axis=0)
+        far_bias = far[pair * 2 + head]
+        mine = (lane < heads) if head == 0 else (lane >= heads)
+        query = jnp.where(mine, queries[...] * 0.125, 0.0).astype(jnp.bfloat16)
+        score = dot_f32(query, keys[...], NT)
+        strips = []
+        for row_block in range(blocks):
+            span = seen_blocks(row_block, blocks)
             pieces = []
             for key_block in range(span):
-                piece = score[:, key_block * BLOCK : (key_block + 1) * BLOCK]
+                piece = score[row_block * BLOCK : (row_block + 1) * BLOCK, key_block * BLOCK : (key_block + 1) * BLOCK]
                 shift = key_block - row_block
                 if shift < -1:
                     piece = piece + far_bias
                 elif shift < 2:
-                    piece = piece + turned[head][:, (2 + shift) * BLOCK : (3 + shift) * BLOCK]
+                    piece = piece + turned[:, (2 + shift) * BLOCK : (3 + shift) * BLOCK]
                 else:
                     raise ValueError(shift)
                 if shift >= 0:
@@ -201,10 +198,13 @@
             for piece in pieces[1:]:
                 mass = mass + piece
             scale = 1.0 / jnp.sum(mass, axis=1, keepdims=True)
-            weights = jnp.concatenate([(piece * scale).astype(jnp.bfloat16) for piece in pieces], axis=1)
-            probs[head, rows, seen] = weights
-            outs.append(dot_f32(weights, values[seen, :]))
-        attended[rows, :] = jnp.where(lane < heads, outs[0], outs[1]).astype(jnp.bfloat16)
+            pieces = [(piece * scale).astype(jnp.bfloat16) for piece in pieces]
+            pieces += [jnp.zeros((BLOCK, BLOCK), jnp.bfloat16)] * (blocks - span)
+            strips.append(jnp.concatenate(pieces, axis=1))
+        weights = jnp.concatenate(strips, axis=0)
+        probs[head] = weights
+        outs.append(dot_f32(weights, values[...]))
+    attended[...] = jnp.where(lane < heads, outs[0], outs[1]).astype(jnp.bfloat16)
 
 
 def attention_forward(far, prefix, qkv_rows, offsets):
@@ -228,53 +228,45 @@
             jax.ShapeDtypeStruct((2 * pairs, length, length), jnp.bfloat16),
         ],
         compiler_params=pltpu.CompilerParams(vmem_limit_bytes=VMEM_BYTES),
-        cost_estimate=cost(17),
+        cost_estimate=cost(13),
         name="attention_forward",
     )(far, prefix, qkv_rows, qkv_rows, qkv_rows, offsets.reshape(pairs, 2, 4 * BLOCK))
 
 
-def attention_backward_kernel(queries, keys, values, grads, probs, grad_rows, bands, flow, *, heads, blocks):
-    lane = lax.broadcasted_iota(jnp.int32, (BLOCK, 2 * heads), 1)
+def attention_backward_kernel(queries, keys, values, grads, probs, grad_rows, bands, *, heads, blocks):
+    lane = lax.broadcasted_iota(jnp.int32, queries.shape, 1)
     query_t = (queries[...] * 0.125).astype(jnp.bfloat16).T
     grad_t = grads[...].T
-    half = blocks // 2
-    dk, dv = [], []
-    dq = [[], []]
+    dq, dk, dv = [], [], []
     for head in range(2):
         mine = (lane < heads) if head == 0 else (lane >= heads)
         sums = [None] * 4
+        grad = jnp.where(mine, grads[...], 0.0).astype(jnp.bfloat16)
+        back = dot_f32(grad, values[...], NT)
+        strips = []
         for row_block in range(blocks):
-            rows = pl.ds(row_block * BLOCK, BLOCK)
             span = seen_blocks(row_block, blocks)
-            seen = pl.ds(0, span * BLOCK)
-            grad = jnp.where(mine, grads[rows, :], 0.0).astype(jnp.bfloat16)
-            soft = probs[head, rows, seen].astype(jnp.float32)
-            back = dot_f32(grad, values[seen, :], NT)
-            inner = jnp.sum(soft * back, axis=1, keepdims=True)
-            score_grad = (soft * (back - inner)).astype(jnp.bfloat16)
-            flow[rows, seen] = score_grad
-            dq[head].append(dot_f32(score_grad, keys[seen, :]) * 0.125)
+            rows = slice(row_block * BLOCK, (row_block + 1) * BLOCK)
+            soft = probs[head, pl.ds(row_block * BLOCK, BLOCK), pl.ds(0, span * BLOCK)].astype(jnp.float32)
+            part = back[rows, : span * BLOCK]
+            inner = jnp.sum(soft * part, axis=1, keepdims=True)
+            score_grad = (soft * (part - inner)).astype(jnp.bfloat16)
             for key_block in range(span):
                 band = max(key_block - row_block, -2)
-                if band > 1:
-                    continue
                 tile = score_grad[:, key_block * BLOCK : (key_block + 1) * BLOCK].astype(jnp.float32)
                 sums[band + 2] = tile if sums[band + 2] is None else sums[band + 2] + tile
+            if span < blocks:
+                rest = jnp.zeros((BLOCK, (blocks - span) * BLOCK), jnp.bfloat16)
+                score_grad = jnp.concatenate([score_grad, rest], axis=1)
+            strips.append(score_grad)
+        flow = jnp.concatenate(strips, axis=0)
         for band in range(4):
             bands[head, band] = sums[band]
         part = slice(head * heads, (head + 1) * heads)
-        key_pieces, value_pieces = [], []
-        for key_block in range(blocks):
-            first = 0 if key_block < half else key_block
-            rows = pl.ds(first * BLOCK, (blocks - first) * BLOCK)
-            cols = pl.ds(key_block * BLOCK, BLOCK)
-            key_pieces.append(dot_f32(query_t[part, first * BLOCK :], flow[rows, cols]))
-            value_pieces.append(dot_f32(grad_t[part, first * BLOCK :], probs[head, rows, cols]))
-        dk.append(jnp.concatenate(key_pieces, axis=1))
-        dv.append(jnp.concatenate(value_pieces, axis=1))
-    for row_block in range(blocks):
-        rows = pl.ds(row_block * BLOCK, BLOCK)
-        grad_rows[0, rows, :] = jnp.where(lane < heads, dq[0][row_block], dq[1][row_block]).astype(jnp.bfloat16)
+        dq.append(dot_f32(flow, keys[...]) * 0.125)
+        dk.append(dot_f32(query_t[part], flow))
+        dv.append(dot_f32(grad_t[part], probs[head]))
+    grad_rows[0] = jnp.where(lane < heads, dq[0], dq[1]).astype(jnp.bfloat16)
     grad_rows[1] = jnp.concatenate(dk, axis=0).T.astype(jnp.bfloat16)
     grad_rows[2] = jnp.concatenate(dv, axis=0).T.astype(jnp.bfloat16)
 
@@ -292,9 +284,8 @@
         out_specs=[pl.BlockSpec((3, length, 128), lambda h: (0, 0, h)), pl.BlockSpec((2, 4, BLOCK, BLOCK), lambda h: (h, 0, 0, 0))],
         out_shape=[jax.ShapeDtypeStruct((3, length, width), jnp.bfloat16)]
         + [jax.ShapeDtypeStruct((2 * pairs, 4, BLOCK, BLOCK), jnp.float32)],
-        scratch_shapes=[pltpu.VMEM((length, length), jnp.bfloat16)],
         compiler_params=pltpu.CompilerParams(vmem_limit_bytes=VMEM_BYTES),
-        cost_estimate=cost(17),
+        cost_estimate=cost(12),
         name="attention_backward",
     )(qkv_rows, qkv_rows, qkv_rows, grads, probs)
 
@@ -827,8 +818,15 @@
     columns = width // 2
     core_index = core.reshape(1).astype(jnp.int32)
     valid_rows = valid_mask.astype(f32)[:, None]
-    counts = partial_sums(jnp.broadcast_to(jnp.sum(valid_rows), (8, 128)))
-    valid_count = counts[-1][0, 0]
+    counts = [jnp.broadcast_to(jnp.sum(valid_rows), (8, 128))]
+    count_trades = [(0, mask) for mask in bits(groups)] + [(mask, 0) for mask in bits(copies)]
+
+    def count_beside(before, value):
+        if len(counts) > len(count_trades):
+            return value
+        counts.append(counts[-1] + swap(after(counts[-1], before), *count_trades[len(counts) - 1]))
+        return after(value, counts[-1])
+
     shards = [
         lax.dynamic_slice_in_dim(part, core * columns, columns, 2)
         for part in (qkv_weight[:2], jnp.concatenate([qkv_weight[2:], out_weight[None]]))
@@ -836,13 +834,13 @@
     if copies > 8:
         mine = lax.all_gather(jnp.concatenate(shards), "dp", axis=1, tiled=True)
     else:
-        mine = join(ring_places(), [gather_ring(shards[0], counts[:3]), gather_ring(shards[1], (slots_t, normed1, counts[3]))])
-    other = swap(mine, 0, 1)
-    qkv_rows = project(core_index, normed1, mine, other, 3)
-    offsets = after(offset_bias(position_bias_table), valid_count)
+        mine = join(ring_places(), [gather_ring(shards[0], ()), gather_ring(shards[1], (slots_t, normed1))])
+    other = count_beside(mine, swap(mine, 0, 1))
+    qkv_rows = count_beside(other, project(core_index, normed1, mine, other, 3))
+    offsets = offset_bias(position_bias_table)
     attended, probs = attention_forward(position_bias_table[:, bucket_far()], prefix, qkv_rows, offsets)
     middle, normed2, gates, *sends = route(
-        core_index, attended, tokens, mine, other, gain_moe, router, routes, slots_t, 2 * chips, capacity
+        core_index, count_beside(qkv_rows, attended), tokens, mine, other, gain_moe, router, routes, slots_t, 2 * chips, capacity
     )
 
     pick = half.reshape(1).astype(jnp.int32)
@@ -850,17 +848,21 @@
 
     def expert(pieces):
         one = not isinstance(pieces, list)
-        hidden_t, slope, rows_t, *results = expert_forward(pick, [pieces] if one else pieces, w_in, w_out)
+        pieces = [pieces] if one else pieces
+        hidden_t, slope, rows_t, *results = expert_forward(pick, pieces, w_in, w_out)
+        hidden_t = count_beside(pieces[-1], hidden_t)
         for kept, value in zip((hidden, slopes, rows_in), (hidden_t, slope, rows_t)):
             kept.append(value)
         return results[0] if one else (hidden_t, results)
 
     back = weave(*through(expert, sends))
+    while len(counts) <= len(count_trades):
+        back[0] = count_beside(back[0], back[0])
+    valid_count = counts[-1][0, 0]
     scale = (total_tokens / valid_count).reshape(1, 1)
     output, grad_y, grad_logits, squares, *sends = combine(
         slots, slots_t, scale, back, middle, teacher, cotangent, valid_rows, gates, routes, expert_count
     )
-    grad_router = jnp.einsum("td,te->de", normed2, grad_logits, preferred_element_type=f32)
 
     out_rows = inner // copies
     in_rows = width // copies
@@ -974,23 +976,23 @@
     )
     away_d, stay_d = near_add(after(got_d, second[1]), keep_d)
     far_d = far_trade(away_d)
-    got_e = swap(after(send_e, away_c), 1, 0)
+    got_e = swap(after(send_e, got_d), 1, 0)
     done_c = finish(after(far_c, away_d), stay_c)
     grad_table = table_gradient(after(bands, second[1]), position_bias_table.shape[1])
 
     chains = [add(after(first[0], away_d, gain_attn_parts), first[1]).reshape((2,) + (2,) * len(dp_masks) + (-1, columns)), None]
     trades = [over_dp(chains[0], dp_masks[0], ()), None]
-    away_e, stay_e = near_add(after(got_e, trades[0][1]), keep_e)
-    far_e = far_trade(away_e)
-    got_f = swap(after(send_f, away_e), 1, 0)
-    chains[1] = add(after(second[0], done_c, grad_table, away_e), second[1]).reshape(chains[0].shape)
+    chains[1] = add(after(second[0], done_c, grad_table), second[1]).reshape(chains[0].shape)
     trades[1] = over_dp(chains[1], dp_masks[0], ())
     trades[0] = (after(trades[0][0], trades[1][1]), trades[0][1])
     total = trades[1][1]
-    out_theirs = swap(after(jnp.concatenate([done_a, done_b]), total), PAIR, 0)
-    away_f, stay_f = near_add(after(got_f, total), keep_f)
-    trades[1] = (after(trades[1][0], away_f), trades[1][1])
-
+    away_e, stay_e = near_add(after(got_e, total), keep_e)
+    far_e = far_trade(away_e)
+    got_f = swap(after(send_f, away_e), 1, 0)
+    trades[1] = (after(trades[1][0], away_e), trades[1][1])
+
+    normed2, squares, gain_moe_parts = after((normed2, squares, gain_moe_parts), second[1])
+    grad_router = jnp.einsum("td,te->de", normed2, grad_logits, preferred_element_type=f32)
     small = [
         jnp.sum(gain_moe_parts, axis=0),
         jnp.sum(gain_attn_parts, axis=0),
@@ -1015,15 +1017,20 @@
         if mask == PAIR:
             done_d = finish(after(far_d, chains[1]), stay_d)
             in_first = swap(done_d, PAIR, 0)
+            out_theirs = swap(after(jnp.concatenate([done_a, done_b]), chains[1]), PAIR, 0)
+            away_f, stay_f = near_add(after(got_f, chains[1]), keep_f)
+            far_f = far_trade(away_f)
         flat = after(flat, chains[1])
     total = jnp.concatenate(chains)
-    far_f = far_trade(after(away_f, total))
     done_e = finish(after(far_e, total), stay_e)
     in_theirs = jnp.concatenate([in_first, swap(done_e[:1], PAIR, 0)])
     for mask in reversed(group_masks):
         bit = (here_group // mask) % 2
         other_part = swap(total, 0, mask)
         total = jnp.concatenate([jnp.where(bit == 0, total, other_part), jnp.where(bit == 0, other_part, total)], axis=1)
+        if mask == group_masks[0]:
+            done_f = finish(after(far_f, total), stay_f)
+            total = after(total, done_f)
         flat = flat + swap(flat, 0, mask)
         total, flat = lax.optimization_barrier((total, flat))
     other_part = swap(total, 0, 1)
@@ -1031,7 +1038,6 @@
     total = jnp.concatenate([jnp.where(core == 0, total, other_part), jnp.where(core == 0, other_part, total)], axis=2)
     weights_done = total.astype(f32)
     grad_qkv, grad_out_weight = weights_done[:3], weights_done[3]
-    done_f = finish(far_f, stay_f)
     flat = flat.reshape(-1)
     starts = [sum(sizes[:place]) for place in range(len(sizes))]
     grad_gain_moe, grad_gain_attn, grad_router, grad_table, square_total = [

time: 429 us -> 422 us (0.984)
  Pallas kernels: 167 us -> 157 us
  starting transfers between devices: 82.1 us -> 90.7 us
  local copies, waits for them, and re-layouts: 34.9 us -> 28 us
    ppermute x66, starting transfers between devices: 64.6 us -> 73.6 us  [swap(): return lax.ppermute(value, AXES, pairs)]
    pallas_call x1, Pallas kernels: 17.3 us -> 11.6 us  [attention_backward(): pl.pallas_call(lambda *refs: attention_backward_kernel(*refs, heads=64, b...]
    unnamed x147 -> x159, local copies, waits for them, and re-layouts: 15.1 us -> 9.85 us
  transfers between devices with their start and end apart: 80 -> 80, of which waited for: 29 -> 30; matrix products, arithmetic and copies ran while one was open for 13% -> 11% of each run, Pallas kernels for 26% -> 29%
where the time goes in v2:
time: 422 us; the launch traced here: 417 us
  Pallas kernels  157 us (37%)
  waiting for transfers between devices  104 us (25%)
  starting transfers between devices  90.7 us (21%)
  local copies, waits for them, and re-layouts  28 us (7%)
  other arithmetic  25.8 us (6%)
  matrix products  6.29 us (1%)
  between operations  6.21 us (1%)
    ppermute x66, waiting for transfers between devices, swap(): return lax.ppermute(value, AXES, pairs)  94.7 us
    ppermute x66, starting transfers between devices, swap(): return lax.ppermute(value, AXES, pairs)  73.6 us
    pallas_call x4, Pallas kernels, weight_part(): pl.pallas_call(lambda *refs: weight_part_kernel(*refs, count=count, plans...  30.7 us
    pallas_call x2, Pallas kernels, expert_forward(): pl.pallas_call(lambda *refs: expert_forward_kernel(*refs, chunk=chunk, co...  27.4 us
    pallas_call x2, Pallas kernels, expert_backward(): pl.pallas_call(lambda *refs: expert_backward_kernel(*refs, chunk=chunk, c...  25.1 us
    ppermute x14, starting transfers between devices, gather_ring(): lax.ppermute(after(held, *due[step - 2:step - 1]) if step > 1 else held,...  17.1 us
    pallas_call x1, Pallas kernels, attention_forward(): pl.pallas_call(lambda *refs: attention_forward_kernel(*refs, heads=64, bl...  12.7 us
    pallas_call x1, Pallas kernels, attention_backward(): pl.pallas_call(lambda *refs: attention_backward_kernel(*refs, heads=64, b...  11.6 us
  transfers between devices with their start and end apart: 80, of which 30 were waited for; matrix products, arithmetic and copies ran while one was open for 11% of the time, Pallas kernels for 29%

profile of v2, /device:TPU:0, one launch (start us, length us, event | category | flops | bytes accessed | tf_op | source)
XLA Modules:
  0.0 417.5 jit_solution(15315158040230650098)
XLA Ops:
  1.7 3.1 collective-permute-start
  34.3 3.3 join.1.mine.refs_15_
  46.4 6.4 %project.1.refs_2_.refs_3_.refs_4_.refs_0_.refs_1_ = bf16[3,512,768]{2,1,0:T(8,128)(2,1)} custom-call(s32[1]{0:T(128)} %bitcast.2.core.refs_0_, bf16[512,768]{1,0:T(8,128)(2,1)} %fusion.6.rows.refs_1_, bf16[4,768,384]{2,1,0:T(8,128)(2,1)} %join.1.mine.refs_15_, bf16[4,768,384]{2,1,0:T(8,128)(2,1)} %copy-done), custom_call_target="tpu_custom_call" | custom-call | flops 1480000000 | tf_op jit(solution)/shard_map/project/pallas_call | solution.py:396
  55.0 12.7 %attention_forward.1 = (bf16[512,768]{1,0:T(8,128)(2,1)}, bf16[12,512,512]{2,1,0:T(8,128)(2,1)}) custom-call(f32[12]{0:T(128)} %slice_reduce_fusion.refs_0_, s32[1]{0:T(128)S(6)} %copy.105.refs_1_, bf16[3,512,768]{2,1,0:T(8,128)(2,1)} %project.1.refs_2_.refs_3_.refs_4_.refs_0_.refs_1_, bf16[3,512,768]{2,1,0:T(8,128)(2,1)} %project.1.refs_2_.refs_3_.refs_4_.refs_0_.refs_1_, ...), custom_call_target="tpu_custom_call" | custom-call | flops 4809999872 | tf_op jit(solution)/shard_map/attention_forward/pallas_call | solution.py:214
  67.7 5.9 %route.1 = (f32[512,768]{1,0:T(8,128)}, bf16[512,768]{1,0:T(8,128)(2,1)}, f32[512,2]{1,0:T(8,128)}, bf16[160,768]{1,0:T(8,128)(2,1)}, bf16[160,768]{1,0:T(8,128)...) custom-call(s32[1]{0:T(128)} %bitcast.2.core.refs_0_, ...), custom_call_target="tpu_custom_call" | custom-call | flops 2220000000 | tf_op jit(solution)/shard_map/route/pallas_call | solution.py:447
  80.0 3.8 collective-permute-done.18.refs_4_
  85.0 4.0 collective-permute-done.20.refs_2_
  91.3 13.6 %expert_forward.2 = (bf16[3072,640]{1,0:T(8,128)(2,1)}, bf16[640,3072]{1,0:T(8,128)(2,1)}, bf16[768,640]{1,0:T(8,128)(2,1)}, bf16[160,768]{1,0:T(8,128)(2,1)}, b...) custom-call(s32[1]{0:T(128)} %bitcast.4.refs_0_, ...), custom_call_target="tpu_custom_call" | custom-call | flops 4809999872 | tf_op jit(solution)/shard_map/expert_forward/pallas_call | solution.py:78
  105.9 4.2 %collective-permute-start.27 = (bf16[160,768]{1,0:T(8,128)(2,1)S(1)}, bf16[160,768]{1,0:T(8,128)(2,1)S(1)}, u32[]{:S(2)}, u32[]{:S(2)}) collective-permute-start(bf16[160,768]{1,0:T(8,128)(2,1)S(1)} %copy-done.71), channel_id=1, source_target_pairs={{0,2},{1,3},{2,0},{3,1},{4,6},{5,7},{6,4},{7,5},{8,10},{9,11},{10,... | collective-permute-start | bytes 737288 | tf_op jit(solution)/shard_map/ppermute | solution.py:748
  112.7 13.7 %expert_forward.3 = (bf16[3072,640]{1,0:T(8,128)(2,1)}, bf16[640,3072]{1,0:T(8,128)(2,1)}, bf16[768,640]{1,0:T(8,128)(2,1)}, bf16[640,768]{1,0:T(8,128)(2,1)}) custom-call(s32[1]{0:T(128)} %bitcast.4.refs_0_, bf16[640,768]{1,0:T(8,128)(2,1)} %copy-done.16, bf16[2,768,3072]{2,1,0:T(8,128)(2,1)} %refs_2_.3, bf16[2,3072,768]{2,1,0:T(8,128)(2,1)} %refs_3_.3), custom_call_target="tpu_custom_call" | custom-call | flops 4809999872 | tf_op jit(solution)/shard_map/expert_forward/pallas_call | solution.py:78
  137.1 5.8 %collective-permute-done.26 = f32[8,128]{1,0:T(8,128)S(1)} collective-permute-done((f32[8,128]{1,0:T(8,128)S(1)}, f32[8,128]{1,0:T(8,128)S(1)}, u32[]{:S(2)}, u32[]{:S(2)}) %collective-permute-start.26) | collective-permute-done | bytes 4128 | tf_op jit(solution)/shard_map/ppermute | solution.py:748
  145.5 8.5 %combine.1 = (bf16[512,768]{1,0:T(8,128)(2,1)}, f32[512,768]{1,0:T(8,128)}, bf16[512,8]{1,0:T(8,128)(2,1)}, f32[8,768]{1,0:T(8,128)}, bf16[160,768]{1,0:T(8,128)...) custom-call(s32[512,2]{1,0:T(8,128)} %multiply_add_fusion.refs_0_.re, ...), custom_call_target="tpu_custom_call" | custom-call | flops 2960000000 | tf_op jit(solution)/shard_map/combine/pallas_call | solution.py:503
  165.7 6.5 %collective-permute-done.36.refs_4_ = bf16[160,768]{1,0:T(8,128)(2,1)S(1)} collective-permute-done((bf16[160,768]{1,0:T(8,128)(2,1)}, bf16[160,768]{1,0:T(8,128)(2,1)S(1)}, u32[]{:S(2)}, u32[]{:S(2)}) %collective-permute-start.36) | collective-permute-done | bytes 245792 | tf_op jit(solution)/shard_map/ppermute | solution.py:748
  173.0 12.5 %expert_backward.2 = (bf16[640,3072]{1,0:T(8,128)(2,1)}, bf16[640,768]{1,0:T(8,128)(2,1)}, bf16[160,768]{1,0:T(8,128)(2,1)}, bf16[160,768]{1,0:T(8,128)(2,1)}, b...) custom-call(s32[1]{0:T(128)} %bitcast.4.refs_0_, bf16[160,768]{1,0:T(8,128)(2,1)} %get-tuple-element.198.refs_1_, ...), custom_call_target="tpu_custom_call" | custom-call | flops 4070000128 | tf_op jit(solution)/shard_map/expert_backward/pallas_call | solution.py:135
  189.2 7.8 %weight_part.4 = (bf16[2,1,128,768]{3,2,1,0:T(8,128)(2,1)}, bf16[2,2,128,768]{3,2,1,0:T(8,128)(2,1)}, bf16[2,3,128,768]{3,2,1,0:T(8,128)(2,1)}) custom-call(s32[4]{0:T(128)} %pad_add_fusion.1.refs_0_, bf16[3072,640]{1,0:T(8,128)(2,1)} %get-tuple-element.180.refs_1_.refs_2_.refs_3_.refs_4_, ...), custom_call_target="tpu_custom_call" | custom-call | flops 1480000000 | tf_op jit(solution)/shard_map/weight_part/pallas_call | solution.py:337
  201.1 12.7 %expert_backward.3 = (bf16[640,3072]{1,0:T(8,128)(2,1)}, bf16[640,768]{1,0:T(8,128)(2,1)}, bf16[640,768]{1,0:T(8,128)(2,1)}) custom-call(s32[1]{0:T(128)} %bitcast.4.refs_0_, bf16[640,768]{1,0:T(8,128)(2,1)} %copy-done.1, bf16[2,768,3072]{2,1,0:T(8,128)(2,1)} %refs_2_.3, bf16[2,3072,768]{2,1,0:T(8,128)(2,1)} %refs_3_.3, ...), custom_call_target="tpu_custom_call" | custom-call | flops 4070000128 | tf_op jit(solution)/shard_map/expert_backward/pallas_call | solution.py:135
  222.4 7.7 %weight_part.5 = (bf16[2,1,128,768]{3,2,1,0:T(8,128)(2,1)}, bf16[2,2,128,768]{3,2,1,0:T(8,128)(2,1)}, bf16[2,3,128,768]{3,2,1,0:T(8,128)(2,1)}) custom-call(s32[4]{0:T(128)} %pad_add_fusion.2.refs_0_, bf16[3072,640]{1,0:T(8,128)(2,1)} %get-tuple-element.180.refs_1_.refs_2_.refs_3_.refs_4_, ...), custom_call_target="tpu_custom_call" | custom-call | flops 1480000000 | tf_op jit(solution)/shard_map/weight_part/pallas_call | solution.py:337
  231.2 7.7 %weight_part.6 = (bf16[2,2,32,3072]{3,2,1,0:T(8,128)(2,1)}, bf16[2,3,32,3072]{3,2,1,0:T(8,128)(2,1)}, bf16[2,1,32,3072]{3,2,1,0:T(8,128)(2,1)}) custom-call(s32[4]{0:T(128)} %pad_add_fusion.1.refs_0_, bf16[768,640]{1,0:T(8,128)(2,1)} %get-tuple-element.204.refs_1_.refs_2_.refs_3_.refs_4_, ...), custom_call_target="tpu_custom_call" | custom-call | flops 1480000000 | tf_op jit(solution)/shard_map/weight_part/pallas_call | solution.py:337
  240.1 8.5 %collect.1 = (f32[512,768]{1,0:T(8,128)}, bf16[512,768]{1,0:T(8,128)(2,1)}, bf16[512,768]{1,0:T(8,128)(2,1)}, f32[8,768]{1,0:T(8,128)}) custom-call(s32[1]{0:T(128)} %bitcast.2.core.refs_0_, s32[512,2]{1,0:T(8,128)} %multiply_add_fusion.refs_0_.refs_1_, bf16[160,768]{1,0:T(8,128)(2,1)} %get-tuple-element.237.refs_2_, ...), custom_call_target="tpu_custom_call" | custom-call | flops 2960000000 | tf_op jit(solution)/shard_map/collect/pallas_call | solution.py:554
  251.3 11.6 %attention_backward.1 = (bf16[3,512,768]{2,1,0:T(8,128)(2,1)}, f32[12,4,128,128]{3,2,1,0:T(8,128)}) custom-call(bf16[3,512,768]{2,1,0:T(8,128)(2,1)} %project.1.refs_2_.refs_3_.refs_4_.refs_0_.refs_1_, bf16[3,512,768]{2,1,0:T(8,128)(2,1)} %project.1.refs_2_.refs_3_.refs_4_.refs_0_.refs_1_, ...), custom_call_target="tpu_custom_call" | custom-call | flops 4440000000 | tf_op jit(solution)/shard_map/attention_backward/pallas_call | solution.py:280
  262.9 3.2 collective-permute-done.51
  269.4 8.4 %outer_halves.1 = (bf16[2,768,384]{2,1,0:T(8,128)(2,1)}, bf16[2,768,384]{2,1,0:T(8,128)(2,1)}, bf16[2,768,384]{2,1,0:T(8,128)(2,1)}, bf16[2,768,384]{2,1,0:T(8,128)(2,1)}) custom-call(s32[1]{0:T(128)} %bitcast.2.core.refs_0_, bf16[512,768]{1,0:T(8,128)(2,1)} %fusion.6.rows.refs_1_, bf16[512,768]{1,0:T(8,128)(2,1)} %get-tuple-element.172.attended.refs_2_, ...), custom_call_target="tpu_custom_call" | custom-call | flops 2220000000 | tf_op jit(solution)/shard_map/outer_halves/pallas_call | solution.py:604
  282.1 7.6 %weight_part.7 = (bf16[2,2,32,3072]{3,2,1,0:T(8,128)(2,1)}, bf16[2,3,32,3072]{3,2,1,0:T(8,128)(2,1)}, bf16[2,1,32,3072]{3,2,1,0:T(8,128)(2,1)}) custom-call(s32[4]{0:T(128)} %pad_add_fusion.2.refs_0_, bf16[768,640]{1,0:T(8,128)(2,1)} %get-tuple-element.204.refs_1_.refs_2_.refs_3_.refs_4_, ...), custom_call_target="tpu_custom_call" | custom-call | flops 1480000000 | tf_op jit(solution)/shard_map/weight_part/pallas_call | solution.py:337
  289.7 8.5 %collective-permute-done.55 = bf16[2,2,32,3072]{3,2,1,0:T(8,128)(2,1)} collective-permute-done((bf16[2,2,32,3072]{3,2,1,0:T(8,128)(2,1)}, bf16[2,2,32,3072]{3,2,1,0:T(8,128)(2,1)}, u32[]{:S(2)}, u32[]{:S(2)}) %collective-permute-start.55) | collective-permute-done | bytes 786464 | tf_op jit(solution)/shard_map/ppermute | solution.py:748
  308.3 8.4 %enter.1 = (f32[512,768]{1,0:T(8,128)}, f32[8,768]{1,0:T(8,128)}) custom-call(s32[1]{0:T(128)} %bitcast.2.core.refs_0_, bf16[3,512,768]{2,1,0:T(8,128)(2,1)} %get-tuple-element.273.refs_3_.grads, bf16[4,768,384]{2,1,0:T(8,128)(2,1)} %join.1.mine.refs_15_, bf16[4,768,384]{2,1,0:T(8,128)(2,1)} %copy-done, bf16[512,768]{1,0:T(8,128)(2,1)} %tokens.3, ...), custom_call_target="tpu_custom_call" | custom-call | flops 2220000000 | tf_op jit(solution)/shard_map/enter/pallas_call | solution.py:650
  317.5 5.3 %fusion.10 = f32[12,32]{1,0:T(8,128)S(1)} fusion(s32[4,128,128]{2,1,0:T(8,128)S(1)} %pad_add_fusion, f32[12,4,128,128]{3,2,1,0:T(8,128)S(1)} %copy-done.3), kind=kOutput, calls=%fused_computation.31 | convolution fusion | flops 304087040 | bytes 3409408 | tf_op jit(solution)/shard_map/hdxy,dxyb->hb/dot_general | solution.py:704
  334.2 17.7 %collective-permute-done.68 = f32[64,128]{1,0:T(8,128)S(1)} collective-permute-done((f32[64,128]{1,0:T(8,128)S(1)}, f32[64,128]{1,0:T(8,128)S(1)}, u32[]{:S(2)}, u32[]{:S(2)}) %collective-permute-start.68) | collective-permute-done | bytes 32800 | tf_op jit(solution)/shard_map/ppermute | solution.py:748
  360.3 7.9 %collective-permute-done.69 = f32[64,128]{1,0:T(8,128)S(1)} collective-permute-done((f32[64,128]{1,0:T(8,128)S(1)}, f32[64,128]{1,0:T(8,128)S(1)}, u32[]{:S(2)}, u32[]{:S(2)}) %collective-permute-start.69) | collective-permute-done | bytes 32800 | tf_op jit(solution)/shard_map/ppermute | solution.py:748
  371.3 5.8 %collective-permute-done.70 = f32[64,128]{1,0:T(8,128)S(1)} collective-permute-done((f32[64,128]{1,0:T(8,128)S(1)}, f32[64,128]{1,0:T(8,128)S(1)}, u32[]{:S(2)}, u32[]{:S(2)}) %collective-permute-start.70) | collective-permute-done | bytes 32800 | tf_op jit(solution)/shard_map/ppermute | solution.py:748
  380.6 8.3 %collective-permute-done.64 = bf16[2,48,384]{2,1,0:T(8,128)(2,1)S(1)} collective-permute-done((bf16[2,48,384]{2,1,0:T(8,128)(2,1)S(1)}, bf16[2,48,384]{2,1,0:T(8,128)(2,1)S(1)}, u32[]{:S(2)}, u32[]{:S(2)}) %collective-permute-start.64) | collective-permute-done | bytes 73760 | tf_op jit(solution)/shard_map/ppermute | solution.py:748
  389.6 3.3 collective-permute-done.71
  393.7 3.5 collective-permute-start.67
  (422 shorter events, 163.5 us)
Async XLA Ops:
  77.2 27.9 %collective-permute-start.24 = (bf16[160,768]{1,0:T(8,128)(2,1)}, bf16[160,768]{1,0:T(8,128)(2,1)S(1)}, u32[]{:S(2)}, u32[]{:S(2)}) collective-permute-start(bf16[160,768]{1,0:T(8,128)(2,1)} %get-tuple-element.186), channel_id=1, source_target_pairs={{0,10},{1,11},{2,8},{3,9},{4,14},{5,15},{6,12},{7,13},{8,2},{9,3},... | collective-permute-start | bytes 737288 | tf_op jit(solution)/shard_map/ppermute | solution.py:748
  79.5 25.6 %collective-permute-start.23 = (bf16[160,768]{1,0:T(8,128)(2,1)}, bf16[160,768]{1,0:T(8,128)(2,1)S(1)}, u32[]{:S(2)}, u32[]{:S(2)}) collective-permute-start(bf16[160,768]{1,0:T(8,128)(2,1)} %get-tuple-element.184), channel_id=1, source_target_pairs={{0,8},{1,9},{2,10},{3,11},{4,12},{5,13},{6,14},{7,15},{8,0},{9,1},... | collective-permute-start | bytes 737288 | tf_op jit(solution)/shard_map/ppermute | solution.py:748
  83.7 21.4 %collective-permute-start.22 = (bf16[160,768]{1,0:T(8,128)(2,1)}, bf16[160,768]{1,0:T(8,128)(2,1)S(1)}, u32[]{:S(2)}, u32[]{:S(2)}) collective-permute-start(bf16[160,768]{1,0:T(8,128)(2,1)} %get-tuple-element.182), channel_id=1, source_target_pairs={{0,2},{1,3},{2,0},{3,1},{4,6},{5,7},{6,4},{7,5},{8,10},{9,11},{10,... | collective-permute-start | bytes 737288 | tf_op jit(solution)/shard_map/ppermute | solution.py:748
  105.9 20.5 %collective-permute-start.27 = (bf16[160,768]{1,0:T(8,128)(2,1)S(1)}, bf16[160,768]{1,0:T(8,128)(2,1)S(1)}, u32[]{:S(2)}, u32[]{:S(2)}) collective-permute-start(bf16[160,768]{1,0:T(8,128)(2,1)S(1)} %copy-done.71), channel_id=1, source_target_pairs={{0,2},{1,3},{2,0},{3,1},{4,6},{5,7},{6,4},{7,5},{8,10},{9,11},{10,... | collective-permute-start | bytes 737288 | tf_op jit(solution)/shard_map/ppermute | solution.py:748
  110.2 16.3 %collective-permute-start.28 = (bf16[160,768]{1,0:T(8,128)(2,1)S(1)}, bf16[160,768]{1,0:T(8,128)(2,1)S(1)}, u32[]{:S(2)}, u32[]{:S(2)}) collective-permute-start(bf16[160,768]{1,0:T(8,128)(2,1)S(1)} %copy-done.70), channel_id=1, source_target_pairs={{0,8},{1,9},{2,10},{3,11},{4,12},{5,13},{6,14},{7,15},{8,0},{9,1},... | collective-permute-start | bytes 737288 | tf_op jit(solution)/shard_map/ppermute | solution.py:748
  110.3 16.3 %collective-permute-start.29 = (bf16[160,768]{1,0:T(8,128)(2,1)S(1)}, bf16[160,768]{1,0:T(8,128)(2,1)S(1)}, u32[]{:S(2)}, u32[]{:S(2)}) collective-permute-start(bf16[160,768]{1,0:T(8,128)(2,1)S(1)} %copy-done.68), channel_id=1, source_target_pairs={{0,10},{1,11},{2,8},{3,9},{4,14},{5,15},{6,12},{7,13},{8,2},{9,3},... | collective-permute-start | bytes 737288 | tf_op jit(solution)/shard_map/ppermute | solution.py:748
  159.8 25.6 %collective-permute-start.39 = (bf16[160,768]{1,0:T(8,128)(2,1)}, bf16[160,768]{1,0:T(8,128)(2,1)S(1)}, u32[]{:S(2)}, u32[]{:S(2)}) collective-permute-start(bf16[160,768]{1,0:T(8,128)(2,1)} %get-tuple-element.214), channel_id=1, source_target_pairs={{0,10},{1,11},{2,8},{3,9},{4,14},{5,15},{6,12},{7,13},{8,2},{9,3},... | collective-permute-start | bytes 737288 | tf_op jit(solution)/shard_map/ppermute | solution.py:748
  161.6 23.9 %collective-permute-start.38 = (bf16[160,768]{1,0:T(8,128)(2,1)}, bf16[160,768]{1,0:T(8,128)(2,1)S(1)}, u32[]{:S(2)}, u32[]{:S(2)}) collective-permute-start(bf16[160,768]{1,0:T(8,128)(2,1)} %get-tuple-element.212), channel_id=1, source_target_pairs={{0,8},{1,9},{2,10},{3,11},{4,12},{5,13},{6,14},{7,15},{8,0},{9,1},... | collective-permute-start | bytes 737288 | tf_op jit(solution)/shard_map/ppermute | solution.py:748
  161.9 23.6 %collective-permute-start.37 = (bf16[160,768]{1,0:T(8,128)(2,1)}, bf16[160,768]{1,0:T(8,128)(2,1)S(1)}, u32[]{:S(2)}, u32[]{:S(2)}) collective-permute-start(bf16[160,768]{1,0:T(8,128)(2,1)} %get-tuple-element.210), channel_id=1, source_target_pairs={{0,2},{1,3},{2,0},{3,1},{4,6},{5,7},{6,4},{7,5},{8,10},{9,11},{10,... | collective-permute-start | bytes 737288 | tf_op jit(solution)/shard_map/ppermute | solution.py:748
  197.0 16.8 %collective-permute-start.41 = (bf16[2,1,128,768]{3,2,1,0:T(8,128)(2,1)}, bf16[2,1,128,768]{3,2,1,0:T(8,128)(2,1)S(1)}, u32[]{:S(2)}, u32[]{:S(2)}) collective-permute-start(bf16[2,1,128,768]{3,2,1,0:T(8,128)(2,1)} %get-tuple-element.223), channel_id=1, source_target_pairs={{0,4},{1,5},{2,6},{3,7},{4,0},{5,1},{6,2},{7,3},{8,12},{9,13},{10,... | collective-permute-start | bytes 1179656 | tf_op jit(solution)/shard_map/ppermute | solution.py:748
  197.5 16.2 %collective-permute-start.42 = (bf16[160,768]{1,0:T(8,128)(2,1)S(1)}, bf16[160,768]{1,0:T(8,128)(2,1)S(1)}, u32[]{:S(2)}, u32[]{:S(2)}) collective-permute-start(bf16[160,768]{1,0:T(8,128)(2,1)S(1)} %copy-done.64), channel_id=1, source_target_pairs={{0,2},{1,3},{2,0},{3,1},{4,6},{5,7},{6,4},{7,5},{8,10},{9,11},{10,... | collective-permute-start | bytes 737288 | tf_op jit(solution)/shard_map/ppermute | solution.py:748
  217.4 21.5 %collective-permute-start.46 = (bf16[160,768]{1,0:T(8,128)(2,1)S(1)}, bf16[160,768]{1,0:T(8,128)(2,1)S(1)}, u32[]{:S(2)}, u32[]{:S(2)}) collective-permute-start(bf16[160,768]{1,0:T(8,128)(2,1)S(1)} %get-tuple-element.345), channel_id=1, source_target_pairs={{0,2},{1,3},{2,0},{3,1},{4,6},{5,7},{6,4},{7,5},{8,10},{9,11},{10,... | collective-permute-start | bytes 737288 | tf_op jit(solution)/shard_map/ppermute | solution.py:748
  217.9 21.0 %collective-permute-start.47 = (bf16[160,768]{1,0:T(8,128)(2,1)S(1)}, bf16[160,768]{1,0:T(8,128)(2,1)S(1)}, u32[]{:S(2)}, u32[]{:S(2)}) collective-permute-start(bf16[160,768]{1,0:T(8,128)(2,1)S(1)} %get-tuple-element.344), channel_id=1, source_target_pairs={{0,8},{1,9},{2,10},{3,11},{4,12},{5,13},{6,14},{7,15},{8,0},{9,1},... | collective-permute-start | bytes 737288 | tf_op jit(solution)/shard_map/ppermute | solution.py:748
  219.7 19.3 %collective-permute-start.48 = (bf16[160,768]{1,0:T(8,128)(2,1)S(1)}, bf16[160,768]{1,0:T(8,128)(2,1)S(1)}, u32[]{:S(2)}, u32[]{:S(2)}) collective-permute-start(bf16[160,768]{1,0:T(8,128)(2,1)S(1)} %get-tuple-element.343), channel_id=1, source_target_pairs={{0,10},{1,11},{2,8},{3,9},{4,14},{5,15},{6,12},{7,13},{8,2},{9,3},... | collective-permute-start | bytes 737288 | tf_op jit(solution)/shard_map/ppermute | solution.py:748
  220.9 27.7 %collective-permute-start.49 = (bf16[2,2,128,768]{3,2,1,0:T(8,128)(2,1)}, bf16[2,2,128,768]{3,2,1,0:T(8,128)(2,1)S(1)}, u32[]{:S(2)}, u32[]{:S(2)}) collective-permute-start(bf16[2,2,128,768]{3,2,1,0:T(8,128)(2,1)} %get-tuple-element.248), channel_id=1, source_target_pairs={{0,4},{1,5},{2,6},{3,7},{4,0},{5,1},{6,2},{7,3},{8,12},{9,13},{10,... | collective-permute-start | bytes 2359304 | tf_op jit(solution)/shard_map/ppermute | solution.py:748
  238.9 27.2 %collective-permute-start.51 = (bf16[2,3,128,768]{3,2,1,0:T(8,128)(2,1)S(1)}, bf16[2,3,128,768]{3,2,1,0:T(8,128)(2,1)S(1)}, u32[]{:S(2)}, u32[]{:S(2)}) collective-permute-start(bf16[2,3,128,768]{3,2,1,0:T(8,128)(2,1)S(1)} %copy-done.55), channel_id=1, source_target_pairs={{0,4},{1,5},{2,6},{3,7},{4,0},{5,1},{6,2},{7,3},{8,12},{9,13},{10,... | collective-permute-start | bytes 3538952 | tf_op jit(solution)/shard_map/ppermute | solution.py:748
  250.4 19.0 %collective-permute-start.52 = (bf16[1,2,128,768]{3,2,1,0:T(8,128)(2,1)S(1)}, bf16[1,2,128,768]{3,2,1,0:T(8,128)(2,1)S(1)}, u32[]{:S(2)}, u32[]{:S(2)}) collective-permute-start(bf16[1,2,128,768]{3,2,1,0:T(8,128)(2,1)S(1)} %constant_dynamic-slice_fusion.6), channel_id=1, source_target_pairs={{0,16},{1,17},{2,18},{3,19},{4,20},{5,21},{6,22},{7,23},{8,24},{9,... | collective-permute-start | bytes 1179656 | tf_op jit(solution)/shard_map/ppermute | solution.py:748
  277.8 21.9 %collective-permute-start.53 = (bf16[2,768,384]{2,1,0:T(8,128)(2,1)}, bf16[2,768,384]{2,1,0:T(8,128)(2,1)S(1)}, u32[]{:S(2)}, u32[]{:S(2)}) collective-permute-start(bf16[2,768,384]{2,1,0:T(8,128)(2,1)} %get-tuple-element.262), channel_id=1, source_target_pairs={{0,1},{1,0},{2,3},{3,2},{4,5},{5,4},{6,7},{7,6},{8,9},{9,8},{10,11... | collective-permute-start | bytes 3538952 | tf_op jit(solution)/shard_map/ppermute | solution.py:748
  277.9 20.3 %collective-permute-start.55 = (bf16[2,2,32,3072]{3,2,1,0:T(8,128)(2,1)}, bf16[2,2,32,3072]{3,2,1,0:T(8,128)(2,1)}, u32[]{:S(2)}, u32[]{:S(2)}) collective-permute-start(bf16[2,2,32,3072]{3,2,1,0:T(8,128)(2,1)} %get-tuple-element.269), channel_id=1, source_target_pairs={{0,4},{1,5},{2,6},{3,7},{4,0},{5,1},{6,2},{7,3},{8,12},{9,13},{10,... | collective-permute-start | bytes 2359304 | tf_op jit(solution)/shard_map/ppermute | solution.py:748
  280.8 20.4 %collective-permute-start.56 = (bf16[2,768,384]{2,1,0:T(8,128)(2,1)}, bf16[2,768,384]{2,1,0:T(8,128)(2,1)S(1)}, u32[]{:S(2)}, u32[]{:S(2)}) collective-permute-start(bf16[2,768,384]{2,1,0:T(8,128)(2,1)} %get-tuple-element.263), channel_id=1, source_target_pairs={{0,1},{1,0},{2,3},{3,2},{4,5},{5,4},{6,7},{7,6},{8,9},{9,8},{10,11... | collective-permute-start | bytes 3538952 | tf_op jit(solution)/shard_map/ppermute | solution.py:748
  282.1 42.0 %collective-permute-start.78 = (bf16[1,3,128,768]{3,2,1,0:T(8,128)(2,1)}, bf16[1,3,128,768]{3,2,1,0:T(8,128)(2,1)}, u32[]{:S(2)}, u32[]{:S(2)}) collective-permute-start(bf16[1,3,128,768]{3,2,1,0:T(8,128)(2,1)} %constant_dynamic-slice_fusion.5), channel_id=1, source_target_pairs={{0,16},{1,17},{2,18},{3,19},{4,20},{5,21},{6,22},{7,23},{8,24},{9,... | collective-permute-start | bytes 1769480 | tf_op jit(solution)/shard_map/ppermute | solution.py:748
  298.2 53.7 %collective-permute-start.62 = (bf16[2,3,32,3072]{3,2,1,0:T(8,128)(2,1)}, bf16[2,3,32,3072]{3,2,1,0:T(8,128)(2,1)}, u32[]{:S(2)}, u32[]{:S(2)}) collective-permute-start(bf16[2,3,32,3072]{3,2,1,0:T(8,128)(2,1)} %get-tuple-element.282), channel_id=1, source_target_pairs={{0,4},{1,5},{2,6},{3,7},{4,0},{5,1},{6,2},{7,3},{8,12},{9,13},{10,... | collective-permute-start | bytes 3538952 | tf_op jit(solution)/shard_map/ppermute | solution.py:748
  303.2 22.8 %collective-permute-start.58 = (bf16[2,8,48,384]{3,2,1,0:T(8,128)(2,1)}, bf16[2,8,48,384]{3,2,1,0:T(8,128)(2,1)}, u32[]{:S(2)}, u32[]{:S(2)}) collective-permute-start(bf16[2,8,48,384]{3,2,1,0:T(8,128)(2,1)} %get-tuple-element.341), channel_id=1, source_target_pairs={{0,2},{1,3},{2,0},{3,1},{4,6},{5,7},{6,4},{7,5},{8,10},{9,11},{10,... | collective-permute-start | bytes 1769480 | tf_op jit(solution)/shard_map/ppermute | solution.py:748
  303.2 27.6 %collective-permute-start.54 = (bf16[2,8,48,384]{3,2,1,0:T(8,128)(2,1)}, bf16[2,8,48,384]{3,2,1,0:T(8,128)(2,1)}, u32[]{:S(2)}, u32[]{:S(2)}) collective-permute-start(bf16[2,8,48,384]{3,2,1,0:T(8,128)(2,1)} %get-tuple-element.339), channel_id=1, source_target_pairs={{0,2},{1,3},{2,0},{3,1},{4,6},{5,7},{6,4},{7,5},{8,10},{9,11},{10,... | collective-permute-start | bytes 1769480 | tf_op jit(solution)/shard_map/ppermute | solution.py:748
  324.1 35.7 %collective-permute-start.75 = (bf16[1,2,32,3072]{3,2,1,0:T(8,128)(2,1)}, bf16[1,2,32,3072]{3,2,1,0:T(8,128)(2,1)S(1)}, u32[]{:S(2)}, u32[]{:S(2)}) collective-permute-start(bf16[1,2,32,3072]{3,2,1,0:T(8,128)(2,1)} %constant_dynamic-slice_fusion.4), channel_id=1, source_target_pairs={{0,16},{1,17},{2,18},{3,19},{4,20},{5,21},{6,22},{7,23},{8,24},{9,... | collective-permute-start | bytes 1179656 | tf_op jit(solution)/shard_map/ppermute | solution.py:748
  327.4 27.1 %collective-permute-start.61 = (bf16[2,2,2,48,384]{4,3,0,1,2:T(8,128)(2,1)S(1)}, bf16[2,2,2,48,384]{4,3,0,1,2:T(8,128)(2,1)S(1)}, u32[]{:S(2)}, u32[]{:S(2)}) collective-permute-start(bf16[2,2,2,48,384]{4,3,0,1,2:T(8,128)(2,1)S(1)} %bitcast.104), channel_id=1, source_target_pairs={{0,8},{1,9},{2,10},{3,11},{4,12},{5,13},{6,14},{7,15},{8,0},{9,1},... | collective-permute-start | bytes 884744 | tf_op jit(solution)/shard_map/ppermute | solution.py:748
  330.8 21.1 %collective-permute-start.68 = (f32[64,128]{1,0:T(8,128)S(1)}, f32[64,128]{1,0:T(8,128)S(1)}, u32[]{:S(2)}, u32[]{:S(2)}) collective-permute-start(f32[64,128]{1,0:T(8,128)S(1)} %pad_bitcast_fusion), channel_id=1, source_target_pairs={{0,8},{1,9},{2,10},{3,11},{4,12},{5,13},{6,14},{7,15},{8,0},{9,1},... | collective-permute-start | bytes 98312 | tf_op jit(solution)/shard_map/ppermute | solution.py:748
  332.1 25.3 %collective-permute-start.57 = (bf16[2,2,2,48,384]{4,3,2,1,0:T(8,128)(2,1)S(1)}, bf16[2,2,2,48,384]{4,3,2,1,0:T(8,128)(2,1)S(1)}, u32[]{:S(2)}, u32[]{:S(2)}) collective-permute-start(bf16[2,2,2,48,384]{4,3,2,1,0:T(8,128)(2,1)S(1)} %dynamic-slice_bitcast_fusion.4), channel_id=1, source_target_pairs={{0,8},{1,9},{2,10},{3,11},{4,12},{5,13},{6,14},{7,15},{8,0},{9,1},... | collective-permute-start | bytes 884744 | tf_op jit(solution)/shard_map/ppermute | solution.py:748
  353.7 47.2 %collective-permute-start.74 = (bf16[1,3,32,3072]{3,2,1,0:T(8,128)(2,1)S(1)}, bf16[1,3,32,3072]{3,2,1,0:T(8,128)(2,1)S(1)}, u32[]{:S(2)}, u32[]{:S(2)}) collective-permute-start(bf16[1,3,32,3072]{3,2,1,0:T(8,128)(2,1)S(1)} %constant_dynamic-slice_fusion.1), channel_id=1, source_target_pairs={{0,16},{1,17},{2,18},{3,19},{4,20},{5,21},{6,22},{7,23},{8,24},{9,... | collective-permute-start | bytes 1769480 | tf_op jit(solution)/shard_map/ppermute | solution.py:748
  353.8 39.7 %collective-permute-start.66 = (bf16[2,1,32,3072]{3,2,1,0:T(8,128)(2,1)S(1)}, bf16[2,1,32,3072]{3,2,1,0:T(8,128)(2,1)S(1)}, u32[]{:S(2)}, u32[]{:S(2)}) collective-permute-start(bf16[2,1,32,3072]{3,2,1,0:T(8,128)(2,1)S(1)} %copy-done.56), channel_id=1, source_target_pairs={{0,4},{1,5},{2,6},{3,7},{4,0},{5,1},{6,2},{7,3},{8,12},{9,13},{10,... | collective-permute-start | bytes 1179656 | tf_op jit(solution)/shard_map/ppermute | solution.py:748
  368.1 42.1 %collective-permute-start.76 = (bf16[2,32,3072]{2,1,0:T(8,128)(2,1)S(1)}, bf16[2,32,3072]{2,1,0:T(8,128)(2,1)}, u32[]{:S(2)}, u32[]{:S(2)}) collective-permute-start(bf16[2,32,3072]{2,1,0:T(8,128)(2,1)S(1)} %fusion.14), channel_id=1, source_target_pairs={{0,8},{1,9},{2,10},{3,11},{4,12},{5,13},{6,14},{7,15},{8,0},{9,1},... | collective-permute-start | bytes 1179656 | tf_op jit(solution)/shard_map/ppermute | solution.py:748
  377.1 31.3 %collective-permute-start.79 = (bf16[3,128,768]{2,1,0:T(8,128)(2,1)S(1)}, bf16[3,128,768]{2,1,0:T(8,128)(2,1)S(1)}, u32[]{:S(2)}, u32[]{:S(2)}) collective-permute-start(bf16[3,128,768]{2,1,0:T(8,128)(2,1)S(1)} %copy-done.22), channel_id=1, source_target_pairs={{0,8},{1,9},{2,10},{3,11},{4,12},{5,13},{6,14},{7,15},{8,0},{9,1},... | collective-permute-start | bytes 1769480 | tf_op jit(solution)/shard_map/ppermute | solution.py:748
  (124 other events, 1061.2 us)

commit v3 on v2

--- a/solution.py
+++ b/solution.py
@@ -899,10 +899,10 @@
         return unit[0]
 
     plan_a, plan_b, plan_c = ((0, 0),), ((0, 1), (0, 2)), ((1, 0), (1, 1), (1, 2))
-    plan_d, plan_e, plan_f = ((0, 0), (0, 1)), ((0, 2), (1, 0), (1, 1)), ((1, 2),)
+    plan_d, plan_e, plan_f = ((0, 0), (0, 1)), ((0, 2), (1, 0)), ((1, 1), (1, 2))
     out_plans, in_plans = (plan_a, plan_b, plan_c), (plan_d, plan_e, plan_f)
 
-    grad_rows, grad_pre, parts = [], [], []
+    grad_rows, grad_pre = [], []
 
     def expert_back(pieces):
         if isinstance(pieces, list):
@@ -911,45 +911,39 @@
             grad_pre.append(grad_pre_rows)
             return grad_pre_rows, results
         grad_rows.append(pieces)
-        parts.extend(weight_part(sent, hidden, grad_rows, out_rows, out_plans, rest, width))
-        parts[0] = swap(parts[0], 1, 0)
-        pieces = after(pieces, parts[1])
         grad_pre_rows, _, results = expert_backward(pick, [pieces], w_in, w_out, slopes[1])
         grad_pre.append(grad_pre_rows)
-        return after(results, parts[0])
+        return results
 
     direct, relay = through(expert_back, sends)
-    got_a, send_b, send_c = parts
-    got_b = swap(after(send_b, relay[0]), 1, 0)
     back = weave(direct, relay)
-    grad_rows, grad_pre = lax.optimization_barrier((grad_rows, grad_pre, relay))[:2]
-    keep_a, keep_b, keep_c = weight_part(kept, hidden, grad_rows, out_rows, out_plans, rest, width)
-    away_a, stay_a = near_add(got_a, keep_a)
-    far_a = far_trade(away_a)
-    grad_pre = after(grad_pre, away_a)
-    send_d, send_e, send_f = weight_part(sent, rows_in, grad_pre, in_rows, in_plans, rest, inner // 2)
-    back = [after(part, send_d) for part in back]
-    got_c = swap(after(send_c, *back), 1, 0)
+    grad_rows = lax.optimization_barrier((grad_rows, relay))[0]
+    send_a, send_b, send_c = weight_part(sent, hidden, grad_rows, out_rows, out_plans, rest, width)
+    got_a = swap(send_a, 1, 0)
+    keep_a, keep_b, keep_c = weight_part(kept, hidden, after(grad_rows, send_a), out_rows, out_plans, rest, width)
+    back = [after(part, keep_a) for part in back]
+    got_b = swap(after(send_b, keep_a), 1, 0)
     grad_middle, grad_attn_proj, grad_attended, gain_moe_parts = collect(
         core_index, slots, back, middle, gain_moe, grad_logits, router, grad_y, mine, other
     )
-    away_b, stay_b = near_add(after(got_b, grad_attended), keep_b)
-    grad_attended, away_b, far_a = lax.optimization_barrier((grad_attended, away_b, far_a))
+    got_c = swap(after(send_c, grad_attended), 1, 0)
+    away_a, stay_a = near_add(after(got_a, grad_attended), keep_a)
+    far_a = far_trade(away_a)
+    grad_qkv_rows, bands = attention_backward(qkv_rows, after(grad_attended, away_a), probs)
+    grad_qkv_rows, got_b = lax.optimization_barrier((grad_qkv_rows, got_b))
+
+    away_b, stay_b = near_add(got_b, keep_b)
     far_b = far_trade(away_b)
+    *weights_away, stay_1, stay_2 = outer_halves(
+        core_index, normed1, attended, after(grad_qkv_rows, away_b), grad_attn_proj
+    )
+    weights_away = lax.optimization_barrier((weights_away, far_a))[0]
     done_a = finish(far_a, stay_a)
-    grad_qkv_rows, bands = attention_backward(qkv_rows, grad_attended, probs)
-    grad_qkv_rows, got_c = lax.optimization_barrier((grad_qkv_rows, got_c))
-
-    away_c, stay_c = near_add(got_c, keep_c)
+    send_d, send_e, send_f = weight_part(sent, rows_in, after(grad_pre, *weights_away), in_rows, in_plans, rest, inner // 2)
+    away_c, stay_c = near_add(after(got_c, send_d), keep_c)
     far_c = far_trade(away_c)
-    got_d = swap(after(send_d, away_c), 1, 0)
-    *weights_away, stay_1, stay_2 = outer_halves(
-        core_index, normed1, attended, after(grad_qkv_rows, far_b, away_c), grad_attn_proj
-    )
-    done_b = finish(far_b, stay_b)
-    keep_d, keep_e, keep_f = weight_part(
-        kept, rows_in, after(grad_pre, *weights_away), in_rows, in_plans, rest, inner // 2
-    )
+    got_d = swap(send_d, 1, 0)
+    got_e = swap(after(send_e, away_c), 1, 0)
     group_masks = bits(groups)[1:]
     dp_masks = sorted(bits(copies), key=lambda mask: (mask != PAIR, mask))
 
@@ -969,26 +963,28 @@
         return swap(away_part, mask, 0), stay_part
 
     weights_got = [swap(part, 0, 1) for part in weights_away]
-    first = over_groups(weights_got[0], stay_1, keep_d)
+    first = over_groups(weights_got[0], stay_1, away_c)
     second = over_groups(weights_got[1], stay_2, first[1])
+    keep_d, keep_e, keep_f = weight_part(
+        kept, rows_in, after(grad_pre, second[1]), in_rows, in_plans, rest, inner // 2
+    )
     grad_input, gain_attn_parts = enter(
-        core_index, after(grad_qkv_rows, second[1]), mine, other, tokens, gain_attn, grad_middle
+        core_index, after(grad_qkv_rows, keep_d), mine, other, tokens, gain_attn, grad_middle
     )
-    away_d, stay_d = near_add(after(got_d, second[1]), keep_d)
+    away_d, stay_d = near_add(after(got_d, gain_attn_parts), keep_d)
     far_d = far_trade(away_d)
-    got_e = swap(after(send_e, got_d), 1, 0)
-    done_c = finish(after(far_c, away_d), stay_c)
+    got_f = swap(after(send_f, away_d, gain_attn_parts), 1, 0)
+    done_b = finish(after(far_b, second[1]), stay_b)
     grad_table = table_gradient(after(bands, second[1]), position_bias_table.shape[1])
 
     chains = [add(after(first[0], away_d, gain_attn_parts), first[1]).reshape((2,) + (2,) * len(dp_masks) + (-1, columns)), None]
     trades = [over_dp(chains[0], dp_masks[0], ()), None]
-    chains[1] = add(after(second[0], done_c, grad_table), second[1]).reshape(chains[0].shape)
+    chains[1] = add(after(second[0], done_b, grad_table), second[1]).reshape(chains[0].shape)
     trades[1] = over_dp(chains[1], dp_masks[0], ())
     trades[0] = (after(trades[0][0], trades[1][1]), trades[0][1])
     total = trades[1][1]
     away_e, stay_e = near_add(after(got_e, total), keep_e)
     far_e = far_trade(away_e)
-    got_f = swap(after(send_f, away_e), 1, 0)
     trades[1] = (after(trades[1][0], away_e), trades[1][1])
 
     normed2, squares, gain_moe_parts = after((normed2, squares, gain_moe_parts), second[1])
@@ -1004,8 +1000,9 @@
     flat = jnp.concatenate([value.reshape(-1) for value in small])
     flat = after(jnp.pad(flat, (0, -sum(sizes) % 1024)).reshape(-1, 128), total)
 
+    flat = flat + swap(flat, 0, 1)
     for place, mask in enumerate(dp_masks):
-        flat_got = swap(flat, mask, 0)
+        flat_got = swap(flat, 0, group_masks[0]) if mask == PAIR else swap(flat, mask, 0)
         chains = [add(*trades[0]), None]
         if place + 1 < len(dp_masks):
             trades_next = [over_dp(chains[0], dp_masks[place + 1], dp_masks[: place + 1]), None]
@@ -1015,6 +1012,7 @@
             trades_next[1] = over_dp(chains[1], dp_masks[place + 1], dp_masks[: place + 1])
             trades = trades_next
         if mask == PAIR:
+            done_c = finish(after(far_c, chains[1]), stay_c)
             done_d = finish(after(far_d, chains[1]), stay_d)
             in_first = swap(done_d, PAIR, 0)
             out_theirs = swap(after(jnp.concatenate([done_a, done_b]), chains[1]), PAIR, 0)
@@ -1031,10 +1029,11 @@
         if mask == group_masks[0]:
             done_f = finish(after(far_f, total), stay_f)
             total = after(total, done_f)
-        flat = flat + swap(flat, 0, mask)
+            flat = flat + swap(flat, PAIR, 0)
+        else:
+            flat = flat + swap(flat, 0, mask)
         total, flat = lax.optimization_barrier((total, flat))
     other_part = swap(total, 0, 1)
-    flat = flat + swap(flat, 0, 1)
     total = jnp.concatenate([jnp.where(core == 0, total, other_part), jnp.where(core == 0, other_part, total)], axis=2)
     weights_done = total.astype(f32)
     grad_qkv, grad_out_weight = weights_done[:3], weights_done[3]

time: 422 us -> 440 us (1.043)
  waiting for transfers between devices: 104 us -> 111 us
  starting transfers between devices: 90.7 us -> 96.6 us
    ppermute x66, waiting for transfers between devices: 94.7 us -> 101 us  [swap(): return lax.ppermute(value, AXES, pairs)]
    ppermute x66, starting transfers between devices: 73.6 us -> 79.5 us  [swap(): return lax.ppermute(value, AXES, pairs)]
    unnamed x159 -> x169, local copies, waits for them, and re-layouts: 9.85 us -> 11.4 us
  transfers between devices with their start and end apart: 80 -> 80, of which waited for: 30 -> 25; matrix products, arithmetic and copies ran while one was open for 11% -> 11% of each run, Pallas kernels for 29% -> 32%
where the time goes in v3:
time: 440 us; the launch traced here: 435 us
  Pallas kernels  157 us (36%)
  waiting for transfers between devices  111 us (25%)
  starting transfers between devices  96.6 us (22%)
  local copies, waits for them, and re-layouts  30.2 us (7%)
  other arithmetic  26.4 us (6%)
  matrix products  8.44 us (2%)
  between operations  6.26 us (1%)
    ppermute x66, waiting for transfers between devices, swap(): return lax.ppermute(value, AXES, pairs)  101 us
    ppermute x66, starting transfers between devices, swap(): return lax.ppermute(value, AXES, pairs)  79.5 us
    pallas_call x4, Pallas kernels, weight_part(): pl.pallas_call(lambda *refs: weight_part_kernel(*refs, count=count, plans...  30.6 us
    pallas_call x2, Pallas kernels, expert_forward(): pl.pallas_call(lambda *refs: expert_forward_kernel(*refs, chunk=chunk, co...  27.5 us
    pallas_call x2, Pallas kernels, expert_backward(): pl.pallas_call(lambda *refs: expert_backward_kernel(*refs, chunk=chunk, c...  25.3 us
    ppermute x14, starting transfers between devices, gather_ring(): lax.ppermute(after(held, *due[step - 2:step - 1]) if step > 1 else held,...  17.1 us
    pallas_call x1, Pallas kernels, attention_forward(): pl.pallas_call(lambda *refs: attention_forward_kernel(*refs, heads=64, bl...  12.6 us
    pallas_call x1, Pallas kernels, attention_backward(): pl.pallas_call(lambda *refs: attention_backward_kernel(*refs, heads=64, b...  11.5 us
  transfers between devices with their start and end apart: 80, of which 25 were waited for; matrix products, arithmetic and copies ran while one was open for 11% of the time, Pallas kernels for 32%

profile of v3, /device:TPU:0, one launch (start us, length us, event | category | flops | bytes accessed | tf_op | source)
XLA Modules:
  0.0 435.4 jit_solution(3118077667379167688)
XLA Ops:
  1.7 3.1 collective-permute-start
  34.3 3.3 join.1.mine.refs_15_
  46.4 6.1 %project.1.refs_2_.refs_3_.refs_4_.refs_0_.refs_1_ = bf16[3,512,768]{2,1,0:T(8,128)(2,1)} custom-call(s32[1]{0:T(128)} %bitcast.2.core.refs_0_, bf16[512,768]{1,0:T(8,128)(2,1)} %fusion.6.rows.refs_1_, bf16[4,768,384]{2,1,0:T(8,128)(2,1)} %join.1.mine.refs_15_, bf16[4,768,384]{2,1,0:T(8,128)(2,1)} %copy-done), custom_call_target="tpu_custom_call" | custom-call | flops 1480000000 | tf_op jit(solution)/shard_map/project/pallas_call | solution.py:396
  54.7 12.6 %attention_forward.1 = (bf16[512,768]{1,0:T(8,128)(2,1)}, bf16[12,512,512]{2,1,0:T(8,128)(2,1)}) custom-call(f32[12]{0:T(128)} %slice_reduce_fusion.refs_0_, s32[1]{0:T(128)S(6)} %copy.105.refs_1_, bf16[3,512,768]{2,1,0:T(8,128)(2,1)} %project.1.refs_2_.refs_3_.refs_4_.refs_0_.refs_1_, bf16[3,512,768]{2,1,0:T(8,128)(2,1)} %project.1.refs_2_.refs_3_.refs_4_.refs_0_.refs_1_, ...), custom_call_target="tpu_custom_call" | custom-call | flops 4809999872 | tf_op jit(solution)/shard_map/attention_forward/pallas_call | solution.py:214
  67.3 5.9 %route.1 = (f32[512,768]{1,0:T(8,128)}, bf16[512,768]{1,0:T(8,128)(2,1)}, f32[512,2]{1,0:T(8,128)}, bf16[160,768]{1,0:T(8,128)(2,1)}, bf16[160,768]{1,0:T(8,128)...) custom-call(s32[1]{0:T(128)} %bitcast.2.core.refs_0_, ...), custom_call_target="tpu_custom_call" | custom-call | flops 2220000000 | tf_op jit(solution)/shard_map/route/pallas_call | solution.py:447
  79.6 3.8 collective-permute-done.18.refs_4_
  84.6 4.0 collective-permute-done.20.refs_2_
  90.9 13.7 %expert_forward.2 = (bf16[3072,640]{1,0:T(8,128)(2,1)}, bf16[640,3072]{1,0:T(8,128)(2,1)}, bf16[768,640]{1,0:T(8,128)(2,1)}, bf16[160,768]{1,0:T(8,128)(2,1)}, b...) custom-call(s32[1]{0:T(128)} %bitcast.4.refs_0_, ...), custom_call_target="tpu_custom_call" | custom-call | flops 4809999872 | tf_op jit(solution)/shard_map/expert_forward/pallas_call | solution.py:78
  105.6 4.2 collective-permute-start.27
  112.4 13.8 %expert_forward.3 = (bf16[3072,640]{1,0:T(8,128)(2,1)}, bf16[640,3072]{1,0:T(8,128)(2,1)}, bf16[768,640]{1,0:T(8,128)(2,1)}, bf16[640,768]{1,0:T(8,128)(2,1)}) custom-call(s32[1]{0:T(128)} %bitcast.4.refs_0_, bf16[640,768]{1,0:T(8,128)(2,1)} %copy-done.16, bf16[2,768,3072]{2,1,0:T(8,128)(2,1)} %refs_2_.3, bf16[2,3072,768]{2,1,0:T(8,128)(2,1)} %refs_3_.3), custom_call_target="tpu_custom_call" | custom-call | flops 4809999872 | tf_op jit(solution)/shard_map/expert_forward/pallas_call | solution.py:78
  136.8 5.9 %collective-permute-done.26 = f32[8,128]{1,0:T(8,128)S(1)} collective-permute-done((f32[8,128]{1,0:T(8,128)S(1)}, f32[8,128]{1,0:T(8,128)S(1)}, u32[]{:S(2)}, u32[]{:S(2)}) %collective-permute-start.26) | collective-permute-done | bytes 4128 | tf_op jit(solution)/shard_map/ppermute | solution.py:748
  145.3 8.5 %combine.1 = (bf16[512,768]{1,0:T(8,128)(2,1)}, f32[512,768]{1,0:T(8,128)}, bf16[512,8]{1,0:T(8,128)(2,1)}, f32[8,768]{1,0:T(8,128)}, bf16[160,768]{1,0:T(8,128)...) custom-call(s32[512,2]{1,0:T(8,128)} %copy-done.15, ...), custom_call_target="tpu_custom_call" | custom-call | flops 2960000000 | tf_op jit(solution)/shard_map/combine/pallas_call | solution.py:503
  155.6 2.8 collective-permute-start.35
  165.5 6.5 %collective-permute-done.36.refs_4_ = bf16[160,768]{1,0:T(8,128)(2,1)S(1)} collective-permute-done((bf16[160,768]{1,0:T(8,128)(2,1)}, bf16[160,768]{1,0:T(8,128)(2,1)S(1)}, u32[]{:S(2)}, u32[]{:S(2)}) %collective-permute-start.36) | collective-permute-done | bytes 245792 | tf_op jit(solution)/shard_map/ppermute | solution.py:748
  172.7 12.5 %expert_backward.2 = (bf16[640,3072]{1,0:T(8,128)(2,1)}, bf16[640,768]{1,0:T(8,128)(2,1)}, bf16[160,768]{1,0:T(8,128)(2,1)}, bf16[160,768]{1,0:T(8,128)(2,1)}, b...) custom-call(s32[1]{0:T(128)} %bitcast.4.refs_0_, bf16[160,768]{1,0:T(8,128)(2,1)} %get-tuple-element.197.refs_1_, ...), custom_call_target="tpu_custom_call" | custom-call | flops 4070000128 | tf_op jit(solution)/shard_map/expert_backward/pallas_call | solution.py:135
  190.7 12.8 %expert_backward.3 = (bf16[640,3072]{1,0:T(8,128)(2,1)}, bf16[640,768]{1,0:T(8,128)(2,1)}, bf16[640,768]{1,0:T(8,128)(2,1)}) custom-call(s32[1]{0:T(128)} %bitcast.4.refs_0_, bf16[640,768]{1,0:T(8,128)(2,1)} %copy-done.1, bf16[2,768,3072]{2,1,0:T(8,128)(2,1)} %refs_2_.3, bf16[2,3072,768]{2,1,0:T(8,128)(2,1)} %refs_3_.3, ...), custom_call_target="tpu_custom_call" | custom-call | flops 4070000128 | tf_op jit(solution)/shard_map/expert_backward/pallas_call | solution.py:135
  210.7 7.7 %weight_part.4 = (bf16[2,1,128,768]{3,2,1,0:T(8,128)(2,1)}, bf16[2,2,128,768]{3,2,1,0:T(8,128)(2,1)}, bf16[2,3,128,768]{3,2,1,0:T(8,128)(2,1)}) custom-call(s32[4]{0:T(128)} %get-tuple-element.360.refs_0_, bf16[3072,640]{1,0:T(8,128)(2,1)} %get-tuple-element.179.refs_1_.refs_2_.refs_3_.refs_4_, ...), custom_call_target="tpu_custom_call" | custom-call | flops 1480000000 | tf_op jit(solution)/shard_map/weight_part/pallas_call | solution.py:337
  219.0 7.8 %weight_part.5 = (bf16[2,1,128,768]{3,2,1,0:T(8,128)(2,1)}, bf16[2,2,128,768]{3,2,1,0:T(8,128)(2,1)}, bf16[2,3,128,768]{3,2,1,0:T(8,128)(2,1)}) custom-call(s32[4]{0:T(128)} %get-tuple-element.359.refs_0_, bf16[3072,640]{1,0:T(8,128)(2,1)} %get-tuple-element.179.refs_1_.refs_2_.refs_3_.refs_4_, ...), custom_call_target="tpu_custom_call" | custom-call | flops 1480000000 | tf_op jit(solution)/shard_map/weight_part/pallas_call | solution.py:337
  229.2 8.5 %collect.1 = (f32[512,768]{1,0:T(8,128)}, bf16[512,768]{1,0:T(8,128)(2,1)}, bf16[512,768]{1,0:T(8,128)(2,1)}, f32[8,768]{1,0:T(8,128)}) custom-call(s32[1]{0:T(128)} %bitcast.2.core.refs_0_, s32[512,2]{1,0:T(8,128)} %copy-done.15, bf16[160,768]{1,0:T(8,128)(2,1)} %get-tuple-element.227.refs_2_, bf16[160,768]{1,0:T(8,128)(2,1)} %get-tuple-element.228.refs_3_, ...), custom_call_target="tpu_custom_call" | custom-call | flops 2960000000 | tf_op jit(solution)/shard_map/collect/pallas_call | solution.py:554
  239.1 11.5 %attention_backward.1 = (bf16[3,512,768]{2,1,0:T(8,128)(2,1)}, f32[12,4,128,128]{3,2,1,0:T(8,128)}) custom-call(bf16[3,512,768]{2,1,0:T(8,128)(2,1)} %project.1.refs_2_.refs_3_.refs_4_.refs_0_.refs_1_, bf16[3,512,768]{2,1,0:T(8,128)(2,1)} %project.1.refs_2_.refs_3_.refs_4_.refs_0_.refs_1_, ...), custom_call_target="tpu_custom_call" | custom-call | flops 4440000000 | tf_op jit(solution)/shard_map/attention_backward/pallas_call | solution.py:280
  251.8 8.3 %outer_halves.1 = (bf16[2,768,384]{2,1,0:T(8,128)(2,1)}, bf16[2,768,384]{2,1,0:T(8,128)(2,1)}, bf16[2,768,384]{2,1,0:T(8,128)(2,1)}, bf16[2,768,384]{2,1,0:T(8,128)(2,1)}) custom-call(s32[1]{0:T(128)} %bitcast.2.core.refs_0_, bf16[512,768]{1,0:T(8,128)(2,1)} %fusion.6.rows.refs_1_, bf16[512,768]{1,0:T(8,128)(2,1)} %get-tuple-element.171.attended.refs_2_, ...), custom_call_target="tpu_custom_call" | custom-call | flops 2220000000 | tf_op jit(solution)/shard_map/outer_halves/pallas_call | solution.py:604
  265.3 7.6 %weight_part.6 = (bf16[2,2,32,3072]{3,2,1,0:T(8,128)(2,1)}, bf16[2,2,32,3072]{3,2,1,0:T(8,128)(2,1)}, bf16[2,2,32,3072]{3,2,1,0:T(8,128)(2,1)}) custom-call(s32[4]{0:T(128)} %get-tuple-element.360.refs_0_, bf16[768,640]{1,0:T(8,128)(2,1)} %get-tuple-element.254.refs_1_.refs_2_.refs_3_.refs_4_, ...), custom_call_target="tpu_custom_call" | custom-call | flops 1480000000 | tf_op jit(solution)/shard_map/weight_part/pallas_call | solution.py:337
  281.7 15.2 %collective-permute-done.58 = bf16[1,2,128,768]{3,2,1,0:T(8,128)(2,1)S(1)} collective-permute-done((bf16[1,2,128,768]{3,2,1,0:T(8,128)(2,1)S(1)}, bf16[1,2,128,768]{3,2,1,0:T(8,128)(2,1)S(1)}, u32[]{:S(2)}, u32[]{:S(2)}) %collective-permute-start.58) | collective-permute-done | bytes 393248 | tf_op jit(solution)/shard_map/ppermute | solution.py:748
  297.4 7.5 %weight_part.7 = (bf16[2,2,32,3072]{3,2,1,0:T(8,128)(2,1)}, bf16[2,2,32,3072]{3,2,1,0:T(8,128)(2,1)}, bf16[2,2,32,3072]{3,2,1,0:T(8,128)(2,1)}) custom-call(s32[4]{0:T(128)} %get-tuple-element.359.refs_0_, bf16[768,640]{1,0:T(8,128)(2,1)} %get-tuple-element.254.refs_1_.refs_2_.refs_3_.refs_4_, ...), custom_call_target="tpu_custom_call" | custom-call | flops 1480000000 | tf_op jit(solution)/shard_map/weight_part/pallas_call | solution.py:337
  304.9 8.4 %enter.1 = (f32[512,768]{1,0:T(8,128)}, f32[8,768]{1,0:T(8,128)}) custom-call(s32[1]{0:T(128)} %bitcast.2.core.refs_0_, bf16[3,512,768]{2,1,0:T(8,128)(2,1)} %get-tuple-element.270.refs_3_.grads, bf16[4,768,384]{2,1,0:T(8,128)(2,1)} %join.1.mine.refs_15_, bf16[4,768,384]{2,1,0:T(8,128)(2,1)} %copy-done, bf16[512,768]{1,0:T(8,128)(2,1)} %tokens.3, ...), custom_call_target="tpu_custom_call" | custom-call | flops 2220000000 | tf_op jit(solution)/shard_map/enter/pallas_call | solution.py:650
  322.0 6.3 %fusion.10 = f32[12,32]{1,0:T(8,128)S(1)} fusion(s32[4,128,128]{2,1,0:T(8,128)} %pad_add_fusion, f32[12,4,128,128]{3,2,1,0:T(8,128)S(1)} %copy-done.3), kind=kOutput, calls=%fused_computation.31 | convolution fusion | flops 304087040 | bytes 3409408 | tf_op jit(solution)/shard_map/hdxy,dxyb->hb/dot_general | solution.py:704
  344.2 6.1 %collective-permute-done.56 = bf16[2,2,2,48,384]{4,3,2,1,0:T(8,128)(2,1)S(1)} collective-permute-done((bf16[2,2,2,48,384]{4,3,2,1,0:T(8,128)(2,1)S(1)}, bf16[2,2,2,48,384]{4,3,2,1,0:T(8,128)(2,1)S(1)}, u32[]{:S(2)}, u32[]{:S(2)}) %collective-permute-start.56) | collective-permute-done | bytes 294944 | tf_op jit(solution)/shard_map/ppermute | solution.py:748
  354.2 16.8 %collective-permute-done.75 = bf16[1,2,32,3072]{3,2,1,0:T(8,128)(2,1)S(1)} collective-permute-done((bf16[1,2,32,3072]{3,2,1,0:T(8,128)(2,1)S(1)}, bf16[1,2,32,3072]{3,2,1,0:T(8,128)(2,1)S(1)}, u32[]{:S(2)}, u32[]{:S(2)}) %collective-permute-start.75) | collective-permute-done | bytes 393248 | tf_op jit(solution)/shard_map/ppermute | solution.py:748
  381.0 18.7 %collective-permute-done.71 = f32[64,128]{1,0:T(8,128)S(1)} collective-permute-done((f32[64,128]{1,0:T(8,128)S(1)}, f32[64,128]{1,0:T(8,128)S(1)}, u32[]{:S(2)}, u32[]{:S(2)}) %collective-permute-start.71) | collective-permute-done | bytes 32800 | tf_op jit(solution)/shard_map/ppermute | solution.py:748
  399.7 2.9 collective-permute-start.64
  402.7 10.4 %collective-permute-done.64 = bf16[2,48,384]{2,1,0:T(8,128)(2,1)S(1)} collective-permute-done((bf16[2,48,384]{2,1,0:T(8,128)(2,1)S(1)}, bf16[2,48,384]{2,1,0:T(8,128)(2,1)S(1)}, u32[]{:S(2)}, u32[]{:S(2)}) %collective-permute-start.64) | collective-permute-done | bytes 73760 | tf_op jit(solution)/shard_map/ppermute | solution.py:748
  414.6 3.8 collective-permute-start.72
  (432 shorter events, 162.1 us)
Async XLA Ops:
  76.8 27.9 %collective-permute-start.24 = (bf16[160,768]{1,0:T(8,128)(2,1)}, bf16[160,768]{1,0:T(8,128)(2,1)S(1)}, u32[]{:S(2)}, u32[]{:S(2)}) collective-permute-start(bf16[160,768]{1,0:T(8,128)(2,1)} %get-tuple-element.185), channel_id=1, source_target_pairs={{0,10},{1,11},{2,8},{3,9},{4,14},{5,15},{6,12},{7,13},{8,2},{9,3},... | collective-permute-start | bytes 737288 | tf_op jit(solution)/shard_map/ppermute | solution.py:748
  79.1 25.6 %collective-permute-start.23 = (bf16[160,768]{1,0:T(8,128)(2,1)}, bf16[160,768]{1,0:T(8,128)(2,1)S(1)}, u32[]{:S(2)}, u32[]{:S(2)}) collective-permute-start(bf16[160,768]{1,0:T(8,128)(2,1)} %get-tuple-element.183), channel_id=1, source_target_pairs={{0,8},{1,9},{2,10},{3,11},{4,12},{5,13},{6,14},{7,15},{8,0},{9,1},... | collective-permute-start | bytes 737288 | tf_op jit(solution)/shard_map/ppermute | solution.py:748
  83.3 21.4 %collective-permute-start.22 = (bf16[160,768]{1,0:T(8,128)(2,1)}, bf16[160,768]{1,0:T(8,128)(2,1)S(1)}, u32[]{:S(2)}, u32[]{:S(2)}) collective-permute-start(bf16[160,768]{1,0:T(8,128)(2,1)} %get-tuple-element.181), channel_id=1, source_target_pairs={{0,2},{1,3},{2,0},{3,1},{4,6},{5,7},{6,4},{7,5},{8,10},{9,11},{10,... | collective-permute-start | bytes 737288 | tf_op jit(solution)/shard_map/ppermute | solution.py:748
  105.6 20.6 %collective-permute-start.27 = (bf16[160,768]{1,0:T(8,128)(2,1)S(1)}, bf16[160,768]{1,0:T(8,128)(2,1)S(1)}, u32[]{:S(2)}, u32[]{:S(2)}) collective-permute-start(bf16[160,768]{1,0:T(8,128)(2,1)S(1)} %copy-done.73), channel_id=1, source_target_pairs={{0,2},{1,3},{2,0},{3,1},{4,6},{5,7},{6,4},{7,5},{8,10},{9,11},{10,... | collective-permute-start | bytes 737288 | tf_op jit(solution)/shard_map/ppermute | solution.py:748
  159.6 25.6 %collective-permute-start.39 = (bf16[160,768]{1,0:T(8,128)(2,1)}, bf16[160,768]{1,0:T(8,128)(2,1)S(1)}, u32[]{:S(2)}, u32[]{:S(2)}) collective-permute-start(bf16[160,768]{1,0:T(8,128)(2,1)} %get-tuple-element.213), channel_id=1, source_target_pairs={{0,10},{1,11},{2,8},{3,9},{4,14},{5,15},{6,12},{7,13},{8,2},{9,3},... | collective-permute-start | bytes 737288 | tf_op jit(solution)/shard_map/ppermute | solution.py:748
  161.3 23.9 %collective-permute-start.38 = (bf16[160,768]{1,0:T(8,128)(2,1)}, bf16[160,768]{1,0:T(8,128)(2,1)S(1)}, u32[]{:S(2)}, u32[]{:S(2)}) collective-permute-start(bf16[160,768]{1,0:T(8,128)(2,1)} %get-tuple-element.211), channel_id=1, source_target_pairs={{0,8},{1,9},{2,10},{3,11},{4,12},{5,13},{6,14},{7,15},{8,0},{9,1},... | collective-permute-start | bytes 737288 | tf_op jit(solution)/shard_map/ppermute | solution.py:748
  161.6 23.6 %collective-permute-start.37 = (bf16[160,768]{1,0:T(8,128)(2,1)}, bf16[160,768]{1,0:T(8,128)(2,1)S(1)}, u32[]{:S(2)}, u32[]{:S(2)}) collective-permute-start(bf16[160,768]{1,0:T(8,128)(2,1)} %get-tuple-element.209), channel_id=1, source_target_pairs={{0,2},{1,3},{2,0},{3,1},{4,6},{5,7},{6,4},{7,5},{8,10},{9,11},{10,... | collective-permute-start | bytes 737288 | tf_op jit(solution)/shard_map/ppermute | solution.py:748
  186.2 17.4 %collective-permute-start.41 = (bf16[160,768]{1,0:T(8,128)(2,1)S(1)}, bf16[160,768]{1,0:T(8,128)(2,1)S(1)}, u32[]{:S(2)}, u32[]{:S(2)}) collective-permute-start(bf16[160,768]{1,0:T(8,128)(2,1)S(1)} %copy-done.64), channel_id=1, source_target_pairs={{0,2},{1,3},{2,0},{3,1},{4,6},{5,7},{6,4},{7,5},{8,10},{9,11},{10,... | collective-permute-start | bytes 737288 | tf_op jit(solution)/shard_map/ppermute | solution.py:748
  186.5 17.1 %collective-permute-start.42 = (bf16[160,768]{1,0:T(8,128)(2,1)S(1)}, bf16[160,768]{1,0:T(8,128)(2,1)S(1)}, u32[]{:S(2)}, u32[]{:S(2)}) collective-permute-start(bf16[160,768]{1,0:T(8,128)(2,1)S(1)} %copy-done.63), channel_id=1, source_target_pairs={{0,8},{1,9},{2,10},{3,11},{4,12},{5,13},{6,14},{7,15},{8,0},{9,1},... | collective-permute-start | bytes 737288 | tf_op jit(solution)/shard_map/ppermute | solution.py:748
  207.2 21.1 %collective-permute-start.45 = (bf16[160,768]{1,0:T(8,128)(2,1)S(1)}, bf16[160,768]{1,0:T(8,128)(2,1)S(1)}, u32[]{:S(2)}, u32[]{:S(2)}) collective-permute-start(bf16[160,768]{1,0:T(8,128)(2,1)S(1)} %get-tuple-element.343), channel_id=1, source_target_pairs={{0,2},{1,3},{2,0},{3,1},{4,6},{5,7},{6,4},{7,5},{8,10},{9,11},{10,... | collective-permute-start | bytes 737288 | tf_op jit(solution)/shard_map/ppermute | solution.py:748
  207.7 20.6 %collective-permute-start.46 = (bf16[160,768]{1,0:T(8,128)(2,1)S(1)}, bf16[160,768]{1,0:T(8,128)(2,1)S(1)}, u32[]{:S(2)}, u32[]{:S(2)}) collective-permute-start(bf16[160,768]{1,0:T(8,128)(2,1)S(1)} %get-tuple-element.342), channel_id=1, source_target_pairs={{0,8},{1,9},{2,10},{3,11},{4,12},{5,13},{6,14},{7,15},{8,0},{9,1},... | collective-permute-start | bytes 737288 | tf_op jit(solution)/shard_map/ppermute | solution.py:748
  209.5 18.9 %collective-permute-start.47 = (bf16[160,768]{1,0:T(8,128)(2,1)S(1)}, bf16[160,768]{1,0:T(8,128)(2,1)S(1)}, u32[]{:S(2)}, u32[]{:S(2)}) collective-permute-start(bf16[160,768]{1,0:T(8,128)(2,1)S(1)} %get-tuple-element.341), channel_id=1, source_target_pairs={{0,10},{1,11},{2,8},{3,9},{4,14},{5,15},{6,12},{7,13},{8,2},{9,3},... | collective-permute-start | bytes 737288 | tf_op jit(solution)/shard_map/ppermute | solution.py:748
  218.4 19.9 %collective-permute-start.48 = (bf16[2,1,128,768]{3,2,1,0:T(8,128)(2,1)}, bf16[2,1,128,768]{3,2,1,0:T(8,128)(2,1)S(1)}, u32[]{:S(2)}, u32[]{:S(2)}) collective-permute-start(bf16[2,1,128,768]{3,2,1,0:T(8,128)(2,1)} %get-tuple-element.223), channel_id=1, source_target_pairs={{0,4},{1,5},{2,6},{3,7},{4,0},{5,1},{6,2},{7,3},{8,12},{9,13},{10,... | collective-permute-start | bytes 1179656 | tf_op jit(solution)/shard_map/ppermute | solution.py:748
  226.8 23.8 %collective-permute-start.49 = (bf16[2,2,128,768]{3,2,1,0:T(8,128)(2,1)S(1)}, bf16[2,2,128,768]{3,2,1,0:T(8,128)(2,1)S(1)}, u32[]{:S(2)}, u32[]{:S(2)}) collective-permute-start(bf16[2,2,128,768]{3,2,1,0:T(8,128)(2,1)S(1)} %copy-done.61), channel_id=1, source_target_pairs={{0,4},{1,5},{2,6},{3,7},{4,0},{5,1},{6,2},{7,3},{8,12},{9,13},{10,... | collective-permute-start | bytes 2359304 | tf_op jit(solution)/shard_map/ppermute | solution.py:748
  237.8 36.7 %collective-permute-start.52 = (bf16[2,3,128,768]{3,2,1,0:T(8,128)(2,1)S(1)}, bf16[2,3,128,768]{3,2,1,0:T(8,128)(2,1)S(1)}, u32[]{:S(2)}, u32[]{:S(2)}) collective-permute-start(bf16[2,3,128,768]{3,2,1,0:T(8,128)(2,1)S(1)} %copy-done.60), channel_id=1, source_target_pairs={{0,4},{1,5},{2,6},{3,7},{4,0},{5,1},{6,2},{7,3},{8,12},{9,13},{10,... | collective-permute-start | bytes 3538952 | tf_op jit(solution)/shard_map/ppermute | solution.py:748
  238.5 21.6 %collective-permute-start.50 = (bf16[1,1,128,768]{3,2,1,0:T(8,128)(2,1)S(1)}, bf16[1,1,128,768]{3,2,1,0:T(8,128)(2,1)S(1)}, u32[]{:S(2)}, u32[]{:S(2)}) collective-permute-start(bf16[1,1,128,768]{3,2,1,0:T(8,128)(2,1)S(1)} %constant_dynamic-slice_fusion.7), channel_id=1, source_target_pairs={{0,16},{1,17},{2,18},{3,19},{4,20},{5,21},{6,22},{7,23},{8,24},{9,... | collective-permute-start | bytes 589832 | tf_op jit(solution)/shard_map/ppermute | solution.py:748
  262.9 33.9 %collective-permute-start.58 = (bf16[1,2,128,768]{3,2,1,0:T(8,128)(2,1)S(1)}, bf16[1,2,128,768]{3,2,1,0:T(8,128)(2,1)S(1)}, u32[]{:S(2)}, u32[]{:S(2)}) collective-permute-start(bf16[1,2,128,768]{3,2,1,0:T(8,128)(2,1)S(1)} %constant_dynamic-slice_fusion.6), channel_id=1, source_target_pairs={{0,16},{1,17},{2,18},{3,19},{4,20},{5,21},{6,22},{7,23},{8,24},{9,... | collective-permute-start | bytes 1179656 | tf_op jit(solution)/shard_map/ppermute | solution.py:748
  272.9 40.4 %collective-permute-start.54 = (bf16[2,2,32,3072]{3,2,1,0:T(8,128)(2,1)}, bf16[2,2,32,3072]{3,2,1,0:T(8,128)(2,1)S(1)}, u32[]{:S(2)}, u32[]{:S(2)}) collective-permute-start(bf16[2,2,32,3072]{3,2,1,0:T(8,128)(2,1)} %get-tuple-element.260), channel_id=1, source_target_pairs={{0,4},{1,5},{2,6},{3,7},{4,0},{5,1},{6,2},{7,3},{8,12},{9,13},{10,... | collective-permute-start | bytes 2359304 | tf_op jit(solution)/shard_map/ppermute | solution.py:748
  275.6 95.5 %collective-permute-start.78 = (bf16[1,3,128,768]{3,2,1,0:T(8,128)(2,1)}, bf16[1,3,128,768]{3,2,1,0:T(8,128)(2,1)}, u32[]{:S(2)}, u32[]{:S(2)}) collective-permute-start(bf16[1,3,128,768]{3,2,1,0:T(8,128)(2,1)} %constant_dynamic-slice_fusion.5), channel_id=1, source_target_pairs={{0,16},{1,17},{2,18},{3,19},{4,20},{5,21},{6,22},{7,23},{8,24},{9,... | collective-permute-start | bytes 1769480 | tf_op jit(solution)/shard_map/ppermute | solution.py:748
  276.2 56.3 %collective-permute-start.62 = (bf16[2,2,32,3072]{3,2,1,0:T(8,128)(2,1)}, bf16[2,2,32,3072]{3,2,1,0:T(8,128)(2,1)}, u32[]{:S(2)}, u32[]{:S(2)}) collective-permute-start(bf16[2,2,32,3072]{3,2,1,0:T(8,128)(2,1)} %get-tuple-element.281), channel_id=1, source_target_pairs={{0,4},{1,5},{2,6},{3,7},{4,0},{5,1},{6,2},{7,3},{8,12},{9,13},{10,... | collective-permute-start | bytes 2359304 | tf_op jit(solution)/shard_map/ppermute | solution.py:748
  280.3 50.7 %collective-permute-start.57 = (bf16[2,8,48,384]{3,2,1,0:T(8,128)(2,1)}, bf16[2,8,48,384]{3,2,1,0:T(8,128)(2,1)}, u32[]{:S(2)}, u32[]{:S(2)}) collective-permute-start(bf16[2,8,48,384]{3,2,1,0:T(8,128)(2,1)} %get-tuple-element.339), channel_id=1, source_target_pairs={{0,2},{1,3},{2,0},{3,1},{4,6},{5,7},{6,4},{7,5},{8,10},{9,11},{10,... | collective-permute-start | bytes 1769480 | tf_op jit(solution)/shard_map/ppermute | solution.py:748
  296.9 35.6 %collective-permute-start.53 = (bf16[2,8,48,384]{3,2,1,0:T(8,128)(2,1)}, bf16[2,8,48,384]{3,2,1,0:T(8,128)(2,1)}, u32[]{:S(2)}, u32[]{:S(2)}) collective-permute-start(bf16[2,8,48,384]{3,2,1,0:T(8,128)(2,1)} %get-tuple-element.337), channel_id=1, source_target_pairs={{0,2},{1,3},{2,0},{3,1},{4,6},{5,7},{6,4},{7,5},{8,10},{9,11},{10,... | collective-permute-start | bytes 1769480 | tf_op jit(solution)/shard_map/ppermute | solution.py:748
  317.3 33.9 %collective-permute-start.66 = (bf16[2,2,32,3072]{3,2,1,0:T(8,128)(2,1)}, bf16[2,2,32,3072]{3,2,1,0:T(8,128)(2,1)}, u32[]{:S(2)}, u32[]{:S(2)}) collective-permute-start(bf16[2,2,32,3072]{3,2,1,0:T(8,128)(2,1)} %get-tuple-element.289), channel_id=1, source_target_pairs={{0,4},{1,5},{2,6},{3,7},{4,0},{5,1},{6,2},{7,3},{8,12},{9,13},{10,... | collective-permute-start | bytes 2359304 | tf_op jit(solution)/shard_map/ppermute | solution.py:748
  341.2 29.8 %collective-permute-start.75 = (bf16[1,2,32,3072]{3,2,1,0:T(8,128)(2,1)S(1)}, bf16[1,2,32,3072]{3,2,1,0:T(8,128)(2,1)S(1)}, u32[]{:S(2)}, u32[]{:S(2)}) collective-permute-start(bf16[1,2,32,3072]{3,2,1,0:T(8,128)(2,1)S(1)} %copy-done.25), channel_id=1, source_target_pairs={{0,16},{1,17},{2,18},{3,19},{4,20},{5,21},{6,22},{7,23},{8,24},{9,... | collective-permute-start | bytes 1179656 | tf_op jit(solution)/shard_map/ppermute | solution.py:748
  342.4 72.2 %collective-permute-start.74 = (bf16[1,2,32,3072]{3,2,1,0:T(8,128)(2,1)S(1)}, bf16[1,2,32,3072]{3,2,1,0:T(8,128)(2,1)S(1)}, u32[]{:S(2)}, u32[]{:S(2)}) collective-permute-start(bf16[1,2,32,3072]{3,2,1,0:T(8,128)(2,1)S(1)} %constant_dynamic-slice_fusion.1), channel_id=1, source_target_pairs={{0,16},{1,17},{2,18},{3,19},{4,20},{5,21},{6,22},{7,23},{8,24},{9,... | collective-permute-start | bytes 1179656 | tf_op jit(solution)/shard_map/ppermute | solution.py:748
  350.6 27.4 %collective-permute-start.63 = (bf16[2,2,48,384]{3,2,0,1:T(8,128)(2,1)S(1)}, bf16[2,2,48,384]{3,2,0,1:T(8,128)(2,1)S(1)}, u32[]{:S(2)}, u32[]{:S(2)}) collective-permute-start(bf16[2,2,48,384]{3,2,0,1:T(8,128)(2,1)S(1)} %dynamic-slice_bitcast_fusion.5), channel_id=1, source_target_pairs={{0,4},{1,5},{2,6},{3,7},{4,0},{5,1},{6,2},{7,3},{8,12},{9,13},{10,... | collective-permute-start | bytes 442376 | tf_op jit(solution)/shard_map/ppermute | solution.py:748
  351.2 26.6 %collective-permute-start.59 = (bf16[2,2,48,384]{3,2,1,0:T(8,128)(2,1)S(1)}, bf16[2,2,48,384]{3,2,1,0:T(8,128)(2,1)S(1)}, u32[]{:S(2)}, u32[]{:S(2)}) collective-permute-start(bf16[2,2,48,384]{3,2,1,0:T(8,128)(2,1)S(1)} %dynamic-slice_bitcast_fusion.6), channel_id=1, source_target_pairs={{0,4},{1,5},{2,6},{3,7},{4,0},{5,1},{6,2},{7,3},{8,12},{9,13},{10,... | collective-permute-start | bytes 442376 | tf_op jit(solution)/shard_map/ppermute | solution.py:748
  371.0 51.6 %collective-permute-start.67 = (bf16[1,2,32,3072]{3,2,1,0:T(8,128)(2,1)S(1)}, bf16[1,2,32,3072]{3,2,1,0:T(8,128)(2,1)S(1)}, u32[]{:S(2)}, u32[]{:S(2)}) collective-permute-start(bf16[1,2,32,3072]{3,2,1,0:T(8,128)(2,1)S(1)} %constant_dynamic-slice_fusion), channel_id=1, source_target_pairs={{0,16},{1,17},{2,18},{3,19},{4,20},{5,21},{6,22},{7,23},{8,24},{9,... | collective-permute-start | bytes 1179656 | tf_op jit(solution)/shard_map/ppermute | solution.py:748
  375.1 51.1 %collective-permute-start.76 = (bf16[2,32,3072]{2,1,0:T(8,128)(2,1)S(1)}, bf16[2,32,3072]{2,1,0:T(8,128)(2,1)}, u32[]{:S(2)}, u32[]{:S(2)}) collective-permute-start(bf16[2,32,3072]{2,1,0:T(8,128)(2,1)S(1)} %fusion.16), channel_id=1, source_target_pairs={{0,8},{1,9},{2,10},{3,11},{4,12},{5,13},{6,14},{7,15},{8,0},{9,1},... | collective-permute-start | bytes 1179656 | tf_op jit(solution)/shard_map/ppermute | solution.py:748
  378.0 21.7 %collective-permute-start.60 = (bf16[2,48,384]{2,1,0:T(8,128)(2,1)S(1)}, bf16[2,48,384]{2,1,0:T(8,128)(2,1)S(1)}, u32[]{:S(2)}, u32[]{:S(2)}) collective-permute-start(bf16[2,48,384]{2,1,0:T(8,128)(2,1)S(1)} %dynamic-slice_bitcast_fusion.8), channel_id=1, source_target_pairs={{0,16},{1,17},{2,18},{3,19},{4,20},{5,21},{6,22},{7,23},{8,24},{9,... | collective-permute-start | bytes 221192 | tf_op jit(solution)/shard_map/ppermute | solution.py:748
  378.3 21.4 %collective-permute-start.71 = (f32[64,128]{1,0:T(8,128)S(1)}, f32[64,128]{1,0:T(8,128)S(1)}, u32[]{:S(2)}, u32[]{:S(2)}) collective-permute-start(f32[64,128]{1,0:T(8,128)S(1)} %add.657), channel_id=1, source_target_pairs={{0,16},{1,17},{2,18},{3,19},{4,20},{5,21},{6,22},{7,23},{8,24},{9,... | collective-permute-start | bytes 98312 | tf_op jit(solution)/shard_map/ppermute | solution.py:748
  399.7 29.8 %collective-permute-start.79 = (bf16[3,128,768]{2,1,0:T(8,128)(2,1)S(1)}, bf16[3,128,768]{2,1,0:T(8,128)(2,1)S(1)}, u32[]{:S(2)}, u32[]{:S(2)}) collective-permute-start(bf16[3,128,768]{2,1,0:T(8,128)(2,1)S(1)} %pad_maximum_fusion.6), channel_id=1, source_target_pairs={{0,8},{1,9},{2,10},{3,11},{4,12},{5,13},{6,14},{7,15},{8,0},{9,1},... | collective-permute-start | bytes 1769480 | tf_op jit(solution)/shard_map/ppermute | solution.py:748
  (129 other events, 1071.5 us)

commit v4 on v2

--- a/solution.py
+++ b/solution.py
@@ -45,7 +45,7 @@
 def expert_forward_kernel(pick, *refs, chunk, count):
     pieces, w_in, w_out = refs[:count], refs[count], refs[count + 1]
     hidden_t, slope, rows_t = refs[count + 2 : count + 5]
-    outs, rows, total = refs[count + 5 : 2 * count + 5], refs[2 * count + 5], refs[2 * count + 6]
+    outs, rows, total = refs[count + 5 : -2], refs[-2], refs[-1]
     step = pl.program_id(0)
 
     @pl.when(step == 0)
@@ -71,7 +71,7 @@
         hand_out(total, outs)
 
 
-def expert_forward(pick, pieces, w_in, w_out, tile=768, chunk=320):
+def expert_forward(pick, pieces, results, w_in, w_out, tile=768, chunk=320):
     many, width = sum(piece.shape[0] for piece in pieces), pieces[0].shape[1]
     inner = w_in.shape[2]
     bf16 = jnp.bfloat16
@@ -90,7 +90,7 @@
                 pl.BlockSpec((many, tile), lambda f, pick: (0, f)),
                 whole((width, many)),
             ]
-            + [whole(piece.shape) for piece in pieces],
+            + [whole((many // results, width))] * results,
             scratch_shapes=[pltpu.VMEM((many, width), bf16), pltpu.VMEM((many, width), jnp.float32)],
         ),
         out_shape=[
@@ -98,7 +98,7 @@
             jax.ShapeDtypeStruct((many, inner), bf16),
             jax.ShapeDtypeStruct((width, many), bf16),
         ]
-        + [jax.ShapeDtypeStruct(piece.shape, bf16) for piece in pieces],
+        + [jax.ShapeDtypeStruct((many // results, width), bf16)] * results,
         compiler_params=pltpu.CompilerParams(vmem_limit_bytes=VMEM_BYTES),
         cost_estimate=cost(13),
         name="expert_forward",
@@ -108,7 +108,7 @@
 def expert_backward_kernel(pick, *refs, chunk, count):
     pieces, w_in, w_out, slope = refs[:count], refs[count], refs[count + 1], refs[count + 2]
     grad_pre, rows = refs[count + 3 : count + 5]
-    outs, total = refs[count + 5 : 2 * count + 5], refs[2 * count + 5]
+    outs, total = refs[count + 5 : -1], refs[-1]
     step = pl.program_id(0)
 
     @pl.when(step == 0)
@@ -128,7 +128,7 @@
         hand_out(total, outs)
 
 
-def expert_backward(pick, pieces, w_in, w_out, slope, tile=768, chunk=640):
+def expert_backward(pick, pieces, results, w_in, w_out, slope, tile=768, chunk=640):
     many, width = sum(piece.shape[0] for piece in pieces), pieces[0].shape[1]
     inner = w_in.shape[2]
     bf16 = jnp.bfloat16
@@ -144,11 +144,11 @@
                 pl.BlockSpec((many, tile), lambda f, pick: (0, f)),
             ],
             out_specs=[pl.BlockSpec((many, tile), lambda f, pick: (0, f)), whole((many, width))]
-            + [whole(piece.shape) for piece in pieces],
+            + [whole((many // results, width))] * results,
             scratch_shapes=[pltpu.VMEM((many, width), jnp.float32)],
         ),
         out_shape=[jax.ShapeDtypeStruct((many, inner), bf16), jax.ShapeDtypeStruct((many, width), bf16)]
-        + [jax.ShapeDtypeStruct(piece.shape, bf16) for piece in pieces],
+        + [jax.ShapeDtypeStruct((many // results, width), bf16)] * results,
         compiler_params=pltpu.CompilerParams(vmem_limit_bytes=VMEM_BYTES),
         cost_estimate=cost(11),
         name="expert_backward",
@@ -771,9 +771,7 @@
         direct = to_chips(direct)
         relay = [after(part, seen) for part in relay]
         passed = visit(swap(jnp.concatenate(relay), 0, 1))
-        passed = swap(after(passed, *direct), 0, 1)
-        relay = [passed[place * capacity : (place + 1) * capacity] for place in range(chips)]
-        return direct, relay
+        return direct, [swap(after(part, *direct), 0, 1) for part in passed]
 
     def weave(direct, relay):
         return [part for pair in zip(direct, to_chips(relay)) for part in pair]
@@ -849,11 +847,11 @@
     def expert(pieces):
         one = not isinstance(pieces, list)
         pieces = [pieces] if one else pieces
-        hidden_t, slope, rows_t, *results = expert_forward(pick, pieces, w_in, w_out)
+        hidden_t, slope, rows_t, *results = expert_forward(pick, pieces, chips, w_in, w_out)
         hidden_t = count_beside(pieces[-1], hidden_t)
         for kept, value in zip((hidden, slopes, rows_in), (hidden_t, slope, rows_t)):
             kept.append(value)
-        return results[0] if one else (hidden_t, results)
+        return results if one else (hidden_t, results)
 
     back = weave(*through(expert, sends))
     while len(counts) <= len(count_trades):
@@ -898,15 +896,15 @@
             unit = add(swap(away_part, mask, 0), stay_part)
         return unit[0]
 
-    plan_a, plan_b, plan_c = ((0, 0),), ((0, 1), (0, 2)), ((1, 0), (1, 1), (1, 2))
-    plan_d, plan_e, plan_f = ((0, 0), (0, 1)), ((0, 2), (1, 0), (1, 1)), ((1, 2),)
+    plan_a, plan_b, plan_c = ((0, 0), (0, 1)), ((0, 2), (1, 0)), ((1, 1), (1, 2))
+    plan_d, plan_e, plan_f = plan_a, plan_b, plan_c
     out_plans, in_plans = (plan_a, plan_b, plan_c), (plan_d, plan_e, plan_f)
 
     grad_rows, grad_pre, parts = [], [], []
 
     def expert_back(pieces):
         if isinstance(pieces, list):
-            grad_pre_rows, grads, *results = expert_backward(pick, pieces, w_in, w_out, slopes[0])
+            grad_pre_rows, grads, *results = expert_backward(pick, pieces, chips, w_in, w_out, slopes[0])
             grad_rows.append(grads)
             grad_pre.append(grad_pre_rows)
             return grad_pre_rows, results
@@ -914,26 +912,27 @@
         parts.extend(weight_part(sent, hidden, grad_rows, out_rows, out_plans, rest, width))
         parts[0] = swap(parts[0], 1, 0)
         pieces = after(pieces, parts[1])
-        grad_pre_rows, _, results = expert_backward(pick, [pieces], w_in, w_out, slopes[1])
+        grad_pre_rows, _, *results = expert_backward(pick, [pieces], chips, w_in, w_out, slopes[1])
         grad_pre.append(grad_pre_rows)
-        return after(results, parts[0])
+        return results
 
     direct, relay = through(expert_back, sends)
     got_a, send_b, send_c = parts
+    relay = [after(part, got_a) for part in relay]
     got_b = swap(after(send_b, relay[0]), 1, 0)
     back = weave(direct, relay)
     grad_rows, grad_pre = lax.optimization_barrier((grad_rows, grad_pre, relay))[:2]
     keep_a, keep_b, keep_c = weight_part(kept, hidden, grad_rows, out_rows, out_plans, rest, width)
     away_a, stay_a = near_add(got_a, keep_a)
     far_a = far_trade(away_a)
-    grad_pre = after(grad_pre, away_a)
-    send_d, send_e, send_f = weight_part(sent, rows_in, grad_pre, in_rows, in_plans, rest, inner // 2)
+    send_d, send_e, send_f = weight_part(sent, rows_in, after(grad_pre, away_a), in_rows, in_plans, rest, inner // 2)
     back = [after(part, send_d) for part in back]
-    got_c = swap(after(send_c, *back), 1, 0)
+    got_c = swap(after(send_c, send_d), 1, 0)
     grad_middle, grad_attn_proj, grad_attended, gain_moe_parts = collect(
         core_index, slots, back, middle, gain_moe, grad_logits, router, grad_y, mine, other
     )
     away_b, stay_b = near_add(after(got_b, grad_attended), keep_b)
+    got_d = swap(after(send_d, grad_attended), 1, 0)
     grad_attended, away_b, far_a = lax.optimization_barrier((grad_attended, away_b, far_a))
     far_b = far_trade(away_b)
     done_a = finish(far_a, stay_a)
@@ -942,11 +941,12 @@
 
     away_c, stay_c = near_add(got_c, keep_c)
     far_c = far_trade(away_c)
-    got_d = swap(after(send_d, away_c), 1, 0)
     *weights_away, stay_1, stay_2 = outer_halves(
-        core_index, normed1, attended, after(grad_qkv_rows, far_b, away_c), grad_attn_proj
+        core_index, normed1, attended, after(grad_qkv_rows, away_c), grad_attn_proj
     )
+    weights_away, far_b, got_d = lax.optimization_barrier((weights_away, far_b, got_d))
     done_b = finish(far_b, stay_b)
+    got_e = swap(after(send_e, got_d), 1, 0)
     keep_d, keep_e, keep_f = weight_part(
         kept, rows_in, after(grad_pre, *weights_away), in_rows, in_plans, rest, inner // 2
     )
@@ -971,25 +971,26 @@
     weights_got = [swap(part, 0, 1) for part in weights_away]
     first = over_groups(weights_got[0], stay_1, keep_d)
     second = over_groups(weights_got[1], stay_2, first[1])
-    grad_input, gain_attn_parts = enter(
-        core_index, after(grad_qkv_rows, second[1]), mine, other, tokens, gain_attn, grad_middle
-    )
     away_d, stay_d = near_add(after(got_d, second[1]), keep_d)
     far_d = far_trade(away_d)
-    got_e = swap(after(send_e, got_d), 1, 0)
-    done_c = finish(after(far_c, away_d), stay_c)
+    grad_input, gain_attn_parts = enter(
+        core_index, after(grad_qkv_rows, away_d), mine, other, tokens, gain_attn, grad_middle
+    )
+    done_c = finish(after(far_c, gain_attn_parts), stay_c)
     grad_table = table_gradient(after(bands, second[1]), position_bias_table.shape[1])
 
     chains = [add(after(first[0], away_d, gain_attn_parts), first[1]).reshape((2,) + (2,) * len(dp_masks) + (-1, columns)), None]
     trades = [over_dp(chains[0], dp_masks[0], ()), None]
-    chains[1] = add(after(second[0], done_c, grad_table), second[1]).reshape(chains[0].shape)
-    trades[1] = over_dp(chains[1], dp_masks[0], ())
-    trades[0] = (after(trades[0][0], trades[1][1]), trades[0][1])
-    total = trades[1][1]
-    away_e, stay_e = near_add(after(got_e, total), keep_e)
+    away_e, stay_e = near_add(after(got_e, chains[0]), keep_e)
     far_e = far_trade(away_e)
     got_f = swap(after(send_f, away_e), 1, 0)
-    trades[1] = (after(trades[1][0], away_e), trades[1][1])
+    chains[1] = add(after(second[0], done_c, grad_table, away_e), second[1]).reshape(chains[0].shape)
+    trades[1] = over_dp(chains[1], dp_masks[0], ())
+    total = trades[1][1]
+    done_d = finish(after(far_d, chains[0]), stay_d)
+    away_f, stay_f = near_add(after(got_f, total), keep_f)
+    far_f = far_trade(away_f)
+    trades = [(after(trades[0][0], total, done_d), trades[0][1]), (after(trades[1][0], away_f), trades[1][1])]
 
     normed2, squares, gain_moe_parts = after((normed2, squares, gain_moe_parts), second[1])
     grad_router = jnp.einsum("td,te->de", normed2, grad_logits, preferred_element_type=f32)
@@ -1004,8 +1005,12 @@
     flat = jnp.concatenate([value.reshape(-1) for value in small])
     flat = after(jnp.pad(flat, (0, -sum(sizes) % 1024)).reshape(-1, 128), total)
 
+    flat = flat + swap(flat, 0, 1)
     for place, mask in enumerate(dp_masks):
-        flat_got = swap(flat, mask, 0)
+        flat_got = swap(flat, 0, group_masks[0]) if mask == PAIR else swap(flat, mask, 0)
+        if place == 1:
+            done_e = finish(far_e, stay_e)
+            trades[1] = (after(trades[1][0], done_e), trades[1][1])
         chains = [add(*trades[0]), None]
         if place + 1 < len(dp_masks):
             trades_next = [over_dp(chains[0], dp_masks[place + 1], dp_masks[: place + 1]), None]
@@ -1015,14 +1020,10 @@
             trades_next[1] = over_dp(chains[1], dp_masks[place + 1], dp_masks[: place + 1])
             trades = trades_next
         if mask == PAIR:
-            done_d = finish(after(far_d, chains[1]), stay_d)
             in_first = swap(done_d, PAIR, 0)
-            out_theirs = swap(after(jnp.concatenate([done_a, done_b]), chains[1]), PAIR, 0)
-            away_f, stay_f = near_add(after(got_f, chains[1]), keep_f)
-            far_f = far_trade(away_f)
+            out_theirs = swap(after(jnp.concatenate([done_a, done_b[:1]]), chains[1]), PAIR, 0)
         flat = after(flat, chains[1])
     total = jnp.concatenate(chains)
-    done_e = finish(after(far_e, total), stay_e)
     in_theirs = jnp.concatenate([in_first, swap(done_e[:1], PAIR, 0)])
     for mask in reversed(group_masks):
         bit = (here_group // mask) % 2
@@ -1031,10 +1032,11 @@
         if mask == group_masks[0]:
             done_f = finish(after(far_f, total), stay_f)
             total = after(total, done_f)
-        flat = flat + swap(flat, 0, mask)
+            flat = flat + swap(flat, PAIR, 0)
+        else:
+            flat = flat + swap(flat, 0, mask)
         total, flat = lax.optimization_barrier((total, flat))
     other_part = swap(total, 0, 1)
-    flat = flat + swap(flat, 0, 1)
     total = jnp.concatenate([jnp.where(core == 0, total, other_part), jnp.where(core == 0, other_part, total)], axis=2)
     weights_done = total.astype(f32)
     grad_qkv, grad_out_weight = weights_done[:3], weights_done[3]
@@ -1044,7 +1046,7 @@
         flat[start : start + value.size].reshape(value.shape) for start, value in zip(starts, small)
     ]
 
-    out_mine, in_mine = done_c, jnp.concatenate([done_e[1:], done_f])
+    out_mine, in_mine = jnp.concatenate([done_b[1:], done_c]), jnp.concatenate([done_e[1:], done_f])
 
     def both_experts(mine, theirs):
         mine, theirs = [part.reshape(-1, part.shape[-1]).astype(f32) for part in (mine, theirs)]

time: 422 us -> 421 us (level)
    ppermute x66 -> x72, waiting for transfers between devices: 94.7 us -> 96.6 us  [swap(): return lax.ppermute(value, AXES, pairs)]
    ppermute x66 -> x72, starting transfers between devices: 73.6 us -> 72.5 us  [swap(): return lax.ppermute(value, AXES, pairs)]
    unnamed x159 -> x157, local copies, waits for them, and re-layouts: 9.85 us -> 9.16 us
  transfers between devices with their start and end apart: 80 -> 86, of which waited for: 30 -> 30; matrix products, arithmetic and copies ran while one was open for 11% -> 11% of each run, Pallas kernels for 29% -> 32%
where the time goes in v4:
time: 421 us; the launch traced here: 416 us
  Pallas kernels  157 us (37%)
  waiting for transfers between devices  105 us (25%)
  starting transfers between devices  89.6 us (21%)
  local copies, waits for them, and re-layouts  26.1 us (6%)
  other arithmetic  25.5 us (6%)
  matrix products  6.29 us (1%)
  between operations  6.11 us (1%)
    ppermute x72, waiting for transfers between devices, swap(): return lax.ppermute(value, AXES, pairs)  96.6 us
    ppermute x72, starting transfers between devices, swap(): return lax.ppermute(value, AXES, pairs)  72.5 us
    pallas_call x4, Pallas kernels, weight_part(): pl.pallas_call(lambda *refs: weight_part_kernel(*refs, count=count, plans...  30.9 us
    pallas_call x2, Pallas kernels, expert_forward(): pl.pallas_call(lambda *refs: expert_forward_kernel(*refs, chunk=chunk, co...  27.4 us
    pallas_call x2, Pallas kernels, expert_backward(): pl.pallas_call(lambda *refs: expert_backward_kernel(*refs, chunk=chunk, c...  25.4 us
    ppermute x14, starting transfers between devices, gather_ring(): lax.ppermute(after(held, *due[step - 2:step - 1]) if step > 1 else held,...  17.1 us
    pallas_call x1, Pallas kernels, attention_forward(): pl.pallas_call(lambda *refs: attention_forward_kernel(*refs, heads=64, bl...  12.7 us
    pallas_call x1, Pallas kernels, attention_backward(): pl.pallas_call(lambda *refs: attention_backward_kernel(*refs, heads=64, b...  11.5 us
  transfers between devices with their start and end apart: 86, of which 30 were waited for; matrix products, arithmetic and copies ran while one was open for 11% of the time, Pallas kernels for 32%

profile of v4, /device:TPU:0, one launch (start us, length us, event | category | flops | bytes accessed | tf_op | source)
XLA Modules:
  0.0 416.2 jit_solution(4014900945906308402)
XLA Ops:
  34.3 3.3 join.1.mine.refs_15_
  46.4 6.4 %project.1.refs_2_.refs_3_.refs_4_.refs_0_.refs_1_ = bf16[3,512,768]{2,1,0:T(8,128)(2,1)} custom-call(s32[1]{0:T(128)} %bitcast.2.core.refs_0_, bf16[512,768]{1,0:T(8,128)(2,1)} %fusion.6.rows.refs_1_, bf16[4,768,384]{2,1,0:T(8,128)(2,1)} %join.1.mine.refs_15_, bf16[4,768,384]{2,1,0:T(8,128)(2,1)} %copy-done), custom_call_target="tpu_custom_call" | custom-call | flops 1480000000 | tf_op jit(solution)/shard_map/project/pallas_call | solution.py:396
  55.0 12.7 %attention_forward.1 = (bf16[512,768]{1,0:T(8,128)(2,1)}, bf16[12,512,512]{2,1,0:T(8,128)(2,1)}) custom-call(f32[12]{0:T(128)} %slice_reduce_fusion.refs_0_, s32[1]{0:T(128)S(6)} %copy.105.refs_1_, bf16[3,512,768]{2,1,0:T(8,128)(2,1)} %project.1.refs_2_.refs_3_.refs_4_.refs_0_.refs_1_, bf16[3,512,768]{2,1,0:T(8,128)(2,1)} %project.1.refs_2_.refs_3_.refs_4_.refs_0_.refs_1_, ...), custom_call_target="tpu_custom_call" | custom-call | flops 4809999872 | tf_op jit(solution)/shard_map/attention_forward/pallas_call | solution.py:214
  67.7 5.9 %route.1 = (f32[512,768]{1,0:T(8,128)}, bf16[512,768]{1,0:T(8,128)(2,1)}, f32[512,2]{1,0:T(8,128)}, bf16[160,768]{1,0:T(8,128)(2,1)}, bf16[160,768]{1,0:T(8,128)...) custom-call(s32[1]{0:T(128)} %bitcast.2.core.refs_0_, ...), custom_call_target="tpu_custom_call" | custom-call | flops 2220000000 | tf_op jit(solution)/shard_map/route/pallas_call | solution.py:447
  80.0 3.8 collective-permute-done.18.refs_4_
  85.0 4.0 collective-permute-done.20.refs_2_
  91.3 13.6 %expert_forward.2 = (bf16[3072,640]{1,0:T(8,128)(2,1)}, bf16[640,3072]{1,0:T(8,128)(2,1)}, bf16[768,640]{1,0:T(8,128)(2,1)}, bf16[160,768]{1,0:T(8,128)(2,1)}, b...) custom-call(s32[1]{0:T(128)} %bitcast.4.refs_0_, ...), custom_call_target="tpu_custom_call" | custom-call | flops 4809999872 | tf_op jit(solution)/shard_map/expert_forward/pallas_call | solution.py:78
  105.9 4.2 %collective-permute-start.27 = (bf16[160,768]{1,0:T(8,128)(2,1)S(1)}, bf16[160,768]{1,0:T(8,128)(2,1)S(1)}, u32[]{:S(2)}, u32[]{:S(2)}) collective-permute-start(bf16[160,768]{1,0:T(8,128)(2,1)S(1)} %copy-done.70), channel_id=1, source_target_pairs={{0,2},{1,3},{2,0},{3,1},{4,6},{5,7},{6,4},{7,5},{8,10},{9,11},{10,... | collective-permute-start | bytes 737288 | tf_op jit(solution)/shard_map/ppermute | solution.py:748
  112.7 13.8 %expert_forward.3 = (bf16[3072,640]{1,0:T(8,128)(2,1)}, bf16[640,3072]{1,0:T(8,128)(2,1)}, bf16[768,640]{1,0:T(8,128)(2,1)}, bf16[160,768]{1,0:T(8,128)(2,1)}, b...) custom-call(s32[1]{0:T(128)} %bitcast.4.refs_0_, bf16[640,768]{1,0:T(8,128)(2,1)} %copy-done.8, ...), custom_call_target="tpu_custom_call" | custom-call | flops 4809999872 | tf_op jit(solution)/shard_map/expert_forward/pallas_call | solution.py:78
  135.5 5.6 %collective-permute-done.26 = f32[8,128]{1,0:T(8,128)S(1)} collective-permute-done((f32[8,128]{1,0:T(8,128)S(1)}, f32[8,128]{1,0:T(8,128)S(1)}, u32[]{:S(2)}, u32[]{:S(2)}) %collective-permute-start.26) | collective-permute-done | bytes 4128 | tf_op jit(solution)/shard_map/ppermute | solution.py:748
  144.1 8.5 %combine.1 = (bf16[512,768]{1,0:T(8,128)(2,1)}, f32[512,768]{1,0:T(8,128)}, bf16[512,8]{1,0:T(8,128)(2,1)}, f32[8,768]{1,0:T(8,128)}, bf16[160,768]{1,0:T(8,128)...) custom-call(s32[512,2]{1,0:T(8,128)} %multiply_add_fusion.refs_0_.re, ...), custom_call_target="tpu_custom_call" | custom-call | flops 2960000000 | tf_op jit(solution)/shard_map/combine/pallas_call | solution.py:503
  154.0 3.2 collective-permute-start.38
  164.3 6.2 %collective-permute-done.39.refs_4_ = bf16[160,768]{1,0:T(8,128)(2,1)S(1)} collective-permute-done((bf16[160,768]{1,0:T(8,128)(2,1)}, bf16[160,768]{1,0:T(8,128)(2,1)S(1)}, u32[]{:S(2)}, u32[]{:S(2)}) %collective-permute-start.39) | collective-permute-done | bytes 245792 | tf_op jit(solution)/shard_map/ppermute | solution.py:748
  171.2 12.5 %expert_backward.2 = (bf16[640,3072]{1,0:T(8,128)(2,1)}, bf16[640,768]{1,0:T(8,128)(2,1)}, bf16[160,768]{1,0:T(8,128)(2,1)}, bf16[160,768]{1,0:T(8,128)(2,1)}, b...) custom-call(s32[1]{0:T(128)} %bitcast.4.refs_0_, bf16[160,768]{1,0:T(8,128)(2,1)} %get-tuple-element.222.refs_1_, ...), custom_call_target="tpu_custom_call" | custom-call | flops 4070000128 | tf_op jit(solution)/shard_map/expert_backward/pallas_call | solution.py:135
  187.4 7.8 %weight_part.4 = (bf16[2,2,128,768]{3,2,1,0:T(8,128)(2,1)}, bf16[2,2,128,768]{3,2,1,0:T(8,128)(2,1)}, bf16[2,2,128,768]{3,2,1,0:T(8,128)(2,1)}) custom-call(s32[4]{0:T(128)} %pad_add_fusion.1.refs_0_, bf16[3072,640]{1,0:T(8,128)(2,1)} %get-tuple-element.198.refs_1_.refs_2_.refs_3_.refs_4_, ...), custom_call_target="tpu_custom_call" | custom-call | flops 1480000000 | tf_op jit(solution)/shard_map/weight_part/pallas_call | solution.py:337
  199.4 12.9 %expert_backward.3 = (bf16[640,3072]{1,0:T(8,128)(2,1)}, bf16[640,768]{1,0:T(8,128)(2,1)}, bf16[160,768]{1,0:T(8,128)(2,1)}, bf16[160,768]{1,0:T(8,128)(2,1)}, b...) custom-call(s32[1]{0:T(128)} %bitcast.4.refs_0_, bf16[640,768]{1,0:T(8,128)(2,1)} %copy-done.1, ...), custom_call_target="tpu_custom_call" | custom-call | flops 4070000128 | tf_op jit(solution)/shard_map/expert_backward/pallas_call | solution.py:135
  220.3 7.8 %weight_part.5 = (bf16[2,2,128,768]{3,2,1,0:T(8,128)(2,1)}, bf16[2,2,128,768]{3,2,1,0:T(8,128)(2,1)}, bf16[2,2,128,768]{3,2,1,0:T(8,128)(2,1)}) custom-call(s32[4]{0:T(128)} %pad_add_fusion.2.refs_0_, bf16[3072,640]{1,0:T(8,128)(2,1)} %get-tuple-element.198.refs_1_.refs_2_.refs_3_.refs_4_, ...), custom_call_target="tpu_custom_call" | custom-call | flops 1480000000 | tf_op jit(solution)/shard_map/weight_part/pallas_call | solution.py:337
  229.5 7.7 %weight_part.6 = (bf16[2,2,32,3072]{3,2,1,0:T(8,128)(2,1)}, bf16[2,2,32,3072]{3,2,1,0:T(8,128)(2,1)}, bf16[2,2,32,3072]{3,2,1,0:T(8,128)(2,1)}) custom-call(s32[4]{0:T(128)} %pad_add_fusion.1.refs_0_, bf16[768,640]{1,0:T(8,128)(2,1)} %get-tuple-element.228.refs_1_.refs_2_.refs_3_.refs_4_, ...), custom_call_target="tpu_custom_call" | custom-call | flops 1480000000 | tf_op jit(solution)/shard_map/weight_part/pallas_call | solution.py:337
  239.1 8.5 %collect.1 = (f32[512,768]{1,0:T(8,128)}, bf16[512,768]{1,0:T(8,128)(2,1)}, bf16[512,768]{1,0:T(8,128)(2,1)}, f32[8,768]{1,0:T(8,128)}) custom-call(s32[1]{0:T(128)} %bitcast.2.core.refs_0_, s32[512,2]{1,0:T(8,128)} %multiply_add_fusion.refs_0_.refs_1_, bf16[160,768]{1,0:T(8,128)(2,1)} %get-tuple-element.270.refs_2_, bf16[160,768]{1,0:T(8,128)(2,1)} %copy-done.57, ...), custom_call_target="tpu_custom_call" | custom-call | flops 2960000000 | tf_op jit(solution)/shard_map/collect/pallas_call | solution.py:554
  249.3 7.5 %collective-permute-done.56 = bf16[1,2,128,768]{3,2,1,0:T(8,128)(2,1)S(1)} collective-permute-done((bf16[1,2,128,768]{3,2,1,0:T(8,128)(2,1)S(1)}, bf16[1,2,128,768]{3,2,1,0:T(8,128)(2,1)S(1)}, u32[]{:S(2)}, u32[]{:S(2)}) %collective-permute-start.56) | collective-permute-done | bytes 393248 | tf_op jit(solution)/shard_map/ppermute | solution.py:748
  256.8 11.5 %attention_backward.1 = (bf16[3,512,768]{2,1,0:T(8,128)(2,1)}, f32[12,4,128,128]{3,2,1,0:T(8,128)}) custom-call(bf16[3,512,768]{2,1,0:T(8,128)(2,1)} %project.1.refs_2_.refs_3_.refs_4_.refs_0_.refs_1_, bf16[3,512,768]{2,1,0:T(8,128)(2,1)} %project.1.refs_2_.refs_3_.refs_4_.refs_0_.refs_1_, ...), custom_call_target="tpu_custom_call" | custom-call | flops 4440000000 | tf_op jit(solution)/shard_map/attention_backward/pallas_call | solution.py:280
  269.5 8.2 %outer_halves.1 = (bf16[2,768,384]{2,1,0:T(8,128)(2,1)}, bf16[2,768,384]{2,1,0:T(8,128)(2,1)}, bf16[2,768,384]{2,1,0:T(8,128)(2,1)}, bf16[2,768,384]{2,1,0:T(8,128)(2,1)}) custom-call(s32[1]{0:T(128)} %bitcast.2.core.refs_0_, bf16[512,768]{1,0:T(8,128)(2,1)} %fusion.6.rows.refs_1_, bf16[512,768]{1,0:T(8,128)(2,1)} %get-tuple-element.190.attended.refs_2_, ...), custom_call_target="tpu_custom_call" | custom-call | flops 2220000000 | tf_op jit(solution)/shard_map/outer_halves/pallas_call | solution.py:604
  277.6 9.7 %collective-permute-done.58 = bf16[1,2,128,768]{3,2,1,0:T(8,128)(2,1)S(1)} collective-permute-done((bf16[1,2,128,768]{3,2,1,0:T(8,128)(2,1)S(1)}, bf16[1,2,128,768]{3,2,1,0:T(8,128)(2,1)S(1)}, u32[]{:S(2)}, u32[]{:S(2)}) %collective-permute-start.58) | collective-permute-done | bytes 393248 | tf_op jit(solution)/shard_map/ppermute | solution.py:748
  291.2 7.6 %weight_part.7 = (bf16[2,2,32,3072]{3,2,1,0:T(8,128)(2,1)}, bf16[2,2,32,3072]{3,2,1,0:T(8,128)(2,1)}, bf16[2,2,32,3072]{3,2,1,0:T(8,128)(2,1)}) custom-call(s32[4]{0:T(128)} %pad_add_fusion.2.refs_0_, bf16[768,640]{1,0:T(8,128)(2,1)} %get-tuple-element.228.refs_1_.refs_2_.refs_3_.refs_4_, ...), custom_call_target="tpu_custom_call" | custom-call | flops 1480000000 | tf_op jit(solution)/shard_map/weight_part/pallas_call | solution.py:337
  308.5 5.3 %fusion.10 = f32[12,32]{1,0:T(8,128)S(1)} fusion(s32[4,128,128]{2,1,0:T(8,128)S(1)} %pad_add_fusion, f32[12,4,128,128]{3,2,1,0:T(8,128)S(1)} %copy-done.3), kind=kOutput, calls=%fused_computation.31 | convolution fusion | flops 304087040 | bytes 3409408 | tf_op jit(solution)/shard_map/hdxy,dxyb->hb/dot_general | solution.py:704
  313.8 8.3 %enter.1 = (f32[512,768]{1,0:T(8,128)}, f32[8,768]{1,0:T(8,128)}) custom-call(s32[1]{0:T(128)} %bitcast.2.core.refs_0_, bf16[3,512,768]{2,1,0:T(8,128)(2,1)} %get-tuple-element.309.refs_3_.grads, bf16[4,768,384]{2,1,0:T(8,128)(2,1)} %join.1.mine.refs_15_, bf16[4,768,384]{2,1,0:T(8,128)(2,1)} %copy-done, bf16[512,768]{1,0:T(8,128)(2,1)} %tokens.3, ...), custom_call_target="tpu_custom_call" | custom-call | flops 2220000000 | tf_op jit(solution)/shard_map/enter/pallas_call | solution.py:650
  325.7 8.3 %collective-permute-done.61 = bf16[2,8,48,384]{3,2,1,0:T(8,128)(2,1)} collective-permute-done((bf16[2,8,48,384]{3,2,1,0:T(8,128)(2,1)}, bf16[2,8,48,384]{3,2,1,0:T(8,128)(2,1)}, u32[]{:S(2)}, u32[]{:S(2)}) %collective-permute-start.61) | collective-permute-done | bytes 589856 | tf_op jit(solution)/shard_map/ppermute | solution.py:748
  347.6 15.4 %collective-permute-done.63 = bf16[2,2,2,48,384]{4,3,2,1,0:T(8,128)(2,1)S(1)} collective-permute-done((bf16[2,2,2,48,384]{4,3,2,1,0:T(8,128)(2,1)S(1)}, bf16[2,2,2,48,384]{4,3,2,1,0:T(8,128)(2,1)S(1)}, u32[]{:S(2)}, u32[]{:S(2)}) %collective-permute-start.63) | collective-permute-done | bytes 294944 | tf_op jit(solution)/shard_map/ppermute | solution.py:748
  365.8 4.0 collective-permute-done.68
  376.9 6.7 %collective-permute-done.69 = bf16[2,48,384]{2,1,0:T(8,128)(2,1)S(1)} collective-permute-done((bf16[2,48,384]{2,1,0:T(8,128)(2,1)S(1)}, bf16[2,48,384]{2,1,0:T(8,128)(2,1)S(1)}, u32[]{:S(2)}, u32[]{:S(2)}) %collective-permute-start.69) | collective-permute-done | bytes 73760 | tf_op jit(solution)/shard_map/ppermute | solution.py:748
  389.2 3.8 collective-permute-done.80
  403.3 6.8 %collective-permute-done.85 = bf16[3,128,768]{2,1,0:T(8,128)(2,1)} collective-permute-done((bf16[3,128,768]{2,1,0:T(8,128)(2,1)S(1)}, bf16[3,128,768]{2,1,0:T(8,128)(2,1)}, u32[]{:S(2)}, u32[]{:S(2)}) %collective-permute-start.85) | collective-permute-done | bytes 589856 | tf_op jit(solution)/shard_map/ppermute | solution.py:748
  (430 shorter events, 158.6 us)
Async XLA Ops:
  77.2 27.9 %collective-permute-start.24 = (bf16[160,768]{1,0:T(8,128)(2,1)}, bf16[160,768]{1,0:T(8,128)(2,1)S(1)}, u32[]{:S(2)}, u32[]{:S(2)}) collective-permute-start(bf16[160,768]{1,0:T(8,128)(2,1)} %get-tuple-element.204), channel_id=1, source_target_pairs={{0,10},{1,11},{2,8},{3,9},{4,14},{5,15},{6,12},{7,13},{8,2},{9,3},... | collective-permute-start | bytes 737288 | tf_op jit(solution)/shard_map/ppermute | solution.py:748
  79.5 25.5 %collective-permute-start.23 = (bf16[160,768]{1,0:T(8,128)(2,1)}, bf16[160,768]{1,0:T(8,128)(2,1)S(1)}, u32[]{:S(2)}, u32[]{:S(2)}) collective-permute-start(bf16[160,768]{1,0:T(8,128)(2,1)} %get-tuple-element.202), channel_id=1, source_target_pairs={{0,8},{1,9},{2,10},{3,11},{4,12},{5,13},{6,14},{7,15},{8,0},{9,1},... | collective-permute-start | bytes 737288 | tf_op jit(solution)/shard_map/ppermute | solution.py:748
  83.7 21.3 %collective-permute-start.22 = (bf16[160,768]{1,0:T(8,128)(2,1)}, bf16[160,768]{1,0:T(8,128)(2,1)S(1)}, u32[]{:S(2)}, u32[]{:S(2)}) collective-permute-start(bf16[160,768]{1,0:T(8,128)(2,1)} %get-tuple-element.200), channel_id=1, source_target_pairs={{0,2},{1,3},{2,0},{3,1},{4,6},{5,7},{6,4},{7,5},{8,10},{9,11},{10,... | collective-permute-start | bytes 737288 | tf_op jit(solution)/shard_map/ppermute | solution.py:748
  89.0 16.0 %collective-permute-start.19 = (f32[8,128]{1,0:T(8,128)S(1)}, f32[8,128]{1,0:T(8,128)S(1)}, u32[]{:S(2)}, u32[]{:S(2)}) collective-permute-start(f32[8,128]{1,0:T(8,128)S(1)} %add.572), channel_id=1, source_target_pairs={{0,8},{1,9},{2,10},{3,11},{4,12},{5,13},{6,14},{7,15},{8,0},{9,1},... | collective-permute-start | bytes 12296 | tf_op jit(solution)/shard_map/ppermute | solution.py:748
  105.9 20.5 %collective-permute-start.27 = (bf16[160,768]{1,0:T(8,128)(2,1)S(1)}, bf16[160,768]{1,0:T(8,128)(2,1)S(1)}, u32[]{:S(2)}, u32[]{:S(2)}) collective-permute-start(bf16[160,768]{1,0:T(8,128)(2,1)S(1)} %copy-done.70), channel_id=1, source_target_pairs={{0,2},{1,3},{2,0},{3,1},{4,6},{5,7},{6,4},{7,5},{8,10},{9,11},{10,... | collective-permute-start | bytes 737288 | tf_op jit(solution)/shard_map/ppermute | solution.py:748
  110.1 16.4 %collective-permute-start.28 = (bf16[160,768]{1,0:T(8,128)(2,1)S(1)}, bf16[160,768]{1,0:T(8,128)(2,1)S(1)}, u32[]{:S(2)}, u32[]{:S(2)}) collective-permute-start(bf16[160,768]{1,0:T(8,128)(2,1)S(1)} %copy-done.68), channel_id=1, source_target_pairs={{0,8},{1,9},{2,10},{3,11},{4,12},{5,13},{6,14},{7,15},{8,0},{9,1},... | collective-permute-start | bytes 737288 | tf_op jit(solution)/shard_map/ppermute | solution.py:748
  110.2 16.3 %collective-permute-start.29 = (bf16[160,768]{1,0:T(8,128)(2,1)S(1)}, bf16[160,768]{1,0:T(8,128)(2,1)S(1)}, u32[]{:S(2)}, u32[]{:S(2)}) collective-permute-start(bf16[160,768]{1,0:T(8,128)(2,1)S(1)} %copy-done.66), channel_id=1, source_target_pairs={{0,10},{1,11},{2,8},{3,9},{4,14},{5,15},{6,12},{7,13},{8,2},{9,3},... | collective-permute-start | bytes 737288 | tf_op jit(solution)/shard_map/ppermute | solution.py:748
  158.1 25.6 %collective-permute-start.42 = (bf16[160,768]{1,0:T(8,128)(2,1)}, bf16[160,768]{1,0:T(8,128)(2,1)S(1)}, u32[]{:S(2)}, u32[]{:S(2)}) collective-permute-start(bf16[160,768]{1,0:T(8,128)(2,1)} %get-tuple-element.238), channel_id=1, source_target_pairs={{0,10},{1,11},{2,8},{3,9},{4,14},{5,15},{6,12},{7,13},{8,2},{9,3},... | collective-permute-start | bytes 737288 | tf_op jit(solution)/shard_map/ppermute | solution.py:748
  160.2 23.5 %collective-permute-start.41 = (bf16[160,768]{1,0:T(8,128)(2,1)}, bf16[160,768]{1,0:T(8,128)(2,1)S(1)}, u32[]{:S(2)}, u32[]{:S(2)}) collective-permute-start(bf16[160,768]{1,0:T(8,128)(2,1)} %get-tuple-element.236), channel_id=1, source_target_pairs={{0,8},{1,9},{2,10},{3,11},{4,12},{5,13},{6,14},{7,15},{8,0},{9,1},... | collective-permute-start | bytes 737288 | tf_op jit(solution)/shard_map/ppermute | solution.py:748
  160.2 23.5 %collective-permute-start.40 = (bf16[160,768]{1,0:T(8,128)(2,1)}, bf16[160,768]{1,0:T(8,128)(2,1)S(1)}, u32[]{:S(2)}, u32[]{:S(2)}) collective-permute-start(bf16[160,768]{1,0:T(8,128)(2,1)} %get-tuple-element.234), channel_id=1, source_target_pairs={{0,2},{1,3},{2,0},{3,1},{4,6},{5,7},{6,4},{7,5},{8,10},{9,11},{10,... | collective-permute-start | bytes 737288 | tf_op jit(solution)/shard_map/ppermute | solution.py:748
  195.3 19.8 %collective-permute-start.48 = (bf16[2,2,128,768]{3,2,1,0:T(8,128)(2,1)}, bf16[2,2,128,768]{3,2,1,0:T(8,128)(2,1)S(1)}, u32[]{:S(2)}, u32[]{:S(2)}) collective-permute-start(bf16[2,2,128,768]{3,2,1,0:T(8,128)(2,1)} %get-tuple-element.251), channel_id=1, source_target_pairs={{0,4},{1,5},{2,6},{3,7},{4,0},{5,1},{6,2},{7,3},{8,12},{9,13},{10,... | collective-permute-start | bytes 2359304 | tf_op jit(solution)/shard_map/ppermute | solution.py:748
  195.8 16.5 %collective-permute-start.44 = (bf16[160,768]{1,0:T(8,128)(2,1)S(1)}, bf16[160,768]{1,0:T(8,128)(2,1)S(1)}, u32[]{:S(2)}, u32[]{:S(2)}) collective-permute-start(bf16[160,768]{1,0:T(8,128)(2,1)S(1)} %copy-done.63), channel_id=1, source_target_pairs={{0,2},{1,3},{2,0},{3,1},{4,6},{5,7},{6,4},{7,5},{8,10},{9,11},{10,... | collective-permute-start | bytes 737288 | tf_op jit(solution)/shard_map/ppermute | solution.py:748
  196.5 15.9 %collective-permute-start.45 = (bf16[160,768]{1,0:T(8,128)(2,1)S(1)}, bf16[160,768]{1,0:T(8,128)(2,1)S(1)}, u32[]{:S(2)}, u32[]{:S(2)}) collective-permute-start(bf16[160,768]{1,0:T(8,128)(2,1)S(1)} %copy-done.62), channel_id=1, source_target_pairs={{0,8},{1,9},{2,10},{3,11},{4,12},{5,13},{6,14},{7,15},{8,0},{9,1},... | collective-permute-start | bytes 737288 | tf_op jit(solution)/shard_map/ppermute | solution.py:748
  215.4 22.4 %collective-permute-start.52 = (bf16[160,768]{1,0:T(8,128)(2,1)}, bf16[160,768]{1,0:T(8,128)(2,1)S(1)}, u32[]{:S(2)}, u32[]{:S(2)}) collective-permute-start(bf16[160,768]{1,0:T(8,128)(2,1)} %collective-permute-done.49), channel_id=1, source_target_pairs={{0,2},{1,3},{2,0},{3,1},{4,6},{5,7},{6,4},{7,5},{8,10},{9,11},{10,... | collective-permute-start | bytes 737288 | tf_op jit(solution)/shard_map/ppermute | solution.py:748
  216.0 22.4 %collective-permute-start.53 = (bf16[160,768]{1,0:T(8,128)(2,1)}, bf16[160,768]{1,0:T(8,128)(2,1)S(1)}, u32[]{:S(2)}, u32[]{:S(2)}) collective-permute-start(bf16[160,768]{1,0:T(8,128)(2,1)} %collective-permute-done.50), channel_id=1, source_target_pairs={{0,8},{1,9},{2,10},{3,11},{4,12},{5,13},{6,14},{7,15},{8,0},{9,1},... | collective-permute-start | bytes 737288 | tf_op jit(solution)/shard_map/ppermute | solution.py:748
  217.9 20.4 %collective-permute-start.54 = (bf16[160,768]{1,0:T(8,128)(2,1)}, bf16[160,768]{1,0:T(8,128)(2,1)S(1)}, u32[]{:S(2)}, u32[]{:S(2)}) collective-permute-start(bf16[160,768]{1,0:T(8,128)(2,1)} %collective-permute-done.51), channel_id=1, source_target_pairs={{0,10},{1,11},{2,8},{3,9},{4,14},{5,15},{6,12},{7,13},{8,2},{9,3},... | collective-permute-start | bytes 737288 | tf_op jit(solution)/shard_map/ppermute | solution.py:748
  218.8 30.3 %collective-permute-start.55 = (bf16[2,2,128,768]{3,2,1,0:T(8,128)(2,1)}, bf16[2,2,128,768]{3,2,1,0:T(8,128)(2,1)S(1)}, u32[]{:S(2)}, u32[]{:S(2)}) collective-permute-start(bf16[2,2,128,768]{3,2,1,0:T(8,128)(2,1)} %get-tuple-element.281), channel_id=1, source_target_pairs={{0,4},{1,5},{2,6},{3,7},{4,0},{5,1},{6,2},{7,3},{8,12},{9,13},{10,... | collective-permute-start | bytes 2359304 | tf_op jit(solution)/shard_map/ppermute | solution.py:748
  237.2 19.6 %collective-permute-start.56 = (bf16[1,2,128,768]{3,2,1,0:T(8,128)(2,1)S(1)}, bf16[1,2,128,768]{3,2,1,0:T(8,128)(2,1)S(1)}, u32[]{:S(2)}, u32[]{:S(2)}) collective-permute-start(bf16[1,2,128,768]{3,2,1,0:T(8,128)(2,1)S(1)} %constant_dynamic-slice_fusion.7), channel_id=1, source_target_pairs={{0,16},{1,17},{2,18},{3,19},{4,20},{5,21},{6,22},{7,23},{8,24},{9,... | collective-permute-start | bytes 1179656 | tf_op jit(solution)/shard_map/ppermute | solution.py:748
  237.8 30.6 %collective-permute-start.57 = (bf16[2,2,128,768]{3,2,1,0:T(8,128)(2,1)S(1)}, bf16[2,2,128,768]{3,2,1,0:T(8,128)(2,1)S(1)}, u32[]{:S(2)}, u32[]{:S(2)}) collective-permute-start(bf16[2,2,128,768]{3,2,1,0:T(8,128)(2,1)S(1)} %copy-done.52), channel_id=1, source_target_pairs={{0,4},{1,5},{2,6},{3,7},{4,0},{5,1},{6,2},{7,3},{8,12},{9,13},{10,... | collective-permute-start | bytes 2359304 | tf_op jit(solution)/shard_map/ppermute | solution.py:748
  247.6 30.0 %collective-permute-start.59 = (bf16[2,2,32,3072]{3,2,1,0:T(8,128)(2,1)}, bf16[2,2,32,3072]{3,2,1,0:T(8,128)(2,1)S(1)}, u32[]{:S(2)}, u32[]{:S(2)}) collective-permute-start(bf16[2,2,32,3072]{3,2,1,0:T(8,128)(2,1)} %get-tuple-element.297), channel_id=1, source_target_pairs={{0,4},{1,5},{2,6},{3,7},{4,0},{5,1},{6,2},{7,3},{8,12},{9,13},{10,... | collective-permute-start | bytes 2359304 | tf_op jit(solution)/shard_map/ppermute | solution.py:748
  268.4 19.0 %collective-permute-start.58 = (bf16[1,2,128,768]{3,2,1,0:T(8,128)(2,1)S(1)}, bf16[1,2,128,768]{3,2,1,0:T(8,128)(2,1)S(1)}, u32[]{:S(2)}, u32[]{:S(2)}) collective-permute-start(bf16[1,2,128,768]{3,2,1,0:T(8,128)(2,1)S(1)} %constant_dynamic-slice_fusion.6), channel_id=1, source_target_pairs={{0,16},{1,17},{2,18},{3,19},{4,20},{5,21},{6,22},{7,23},{8,24},{9,... | collective-permute-start | bytes 1179656 | tf_op jit(solution)/shard_map/ppermute | solution.py:748
  288.1 35.0 %collective-permute-start.65 = (bf16[1,2,128,768]{3,2,1,0:T(8,128)(2,1)}, bf16[1,2,128,768]{3,2,1,0:T(8,128)(2,1)}, u32[]{:S(2)}, u32[]{:S(2)}) collective-permute-start(bf16[1,2,128,768]{3,2,1,0:T(8,128)(2,1)} %constant_dynamic-slice_fusion.5), channel_id=1, source_target_pairs={{0,16},{1,17},{2,18},{3,19},{4,20},{5,21},{6,22},{7,23},{8,24},{9,... | collective-permute-start | bytes 1179656 | tf_op jit(solution)/shard_map/ppermute | solution.py:748
  288.9 46.3 %collective-permute-start.66 = (bf16[2,2,32,3072]{3,2,1,0:T(8,128)(2,1)}, bf16[2,2,32,3072]{3,2,1,0:T(8,128)(2,1)}, u32[]{:S(2)}, u32[]{:S(2)}) collective-permute-start(bf16[2,2,32,3072]{3,2,1,0:T(8,128)(2,1)} %get-tuple-element.317), channel_id=1, source_target_pairs={{0,4},{1,5},{2,6},{3,7},{4,0},{5,1},{6,2},{7,3},{8,12},{9,13},{10,... | collective-permute-start | bytes 2359304 | tf_op jit(solution)/shard_map/ppermute | solution.py:748
  303.4 38.2 %collective-permute-start.67 = (bf16[1,2,32,3072]{3,2,1,0:T(8,128)(2,1)}, bf16[1,2,32,3072]{3,2,1,0:T(8,128)(2,1)}, u32[]{:S(2)}, u32[]{:S(2)}) collective-permute-start(bf16[1,2,32,3072]{3,2,1,0:T(8,128)(2,1)} %constant_dynamic-slice_fusion.4), channel_id=1, source_target_pairs={{0,16},{1,17},{2,18},{3,19},{4,20},{5,21},{6,22},{7,23},{8,24},{9,... | collective-permute-start | bytes 1179656 | tf_op jit(solution)/shard_map/ppermute | solution.py:748
  306.0 30.5 %collective-permute-start.64 = (bf16[2,8,48,384]{3,2,1,0:T(8,128)(2,1)}, bf16[2,8,48,384]{3,2,1,0:T(8,128)(2,1)}, u32[]{:S(2)}, u32[]{:S(2)}) collective-permute-start(bf16[2,8,48,384]{3,2,1,0:T(8,128)(2,1)} %get-tuple-element.377), channel_id=1, source_target_pairs={{0,2},{1,3},{2,0},{3,1},{4,6},{5,7},{6,4},{7,5},{8,10},{9,11},{10,... | collective-permute-start | bytes 1769480 | tf_op jit(solution)/shard_map/ppermute | solution.py:748
  306.3 27.6 %collective-permute-start.61 = (bf16[2,8,48,384]{3,2,1,0:T(8,128)(2,1)}, bf16[2,8,48,384]{3,2,1,0:T(8,128)(2,1)}, u32[]{:S(2)}, u32[]{:S(2)}) collective-permute-start(bf16[2,8,48,384]{3,2,1,0:T(8,128)(2,1)} %get-tuple-element.375), channel_id=1, source_target_pairs={{0,2},{1,3},{2,0},{3,1},{4,6},{5,7},{6,4},{7,5},{8,10},{9,11},{10,... | collective-permute-start | bytes 1769480 | tf_op jit(solution)/shard_map/ppermute | solution.py:748
  338.0 26.7 %collective-permute-start.82 = (bf16[1,2,32,3072]{3,2,1,0:T(8,128)(2,1)S(1)}, bf16[1,2,32,3072]{3,2,1,0:T(8,128)(2,1)S(1)}, u32[]{:S(2)}, u32[]{:S(2)}) collective-permute-start(bf16[1,2,32,3072]{3,2,1,0:T(8,128)(2,1)S(1)} %constant_dynamic-slice_fusion.3), channel_id=1, source_target_pairs={{0,16},{1,17},{2,18},{3,19},{4,20},{5,21},{6,22},{7,23},{8,24},{9,... | collective-permute-start | bytes 1179656 | tf_op jit(solution)/shard_map/ppermute | solution.py:748
  338.4 26.7 %collective-permute-start.70 = (bf16[2,2,2,48,384]{4,3,0,1,2:T(8,128)(2,1)S(1)}, bf16[2,2,2,48,384]{4,3,0,1,2:T(8,128)(2,1)S(1)}, u32[]{:S(2)}, u32[]{:S(2)}) collective-permute-start(bf16[2,2,2,48,384]{4,3,0,1,2:T(8,128)(2,1)S(1)} %bitcast.102), channel_id=1, source_target_pairs={{0,8},{1,9},{2,10},{3,11},{4,12},{5,13},{6,14},{7,15},{8,0},{9,1},... | collective-permute-start | bytes 884744 | tf_op jit(solution)/shard_map/ppermute | solution.py:748
  340.1 24.7 %collective-permute-start.71 = (bf16[2,2,32,3072]{3,2,1,0:T(8,128)(2,1)S(1)}, bf16[2,2,32,3072]{3,2,1,0:T(8,128)(2,1)S(1)}, u32[]{:S(2)}, u32[]{:S(2)}) collective-permute-start(bf16[2,2,32,3072]{3,2,1,0:T(8,128)(2,1)S(1)} %copy-done.53), channel_id=1, source_target_pairs={{0,4},{1,5},{2,6},{3,7},{4,0},{5,1},{6,2},{7,3},{8,12},{9,13},{10,... | collective-permute-start | bytes 2359304 | tf_op jit(solution)/shard_map/ppermute | solution.py:748
  341.6 21.5 %collective-permute-start.63 = (bf16[2,2,2,48,384]{4,3,2,1,0:T(8,128)(2,1)S(1)}, bf16[2,2,2,48,384]{4,3,2,1,0:T(8,128)(2,1)S(1)}, u32[]{:S(2)}, u32[]{:S(2)}) collective-permute-start(bf16[2,2,2,48,384]{4,3,2,1,0:T(8,128)(2,1)S(1)} %dynamic-slice_bitcast_fusion.4), channel_id=1, source_target_pairs={{0,8},{1,9},{2,10},{3,11},{4,12},{5,13},{6,14},{7,15},{8,0},{9,1},... | collective-permute-start | bytes 884744 | tf_op jit(solution)/shard_map/ppermute | solution.py:748
  346.0 53.7 %collective-permute-start.83 = (bf16[2,32,3072]{2,1,0:T(8,128)(2,1)S(1)}, bf16[2,32,3072]{2,1,0:T(8,128)(2,1)}, u32[]{:S(2)}, u32[]{:S(2)}) collective-permute-start(bf16[2,32,3072]{2,1,0:T(8,128)(2,1)S(1)} %fusion.15), channel_id=1, source_target_pairs={{0,8},{1,9},{2,10},{3,11},{4,12},{5,13},{6,14},{7,15},{8,0},{9,1},... | collective-permute-start | bytes 1179656 | tf_op jit(solution)/shard_map/ppermute | solution.py:748
  393.0 17.1 %collective-permute-start.85 = (bf16[3,128,768]{2,1,0:T(8,128)(2,1)S(1)}, bf16[3,128,768]{2,1,0:T(8,128)(2,1)}, u32[]{:S(2)}, u32[]{:S(2)}) collective-permute-start(bf16[3,128,768]{2,1,0:T(8,128)(2,1)S(1)} %copy-done.20), channel_id=1, source_target_pairs={{0,8},{1,9},{2,10},{3,11},{4,12},{5,13},{6,14},{7,15},{8,0},{9,1},... | collective-permute-start | bytes 1769480 | tf_op jit(solution)/shard_map/ppermute | solution.py:748
  (129 other events, 1081.1 us)

commit v5 on v4

--- a/solution.py
+++ b/solution.py
@@ -285,7 +285,7 @@
         out_shape=[jax.ShapeDtypeStruct((3, length, width), jnp.bfloat16)]
         + [jax.ShapeDtypeStruct((2 * pairs, 4, BLOCK, BLOCK), jnp.float32)],
         compiler_params=pltpu.CompilerParams(vmem_limit_bytes=VMEM_BYTES),
-        cost_estimate=cost(12),
+        cost_estimate=cost(4),
         name="attention_backward",
     )(qkv_rows, qkv_rows, qkv_rows, grads, probs)
 
@@ -617,7 +617,7 @@
         ),
         out_shape=[shape] * 4,
         compiler_params=pltpu.CompilerParams(vmem_limit_bytes=VMEM_BYTES),
-        cost_estimate=cost(6),
+        cost_estimate=cost(2),
         name="outer_halves",
     )(core, normed, attended, rights, last)
 
@@ -933,19 +933,18 @@
     )
     away_b, stay_b = near_add(after(got_b, grad_attended), keep_b)
     got_d = swap(after(send_d, grad_attended), 1, 0)
-    grad_attended, away_b, far_a = lax.optimization_barrier((grad_attended, away_b, far_a))
-    far_b = far_trade(away_b)
+    grad_attended, away_b = lax.optimization_barrier((grad_attended, away_b))
+    grad_qkv_rows, bands = attention_backward(qkv_rows, grad_attended, probs)
+    grad_qkv_rows, got_c, far_a = lax.optimization_barrier((grad_qkv_rows, got_c, far_a))
     done_a = finish(far_a, stay_a)
-    grad_qkv_rows, bands = attention_backward(qkv_rows, grad_attended, probs)
-    grad_qkv_rows, got_c = lax.optimization_barrier((grad_qkv_rows, got_c))
 
     away_c, stay_c = near_add(got_c, keep_c)
-    far_c = far_trade(away_c)
+    far_c = far_trade(jnp.concatenate([away_b, away_c], axis=1))
+    stay_c = jnp.concatenate([stay_b, stay_c], axis=1)
     *weights_away, stay_1, stay_2 = outer_halves(
         core_index, normed1, attended, after(grad_qkv_rows, away_c), grad_attn_proj
     )
-    weights_away, far_b, got_d = lax.optimization_barrier((weights_away, far_b, got_d))
-    done_b = finish(far_b, stay_b)
+    weights_away, got_d = lax.optimization_barrier((weights_away, got_d))
     got_e = swap(after(send_e, got_d), 1, 0)
     keep_d, keep_e, keep_f = weight_part(
         kept, rows_in, after(grad_pre, *weights_away), in_rows, in_plans, rest, inner // 2
@@ -982,11 +981,11 @@
     chains = [add(after(first[0], away_d, gain_attn_parts), first[1]).reshape((2,) + (2,) * len(dp_masks) + (-1, columns)), None]
     trades = [over_dp(chains[0], dp_masks[0], ()), None]
     away_e, stay_e = near_add(after(got_e, chains[0]), keep_e)
-    far_e = far_trade(away_e)
     got_f = swap(after(send_f, away_e), 1, 0)
     chains[1] = add(after(second[0], done_c, grad_table, away_e), second[1]).reshape(chains[0].shape)
     trades[1] = over_dp(chains[1], dp_masks[0], ())
     total = trades[1][1]
+    far_e = far_trade(after(away_e, total))
     done_d = finish(after(far_d, chains[0]), stay_d)
     away_f, stay_f = near_add(after(got_f, total), keep_f)
     far_f = far_trade(away_f)
@@ -1008,8 +1007,10 @@
     flat = flat + swap(flat, 0, 1)
     for place, mask in enumerate(dp_masks):
         flat_got = swap(flat, 0, group_masks[0]) if mask == PAIR else swap(flat, mask, 0)
+        if place + 1 == len(dp_masks):
+            trades[1] = (after(trades[1][0], out_theirs), trades[1][1])
         if place == 1:
-            done_e = finish(far_e, stay_e)
+            done_e = finish(after(far_e, chains[1]), stay_e)
             trades[1] = (after(trades[1][0], done_e), trades[1][1])
         chains = [add(*trades[0]), None]
         if place + 1 < len(dp_masks):
@@ -1021,7 +1022,7 @@
             trades = trades_next
         if mask == PAIR:
             in_first = swap(done_d, PAIR, 0)
-            out_theirs = swap(after(jnp.concatenate([done_a, done_b[:1]]), chains[1]), PAIR, 0)
+            out_theirs = swap(after(jnp.concatenate([done_a, done_c[:1]]), chains[1]), PAIR, 0)
         flat = after(flat, chains[1])
     total = jnp.concatenate(chains)
     in_theirs = jnp.concatenate([in_first, swap(done_e[:1], PAIR, 0)])
@@ -1046,7 +1047,7 @@
         flat[start : start + value.size].reshape(value.shape) for start, value in zip(starts, small)
     ]
 
-    out_mine, in_mine = jnp.concatenate([done_b[1:], done_c]), jnp.concatenate([done_e[1:], done_f])
+    out_mine, in_mine = done_c[1:], jnp.concatenate([done_e[1:], done_f])
 
     def both_experts(mine, theirs):
         mine, theirs = [part.reshape(-1, part.shape[-1]).astype(f32) for part in (mine, theirs)]

time: 421 us -> 428 us (1.017)
  local copies, waits for them, and re-layouts: 26.1 us -> 33.7 us
  waiting for transfers between devices: 105 us -> 99.5 us
    ppermute x72 -> x71, waiting for transfers between devices: 96.6 us -> 90.7 us  [swap(): return lax.ppermute(value, AXES, pairs)]
    unnamed x157 -> x167, local copies, waits for them, and re-layouts: 9.16 us -> 14 us
    ppermute x72 -> x71, starting transfers between devices: 72.5 us -> 74.8 us  [swap(): return lax.ppermute(value, AXES, pairs)]
  transfers between devices with their start and end apart: 86 -> 85, of which waited for: 30 -> 28; matrix products, arithmetic and copies ran while one was open for 11% -> 13% of each run, Pallas kernels for 32% -> 31%
where the time goes in v5:
time: 428 us; the launch traced here: 423 us
  Pallas kernels  157 us (37%)
  waiting for transfers between devices  99.5 us (23%)
  starting transfers between devices  91.9 us (21%)
  local copies, waits for them, and re-layouts  33.7 us (8%)
  other arithmetic  26.5 us (6%)
  matrix products  8.02 us (2%)
  between operations  6.12 us (1%)
    ppermute x71, waiting for transfers between devices, swap(): return lax.ppermute(value, AXES, pairs)  90.7 us
    ppermute x71, starting transfers between devices, swap(): return lax.ppermute(value, AXES, pairs)  74.8 us
    pallas_call x4, Pallas kernels, weight_part(): pl.pallas_call(lambda *refs: weight_part_kernel(*refs, count=count, plans...  30.8 us
    pallas_call x2, Pallas kernels, expert_forward(): pl.pallas_call(lambda *refs: expert_forward_kernel(*refs, chunk=chunk, co...  27.4 us
    pallas_call x2, Pallas kernels, expert_backward(): pl.pallas_call(lambda *refs: expert_backward_kernel(*refs, chunk=chunk, c...  25.2 us
    ppermute x14, starting transfers between devices, gather_ring(): lax.ppermute(after(held, *due[step - 2:step - 1]) if step > 1 else held,...  17.1 us
    unnamed x167, local copies, waits for them, and re-layouts  14 us
    pallas_call x1, Pallas kernels, attention_forward(): pl.pallas_call(lambda *refs: attention_forward_kernel(*refs, heads=64, bl...  12.6 us
  transfers between devices with their start and end apart: 85, of which 28 were waited for; matrix products, arithmetic and copies ran while one was open for 13% of the time, Pallas kernels for 31%

profile of v5, /device:TPU:0, one launch (start us, length us, event | category | flops | bytes accessed | tf_op | source)
XLA Modules:
  0.0 422.8 jit_solution(5110765979883035030)
XLA Ops:
  1.7 3.1 collective-permute-start
  34.3 3.3 join.1.mine.refs_15_
  46.4 6.4 %project.1.refs_2_.refs_3_.refs_4_.refs_0_.refs_1_ = bf16[3,512,768]{2,1,0:T(8,128)(2,1)} custom-call(s32[1]{0:T(128)} %bitcast.2.core.refs_0_, bf16[512,768]{1,0:T(8,128)(2,1)} %fusion.6.rows.refs_1_, bf16[4,768,384]{2,1,0:T(8,128)(2,1)} %join.1.mine.refs_15_, bf16[4,768,384]{2,1,0:T(8,128)(2,1)} %copy-done), custom_call_target="tpu_custom_call" | custom-call | flops 1480000000 | tf_op jit(solution)/shard_map/project/pallas_call | solution.py:396
  55.0 12.6 %attention_forward.1 = (bf16[512,768]{1,0:T(8,128)(2,1)}, bf16[12,512,512]{2,1,0:T(8,128)(2,1)}) custom-call(f32[12]{0:T(128)} %slice_reduce_fusion.refs_0_, s32[1]{0:T(128)S(6)} %copy.105.refs_1_, bf16[3,512,768]{2,1,0:T(8,128)(2,1)} %project.1.refs_2_.refs_3_.refs_4_.refs_0_.refs_1_, bf16[3,512,768]{2,1,0:T(8,128)(2,1)} %project.1.refs_2_.refs_3_.refs_4_.refs_0_.refs_1_, ...), custom_call_target="tpu_custom_call" | custom-call | flops 4809999872 | tf_op jit(solution)/shard_map/attention_forward/pallas_call | solution.py:214
  67.7 5.9 %route.1 = (f32[512,768]{1,0:T(8,128)}, bf16[512,768]{1,0:T(8,128)(2,1)}, f32[512,2]{1,0:T(8,128)}, bf16[160,768]{1,0:T(8,128)(2,1)}, bf16[160,768]{1,0:T(8,128)...) custom-call(s32[1]{0:T(128)} %bitcast.2.core.refs_0_, ...), custom_call_target="tpu_custom_call" | custom-call | flops 2220000000 | tf_op jit(solution)/shard_map/route/pallas_call | solution.py:447
  79.9 3.8 collective-permute-done.18.refs_4_
  85.0 4.0 collective-permute-done.20.refs_2_
  91.3 13.7 %expert_forward.2 = (bf16[3072,640]{1,0:T(8,128)(2,1)}, bf16[640,3072]{1,0:T(8,128)(2,1)}, bf16[768,640]{1,0:T(8,128)(2,1)}, bf16[160,768]{1,0:T(8,128)(2,1)}, b...) custom-call(s32[1]{0:T(128)} %bitcast.4.refs_0_, ...), custom_call_target="tpu_custom_call" | custom-call | flops 4809999872 | tf_op jit(solution)/shard_map/expert_forward/pallas_call | solution.py:78
  105.9 4.2 collective-permute-start.27
  112.6 13.8 %expert_forward.3 = (bf16[3072,640]{1,0:T(8,128)(2,1)}, bf16[640,3072]{1,0:T(8,128)(2,1)}, bf16[768,640]{1,0:T(8,128)(2,1)}, bf16[160,768]{1,0:T(8,128)(2,1)}, b...) custom-call(s32[1]{0:T(128)} %bitcast.4.refs_0_, bf16[640,768]{1,0:T(8,128)(2,1)} %copy-done.14, ...), custom_call_target="tpu_custom_call" | custom-call | flops 4809999872 | tf_op jit(solution)/shard_map/expert_forward/pallas_call | solution.py:78
  135.4 5.6 %collective-permute-done.26 = f32[8,128]{1,0:T(8,128)S(1)} collective-permute-done((f32[8,128]{1,0:T(8,128)S(1)}, f32[8,128]{1,0:T(8,128)S(1)}, u32[]{:S(2)}, u32[]{:S(2)}) %collective-permute-start.26) | collective-permute-done | bytes 4128 | tf_op jit(solution)/shard_map/ppermute | solution.py:748
  144.0 8.5 %combine.1 = (bf16[512,768]{1,0:T(8,128)(2,1)}, f32[512,768]{1,0:T(8,128)}, bf16[512,8]{1,0:T(8,128)(2,1)}, f32[8,768]{1,0:T(8,128)}, bf16[160,768]{1,0:T(8,128)...) custom-call(s32[512,2]{1,0:T(8,128)} %multiply_add_fusion.refs_0_.re, ...), custom_call_target="tpu_custom_call" | custom-call | flops 2960000000 | tf_op jit(solution)/shard_map/combine/pallas_call | solution.py:503
  154.0 3.3 collective-permute-start.38
  164.3 6.2 %collective-permute-done.39.refs_4_ = bf16[160,768]{1,0:T(8,128)(2,1)S(1)} collective-permute-done((bf16[160,768]{1,0:T(8,128)(2,1)}, bf16[160,768]{1,0:T(8,128)(2,1)S(1)}, u32[]{:S(2)}, u32[]{:S(2)}) %collective-permute-start.39) | collective-permute-done | bytes 245792 | tf_op jit(solution)/shard_map/ppermute | solution.py:748
  171.2 12.5 %expert_backward.2 = (bf16[640,3072]{1,0:T(8,128)(2,1)}, bf16[640,768]{1,0:T(8,128)(2,1)}, bf16[160,768]{1,0:T(8,128)(2,1)}, bf16[160,768]{1,0:T(8,128)(2,1)}, b...) custom-call(s32[1]{0:T(128)} %bitcast.4.refs_0_, bf16[160,768]{1,0:T(8,128)(2,1)} %get-tuple-element.224.refs_1_, ...), custom_call_target="tpu_custom_call" | custom-call | flops 4070000128 | tf_op jit(solution)/shard_map/expert_backward/pallas_call | solution.py:135
  187.4 7.8 %weight_part.4 = (bf16[2,2,128,768]{3,2,1,0:T(8,128)(2,1)}, bf16[2,2,128,768]{3,2,1,0:T(8,128)(2,1)}, bf16[2,2,128,768]{3,2,1,0:T(8,128)(2,1)}) custom-call(s32[4]{0:T(128)} %pad_add_fusion.1.refs_0_, bf16[3072,640]{1,0:T(8,128)(2,1)} %get-tuple-element.200.refs_1_.refs_2_.refs_3_.refs_4_, ...), custom_call_target="tpu_custom_call" | custom-call | flops 1480000000 | tf_op jit(solution)/shard_map/weight_part/pallas_call | solution.py:337
  199.3 12.7 %expert_backward.3 = (bf16[640,3072]{1,0:T(8,128)(2,1)}, bf16[640,768]{1,0:T(8,128)(2,1)}, bf16[160,768]{1,0:T(8,128)(2,1)}, bf16[160,768]{1,0:T(8,128)(2,1)}, b...) custom-call(s32[1]{0:T(128)} %bitcast.4.refs_0_, bf16[640,768]{1,0:T(8,128)(2,1)} %copy-done.1, ...), custom_call_target="tpu_custom_call" | custom-call | flops 4070000128 | tf_op jit(solution)/shard_map/expert_backward/pallas_call | solution.py:135
  220.1 7.8 %weight_part.5 = (bf16[2,2,128,768]{3,2,1,0:T(8,128)(2,1)}, bf16[2,2,128,768]{3,2,1,0:T(8,128)(2,1)}, bf16[2,2,128,768]{3,2,1,0:T(8,128)(2,1)}) custom-call(s32[4]{0:T(128)} %pad_add_fusion.2.refs_0_, bf16[3072,640]{1,0:T(8,128)(2,1)} %get-tuple-element.200.refs_1_.refs_2_.refs_3_.refs_4_, ...), custom_call_target="tpu_custom_call" | custom-call | flops 1480000000 | tf_op jit(solution)/shard_map/weight_part/pallas_call | solution.py:337
  229.3 7.7 %weight_part.6 = (bf16[2,2,32,3072]{3,2,1,0:T(8,128)(2,1)}, bf16[2,2,32,3072]{3,2,1,0:T(8,128)(2,1)}, bf16[2,2,32,3072]{3,2,1,0:T(8,128)(2,1)}) custom-call(s32[4]{0:T(128)} %pad_add_fusion.1.refs_0_, bf16[768,640]{1,0:T(8,128)(2,1)} %get-tuple-element.230.refs_1_.refs_2_.refs_3_.refs_4_, ...), custom_call_target="tpu_custom_call" | custom-call | flops 1480000000 | tf_op jit(solution)/shard_map/weight_part/pallas_call | solution.py:337
  239.0 8.5 %collect.1 = (f32[512,768]{1,0:T(8,128)}, bf16[512,768]{1,0:T(8,128)(2,1)}, bf16[512,768]{1,0:T(8,128)(2,1)}, f32[8,768]{1,0:T(8,128)}) custom-call(s32[1]{0:T(128)} %bitcast.2.core.refs_0_, s32[512,2]{1,0:T(8,128)} %multiply_add_fusion.refs_0_.refs_1_, bf16[160,768]{1,0:T(8,128)(2,1)} %get-tuple-element.272.refs_2_, bf16[160,768]{1,0:T(8,128)(2,1)} %copy-done.62, ...), custom_call_target="tpu_custom_call" | custom-call | flops 2960000000 | tf_op jit(solution)/shard_map/collect/pallas_call | solution.py:554
  249.2 11.5 %attention_backward.1 = (bf16[3,512,768]{2,1,0:T(8,128)(2,1)}, f32[12,4,128,128]{3,2,1,0:T(8,128)}) custom-call(bf16[3,512,768]{2,1,0:T(8,128)(2,1)} %project.1.refs_2_.refs_3_.refs_4_.refs_0_.refs_1_, bf16[3,512,768]{2,1,0:T(8,128)(2,1)} %project.1.refs_2_.refs_3_.refs_4_.refs_0_.refs_1_, ...), custom_call_target="tpu_custom_call" | custom-call | flops 1480000000 | tf_op jit(solution)/shard_map/attention_backward/pallas_call | solution.py:280
  261.8 8.4 %outer_halves.1 = (bf16[2,768,384]{2,1,0:T(8,128)(2,1)}, bf16[2,768,384]{2,1,0:T(8,128)(2,1)}, bf16[2,768,384]{2,1,0:T(8,128)(2,1)}, bf16[2,768,384]{2,1,0:T(8,128)(2,1)}) custom-call(s32[1]{0:T(128)} %bitcast.2.core.refs_0_, bf16[512,768]{1,0:T(8,128)(2,1)} %fusion.6.rows.refs_1_, bf16[512,768]{1,0:T(8,128)(2,1)} %get-tuple-element.192.attended.refs_2_, ...), custom_call_target="tpu_custom_call" | custom-call | flops 740000000 | tf_op jit(solution)/shard_map/outer_halves/pallas_call | solution.py:604
  279.9 7.5 %weight_part.7 = (bf16[2,2,32,3072]{3,2,1,0:T(8,128)(2,1)}, bf16[2,2,32,3072]{3,2,1,0:T(8,128)(2,1)}, bf16[2,2,32,3072]{3,2,1,0:T(8,128)(2,1)}) custom-call(s32[4]{0:T(128)} %pad_add_fusion.2.refs_0_, bf16[768,640]{1,0:T(8,128)(2,1)} %get-tuple-element.230.refs_1_.refs_2_.refs_3_.refs_4_, ...), custom_call_target="tpu_custom_call" | custom-call | flops 1480000000 | tf_op jit(solution)/shard_map/weight_part/pallas_call | solution.py:337
  296.5 8.4 %enter.1 = (f32[512,768]{1,0:T(8,128)}, f32[8,768]{1,0:T(8,128)}) custom-call(s32[1]{0:T(128)} %bitcast.2.core.refs_0_, bf16[3,512,768]{2,1,0:T(8,128)(2,1)} %get-tuple-element.310.refs_3_.grads, bf16[4,768,384]{2,1,0:T(8,128)(2,1)} %join.1.mine.refs_15_, bf16[4,768,384]{2,1,0:T(8,128)(2,1)} %copy-done, bf16[512,768]{1,0:T(8,128)(2,1)} %tokens.3, ...), custom_call_target="tpu_custom_call" | custom-call | flops 2220000000 | tf_op jit(solution)/shard_map/enter/pallas_call | solution.py:650
  310.1 6.2 %fusion.10 = f32[12,32]{1,0:T(8,128)S(1)} fusion(s32[4,128,128]{2,1,0:T(8,128)} %pad_add_fusion, f32[12,4,128,128]{3,2,1,0:T(8,128)S(1)} %copy-done.3), kind=kOutput, calls=%fused_computation.32 | convolution fusion | flops 304087040 | bytes 3409408 | tf_op jit(solution)/shard_map/hdxy,dxyb->hb/dot_general | solution.py:704
  317.0 5.9 %collective-permute-done.72 = bf16[1,4,128,768]{3,2,1,0:T(8,128)(2,1)} collective-permute-done((bf16[1,4,128,768]{3,2,1,0:T(8,128)(2,1)}, bf16[1,4,128,768]{3,2,1,0:T(8,128)(2,1)}, u32[]{:S(2)}, u32[]{:S(2)}) %collective-permute-start.72) | collective-permute-done | bytes 786464 | tf_op jit(solution)/shard_map/ppermute | solution.py:748
  336.0 4.3 %collective-permute-done.62 = bf16[2,2,2,48,384]{4,3,2,1,0:T(8,128)(2,1)S(1)} collective-permute-done((bf16[2,2,2,48,384]{4,3,2,1,0:T(8,128)(2,1)S(1)}, bf16[2,2,2,48,384]{4,3,2,1,0:T(8,128)(2,1)S(1)}, u32[]{:S(2)}, u32[]{:S(2)}) %collective-permute-start.62) | collective-permute-done | bytes 294944 | tf_op jit(solution)/shard_map/ppermute | solution.py:748
  343.9 9.8 %collective-permute-done.66 = bf16[2,2,48,384]{3,2,1,0:T(8,128)(2,1)S(1)} collective-permute-done((bf16[2,2,48,384]{3,2,1,0:T(8,128)(2,1)S(1)}, bf16[2,2,48,384]{3,2,1,0:T(8,128)(2,1)S(1)}, u32[]{:S(2)}, u32[]{:S(2)}) %collective-permute-start.66) | collective-permute-done | bytes 147488 | tf_op jit(solution)/shard_map/ppermute | solution.py:748
  354.0 4.9 %collective-permute-start.83 = (bf16[2,32,3072]{2,1,0:T(8,128)(2,1)S(1)}, bf16[2,32,3072]{2,1,0:T(8,128)(2,1)S(1)}, u32[]{:S(2)}, u32[]{:S(2)}) collective-permute-start(bf16[2,32,3072]{2,1,0:T(8,128)(2,1)S(1)} %fusion.14), channel_id=1, source_target_pairs={{0,8},{1,9},{2,10},{3,11},{4,12},{5,13},{6,14},{7,15},{8,0},{9,1},... | collective-permute-start | bytes 1179656 | tf_op jit(solution)/shard_map/ppermute | solution.py:748
  362.4 25.0 %collective-permute-done.68 = bf16[2,2,2,48,384]{4,3,0,1,2:T(8,128)(2,1)S(1)} collective-permute-done((bf16[2,2,2,48,384]{4,3,0,1,2:T(8,128)(2,1)S(1)}, bf16[2,2,2,48,384]{4,3,0,1,2:T(8,128)(2,1)S(1)}, u32[]{:S(2)}, u32[]{:S(2)}) %collective-permute-start.68) | collective-permute-done | bytes 294944 | tf_op jit(solution)/shard_map/ppermute | solution.py:748
  389.7 3.4 collective-permute-done.78
  396.1 8.2 %collective-permute-done.79 = f32[64,128]{1,0:T(8,128)S(1)} collective-permute-done((f32[64,128]{1,0:T(8,128)S(1)}, f32[64,128]{1,0:T(8,128)S(1)}, u32[]{:S(2)}, u32[]{:S(2)}) %collective-permute-start.79) | collective-permute-done | bytes 32800 | tf_op jit(solution)/shard_map/ppermute | solution.py:748
  (440 shorter events, 161.7 us)
Async XLA Ops:
  77.1 27.9 %collective-permute-start.24 = (bf16[160,768]{1,0:T(8,128)(2,1)}, bf16[160,768]{1,0:T(8,128)(2,1)S(1)}, u32[]{:S(2)}, u32[]{:S(2)}) collective-permute-start(bf16[160,768]{1,0:T(8,128)(2,1)} %get-tuple-element.206), channel_id=1, source_target_pairs={{0,10},{1,11},{2,8},{3,9},{4,14},{5,15},{6,12},{7,13},{8,2},{9,3},... | collective-permute-start | bytes 737288 | tf_op jit(solution)/shard_map/ppermute | solution.py:748
  79.4 25.6 %collective-permute-start.23 = (bf16[160,768]{1,0:T(8,128)(2,1)}, bf16[160,768]{1,0:T(8,128)(2,1)S(1)}, u32[]{:S(2)}, u32[]{:S(2)}) collective-permute-start(bf16[160,768]{1,0:T(8,128)(2,1)} %get-tuple-element.204), channel_id=1, source_target_pairs={{0,8},{1,9},{2,10},{3,11},{4,12},{5,13},{6,14},{7,15},{8,0},{9,1},... | collective-permute-start | bytes 737288 | tf_op jit(solution)/shard_map/ppermute | solution.py:748
  83.7 21.4 %collective-permute-start.22 = (bf16[160,768]{1,0:T(8,128)(2,1)}, bf16[160,768]{1,0:T(8,128)(2,1)S(1)}, u32[]{:S(2)}, u32[]{:S(2)}) collective-permute-start(bf16[160,768]{1,0:T(8,128)(2,1)} %get-tuple-element.202), channel_id=1, source_target_pairs={{0,2},{1,3},{2,0},{3,1},{4,6},{5,7},{6,4},{7,5},{8,10},{9,11},{10,... | collective-permute-start | bytes 737288 | tf_op jit(solution)/shard_map/ppermute | solution.py:748
  89.0 16.0 %collective-permute-start.19 = (f32[8,128]{1,0:T(8,128)S(1)}, f32[8,128]{1,0:T(8,128)S(1)}, u32[]{:S(2)}, u32[]{:S(2)}) collective-permute-start(f32[8,128]{1,0:T(8,128)S(1)} %add.569), channel_id=1, source_target_pairs={{0,8},{1,9},{2,10},{3,11},{4,12},{5,13},{6,14},{7,15},{8,0},{9,1},... | collective-permute-start | bytes 12296 | tf_op jit(solution)/shard_map/ppermute | solution.py:748
  105.9 20.5 %collective-permute-start.27 = (bf16[160,768]{1,0:T(8,128)(2,1)S(1)}, bf16[160,768]{1,0:T(8,128)(2,1)S(1)}, u32[]{:S(2)}, u32[]{:S(2)}) collective-permute-start(bf16[160,768]{1,0:T(8,128)(2,1)S(1)} %copy-done.75), channel_id=1, source_target_pairs={{0,2},{1,3},{2,0},{3,1},{4,6},{5,7},{6,4},{7,5},{8,10},{9,11},{10,... | collective-permute-start | bytes 737288 | tf_op jit(solution)/shard_map/ppermute | solution.py:748
  110.1 16.3 %collective-permute-start.28 = (bf16[160,768]{1,0:T(8,128)(2,1)S(1)}, bf16[160,768]{1,0:T(8,128)(2,1)S(1)}, u32[]{:S(2)}, u32[]{:S(2)}) collective-permute-start(bf16[160,768]{1,0:T(8,128)(2,1)S(1)} %copy-done.73), channel_id=1, source_target_pairs={{0,8},{1,9},{2,10},{3,11},{4,12},{5,13},{6,14},{7,15},{8,0},{9,1},... | collective-permute-start | bytes 737288 | tf_op jit(solution)/shard_map/ppermute | solution.py:748
  110.2 16.3 %collective-permute-start.29 = (bf16[160,768]{1,0:T(8,128)(2,1)S(1)}, bf16[160,768]{1,0:T(8,128)(2,1)S(1)}, u32[]{:S(2)}, u32[]{:S(2)}) collective-permute-start(bf16[160,768]{1,0:T(8,128)(2,1)S(1)} %copy-done.71), channel_id=1, source_target_pairs={{0,10},{1,11},{2,8},{3,9},{4,14},{5,15},{6,12},{7,13},{8,2},{9,3},... | collective-permute-start | bytes 737288 | tf_op jit(solution)/shard_map/ppermute | solution.py:748
  158.1 25.6 %collective-permute-start.42 = (bf16[160,768]{1,0:T(8,128)(2,1)}, bf16[160,768]{1,0:T(8,128)(2,1)S(1)}, u32[]{:S(2)}, u32[]{:S(2)}) collective-permute-start(bf16[160,768]{1,0:T(8,128)(2,1)} %get-tuple-element.240), channel_id=1, source_target_pairs={{0,10},{1,11},{2,8},{3,9},{4,14},{5,15},{6,12},{7,13},{8,2},{9,3},... | collective-permute-start | bytes 737288 | tf_op jit(solution)/shard_map/ppermute | solution.py:748
  160.2 23.5 %collective-permute-start.41 = (bf16[160,768]{1,0:T(8,128)(2,1)}, bf16[160,768]{1,0:T(8,128)(2,1)S(1)}, u32[]{:S(2)}, u32[]{:S(2)}) collective-permute-start(bf16[160,768]{1,0:T(8,128)(2,1)} %get-tuple-element.238), channel_id=1, source_target_pairs={{0,8},{1,9},{2,10},{3,11},{4,12},{5,13},{6,14},{7,15},{8,0},{9,1},... | collective-permute-start | bytes 737288 | tf_op jit(solution)/shard_map/ppermute | solution.py:748
  160.2 23.5 %collective-permute-start.40 = (bf16[160,768]{1,0:T(8,128)(2,1)}, bf16[160,768]{1,0:T(8,128)(2,1)S(1)}, u32[]{:S(2)}, u32[]{:S(2)}) collective-permute-start(bf16[160,768]{1,0:T(8,128)(2,1)} %get-tuple-element.236), channel_id=1, source_target_pairs={{0,2},{1,3},{2,0},{3,1},{4,6},{5,7},{6,4},{7,5},{8,10},{9,11},{10,... | collective-permute-start | bytes 737288 | tf_op jit(solution)/shard_map/ppermute | solution.py:748
  195.2 19.8 %collective-permute-start.48 = (bf16[2,2,128,768]{3,2,1,0:T(8,128)(2,1)}, bf16[2,2,128,768]{3,2,1,0:T(8,128)(2,1)S(1)}, u32[]{:S(2)}, u32[]{:S(2)}) collective-permute-start(bf16[2,2,128,768]{3,2,1,0:T(8,128)(2,1)} %get-tuple-element.253), channel_id=1, source_target_pairs={{0,4},{1,5},{2,6},{3,7},{4,0},{5,1},{6,2},{7,3},{8,12},{9,13},{10,... | collective-permute-start | bytes 2359304 | tf_op jit(solution)/shard_map/ppermute | solution.py:748
  195.8 16.3 %collective-permute-start.44 = (bf16[160,768]{1,0:T(8,128)(2,1)S(1)}, bf16[160,768]{1,0:T(8,128)(2,1)S(1)}, u32[]{:S(2)}, u32[]{:S(2)}) collective-permute-start(bf16[160,768]{1,0:T(8,128)(2,1)S(1)} %copy-done.68), channel_id=1, source_target_pairs={{0,2},{1,3},{2,0},{3,1},{4,6},{5,7},{6,4},{7,5},{8,10},{9,11},{10,... | collective-permute-start | bytes 737288 | tf_op jit(solution)/shard_map/ppermute | solution.py:748
  215.1 22.5 %collective-permute-start.52 = (bf16[160,768]{1,0:T(8,128)(2,1)}, bf16[160,768]{1,0:T(8,128)(2,1)S(1)}, u32[]{:S(2)}, u32[]{:S(2)}) collective-permute-start(bf16[160,768]{1,0:T(8,128)(2,1)} %collective-permute-done.49), channel_id=1, source_target_pairs={{0,2},{1,3},{2,0},{3,1},{4,6},{5,7},{6,4},{7,5},{8,10},{9,11},{10,... | collective-permute-start | bytes 737288 | tf_op jit(solution)/shard_map/ppermute | solution.py:748
  215.8 22.4 %collective-permute-start.53 = (bf16[160,768]{1,0:T(8,128)(2,1)}, bf16[160,768]{1,0:T(8,128)(2,1)S(1)}, u32[]{:S(2)}, u32[]{:S(2)}) collective-permute-start(bf16[160,768]{1,0:T(8,128)(2,1)} %collective-permute-done.50), channel_id=1, source_target_pairs={{0,8},{1,9},{2,10},{3,11},{4,12},{5,13},{6,14},{7,15},{8,0},{9,1},... | collective-permute-start | bytes 737288 | tf_op jit(solution)/shard_map/ppermute | solution.py:748
  217.8 20.4 %collective-permute-start.54 = (bf16[160,768]{1,0:T(8,128)(2,1)}, bf16[160,768]{1,0:T(8,128)(2,1)S(1)}, u32[]{:S(2)}, u32[]{:S(2)}) collective-permute-start(bf16[160,768]{1,0:T(8,128)(2,1)} %collective-permute-done.51), channel_id=1, source_target_pairs={{0,10},{1,11},{2,8},{3,9},{4,14},{5,15},{6,12},{7,13},{8,2},{9,3},... | collective-permute-start | bytes 737288 | tf_op jit(solution)/shard_map/ppermute | solution.py:748
  218.6 30.3 %collective-permute-start.55 = (bf16[2,2,128,768]{3,2,1,0:T(8,128)(2,1)S(1)}, bf16[2,2,128,768]{3,2,1,0:T(8,128)(2,1)S(1)}, u32[]{:S(2)}, u32[]{:S(2)}) collective-permute-start(bf16[2,2,128,768]{3,2,1,0:T(8,128)(2,1)S(1)} %copy-done.57), channel_id=1, source_target_pairs={{0,4},{1,5},{2,6},{3,7},{4,0},{5,1},{6,2},{7,3},{8,12},{9,13},{10,... | collective-permute-start | bytes 2359304 | tf_op jit(solution)/shard_map/ppermute | solution.py:748
  237.0 23.7 %collective-permute-start.57 = (bf16[1,2,128,768]{3,2,1,0:T(8,128)(2,1)S(1)}, bf16[1,2,128,768]{3,2,1,0:T(8,128)(2,1)S(1)}, u32[]{:S(2)}, u32[]{:S(2)}) collective-permute-start(bf16[1,2,128,768]{3,2,1,0:T(8,128)(2,1)S(1)} %constant_dynamic-slice_fusion.9), channel_id=1, source_target_pairs={{0,16},{1,17},{2,18},{3,19},{4,20},{5,21},{6,22},{7,23},{8,24},{9,... | collective-permute-start | bytes 1179656 | tf_op jit(solution)/shard_map/ppermute | solution.py:748
  237.6 23.2 %collective-permute-start.56 = (bf16[2,2,128,768]{3,2,1,0:T(8,128)(2,1)S(1)}, bf16[2,2,128,768]{3,2,1,0:T(8,128)(2,1)S(1)}, u32[]{:S(2)}, u32[]{:S(2)}) collective-permute-start(bf16[2,2,128,768]{3,2,1,0:T(8,128)(2,1)S(1)} %copy-done.56), channel_id=1, source_target_pairs={{0,4},{1,5},{2,6},{3,7},{4,0},{5,1},{6,2},{7,3},{8,12},{9,13},{10,... | collective-permute-start | bytes 2359304 | tf_op jit(solution)/shard_map/ppermute | solution.py:748
  247.5 25.2 %collective-permute-start.58 = (bf16[2,2,32,3072]{3,2,1,0:T(8,128)(2,1)}, bf16[2,2,32,3072]{3,2,1,0:T(8,128)(2,1)S(1)}, u32[]{:S(2)}, u32[]{:S(2)}) collective-permute-start(bf16[2,2,32,3072]{3,2,1,0:T(8,128)(2,1)} %get-tuple-element.298), channel_id=1, source_target_pairs={{0,4},{1,5},{2,6},{3,7},{4,0},{5,1},{6,2},{7,3},{8,12},{9,13},{10,... | collective-permute-start | bytes 2359304 | tf_op jit(solution)/shard_map/ppermute | solution.py:748
  272.9 16.0 %collective-permute-start.61 = (bf16[2,768,384]{2,1,0:T(8,128)(2,1)}, bf16[2,768,384]{2,1,0:T(8,128)(2,1)S(1)}, u32[]{:S(2)}, u32[]{:S(2)}) collective-permute-start(bf16[2,768,384]{2,1,0:T(8,128)(2,1)} %get-tuple-element.300), channel_id=1, source_target_pairs={{0,1},{1,0},{2,3},{3,2},{4,5},{5,4},{6,7},{7,6},{8,9},{9,8},{10,11... | collective-permute-start | bytes 3538952 | tf_op jit(solution)/shard_map/ppermute | solution.py:748
  276.0 46.9 %collective-permute-start.72 = (bf16[1,4,128,768]{3,2,1,0:T(8,128)(2,1)}, bf16[1,4,128,768]{3,2,1,0:T(8,128)(2,1)}, u32[]{:S(2)}, u32[]{:S(2)}) collective-permute-start(bf16[1,4,128,768]{3,2,1,0:T(8,128)(2,1)} %pad_maximum_fusion.4), channel_id=1, source_target_pairs={{0,16},{1,17},{2,18},{3,19},{4,20},{5,21},{6,22},{7,23},{8,24},{9,... | collective-permute-start | bytes 2359304 | tf_op jit(solution)/shard_map/ppermute | solution.py:748
  279.4 51.9 %collective-permute-start.64 = (bf16[2,2,32,3072]{3,2,1,0:T(8,128)(2,1)}, bf16[2,2,32,3072]{3,2,1,0:T(8,128)(2,1)}, u32[]{:S(2)}, u32[]{:S(2)}) collective-permute-start(bf16[2,2,32,3072]{3,2,1,0:T(8,128)(2,1)} %get-tuple-element.317), channel_id=1, source_target_pairs={{0,4},{1,5},{2,6},{3,7},{4,0},{5,1},{6,2},{7,3},{8,12},{9,13},{10,... | collective-permute-start | bytes 2359304 | tf_op jit(solution)/shard_map/ppermute | solution.py:748
  293.0 40.5 %collective-permute-start.65 = (bf16[1,2,32,3072]{3,2,1,0:T(8,128)(2,1)}, bf16[1,2,32,3072]{3,2,1,0:T(8,128)(2,1)}, u32[]{:S(2)}, u32[]{:S(2)}) collective-permute-start(bf16[1,2,32,3072]{3,2,1,0:T(8,128)(2,1)} %constant_dynamic-slice_fusion.6), channel_id=1, source_target_pairs={{0,16},{1,17},{2,18},{3,19},{4,20},{5,21},{6,22},{7,23},{8,24},{9,... | collective-permute-start | bytes 1179656 | tf_op jit(solution)/shard_map/ppermute | solution.py:748
  293.3 39.5 %collective-permute-start.63 = (bf16[2,8,48,384]{3,2,1,0:T(8,128)(2,1)}, bf16[2,8,48,384]{3,2,1,0:T(8,128)(2,1)}, u32[]{:S(2)}, u32[]{:S(2)}) collective-permute-start(bf16[2,8,48,384]{3,2,1,0:T(8,128)(2,1)} %get-tuple-element.381), channel_id=1, source_target_pairs={{0,2},{1,3},{2,0},{3,1},{4,6},{5,7},{6,4},{7,5},{8,10},{9,11},{10,... | collective-permute-start | bytes 1769480 | tf_op jit(solution)/shard_map/ppermute | solution.py:748
  294.6 35.1 %collective-permute-start.60 = (bf16[2,8,48,384]{3,2,1,0:T(8,128)(2,1)}, bf16[2,8,48,384]{3,2,1,0:T(8,128)(2,1)}, u32[]{:S(2)}, u32[]{:S(2)}) collective-permute-start(bf16[2,8,48,384]{3,2,1,0:T(8,128)(2,1)} %get-tuple-element.379), channel_id=1, source_target_pairs={{0,2},{1,3},{2,0},{3,1},{4,6},{5,7},{6,4},{7,5},{8,10},{9,11},{10,... | collective-permute-start | bytes 1769480 | tf_op jit(solution)/shard_map/ppermute | solution.py:748
  332.8 27.0 %collective-permute-start.69 = (bf16[2,2,32,3072]{3,2,1,0:T(8,128)(2,1)S(1)}, bf16[2,2,32,3072]{3,2,1,0:T(8,128)(2,1)S(1)}, u32[]{:S(2)}, u32[]{:S(2)}) collective-permute-start(bf16[2,2,32,3072]{3,2,1,0:T(8,128)(2,1)S(1)} %copy-done.58), channel_id=1, source_target_pairs={{0,4},{1,5},{2,6},{3,7},{4,0},{5,1},{6,2},{7,3},{8,12},{9,13},{10,... | collective-permute-start | bytes 2359304 | tf_op jit(solution)/shard_map/ppermute | solution.py:748
  342.1 16.9 %collective-permute-start.77 = (f32[64,128]{1,0:T(8,128)S(1)}, f32[64,128]{1,0:T(8,128)S(1)}, u32[]{:S(2)}, u32[]{:S(2)}) collective-permute-start(f32[64,128]{1,0:T(8,128)S(1)} %add.652), channel_id=1, source_target_pairs={{0,2},{1,3},{2,0},{3,1},{4,6},{5,7},{6,4},{7,5},{8,10},{9,11},{10,... | collective-permute-start | bytes 98312 | tf_op jit(solution)/shard_map/ppermute | solution.py:748
  354.0 60.4 %collective-permute-start.83 = (bf16[2,32,3072]{2,1,0:T(8,128)(2,1)S(1)}, bf16[2,32,3072]{2,1,0:T(8,128)(2,1)S(1)}, u32[]{:S(2)}, u32[]{:S(2)}) collective-permute-start(bf16[2,32,3072]{2,1,0:T(8,128)(2,1)S(1)} %fusion.14), channel_id=1, source_target_pairs={{0,8},{1,9},{2,10},{3,11},{4,12},{5,13},{6,14},{7,15},{8,0},{9,1},... | collective-permute-start | bytes 1179656 | tf_op jit(solution)/shard_map/ppermute | solution.py:748
  358.9 28.4 %collective-permute-start.68 = (bf16[2,2,2,48,384]{4,3,0,1,2:T(8,128)(2,1)S(1)}, bf16[2,2,2,48,384]{4,3,0,1,2:T(8,128)(2,1)S(1)}, u32[]{:S(2)}, u32[]{:S(2)}) collective-permute-start(bf16[2,2,2,48,384]{4,3,0,1,2:T(8,128)(2,1)S(1)} %bitcast.104), channel_id=1, source_target_pairs={{0,8},{1,9},{2,10},{3,11},{4,12},{5,13},{6,14},{7,15},{8,0},{9,1},... | collective-permute-start | bytes 884744 | tf_op jit(solution)/shard_map/ppermute | solution.py:748
  359.0 29.0 %collective-permute-start.82 = (bf16[1,2,32,3072]{3,2,1,0:T(8,128)(2,1)S(1)}, bf16[1,2,32,3072]{3,2,1,0:T(8,128)(2,1)S(1)}, u32[]{:S(2)}, u32[]{:S(2)}) collective-permute-start(bf16[1,2,32,3072]{3,2,1,0:T(8,128)(2,1)S(1)} %constant_dynamic-slice_fusion.5), channel_id=1, source_target_pairs={{0,16},{1,17},{2,18},{3,19},{4,20},{5,21},{6,22},{7,23},{8,24},{9,... | collective-permute-start | bytes 1179656 | tf_op jit(solution)/shard_map/ppermute | solution.py:748
  360.1 54.0 %collective-permute-start.75 = (bf16[1,2,32,3072]{3,2,1,0:T(8,128)(2,1)S(1)}, bf16[1,2,32,3072]{3,2,1,0:T(8,128)(2,1)S(1)}, u32[]{:S(2)}, u32[]{:S(2)}) collective-permute-start(bf16[1,2,32,3072]{3,2,1,0:T(8,128)(2,1)S(1)} %constant_dynamic-slice_fusion.2), channel_id=1, source_target_pairs={{0,16},{1,17},{2,18},{3,19},{4,20},{5,21},{6,22},{7,23},{8,24},{9,... | collective-permute-start | bytes 1179656 | tf_op jit(solution)/shard_map/ppermute | solution.py:748
  388.0 20.8 %collective-permute-start.73 = (bf16[3,128,768]{2,1,0:T(8,128)(2,1)S(1)}, bf16[3,128,768]{2,1,0:T(8,128)(2,1)S(1)}, u32[]{:S(2)}, u32[]{:S(2)}) collective-permute-start(bf16[3,128,768]{2,1,0:T(8,128)(2,1)S(1)} %pad_maximum_fusion.5), channel_id=1, source_target_pairs={{0,8},{1,9},{2,10},{3,11},{4,12},{5,13},{6,14},{7,15},{8,0},{9,1},... | collective-permute-start | bytes 1769480 | tf_op jit(solution)/shard_map/ppermute | solution.py:748
  (134 other events, 1087.8 us)

commit v6 on v5

--- a/solution.py
+++ b/solution.py
@@ -952,14 +952,6 @@
     group_masks = bits(groups)[1:]
     dp_masks = sorted(bits(copies), key=lambda mask: (mask != PAIR, mask))
 
-    def over_groups(got, stay, *due):
-        got = add(after(got, *due), stay).reshape(2, copies, in_rows, columns)
-        for mask in group_masks[:-1]:
-            away_part, stay_part = fold(got, (here_group // mask) % 2, 2)
-            got = add(swap(away_part, 0, mask), stay_part)
-        away_part, stay_part = fold(got, (here_group // group_masks[-1]) % 2, 2)
-        return swap(away_part, 0, group_masks[-1]), stay_part
-
     def over_dp(total, mask, passed):
         axis = 1 + sorted([other for other in dp_masks if other not in passed], reverse=True).index(mask)
         bit = (here_dp // mask) % 2
@@ -968,30 +960,25 @@
         return swap(away_part, mask, 0), stay_part
 
     weights_got = [swap(part, 0, 1) for part in weights_away]
-    first = over_groups(weights_got[0], stay_1, keep_d)
-    second = over_groups(weights_got[1], stay_2, first[1])
-    away_d, stay_d = near_add(after(got_d, second[1]), keep_d)
+    halves_sum = [
+        add(after(got, keep_d), stay).reshape(2, copies, in_rows, columns) for got, stay in zip(weights_got, (stay_1, stay_2))
+    ]
+    for mask in group_masks[:-1]:
+        folded = [fold(part, (here_group // mask) % 2, 2) for part in halves_sum]
+        halves_sum = [add(swap(away_part, 0, mask), stay_part) for away_part, stay_part in folded]
+    folded = [fold(part, (here_group // group_masks[-1]) % 2, 2) for part in halves_sum]
+    y_stay = jnp.concatenate([stay_part for _, stay_part in folded])
+    y_got = swap(jnp.concatenate([away_part for away_part, _ in folded]), 0, group_masks[-1])
+    away_d, stay_d = near_add(after(got_d, y_stay), keep_d)
     far_d = far_trade(away_d)
     grad_input, gain_attn_parts = enter(
         core_index, after(grad_qkv_rows, away_d), mine, other, tokens, gain_attn, grad_middle
     )
-    done_c = finish(after(far_c, gain_attn_parts), stay_c)
-    grad_table = table_gradient(after(bands, second[1]), position_bias_table.shape[1])
-
-    chains = [add(after(first[0], away_d, gain_attn_parts), first[1]).reshape((2,) + (2,) * len(dp_masks) + (-1, columns)), None]
-    trades = [over_dp(chains[0], dp_masks[0], ()), None]
-    away_e, stay_e = near_add(after(got_e, chains[0]), keep_e)
+    grad_table = table_gradient(after(bands, y_stay), position_bias_table.shape[1])
+
+    away_e, stay_e = near_add(after(got_e, gain_attn_parts), keep_e)
     got_f = swap(after(send_f, away_e), 1, 0)
-    chains[1] = add(after(second[0], done_c, grad_table, away_e), second[1]).reshape(chains[0].shape)
-    trades[1] = over_dp(chains[1], dp_masks[0], ())
-    total = trades[1][1]
-    far_e = far_trade(after(away_e, total))
-    done_d = finish(after(far_d, chains[0]), stay_d)
-    away_f, stay_f = near_add(after(got_f, total), keep_f)
-    far_f = far_trade(away_f)
-    trades = [(after(trades[0][0], total, done_d), trades[0][1]), (after(trades[1][0], away_f), trades[1][1])]
-
-    normed2, squares, gain_moe_parts = after((normed2, squares, gain_moe_parts), second[1])
+    normed2, squares, gain_moe_parts = after((normed2, squares, gain_moe_parts), y_stay)
     grad_router = jnp.einsum("td,te->de", normed2, grad_logits, preferred_element_type=f32)
     small = [
         jnp.sum(gain_moe_parts, axis=0),
@@ -1002,29 +989,32 @@
     ]
     sizes = [value.size for value in small]
     flat = jnp.concatenate([value.reshape(-1) for value in small])
-    flat = after(jnp.pad(flat, (0, -sum(sizes) % 1024)).reshape(-1, 128), total)
-
+    flat = jnp.pad(flat, (0, -sum(sizes) % 1024)).reshape(-1, 128)
     flat = flat + swap(flat, 0, 1)
-    for place, mask in enumerate(dp_masks):
-        flat_got = swap(flat, 0, group_masks[0]) if mask == PAIR else swap(flat, mask, 0)
-        if place + 1 == len(dp_masks):
-            trades[1] = (after(trades[1][0], out_theirs), trades[1][1])
-        if place == 1:
-            done_e = finish(after(far_e, chains[1]), stay_e)
-            trades[1] = (after(trades[1][0], done_e), trades[1][1])
-        chains = [add(*trades[0]), None]
-        if place + 1 < len(dp_masks):
-            trades_next = [over_dp(chains[0], dp_masks[place + 1], dp_masks[: place + 1]), None]
-        chains[1] = add(after(trades[1][0], chains[0]), trades[1][1])
+    done_c = finish(after(far_c, away_e), stay_c)
+    total = add(after(y_got, away_e, flat, done_c), y_stay)
+    total = total.reshape((4,) + (2,) * len(dp_masks) + (-1, columns))
+
+
+    passed_masks = []
+    for mask in dp_masks:
+        got, stay = over_dp(total, mask, passed_masks)
+        passed_masks.append(mask)
+        flat_got = swap(after(flat, stay), 0, group_masks[0]) if mask == PAIR else swap(flat, mask, 0)
+        if mask == PAIR:
+            far_e = far_trade(after(away_e, stay))
+            away_f, stay_f = near_add(after(got_f, stay), keep_f)
+            far_f = far_trade(away_f)
+            got = after(got, away_f)
+        total = add(got, stay)
         flat = flat + flat_got
-        if place + 1 < len(dp_masks):
-            trades_next[1] = over_dp(chains[1], dp_masks[place + 1], dp_masks[: place + 1])
-            trades = trades_next
         if mask == PAIR:
+            done_d = finish(after(far_d, total), stay_d)
             in_first = swap(done_d, PAIR, 0)
-            out_theirs = swap(after(jnp.concatenate([done_a, done_c[:1]]), chains[1]), PAIR, 0)
-        flat = after(flat, chains[1])
-    total = jnp.concatenate(chains)
+            out_theirs = swap(after(jnp.concatenate([done_a, done_c[:1]]), total), PAIR, 0)
+        elif len(passed_masks) == 2:
+            done_e = finish(after(far_e, total), stay_e)
+        flat = after(flat, total)
     in_theirs = jnp.concatenate([in_first, swap(done_e[:1], PAIR, 0)])
     for mask in reversed(group_masks):
         bit = (here_group // mask) % 2

time: 428 us -> 417 us (0.974)
  waiting for transfers between devices: 99.5 us -> 84.5 us
    ppermute x71 -> x67, waiting for transfers between devices: 90.7 us -> 75.7 us  [swap(): return lax.ppermute(value, AXES, pairs)]
    unnamed x167 -> x157, local copies, waits for them, and re-layouts: 14 us -> 16.9 us
    convert_element_type x18 -> x14, other arithmetic: 8.69 us -> 7.61 us  [add(): return (left.astype(f32) + right.astype(f32)).astype(bf16)]
    ppermute x71 -> x67, starting transfers between devices: 74.8 us -> 73.9 us  [swap(): return lax.ppermute(value, AXES, pairs)]
  transfers between devices with their start and end apart: 85 -> 81, of which waited for: 28 -> 24; matrix products, arithmetic and copies ran while one was open for 13% -> 15% of each run, Pallas kernels for 31% -> 32%
where the time goes in v6:
time: 417 us; the launch traced here: 412 us
  Pallas kernels  157 us (38%)
  starting transfers between devices  91 us (22%)
  waiting for transfers between devices  84.5 us (20%)
  local copies, waits for them, and re-layouts  36 us (9%)
  other arithmetic  28.2 us (7%)
  matrix products  9.14 us (2%)
  between operations  5.97 us (1%)
    ppermute x67, waiting for transfers between devices, swap(): return lax.ppermute(value, AXES, pairs)  75.7 us
    ppermute x67, starting transfers between devices, swap(): return lax.ppermute(value, AXES, pairs)  73.9 us
    pallas_call x4, Pallas kernels, weight_part(): pl.pallas_call(lambda *refs: weight_part_kernel(*refs, count=count, plans...  30.7 us
    pallas_call x2, Pallas kernels, expert_forward(): pl.pallas_call(lambda *refs: expert_forward_kernel(*refs, chunk=chunk, co...  27.4 us
    pallas_call x2, Pallas kernels, expert_backward(): pl.pallas_call(lambda *refs: expert_backward_kernel(*refs, chunk=chunk, c...  25.2 us
    ppermute x14, starting transfers between devices, gather_ring(): lax.ppermute(after(held, *due[step - 2:step - 1]) if step > 1 else held,...  17.1 us
    unnamed x157, local copies, waits for them, and re-layouts  16.9 us
    pallas_call x1, Pallas kernels, attention_forward(): pl.pallas_call(lambda *refs: attention_forward_kernel(*refs, heads=64, bl...  12.6 us
  transfers between devices with their start and end apart: 81, of which 24 were waited for; matrix products, arithmetic and copies ran while one was open for 15% of the time, Pallas kernels for 32%

profile of v6, /device:TPU:0, one launch (start us, length us, event | category | flops | bytes accessed | tf_op | source)
XLA Modules:
  0.0 411.9 jit_solution(15284683628633366877)
XLA Ops:
  1.7 3.1 collective-permute-start
  34.3 3.3 join.1.mine.refs_15_
  46.4 6.4 %project.1.refs_2_.refs_3_.refs_4_.refs_0_.refs_1_ = bf16[3,512,768]{2,1,0:T(8,128)(2,1)} custom-call(s32[1]{0:T(128)} %bitcast.2.core.refs_0_, bf16[512,768]{1,0:T(8,128)(2,1)} %fusion.6.rows.refs_1_, bf16[4,768,384]{2,1,0:T(8,128)(2,1)} %join.1.mine.refs_15_, bf16[4,768,384]{2,1,0:T(8,128)(2,1)} %copy-done), custom_call_target="tpu_custom_call" | custom-call | flops 1480000000 | tf_op jit(solution)/shard_map/project/pallas_call | solution.py:396
  55.0 12.6 %attention_forward.1 = (bf16[512,768]{1,0:T(8,128)(2,1)}, bf16[12,512,512]{2,1,0:T(8,128)(2,1)}) custom-call(f32[12]{0:T(128)} %slice_reduce_fusion.refs_0_, s32[1]{0:T(128)S(6)} %copy.109.refs_1_, bf16[3,512,768]{2,1,0:T(8,128)(2,1)} %project.1.refs_2_.refs_3_.refs_4_.refs_0_.refs_1_, bf16[3,512,768]{2,1,0:T(8,128)(2,1)} %project.1.refs_2_.refs_3_.refs_4_.refs_0_.refs_1_, ...), custom_call_target="tpu_custom_call" | custom-call | flops 4809999872 | tf_op jit(solution)/shard_map/attention_forward/pallas_call | solution.py:214
  67.7 5.9 %route.1 = (f32[512,768]{1,0:T(8,128)}, bf16[512,768]{1,0:T(8,128)(2,1)}, f32[512,2]{1,0:T(8,128)}, bf16[160,768]{1,0:T(8,128)(2,1)}, bf16[160,768]{1,0:T(8,128)...) custom-call(s32[1]{0:T(128)} %bitcast.2.core.refs_0_, ...), custom_call_target="tpu_custom_call" | custom-call | flops 2220000000 | tf_op jit(solution)/shard_map/route/pallas_call | solution.py:447
  79.9 3.8 collective-permute-done.18.refs_4_
  85.0 4.0 collective-permute-done.20.refs_2_
  91.3 13.7 %expert_forward.2 = (bf16[3072,640]{1,0:T(8,128)(2,1)}, bf16[640,3072]{1,0:T(8,128)(2,1)}, bf16[768,640]{1,0:T(8,128)(2,1)}, bf16[160,768]{1,0:T(8,128)(2,1)}, b...) custom-call(s32[1]{0:T(128)} %bitcast.4.refs_0_, ...), custom_call_target="tpu_custom_call" | custom-call | flops 4809999872 | tf_op jit(solution)/shard_map/expert_forward/pallas_call | solution.py:78
  105.9 4.2 %collective-permute-start.27 = (bf16[160,768]{1,0:T(8,128)(2,1)S(1)}, bf16[160,768]{1,0:T(8,128)(2,1)S(1)}, u32[]{:S(2)}, u32[]{:S(2)}) collective-permute-start(bf16[160,768]{1,0:T(8,128)(2,1)S(1)} %copy-done.70), channel_id=1, source_target_pairs={{0,2},{1,3},{2,0},{3,1},{4,6},{5,7},{6,4},{7,5},{8,10},{9,11},{10,... | collective-permute-start | bytes 737288 | tf_op jit(solution)/shard_map/ppermute | solution.py:748
  112.7 13.8 %expert_forward.3 = (bf16[3072,640]{1,0:T(8,128)(2,1)}, bf16[640,3072]{1,0:T(8,128)(2,1)}, bf16[768,640]{1,0:T(8,128)(2,1)}, bf16[160,768]{1,0:T(8,128)(2,1)}, b...) custom-call(s32[1]{0:T(128)} %bitcast.4.refs_0_, bf16[640,768]{1,0:T(8,128)(2,1)} %copy-done.15, ...), custom_call_target="tpu_custom_call" | custom-call | flops 4809999872 | tf_op jit(solution)/shard_map/expert_forward/pallas_call | solution.py:78
  135.5 5.6 %collective-permute-done.26 = f32[8,128]{1,0:T(8,128)S(1)} collective-permute-done((f32[8,128]{1,0:T(8,128)S(1)}, f32[8,128]{1,0:T(8,128)S(1)}, u32[]{:S(2)}, u32[]{:S(2)}) %collective-permute-start.26) | collective-permute-done | bytes 4128 | tf_op jit(solution)/shard_map/ppermute | solution.py:748
  144.1 8.5 %combine.1 = (bf16[512,768]{1,0:T(8,128)(2,1)}, f32[512,768]{1,0:T(8,128)}, bf16[512,8]{1,0:T(8,128)(2,1)}, f32[8,768]{1,0:T(8,128)}, bf16[160,768]{1,0:T(8,128)...) custom-call(s32[512,2]{1,0:T(8,128)} %multiply_add_fusion.refs_0_.re, ...), custom_call_target="tpu_custom_call" | custom-call | flops 2960000000 | tf_op jit(solution)/shard_map/combine/pallas_call | solution.py:503
  154.0 3.3 collective-permute-start.38
  161.7 2.7 collective-permute-done.38.refs_3_
  164.4 6.2 %collective-permute-done.39.refs_4_ = bf16[160,768]{1,0:T(8,128)(2,1)S(1)} collective-permute-done((bf16[160,768]{1,0:T(8,128)(2,1)}, bf16[160,768]{1,0:T(8,128)(2,1)S(1)}, u32[]{:S(2)}, u32[]{:S(2)}) %collective-permute-start.39) | collective-permute-done | bytes 245792 | tf_op jit(solution)/shard_map/ppermute | solution.py:748
  171.2 12.5 %expert_backward.2 = (bf16[640,3072]{1,0:T(8,128)(2,1)}, bf16[640,768]{1,0:T(8,128)(2,1)}, bf16[160,768]{1,0:T(8,128)(2,1)}, bf16[160,768]{1,0:T(8,128)(2,1)}, b...) custom-call(s32[1]{0:T(128)} %bitcast.4.refs_0_, bf16[160,768]{1,0:T(8,128)(2,1)} %get-tuple-element.218.refs_1_, ...), custom_call_target="tpu_custom_call" | custom-call | flops 4070000128 | tf_op jit(solution)/shard_map/expert_backward/pallas_call | solution.py:135
  187.4 7.8 %weight_part.4 = (bf16[2,2,128,768]{3,2,1,0:T(8,128)(2,1)}, bf16[2,2,128,768]{3,2,1,0:T(8,128)(2,1)}, bf16[2,2,128,768]{3,2,1,0:T(8,128)(2,1)}) custom-call(s32[4]{0:T(128)} %pad_add_fusion.1.refs_0_, bf16[3072,640]{1,0:T(8,128)(2,1)} %get-tuple-element.194.refs_1_.refs_2_.refs_3_.refs_4_, ...), custom_call_target="tpu_custom_call" | custom-call | flops 1480000000 | tf_op jit(solution)/shard_map/weight_part/pallas_call | solution.py:337
  199.4 12.7 %expert_backward.3 = (bf16[640,3072]{1,0:T(8,128)(2,1)}, bf16[640,768]{1,0:T(8,128)(2,1)}, bf16[160,768]{1,0:T(8,128)(2,1)}, bf16[160,768]{1,0:T(8,128)(2,1)}, b...) custom-call(s32[1]{0:T(128)} %bitcast.4.refs_0_, bf16[640,768]{1,0:T(8,128)(2,1)} %copy-done.1, ...), custom_call_target="tpu_custom_call" | custom-call | flops 4070000128 | tf_op jit(solution)/shard_map/expert_backward/pallas_call | solution.py:135
  220.1 7.8 %weight_part.5 = (bf16[2,2,128,768]{3,2,1,0:T(8,128)(2,1)}, bf16[2,2,128,768]{3,2,1,0:T(8,128)(2,1)}, bf16[2,2,128,768]{3,2,1,0:T(8,128)(2,1)}) custom-call(s32[4]{0:T(128)} %pad_add_fusion.2.refs_0_, bf16[3072,640]{1,0:T(8,128)(2,1)} %get-tuple-element.194.refs_1_.refs_2_.refs_3_.refs_4_, ...), custom_call_target="tpu_custom_call" | custom-call | flops 1480000000 | tf_op jit(solution)/shard_map/weight_part/pallas_call | solution.py:337
  229.3 7.6 %weight_part.6 = (bf16[2,2,32,3072]{3,2,1,0:T(8,128)(2,1)}, bf16[2,2,32,3072]{3,2,1,0:T(8,128)(2,1)}, bf16[2,2,32,3072]{3,2,1,0:T(8,128)(2,1)}) custom-call(s32[4]{0:T(128)} %pad_add_fusion.1.refs_0_, bf16[768,640]{1,0:T(8,128)(2,1)} %get-tuple-element.224.refs_1_.refs_2_.refs_3_.refs_4_, ...), custom_call_target="tpu_custom_call" | custom-call | flops 1480000000 | tf_op jit(solution)/shard_map/weight_part/pallas_call | solution.py:337
  238.9 8.5 %collect.1 = (f32[512,768]{1,0:T(8,128)}, bf16[512,768]{1,0:T(8,128)(2,1)}, bf16[512,768]{1,0:T(8,128)(2,1)}, f32[8,768]{1,0:T(8,128)}) custom-call(s32[1]{0:T(128)} %bitcast.2.core.refs_0_, s32[512,2]{1,0:T(8,128)} %multiply_add_fusion.refs_0_.refs_1_, bf16[160,768]{1,0:T(8,128)(2,1)} %get-tuple-element.266.refs_2_, bf16[160,768]{1,0:T(8,128)(2,1)} %copy-done.57, ...), custom_call_target="tpu_custom_call" | custom-call | flops 2960000000 | tf_op jit(solution)/shard_map/collect/pallas_call | solution.py:554
  249.1 11.5 %attention_backward.1 = (bf16[3,512,768]{2,1,0:T(8,128)(2,1)}, f32[12,4,128,128]{3,2,1,0:T(8,128)}) custom-call(bf16[3,512,768]{2,1,0:T(8,128)(2,1)} %project.1.refs_2_.refs_3_.refs_4_.refs_0_.refs_1_, bf16[3,512,768]{2,1,0:T(8,128)(2,1)} %project.1.refs_2_.refs_3_.refs_4_.refs_0_.refs_1_, ...), custom_call_target="tpu_custom_call" | custom-call | flops 1480000000 | tf_op jit(solution)/shard_map/attention_backward/pallas_call | solution.py:280
  261.7 8.4 %outer_halves.1 = (bf16[2,768,384]{2,1,0:T(8,128)(2,1)}, bf16[2,768,384]{2,1,0:T(8,128)(2,1)}, bf16[2,768,384]{2,1,0:T(8,128)(2,1)}, bf16[2,768,384]{2,1,0:T(8,128)(2,1)}) custom-call(s32[1]{0:T(128)} %bitcast.2.core.refs_0_, bf16[512,768]{1,0:T(8,128)(2,1)} %fusion.6.rows.refs_1_, bf16[512,768]{1,0:T(8,128)(2,1)} %get-tuple-element.186.attended.refs_2_, ...), custom_call_target="tpu_custom_call" | custom-call | flops 740000000 | tf_op jit(solution)/shard_map/outer_halves/pallas_call | solution.py:604
  279.7 7.5 %weight_part.7 = (bf16[2,2,32,3072]{3,2,1,0:T(8,128)(2,1)}, bf16[2,2,32,3072]{3,2,1,0:T(8,128)(2,1)}, bf16[2,2,32,3072]{3,2,1,0:T(8,128)(2,1)}) custom-call(s32[4]{0:T(128)} %pad_add_fusion.2.refs_0_, bf16[768,640]{1,0:T(8,128)(2,1)} %get-tuple-element.224.refs_1_.refs_2_.refs_3_.refs_4_, ...), custom_call_target="tpu_custom_call" | custom-call | flops 1480000000 | tf_op jit(solution)/shard_map/weight_part/pallas_call | solution.py:337
  295.8 8.4 %enter.1 = (f32[512,768]{1,0:T(8,128)}, f32[8,768]{1,0:T(8,128)}) custom-call(s32[1]{0:T(128)} %bitcast.2.core.refs_0_, bf16[3,512,768]{2,1,0:T(8,128)(2,1)} %get-tuple-element.306.refs_3_.grads, bf16[4,768,384]{2,1,0:T(8,128)(2,1)} %join.1.mine.refs_15_, bf16[4,768,384]{2,1,0:T(8,128)(2,1)} %copy-done, bf16[512,768]{1,0:T(8,128)(2,1)} %tokens.3, ...), custom_call_target="tpu_custom_call" | custom-call | flops 2220000000 | tf_op jit(solution)/shard_map/enter/pallas_call | solution.py:650
  309.8 6.2 %fusion.10 = f32[12,32]{1,0:T(8,128)S(1)} fusion(s32[4,128,128]{2,1,0:T(8,128)} %pad_add_fusion, f32[12,4,128,128]{3,2,1,0:T(8,128)S(1)} %copy-done.3), kind=kOutput, calls=%fused_computation.34 | convolution fusion | flops 304087040 | bytes 3409408 | tf_op jit(solution)/shard_map/hdxy,dxyb->hb/dot_general | solution.py:704
  334.4 12.7 %collective-permute-done.65 = bf16[2,2,32,3072]{3,2,1,0:T(8,128)(2,1)S(1)} collective-permute-done((bf16[2,2,32,3072]{3,2,1,0:T(8,128)(2,1)S(1)}, bf16[2,2,32,3072]{3,2,1,0:T(8,128)(2,1)S(1)}, u32[]{:S(2)}, u32[]{:S(2)}) %collective-permute-start.65) | collective-permute-done | bytes 786464 | tf_op jit(solution)/shard_map/ppermute | solution.py:748
  348.0 2.7 collective-permute-start.69
  356.3 3.6 collective-permute-done.71
  361.7 2.6 collective-permute-start.67
  364.4 21.8 %collective-permute-done.75 = bf16[1,2,32,3072]{3,2,1,0:T(8,128)(2,1)S(1)} collective-permute-done((bf16[1,2,32,3072]{3,2,1,0:T(8,128)(2,1)S(1)}, bf16[1,2,32,3072]{3,2,1,0:T(8,128)(2,1)S(1)}, u32[]{:S(2)}, u32[]{:S(2)}) %collective-permute-start.75) | collective-permute-done | bytes 393248 | tf_op jit(solution)/shard_map/ppermute | solution.py:748
  386.3 5.8 %collective-permute-done.72 = f32[64,128]{1,0:T(8,128)S(1)} collective-permute-done((f32[64,128]{1,0:T(8,128)S(1)}, f32[64,128]{1,0:T(8,128)S(1)}, u32[]{:S(2)}, u32[]{:S(2)}) %collective-permute-start.72) | collective-permute-done | bytes 32800 | tf_op jit(solution)/shard_map/ppermute | solution.py:748
  (414 shorter events, 160.6 us)
Async XLA Ops:
  77.1 27.9 %collective-permute-start.24 = (bf16[160,768]{1,0:T(8,128)(2,1)}, bf16[160,768]{1,0:T(8,128)(2,1)S(1)}, u32[]{:S(2)}, u32[]{:S(2)}) collective-permute-start(bf16[160,768]{1,0:T(8,128)(2,1)} %get-tuple-element.200), channel_id=1, source_target_pairs={{0,10},{1,11},{2,8},{3,9},{4,14},{5,15},{6,12},{7,13},{8,2},{9,3},... | collective-permute-start | bytes 737288 | tf_op jit(solution)/shard_map/ppermute | solution.py:748
  79.5 25.6 %collective-permute-start.23 = (bf16[160,768]{1,0:T(8,128)(2,1)}, bf16[160,768]{1,0:T(8,128)(2,1)S(1)}, u32[]{:S(2)}, u32[]{:S(2)}) collective-permute-start(bf16[160,768]{1,0:T(8,128)(2,1)} %get-tuple-element.198), channel_id=1, source_target_pairs={{0,8},{1,9},{2,10},{3,11},{4,12},{5,13},{6,14},{7,15},{8,0},{9,1},... | collective-permute-start | bytes 737288 | tf_op jit(solution)/shard_map/ppermute | solution.py:748
  83.7 21.4 %collective-permute-start.22 = (bf16[160,768]{1,0:T(8,128)(2,1)}, bf16[160,768]{1,0:T(8,128)(2,1)S(1)}, u32[]{:S(2)}, u32[]{:S(2)}) collective-permute-start(bf16[160,768]{1,0:T(8,128)(2,1)} %get-tuple-element.196), channel_id=1, source_target_pairs={{0,2},{1,3},{2,0},{3,1},{4,6},{5,7},{6,4},{7,5},{8,10},{9,11},{10,... | collective-permute-start | bytes 737288 | tf_op jit(solution)/shard_map/ppermute | solution.py:748
  89.0 16.0 %collective-permute-start.19 = (f32[8,128]{1,0:T(8,128)S(1)}, f32[8,128]{1,0:T(8,128)S(1)}, u32[]{:S(2)}, u32[]{:S(2)}) collective-permute-start(f32[8,128]{1,0:T(8,128)S(1)} %add.548), channel_id=1, source_target_pairs={{0,8},{1,9},{2,10},{3,11},{4,12},{5,13},{6,14},{7,15},{8,0},{9,1},... | collective-permute-start | bytes 12296 | tf_op jit(solution)/shard_map/ppermute | solution.py:748
  105.9 20.5 %collective-permute-start.27 = (bf16[160,768]{1,0:T(8,128)(2,1)S(1)}, bf16[160,768]{1,0:T(8,128)(2,1)S(1)}, u32[]{:S(2)}, u32[]{:S(2)}) collective-permute-start(bf16[160,768]{1,0:T(8,128)(2,1)S(1)} %copy-done.70), channel_id=1, source_target_pairs={{0,2},{1,3},{2,0},{3,1},{4,6},{5,7},{6,4},{7,5},{8,10},{9,11},{10,... | collective-permute-start | bytes 737288 | tf_op jit(solution)/shard_map/ppermute | solution.py:748
  110.1 16.3 %collective-permute-start.28 = (bf16[160,768]{1,0:T(8,128)(2,1)S(1)}, bf16[160,768]{1,0:T(8,128)(2,1)S(1)}, u32[]{:S(2)}, u32[]{:S(2)}) collective-permute-start(bf16[160,768]{1,0:T(8,128)(2,1)S(1)} %copy-done.68), channel_id=1, source_target_pairs={{0,8},{1,9},{2,10},{3,11},{4,12},{5,13},{6,14},{7,15},{8,0},{9,1},... | collective-permute-start | bytes 737288 | tf_op jit(solution)/shard_map/ppermute | solution.py:748
  110.2 16.3 %collective-permute-start.29 = (bf16[160,768]{1,0:T(8,128)(2,1)S(1)}, bf16[160,768]{1,0:T(8,128)(2,1)S(1)}, u32[]{:S(2)}, u32[]{:S(2)}) collective-permute-start(bf16[160,768]{1,0:T(8,128)(2,1)S(1)} %copy-done.66), channel_id=1, source_target_pairs={{0,10},{1,11},{2,8},{3,9},{4,14},{5,15},{6,12},{7,13},{8,2},{9,3},... | collective-permute-start | bytes 737288 | tf_op jit(solution)/shard_map/ppermute | solution.py:748
  127.2 15.1 %collective-permute-start.30 = (bf16[160,768]{1,0:T(8,128)(2,1)}, bf16[160,768]{1,0:T(8,128)(2,1)S(1)}, u32[]{:S(2)}, u32[]{:S(2)}) collective-permute-start(bf16[160,768]{1,0:T(8,128)(2,1)} %get-tuple-element.208), channel_id=1, source_target_pairs={{0,1},{1,0},{2,3},{3,2},{4,5},{5,4},{6,7},{7,6},{8,9},{9,8},{10,11... | collective-permute-start | bytes 737288 | tf_op jit(solution)/shard_map/ppermute | solution.py:748
  158.1 25.7 %collective-permute-start.42 = (bf16[160,768]{1,0:T(8,128)(2,1)}, bf16[160,768]{1,0:T(8,128)(2,1)S(1)}, u32[]{:S(2)}, u32[]{:S(2)}) collective-permute-start(bf16[160,768]{1,0:T(8,128)(2,1)} %get-tuple-element.234), channel_id=1, source_target_pairs={{0,10},{1,11},{2,8},{3,9},{4,14},{5,15},{6,12},{7,13},{8,2},{9,3},... | collective-permute-start | bytes 737288 | tf_op jit(solution)/shard_map/ppermute | solution.py:748
  160.2 23.5 %collective-permute-start.41 = (bf16[160,768]{1,0:T(8,128)(2,1)}, bf16[160,768]{1,0:T(8,128)(2,1)S(1)}, u32[]{:S(2)}, u32[]{:S(2)}) collective-permute-start(bf16[160,768]{1,0:T(8,128)(2,1)} %get-tuple-element.232), channel_id=1, source_target_pairs={{0,8},{1,9},{2,10},{3,11},{4,12},{5,13},{6,14},{7,15},{8,0},{9,1},... | collective-permute-start | bytes 737288 | tf_op jit(solution)/shard_map/ppermute | solution.py:748
  160.2 23.5 %collective-permute-start.40 = (bf16[160,768]{1,0:T(8,128)(2,1)}, bf16[160,768]{1,0:T(8,128)(2,1)S(1)}, u32[]{:S(2)}, u32[]{:S(2)}) collective-permute-start(bf16[160,768]{1,0:T(8,128)(2,1)} %get-tuple-element.230), channel_id=1, source_target_pairs={{0,2},{1,3},{2,0},{3,1},{4,6},{5,7},{6,4},{7,5},{8,10},{9,11},{10,... | collective-permute-start | bytes 737288 | tf_op jit(solution)/shard_map/ppermute | solution.py:748
  195.3 19.8 %collective-permute-start.48 = (bf16[2,2,128,768]{3,2,1,0:T(8,128)(2,1)}, bf16[2,2,128,768]{3,2,1,0:T(8,128)(2,1)S(1)}, u32[]{:S(2)}, u32[]{:S(2)}) collective-permute-start(bf16[2,2,128,768]{3,2,1,0:T(8,128)(2,1)} %get-tuple-element.247), channel_id=1, source_target_pairs={{0,4},{1,5},{2,6},{3,7},{4,0},{5,1},{6,2},{7,3},{8,12},{9,13},{10,... | collective-permute-start | bytes 2359304 | tf_op jit(solution)/shard_map/ppermute | solution.py:748
  195.8 16.3 %collective-permute-start.44 = (bf16[160,768]{1,0:T(8,128)(2,1)S(1)}, bf16[160,768]{1,0:T(8,128)(2,1)S(1)}, u32[]{:S(2)}, u32[]{:S(2)}) collective-permute-start(bf16[160,768]{1,0:T(8,128)(2,1)S(1)} %copy-done.63), channel_id=1, source_target_pairs={{0,2},{1,3},{2,0},{3,1},{4,6},{5,7},{6,4},{7,5},{8,10},{9,11},{10,... | collective-permute-start | bytes 737288 | tf_op jit(solution)/shard_map/ppermute | solution.py:748
  196.5 15.7 %collective-permute-start.45 = (bf16[160,768]{1,0:T(8,128)(2,1)S(1)}, bf16[160,768]{1,0:T(8,128)(2,1)S(1)}, u32[]{:S(2)}, u32[]{:S(2)}) collective-permute-start(bf16[160,768]{1,0:T(8,128)(2,1)S(1)} %copy-done.62), channel_id=1, source_target_pairs={{0,8},{1,9},{2,10},{3,11},{4,12},{5,13},{6,14},{7,15},{8,0},{9,1},... | collective-permute-start | bytes 737288 | tf_op jit(solution)/shard_map/ppermute | solution.py:748
  215.1 22.3 %collective-permute-start.52 = (bf16[160,768]{1,0:T(8,128)(2,1)}, bf16[160,768]{1,0:T(8,128)(2,1)S(1)}, u32[]{:S(2)}, u32[]{:S(2)}) collective-permute-start(bf16[160,768]{1,0:T(8,128)(2,1)} %collective-permute-done.49), channel_id=1, source_target_pairs={{0,2},{1,3},{2,0},{3,1},{4,6},{5,7},{6,4},{7,5},{8,10},{9,11},{10,... | collective-permute-start | bytes 737288 | tf_op jit(solution)/shard_map/ppermute | solution.py:748
  215.8 22.3 %collective-permute-start.53 = (bf16[160,768]{1,0:T(8,128)(2,1)}, bf16[160,768]{1,0:T(8,128)(2,1)S(1)}, u32[]{:S(2)}, u32[]{:S(2)}) collective-permute-start(bf16[160,768]{1,0:T(8,128)(2,1)} %collective-permute-done.50), channel_id=1, source_target_pairs={{0,8},{1,9},{2,10},{3,11},{4,12},{5,13},{6,14},{7,15},{8,0},{9,1},... | collective-permute-start | bytes 737288 | tf_op jit(solution)/shard_map/ppermute | solution.py:748
  217.8 20.3 %collective-permute-start.54 = (bf16[160,768]{1,0:T(8,128)(2,1)}, bf16[160,768]{1,0:T(8,128)(2,1)S(1)}, u32[]{:S(2)}, u32[]{:S(2)}) collective-permute-start(bf16[160,768]{1,0:T(8,128)(2,1)} %collective-permute-done.51), channel_id=1, source_target_pairs={{0,10},{1,11},{2,8},{3,9},{4,14},{5,15},{6,12},{7,13},{8,2},{9,3},... | collective-permute-start | bytes 737288 | tf_op jit(solution)/shard_map/ppermute | solution.py:748
  218.6 30.2 %collective-permute-start.55 = (bf16[2,2,128,768]{3,2,1,0:T(8,128)(2,1)S(1)}, bf16[2,2,128,768]{3,2,1,0:T(8,128)(2,1)S(1)}, u32[]{:S(2)}, u32[]{:S(2)}) collective-permute-start(bf16[2,2,128,768]{3,2,1,0:T(8,128)(2,1)S(1)} %copy-done.52), channel_id=1, source_target_pairs={{0,4},{1,5},{2,6},{3,7},{4,0},{5,1},{6,2},{7,3},{8,12},{9,13},{10,... | collective-permute-start | bytes 2359304 | tf_op jit(solution)/shard_map/ppermute | solution.py:748
  236.9 23.7 %collective-permute-start.57 = (bf16[1,2,128,768]{3,2,1,0:T(8,128)(2,1)S(1)}, bf16[1,2,128,768]{3,2,1,0:T(8,128)(2,1)S(1)}, u32[]{:S(2)}, u32[]{:S(2)}) collective-permute-start(bf16[1,2,128,768]{3,2,1,0:T(8,128)(2,1)S(1)} %constant_dynamic-slice_fusion.7), channel_id=1, source_target_pairs={{0,16},{1,17},{2,18},{3,19},{4,20},{5,21},{6,22},{7,23},{8,24},{9,... | collective-permute-start | bytes 1179656 | tf_op jit(solution)/shard_map/ppermute | solution.py:748
  237.5 23.2 %collective-permute-start.56 = (bf16[2,2,128,768]{3,2,1,0:T(8,128)(2,1)S(1)}, bf16[2,2,128,768]{3,2,1,0:T(8,128)(2,1)S(1)}, u32[]{:S(2)}, u32[]{:S(2)}) collective-permute-start(bf16[2,2,128,768]{3,2,1,0:T(8,128)(2,1)S(1)} %copy-done.51), channel_id=1, source_target_pairs={{0,4},{1,5},{2,6},{3,7},{4,0},{5,1},{6,2},{7,3},{8,12},{9,13},{10,... | collective-permute-start | bytes 2359304 | tf_op jit(solution)/shard_map/ppermute | solution.py:748
  247.4 25.2 %collective-permute-start.58 = (bf16[2,2,32,3072]{3,2,1,0:T(8,128)(2,1)}, bf16[2,2,32,3072]{3,2,1,0:T(8,128)(2,1)S(1)}, u32[]{:S(2)}, u32[]{:S(2)}) collective-permute-start(bf16[2,2,32,3072]{3,2,1,0:T(8,128)(2,1)} %get-tuple-element.292), channel_id=1, source_target_pairs={{0,4},{1,5},{2,6},{3,7},{4,0},{5,1},{6,2},{7,3},{8,12},{9,13},{10,... | collective-permute-start | bytes 2359304 | tf_op jit(solution)/shard_map/ppermute | solution.py:748
  275.7 53.0 %collective-permute-start.79 = (bf16[1,4,128,768]{3,2,1,0:T(8,128)(2,1)}, bf16[1,4,128,768]{3,2,1,0:T(8,128)(2,1)}, u32[]{:S(2)}, u32[]{:S(2)}) collective-permute-start(bf16[1,4,128,768]{3,2,1,0:T(8,128)(2,1)} %pad_maximum_fusion.6), channel_id=1, source_target_pairs={{0,16},{1,17},{2,18},{3,19},{4,20},{5,21},{6,22},{7,23},{8,24},{9,... | collective-permute-start | bytes 2359304 | tf_op jit(solution)/shard_map/ppermute | solution.py:748
  279.2 25.1 %collective-permute-start.62 = (bf16[2,2,32,3072]{3,2,1,0:T(8,128)(2,1)}, bf16[2,2,32,3072]{3,2,1,0:T(8,128)(2,1)}, u32[]{:S(2)}, u32[]{:S(2)}) collective-permute-start(bf16[2,2,32,3072]{3,2,1,0:T(8,128)(2,1)} %get-tuple-element.304), channel_id=1, source_target_pairs={{0,4},{1,5},{2,6},{3,7},{4,0},{5,1},{6,2},{7,3},{8,12},{9,13},{10,... | collective-permute-start | bytes 2359304 | tf_op jit(solution)/shard_map/ppermute | solution.py:748
  293.0 60.4 %collective-permute-start.76 = (bf16[1,2,32,3072]{3,2,1,0:T(8,128)(2,1)}, bf16[1,2,32,3072]{3,2,1,0:T(8,128)(2,1)}, u32[]{:S(2)}, u32[]{:S(2)}) collective-permute-start(bf16[1,2,32,3072]{3,2,1,0:T(8,128)(2,1)} %constant_dynamic-slice_fusion.4), channel_id=1, source_target_pairs={{0,16},{1,17},{2,18},{3,19},{4,20},{5,21},{6,22},{7,23},{8,24},{9,... | collective-permute-start | bytes 1179656 | tf_op jit(solution)/shard_map/ppermute | solution.py:748
  294.5 36.3 %collective-permute-start.61 = (bf16[4,8,48,384]{3,2,1,0:T(8,128)(2,1)}, bf16[4,8,48,384]{3,2,1,0:T(8,128)(2,1)}, u32[]{:S(2)}, u32[]{:S(2)}) collective-permute-start(bf16[4,8,48,384]{3,2,1,0:T(8,128)(2,1)} %pad_maximum_fusion.2), channel_id=1, source_target_pairs={{0,2},{1,3},{2,0},{3,1},{4,6},{5,7},{6,4},{7,5},{8,10},{9,11},{10,... | collective-permute-start | bytes 3538952 | tf_op jit(solution)/shard_map/ppermute | solution.py:748
  327.1 20.0 %collective-permute-start.65 = (bf16[2,2,32,3072]{3,2,1,0:T(8,128)(2,1)S(1)}, bf16[2,2,32,3072]{3,2,1,0:T(8,128)(2,1)S(1)}, u32[]{:S(2)}, u32[]{:S(2)}) collective-permute-start(bf16[2,2,32,3072]{3,2,1,0:T(8,128)(2,1)S(1)} %copy-done.53), channel_id=1, source_target_pairs={{0,4},{1,5},{2,6},{3,7},{4,0},{5,1},{6,2},{7,3},{8,12},{9,13},{10,... | collective-permute-start | bytes 2359304 | tf_op jit(solution)/shard_map/ppermute | solution.py:748
  333.3 17.8 %collective-permute-start.64 = (bf16[4,2,2,48,384]{4,3,2,1,0:T(8,128)(2,1)S(1)}, bf16[4,2,2,48,384]{4,3,2,1,0:T(8,128)(2,1)S(1)}, u32[]{:S(2)}, u32[]{:S(2)}) collective-permute-start(bf16[4,2,2,48,384]{4,3,2,1,0:T(8,128)(2,1)S(1)} %get-tuple-element.378), channel_id=1, source_target_pairs={{0,8},{1,9},{2,10},{3,11},{4,12},{5,13},{6,14},{7,15},{8,0},{9,1},... | collective-permute-start | bytes 1769480 | tf_op jit(solution)/shard_map/ppermute | solution.py:748
  348.0 51.6 %collective-permute-start.69 = (bf16[1,2,32,3072]{3,2,1,0:T(8,128)(2,1)S(1)}, bf16[1,2,32,3072]{3,2,1,0:T(8,128)(2,1)S(1)}, u32[]{:S(2)}, u32[]{:S(2)}) collective-permute-start(bf16[1,2,32,3072]{3,2,1,0:T(8,128)(2,1)S(1)} %constant_dynamic-slice_fusion.2), channel_id=1, source_target_pairs={{0,16},{1,17},{2,18},{3,19},{4,20},{5,21},{6,22},{7,23},{8,24},{9,... | collective-permute-start | bytes 1179656 | tf_op jit(solution)/shard_map/ppermute | solution.py:748
  350.7 35.5 %collective-permute-start.75 = (bf16[1,2,32,3072]{3,2,1,0:T(8,128)(2,1)S(1)}, bf16[1,2,32,3072]{3,2,1,0:T(8,128)(2,1)S(1)}, u32[]{:S(2)}, u32[]{:S(2)}) collective-permute-start(bf16[1,2,32,3072]{3,2,1,0:T(8,128)(2,1)S(1)} %constant_dynamic-slice_fusion.3), channel_id=1, source_target_pairs={{0,16},{1,17},{2,18},{3,19},{4,20},{5,21},{6,22},{7,23},{8,24},{9,... | collective-permute-start | bytes 1179656 | tf_op jit(solution)/shard_map/ppermute | solution.py:748
  354.5 48.2 %collective-permute-start.77 = (bf16[2,32,3072]{2,1,0:T(8,128)(2,1)S(1)}, bf16[2,32,3072]{2,1,0:T(8,128)(2,1)}, u32[]{:S(2)}, u32[]{:S(2)}) collective-permute-start(bf16[2,32,3072]{2,1,0:T(8,128)(2,1)S(1)} %fusion.15), channel_id=1, source_target_pairs={{0,8},{1,9},{2,10},{3,11},{4,12},{5,13},{6,14},{7,15},{8,0},{9,1},... | collective-permute-start | bytes 1179656 | tf_op jit(solution)/shard_map/ppermute | solution.py:748
  359.9 47.0 %collective-permute-start.80 = (bf16[3,128,768]{2,1,0:T(8,128)(2,1)S(1)}, bf16[3,128,768]{2,1,0:T(8,128)(2,1)S(1)}, u32[]{:S(2)}, u32[]{:S(2)}) collective-permute-start(bf16[3,128,768]{2,1,0:T(8,128)(2,1)S(1)} %pad_maximum_fusion.9), channel_id=1, source_target_pairs={{0,8},{1,9},{2,10},{3,11},{4,12},{5,13},{6,14},{7,15},{8,0},{9,1},... | collective-permute-start | bytes 1769480 | tf_op jit(solution)/shard_map/ppermute | solution.py:748
  361.7 30.4 %collective-permute-start.67 = (bf16[4,48,384]{2,1,0:T(8,128)(2,1)S(1)}, bf16[4,48,384]{2,1,0:T(8,128)(2,1)S(1)}, u32[]{:S(2)}, u32[]{:S(2)}) collective-permute-start(bf16[4,48,384]{2,1,0:T(8,128)(2,1)S(1)} %dynamic-slice_bitcast_fusion.7), channel_id=1, source_target_pairs={{0,16},{1,17},{2,18},{3,19},{4,20},{5,21},{6,22},{7,23},{8,24},{9,... | collective-permute-start | bytes 442376 | tf_op jit(solution)/shard_map/ppermute | solution.py:748
  (125 other events, 956.8 us)

commit v7 on v6

--- a/solution.py
+++ b/solution.py
@@ -974,10 +974,11 @@
     grad_input, gain_attn_parts = enter(
         core_index, after(grad_qkv_rows, away_d), mine, other, tokens, gain_attn, grad_middle
     )
-    grad_table = table_gradient(after(bands, y_stay), position_bias_table.shape[1])
 
     away_e, stay_e = near_add(after(got_e, gain_attn_parts), keep_e)
     got_f = swap(after(send_f, away_e), 1, 0)
+    away_f, stay_f = near_add(after(got_f, away_e), keep_f)
+    grad_table = table_gradient(after(bands, away_e), position_bias_table.shape[1])
     normed2, squares, gain_moe_parts = after((normed2, squares, gain_moe_parts), y_stay)
     grad_router = jnp.einsum("td,te->de", normed2, grad_logits, preferred_element_type=f32)
     small = [
@@ -990,44 +991,42 @@
     sizes = [value.size for value in small]
     flat = jnp.concatenate([value.reshape(-1) for value in small])
     flat = jnp.pad(flat, (0, -sum(sizes) % 1024)).reshape(-1, 128)
-    flat = flat + swap(flat, 0, 1)
     done_c = finish(after(far_c, away_e), stay_c)
-    total = add(after(y_got, away_e, flat, done_c), y_stay)
+    total = add(after(y_got, away_f, far_c, grad_table), y_stay)
     total = total.reshape((4,) + (2,) * len(dp_masks) + (-1, columns))
 
 
+    small_trades = [(0, 1), (0, group_masks[0])] + [(mask, 0) for mask in dp_masks if mask != PAIR] + [(PAIR, 0)]
+    small_trades += [(0, mask) for mask in group_masks[1:]]
     passed_masks = []
     for mask in dp_masks:
         got, stay = over_dp(total, mask, passed_masks)
         passed_masks.append(mask)
-        flat_got = swap(after(flat, stay), 0, group_masks[0]) if mask == PAIR else swap(flat, mask, 0)
+        flat_got = swap(after(flat, stay), *small_trades.pop(0))
         if mask == PAIR:
-            far_e = far_trade(after(away_e, stay))
-            away_f, stay_f = near_add(after(got_f, stay), keep_f)
-            far_f = far_trade(away_f)
-            got = after(got, away_f)
+            far_e, far_f = far_trade(after(away_e, stay)), far_trade(after(away_f, stay))
+            got = after(got, far_e)
+            done_e = finish(far_e, stay_e)
+        elif len(passed_masks) == len(dp_masks):
+            got = after(got, far_f)
+            done_f = finish(far_f, stay_f)
         total = add(got, stay)
         flat = flat + flat_got
         if mask == PAIR:
             done_d = finish(after(far_d, total), stay_d)
             in_first = swap(done_d, PAIR, 0)
             out_theirs = swap(after(jnp.concatenate([done_a, done_c[:1]]), total), PAIR, 0)
-        elif len(passed_masks) == 2:
-            done_e = finish(after(far_e, total), stay_e)
         flat = after(flat, total)
     in_theirs = jnp.concatenate([in_first, swap(done_e[:1], PAIR, 0)])
     for mask in reversed(group_masks):
         bit = (here_group // mask) % 2
         other_part = swap(total, 0, mask)
         total = jnp.concatenate([jnp.where(bit == 0, total, other_part), jnp.where(bit == 0, other_part, total)], axis=1)
-        if mask == group_masks[0]:
-            done_f = finish(after(far_f, total), stay_f)
-            total = after(total, done_f)
-            flat = flat + swap(flat, PAIR, 0)
-        else:
-            flat = flat + swap(flat, 0, mask)
+        flat = flat + swap(flat, *small_trades.pop(0))
         total, flat = lax.optimization_barrier((total, flat))
     other_part = swap(total, 0, 1)
+    for trade in small_trades:
+        flat = flat + swap(flat, *trade)
     total = jnp.concatenate([jnp.where(core == 0, total, other_part), jnp.where(core == 0, other_part, total)], axis=2)
     weights_done = total.astype(f32)
     grad_qkv, grad_out_weight = weights_done[:3], weights_done[3]

time: 417 us -> 410 us (0.983)
    unnamed x157 -> x165, local copies, waits for them, and re-layouts: 16.9 us -> 16.8 us
  transfers between devices with their start and end apart: 81 -> 81, of which waited for: 24 -> 27; matrix products, arithmetic and copies ran while one was open for 15% -> 14% of each run, Pallas kernels for 32% -> 32%
where the time goes in v7:
time: 410 us; the launch traced here: 405 us
  Pallas kernels  157 us (38%)
  starting transfers between devices  88.7 us (22%)
  waiting for transfers between devices  80.9 us (20%)
  local copies, waits for them, and re-layouts  34.8 us (8%)
  other arithmetic  28.4 us (7%)
  matrix products  9.14 us (2%)
  between operations  6.04 us (1%)
    ppermute x67, waiting for transfers between devices, swap(): return lax.ppermute(value, AXES, pairs)  72 us
    ppermute x67, starting transfers between devices, swap(): return lax.ppermute(value, AXES, pairs)  71.7 us
    pallas_call x4, Pallas kernels, weight_part(): pl.pallas_call(lambda *refs: weight_part_kernel(*refs, count=count, plans...  30.8 us
    pallas_call x2, Pallas kernels, expert_forward(): pl.pallas_call(lambda *refs: expert_forward_kernel(*refs, chunk=chunk, co...  27.6 us
    pallas_call x2, Pallas kernels, expert_backward(): pl.pallas_call(lambda *refs: expert_backward_kernel(*refs, chunk=chunk, c...  25.3 us
    ppermute x14, starting transfers between devices, gather_ring(): lax.ppermute(after(held, *due[step - 2:step - 1]) if step > 1 else held,...  17.1 us
    unnamed x165, local copies, waits for them, and re-layouts  16.8 us
    pallas_call x1, Pallas kernels, attention_forward(): pl.pallas_call(lambda *refs: attention_forward_kernel(*refs, heads=64, bl...  12.7 us
  transfers between devices with their start and end apart: 81, of which 27 were waited for; matrix products, arithmetic and copies ran while one was open for 14% of the time, Pallas kernels for 32%

profile of v7, /device:TPU:0, one launch (start us, length us, event | category | flops | bytes accessed | tf_op | source)
XLA Modules:
  0.0 405.2 jit_solution(3029088600237118927)
XLA Ops:
  1.7 3.1 collective-permute-start
  34.3 3.3 join.1.mine.refs_15_
  46.4 6.4 %project.1.refs_2_.refs_3_.refs_4_.refs_0_.refs_1_ = bf16[3,512,768]{2,1,0:T(8,128)(2,1)} custom-call(s32[1]{0:T(128)} %bitcast.2.core.refs_0_, bf16[512,768]{1,0:T(8,128)(2,1)} %fusion.6.rows.refs_1_, bf16[4,768,384]{2,1,0:T(8,128)(2,1)} %join.1.mine.refs_15_, bf16[4,768,384]{2,1,0:T(8,128)(2,1)} %copy-done), custom_call_target="tpu_custom_call" | custom-call | flops 1480000000 | tf_op jit(solution)/shard_map/project/pallas_call | solution.py:396
  55.0 12.7 %attention_forward.1 = (bf16[512,768]{1,0:T(8,128)(2,1)}, bf16[12,512,512]{2,1,0:T(8,128)(2,1)}) custom-call(f32[12]{0:T(128)} %slice_reduce_fusion.refs_0_, s32[1]{0:T(128)S(6)} %copy.107.refs_1_, bf16[3,512,768]{2,1,0:T(8,128)(2,1)} %project.1.refs_2_.refs_3_.refs_4_.refs_0_.refs_1_, bf16[3,512,768]{2,1,0:T(8,128)(2,1)} %project.1.refs_2_.refs_3_.refs_4_.refs_0_.refs_1_, ...), custom_call_target="tpu_custom_call" | custom-call | flops 4809999872 | tf_op jit(solution)/shard_map/attention_forward/pallas_call | solution.py:214
  67.7 5.9 %route.1 = (f32[512,768]{1,0:T(8,128)}, bf16[512,768]{1,0:T(8,128)(2,1)}, f32[512,2]{1,0:T(8,128)}, bf16[160,768]{1,0:T(8,128)(2,1)}, bf16[160,768]{1,0:T(8,128)...) custom-call(s32[1]{0:T(128)} %bitcast.2.core.refs_0_, ...), custom_call_target="tpu_custom_call" | custom-call | flops 2220000000 | tf_op jit(solution)/shard_map/route/pallas_call | solution.py:447
  80.0 3.8 collective-permute-done.18.refs_4_
  85.0 4.0 collective-permute-done.20.refs_2_
  91.3 13.8 %expert_forward.2 = (bf16[3072,640]{1,0:T(8,128)(2,1)}, bf16[640,3072]{1,0:T(8,128)(2,1)}, bf16[768,640]{1,0:T(8,128)(2,1)}, bf16[160,768]{1,0:T(8,128)(2,1)}, b...) custom-call(s32[1]{0:T(128)} %bitcast.4.refs_0_, ...), custom_call_target="tpu_custom_call" | custom-call | flops 4809999872 | tf_op jit(solution)/shard_map/expert_forward/pallas_call | solution.py:78
  106.1 4.2 %collective-permute-start.27 = (bf16[160,768]{1,0:T(8,128)(2,1)S(1)}, bf16[160,768]{1,0:T(8,128)(2,1)S(1)}, u32[]{:S(2)}, u32[]{:S(2)}) collective-permute-start(bf16[160,768]{1,0:T(8,128)(2,1)S(1)} %copy-done.74), channel_id=1, source_target_pairs={{0,2},{1,3},{2,0},{3,1},{4,6},{5,7},{6,4},{7,5},{8,10},{9,11},{10,... | collective-permute-start | bytes 737288 | tf_op jit(solution)/shard_map/ppermute | solution.py:748
  112.9 13.8 %expert_forward.3 = (bf16[3072,640]{1,0:T(8,128)(2,1)}, bf16[640,3072]{1,0:T(8,128)(2,1)}, bf16[768,640]{1,0:T(8,128)(2,1)}, bf16[160,768]{1,0:T(8,128)(2,1)}, b...) custom-call(s32[1]{0:T(128)} %bitcast.4.refs_0_, bf16[640,768]{1,0:T(8,128)(2,1)} %copy-done.16, ...), custom_call_target="tpu_custom_call" | custom-call | flops 4809999872 | tf_op jit(solution)/shard_map/expert_forward/pallas_call | solution.py:78
  135.7 5.6 %collective-permute-done.26 = f32[8,128]{1,0:T(8,128)S(1)} collective-permute-done((f32[8,128]{1,0:T(8,128)S(1)}, f32[8,128]{1,0:T(8,128)S(1)}, u32[]{:S(2)}, u32[]{:S(2)}) %collective-permute-start.26) | collective-permute-done | bytes 4128 | tf_op jit(solution)/shard_map/ppermute | solution.py:748
  144.3 8.5 %combine.1 = (bf16[512,768]{1,0:T(8,128)(2,1)}, f32[512,768]{1,0:T(8,128)}, bf16[512,8]{1,0:T(8,128)(2,1)}, f32[8,768]{1,0:T(8,128)}, bf16[160,768]{1,0:T(8,128)...) custom-call(s32[512,2]{1,0:T(8,128)} %multiply_add_fusion.refs_0_.re, ...), custom_call_target="tpu_custom_call" | custom-call | flops 2960000000 | tf_op jit(solution)/shard_map/combine/pallas_call | solution.py:503
  154.2 3.3 collective-permute-start.38
  161.8 2.7 collective-permute-done.38.refs_3_
  164.5 6.2 %collective-permute-done.39.refs_4_ = bf16[160,768]{1,0:T(8,128)(2,1)S(1)} collective-permute-done((bf16[160,768]{1,0:T(8,128)(2,1)}, bf16[160,768]{1,0:T(8,128)(2,1)S(1)}, u32[]{:S(2)}, u32[]{:S(2)}) %collective-permute-start.39) | collective-permute-done | bytes 245792 | tf_op jit(solution)/shard_map/ppermute | solution.py:748
  171.4 12.5 %expert_backward.2 = (bf16[640,3072]{1,0:T(8,128)(2,1)}, bf16[640,768]{1,0:T(8,128)(2,1)}, bf16[160,768]{1,0:T(8,128)(2,1)}, bf16[160,768]{1,0:T(8,128)(2,1)}, b...) custom-call(s32[1]{0:T(128)} %bitcast.4.refs_0_, bf16[160,768]{1,0:T(8,128)(2,1)} %get-tuple-element.219.refs_1_, ...), custom_call_target="tpu_custom_call" | custom-call | flops 4070000128 | tf_op jit(solution)/shard_map/expert_backward/pallas_call | solution.py:135
  187.6 7.8 %weight_part.4 = (bf16[2,2,128,768]{3,2,1,0:T(8,128)(2,1)}, bf16[2,2,128,768]{3,2,1,0:T(8,128)(2,1)}, bf16[2,2,128,768]{3,2,1,0:T(8,128)(2,1)}) custom-call(s32[4]{0:T(128)} %pad_add_fusion.1.refs_0_, bf16[3072,640]{1,0:T(8,128)(2,1)} %get-tuple-element.195.refs_1_.refs_2_.refs_3_.refs_4_, ...), custom_call_target="tpu_custom_call" | custom-call | flops 1480000000 | tf_op jit(solution)/shard_map/weight_part/pallas_call | solution.py:337
  199.6 12.8 %expert_backward.3 = (bf16[640,3072]{1,0:T(8,128)(2,1)}, bf16[640,768]{1,0:T(8,128)(2,1)}, bf16[160,768]{1,0:T(8,128)(2,1)}, bf16[160,768]{1,0:T(8,128)(2,1)}, b...) custom-call(s32[1]{0:T(128)} %bitcast.4.refs_0_, bf16[640,768]{1,0:T(8,128)(2,1)} %copy-done.1, ...), custom_call_target="tpu_custom_call" | custom-call | flops 4070000128 | tf_op jit(solution)/shard_map/expert_backward/pallas_call | solution.py:135
  220.4 7.8 %weight_part.5 = (bf16[2,2,128,768]{3,2,1,0:T(8,128)(2,1)}, bf16[2,2,128,768]{3,2,1,0:T(8,128)(2,1)}, bf16[2,2,128,768]{3,2,1,0:T(8,128)(2,1)}) custom-call(s32[4]{0:T(128)} %pad_add_fusion.2.refs_0_, bf16[3072,640]{1,0:T(8,128)(2,1)} %get-tuple-element.195.refs_1_.refs_2_.refs_3_.refs_4_, ...), custom_call_target="tpu_custom_call" | custom-call | flops 1480000000 | tf_op jit(solution)/shard_map/weight_part/pallas_call | solution.py:337
  229.6 7.7 %weight_part.6 = (bf16[2,2,32,3072]{3,2,1,0:T(8,128)(2,1)}, bf16[2,2,32,3072]{3,2,1,0:T(8,128)(2,1)}, bf16[2,2,32,3072]{3,2,1,0:T(8,128)(2,1)}) custom-call(s32[4]{0:T(128)} %pad_add_fusion.1.refs_0_, bf16[768,640]{1,0:T(8,128)(2,1)} %get-tuple-element.225.refs_1_.refs_2_.refs_3_.refs_4_, ...), custom_call_target="tpu_custom_call" | custom-call | flops 1480000000 | tf_op jit(solution)/shard_map/weight_part/pallas_call | solution.py:337
  239.2 8.5 %collect.1 = (f32[512,768]{1,0:T(8,128)}, bf16[512,768]{1,0:T(8,128)(2,1)}, bf16[512,768]{1,0:T(8,128)(2,1)}, f32[8,768]{1,0:T(8,128)}) custom-call(s32[1]{0:T(128)} %bitcast.2.core.refs_0_, s32[512,2]{1,0:T(8,128)} %multiply_add_fusion.refs_0_.refs_1_, bf16[160,768]{1,0:T(8,128)(2,1)} %get-tuple-element.267.refs_2_, bf16[160,768]{1,0:T(8,128)(2,1)} %copy-done.61, ...), custom_call_target="tpu_custom_call" | custom-call | flops 2960000000 | tf_op jit(solution)/shard_map/collect/pallas_call | solution.py:554
  249.4 11.6 %attention_backward.1 = (bf16[3,512,768]{2,1,0:T(8,128)(2,1)}, f32[12,4,128,128]{3,2,1,0:T(8,128)}) custom-call(bf16[3,512,768]{2,1,0:T(8,128)(2,1)} %project.1.refs_2_.refs_3_.refs_4_.refs_0_.refs_1_, bf16[3,512,768]{2,1,0:T(8,128)(2,1)} %project.1.refs_2_.refs_3_.refs_4_.refs_0_.refs_1_, ...), custom_call_target="tpu_custom_call" | custom-call | flops 1480000000 | tf_op jit(solution)/shard_map/attention_backward/pallas_call | solution.py:280
  262.1 8.4 %outer_halves.1 = (bf16[2,768,384]{2,1,0:T(8,128)(2,1)}, bf16[2,768,384]{2,1,0:T(8,128)(2,1)}, bf16[2,768,384]{2,1,0:T(8,128)(2,1)}, bf16[2,768,384]{2,1,0:T(8,128)(2,1)}) custom-call(s32[1]{0:T(128)} %bitcast.2.core.refs_0_, bf16[512,768]{1,0:T(8,128)(2,1)} %fusion.6.rows.refs_1_, bf16[512,768]{1,0:T(8,128)(2,1)} %get-tuple-element.187.attended.refs_2_, ...), custom_call_target="tpu_custom_call" | custom-call | flops 740000000 | tf_op jit(solution)/shard_map/outer_halves/pallas_call | solution.py:604
  280.1 7.5 %weight_part.7 = (bf16[2,2,32,3072]{3,2,1,0:T(8,128)(2,1)}, bf16[2,2,32,3072]{3,2,1,0:T(8,128)(2,1)}, bf16[2,2,32,3072]{3,2,1,0:T(8,128)(2,1)}) custom-call(s32[4]{0:T(128)} %pad_add_fusion.2.refs_0_, bf16[768,640]{1,0:T(8,128)(2,1)} %get-tuple-element.225.refs_1_.refs_2_.refs_3_.refs_4_, ...), custom_call_target="tpu_custom_call" | custom-call | flops 1480000000 | tf_op jit(solution)/shard_map/weight_part/pallas_call | solution.py:337
  296.2 8.3 %enter.1 = (f32[512,768]{1,0:T(8,128)}, f32[8,768]{1,0:T(8,128)}) custom-call(s32[1]{0:T(128)} %bitcast.2.core.refs_0_, bf16[3,512,768]{2,1,0:T(8,128)(2,1)} %get-tuple-element.308.refs_3_.grads, bf16[4,768,384]{2,1,0:T(8,128)(2,1)} %join.1.mine.refs_15_, bf16[4,768,384]{2,1,0:T(8,128)(2,1)} %copy-done, bf16[512,768]{1,0:T(8,128)(2,1)} %tokens.3, ...), custom_call_target="tpu_custom_call" | custom-call | flops 2220000000 | tf_op jit(solution)/shard_map/enter/pallas_call | solution.py:650
  315.6 6.2 %fusion.10 = f32[12,32]{1,0:T(8,128)S(1)} fusion(s32[4,128,128]{2,1,0:T(8,128)} %pad_add_fusion, f32[12,4,128,128]{3,2,1,0:T(8,128)S(1)} %copy-done.3), kind=kOutput, calls=%fused_computation.34 | convolution fusion | flops 304087040 | bytes 3409408 | tf_op jit(solution)/shard_map/hdxy,dxyb->hb/dot_general | solution.py:704
  337.8 15.9 %collective-permute-done.66 = bf16[1,2,32,3072]{3,2,1,0:T(8,128)(2,1)S(1)} collective-permute-done((bf16[1,2,32,3072]{3,2,1,0:T(8,128)(2,1)S(1)}, bf16[1,2,32,3072]{3,2,1,0:T(8,128)(2,1)S(1)}, u32[]{:S(2)}, u32[]{:S(2)}) %collective-permute-start.66) | collective-permute-done | bytes 393248 | tf_op jit(solution)/shard_map/ppermute | solution.py:748
  354.0 10.6 %collective-permute-done.65 = bf16[4,2,2,48,384]{4,3,0,1,2:T(8,128)(2,1)S(1)} collective-permute-done((bf16[4,2,2,48,384]{4,3,0,1,2:T(8,128)(2,1)S(1)}, bf16[4,2,2,48,384]{4,3,0,1,2:T(8,128)(2,1)S(1)}, u32[]{:S(2)}, u32[]{:S(2)}) %collective-permute-start.65) | collective-permute-done | bytes 589856 | tf_op jit(solution)/shard_map/ppermute | solution.py:748
  366.6 6.4 %collective-permute-done.67 = bf16[4,2,48,384]{3,2,0,1:T(8,128)(2,1)S(1)} collective-permute-done((bf16[4,2,48,384]{3,2,0,1:T(8,128)(2,1)S(1)}, bf16[4,2,48,384]{3,2,0,1:T(8,128)(2,1)S(1)}, u32[]{:S(2)}, u32[]{:S(2)}) %collective-permute-start.67) | collective-permute-done | bytes 294944 | tf_op jit(solution)/shard_map/ppermute | solution.py:748
  377.2 4.4 %collective-permute-done.68 = bf16[4,48,384]{2,1,0:T(8,128)(2,1)S(1)} collective-permute-done((bf16[4,48,384]{2,1,0:T(8,128)(2,1)S(1)}, bf16[4,48,384]{2,1,0:T(8,128)(2,1)S(1)}, u32[]{:S(2)}, u32[]{:S(2)}) %collective-permute-start.68) | collective-permute-done | bytes 147488 | tf_op jit(solution)/shard_map/ppermute | solution.py:748
  385.7 3.4 collective-permute-start.74
  393.0 3.1 collective-permute-start.75
  (423 shorter events, 159.1 us)
Async XLA Ops:
  77.2 28.0 %collective-permute-start.24 = (bf16[160,768]{1,0:T(8,128)(2,1)}, bf16[160,768]{1,0:T(8,128)(2,1)S(1)}, u32[]{:S(2)}, u32[]{:S(2)}) collective-permute-start(bf16[160,768]{1,0:T(8,128)(2,1)} %get-tuple-element.201), channel_id=1, source_target_pairs={{0,10},{1,11},{2,8},{3,9},{4,14},{5,15},{6,12},{7,13},{8,2},{9,3},... | collective-permute-start | bytes 737288 | tf_op jit(solution)/shard_map/ppermute | solution.py:748
  79.5 25.7 %collective-permute-start.23 = (bf16[160,768]{1,0:T(8,128)(2,1)}, bf16[160,768]{1,0:T(8,128)(2,1)S(1)}, u32[]{:S(2)}, u32[]{:S(2)}) collective-permute-start(bf16[160,768]{1,0:T(8,128)(2,1)} %get-tuple-element.199), channel_id=1, source_target_pairs={{0,8},{1,9},{2,10},{3,11},{4,12},{5,13},{6,14},{7,15},{8,0},{9,1},... | collective-permute-start | bytes 737288 | tf_op jit(solution)/shard_map/ppermute | solution.py:748
  83.7 21.5 %collective-permute-start.22 = (bf16[160,768]{1,0:T(8,128)(2,1)}, bf16[160,768]{1,0:T(8,128)(2,1)S(1)}, u32[]{:S(2)}, u32[]{:S(2)}) collective-permute-start(bf16[160,768]{1,0:T(8,128)(2,1)} %get-tuple-element.197), channel_id=1, source_target_pairs={{0,2},{1,3},{2,0},{3,1},{4,6},{5,7},{6,4},{7,5},{8,10},{9,11},{10,... | collective-permute-start | bytes 737288 | tf_op jit(solution)/shard_map/ppermute | solution.py:748
  89.1 16.1 %collective-permute-start.19 = (f32[8,128]{1,0:T(8,128)S(1)}, f32[8,128]{1,0:T(8,128)S(1)}, u32[]{:S(2)}, u32[]{:S(2)}) collective-permute-start(f32[8,128]{1,0:T(8,128)S(1)} %add.548), channel_id=1, source_target_pairs={{0,8},{1,9},{2,10},{3,11},{4,12},{5,13},{6,14},{7,15},{8,0},{9,1},... | collective-permute-start | bytes 12296 | tf_op jit(solution)/shard_map/ppermute | solution.py:748
  106.1 20.6 %collective-permute-start.27 = (bf16[160,768]{1,0:T(8,128)(2,1)S(1)}, bf16[160,768]{1,0:T(8,128)(2,1)S(1)}, u32[]{:S(2)}, u32[]{:S(2)}) collective-permute-start(bf16[160,768]{1,0:T(8,128)(2,1)S(1)} %copy-done.74), channel_id=1, source_target_pairs={{0,2},{1,3},{2,0},{3,1},{4,6},{5,7},{6,4},{7,5},{8,10},{9,11},{10,... | collective-permute-start | bytes 737288 | tf_op jit(solution)/shard_map/ppermute | solution.py:748
  110.3 16.4 %collective-permute-start.28 = (bf16[160,768]{1,0:T(8,128)(2,1)S(1)}, bf16[160,768]{1,0:T(8,128)(2,1)S(1)}, u32[]{:S(2)}, u32[]{:S(2)}) collective-permute-start(bf16[160,768]{1,0:T(8,128)(2,1)S(1)} %copy-done.72), channel_id=1, source_target_pairs={{0,8},{1,9},{2,10},{3,11},{4,12},{5,13},{6,14},{7,15},{8,0},{9,1},... | collective-permute-start | bytes 737288 | tf_op jit(solution)/shard_map/ppermute | solution.py:748
  110.4 16.3 %collective-permute-start.29 = (bf16[160,768]{1,0:T(8,128)(2,1)S(1)}, bf16[160,768]{1,0:T(8,128)(2,1)S(1)}, u32[]{:S(2)}, u32[]{:S(2)}) collective-permute-start(bf16[160,768]{1,0:T(8,128)(2,1)S(1)} %copy-done.70), channel_id=1, source_target_pairs={{0,10},{1,11},{2,8},{3,9},{4,14},{5,15},{6,12},{7,13},{8,2},{9,3},... | collective-permute-start | bytes 737288 | tf_op jit(solution)/shard_map/ppermute | solution.py:748
  127.4 15.1 %collective-permute-start.30 = (bf16[160,768]{1,0:T(8,128)(2,1)}, bf16[160,768]{1,0:T(8,128)(2,1)S(1)}, u32[]{:S(2)}, u32[]{:S(2)}) collective-permute-start(bf16[160,768]{1,0:T(8,128)(2,1)} %get-tuple-element.209), channel_id=1, source_target_pairs={{0,1},{1,0},{2,3},{3,2},{4,5},{5,4},{6,7},{7,6},{8,9},{9,8},{10,11... | collective-permute-start | bytes 737288 | tf_op jit(solution)/shard_map/ppermute | solution.py:748
  158.3 25.7 %collective-permute-start.42 = (bf16[160,768]{1,0:T(8,128)(2,1)}, bf16[160,768]{1,0:T(8,128)(2,1)S(1)}, u32[]{:S(2)}, u32[]{:S(2)}) collective-permute-start(bf16[160,768]{1,0:T(8,128)(2,1)} %get-tuple-element.235), channel_id=1, source_target_pairs={{0,10},{1,11},{2,8},{3,9},{4,14},{5,15},{6,12},{7,13},{8,2},{9,3},... | collective-permute-start | bytes 737288 | tf_op jit(solution)/shard_map/ppermute | solution.py:748
  160.4 23.6 %collective-permute-start.41 = (bf16[160,768]{1,0:T(8,128)(2,1)}, bf16[160,768]{1,0:T(8,128)(2,1)S(1)}, u32[]{:S(2)}, u32[]{:S(2)}) collective-permute-start(bf16[160,768]{1,0:T(8,128)(2,1)} %get-tuple-element.233), channel_id=1, source_target_pairs={{0,8},{1,9},{2,10},{3,11},{4,12},{5,13},{6,14},{7,15},{8,0},{9,1},... | collective-permute-start | bytes 737288 | tf_op jit(solution)/shard_map/ppermute | solution.py:748
  160.4 23.6 %collective-permute-start.40 = (bf16[160,768]{1,0:T(8,128)(2,1)}, bf16[160,768]{1,0:T(8,128)(2,1)S(1)}, u32[]{:S(2)}, u32[]{:S(2)}) collective-permute-start(bf16[160,768]{1,0:T(8,128)(2,1)} %get-tuple-element.231), channel_id=1, source_target_pairs={{0,2},{1,3},{2,0},{3,1},{4,6},{5,7},{6,4},{7,5},{8,10},{9,11},{10,... | collective-permute-start | bytes 737288 | tf_op jit(solution)/shard_map/ppermute | solution.py:748
  195.5 19.8 %collective-permute-start.48 = (bf16[2,2,128,768]{3,2,1,0:T(8,128)(2,1)}, bf16[2,2,128,768]{3,2,1,0:T(8,128)(2,1)S(1)}, u32[]{:S(2)}, u32[]{:S(2)}) collective-permute-start(bf16[2,2,128,768]{3,2,1,0:T(8,128)(2,1)} %get-tuple-element.248), channel_id=1, source_target_pairs={{0,4},{1,5},{2,6},{3,7},{4,0},{5,1},{6,2},{7,3},{8,12},{9,13},{10,... | collective-permute-start | bytes 2359304 | tf_op jit(solution)/shard_map/ppermute | solution.py:748
  196.0 16.3 %collective-permute-start.44 = (bf16[160,768]{1,0:T(8,128)(2,1)S(1)}, bf16[160,768]{1,0:T(8,128)(2,1)S(1)}, u32[]{:S(2)}, u32[]{:S(2)}) collective-permute-start(bf16[160,768]{1,0:T(8,128)(2,1)S(1)} %copy-done.67), channel_id=1, source_target_pairs={{0,2},{1,3},{2,0},{3,1},{4,6},{5,7},{6,4},{7,5},{8,10},{9,11},{10,... | collective-permute-start | bytes 737288 | tf_op jit(solution)/shard_map/ppermute | solution.py:748
  196.7 15.7 %collective-permute-start.45 = (bf16[160,768]{1,0:T(8,128)(2,1)S(1)}, bf16[160,768]{1,0:T(8,128)(2,1)S(1)}, u32[]{:S(2)}, u32[]{:S(2)}) collective-permute-start(bf16[160,768]{1,0:T(8,128)(2,1)S(1)} %copy-done.66), channel_id=1, source_target_pairs={{0,8},{1,9},{2,10},{3,11},{4,12},{5,13},{6,14},{7,15},{8,0},{9,1},... | collective-permute-start | bytes 737288 | tf_op jit(solution)/shard_map/ppermute | solution.py:748
  215.4 22.4 %collective-permute-start.52 = (bf16[160,768]{1,0:T(8,128)(2,1)}, bf16[160,768]{1,0:T(8,128)(2,1)S(1)}, u32[]{:S(2)}, u32[]{:S(2)}) collective-permute-start(bf16[160,768]{1,0:T(8,128)(2,1)} %collective-permute-done.49), channel_id=1, source_target_pairs={{0,2},{1,3},{2,0},{3,1},{4,6},{5,7},{6,4},{7,5},{8,10},{9,11},{10,... | collective-permute-start | bytes 737288 | tf_op jit(solution)/shard_map/ppermute | solution.py:748
  216.0 22.4 %collective-permute-start.53 = (bf16[160,768]{1,0:T(8,128)(2,1)}, bf16[160,768]{1,0:T(8,128)(2,1)S(1)}, u32[]{:S(2)}, u32[]{:S(2)}) collective-permute-start(bf16[160,768]{1,0:T(8,128)(2,1)} %collective-permute-done.50), channel_id=1, source_target_pairs={{0,8},{1,9},{2,10},{3,11},{4,12},{5,13},{6,14},{7,15},{8,0},{9,1},... | collective-permute-start | bytes 737288 | tf_op jit(solution)/shard_map/ppermute | solution.py:748
  218.0 20.5 %collective-permute-start.54 = (bf16[160,768]{1,0:T(8,128)(2,1)}, bf16[160,768]{1,0:T(8,128)(2,1)S(1)}, u32[]{:S(2)}, u32[]{:S(2)}) collective-permute-start(bf16[160,768]{1,0:T(8,128)(2,1)} %collective-permute-done.51), channel_id=1, source_target_pairs={{0,10},{1,11},{2,8},{3,9},{4,14},{5,15},{6,12},{7,13},{8,2},{9,3},... | collective-permute-start | bytes 737288 | tf_op jit(solution)/shard_map/ppermute | solution.py:748
  218.9 30.3 %collective-permute-start.55 = (bf16[2,2,128,768]{3,2,1,0:T(8,128)(2,1)S(1)}, bf16[2,2,128,768]{3,2,1,0:T(8,128)(2,1)S(1)}, u32[]{:S(2)}, u32[]{:S(2)}) collective-permute-start(bf16[2,2,128,768]{3,2,1,0:T(8,128)(2,1)S(1)} %copy-done.56), channel_id=1, source_target_pairs={{0,4},{1,5},{2,6},{3,7},{4,0},{5,1},{6,2},{7,3},{8,12},{9,13},{10,... | collective-permute-start | bytes 2359304 | tf_op jit(solution)/shard_map/ppermute | solution.py:748
  237.3 23.7 %collective-permute-start.57 = (bf16[1,2,128,768]{3,2,1,0:T(8,128)(2,1)S(1)}, bf16[1,2,128,768]{3,2,1,0:T(8,128)(2,1)S(1)}, u32[]{:S(2)}, u32[]{:S(2)}) collective-permute-start(bf16[1,2,128,768]{3,2,1,0:T(8,128)(2,1)S(1)} %constant_dynamic-slice_fusion.9), channel_id=1, source_target_pairs={{0,16},{1,17},{2,18},{3,19},{4,20},{5,21},{6,22},{7,23},{8,24},{9,... | collective-permute-start | bytes 1179656 | tf_op jit(solution)/shard_map/ppermute | solution.py:748
  237.8 23.2 %collective-permute-start.56 = (bf16[2,2,128,768]{3,2,1,0:T(8,128)(2,1)S(1)}, bf16[2,2,128,768]{3,2,1,0:T(8,128)(2,1)S(1)}, u32[]{:S(2)}, u32[]{:S(2)}) collective-permute-start(bf16[2,2,128,768]{3,2,1,0:T(8,128)(2,1)S(1)} %copy-done.55), channel_id=1, source_target_pairs={{0,4},{1,5},{2,6},{3,7},{4,0},{5,1},{6,2},{7,3},{8,12},{9,13},{10,... | collective-permute-start | bytes 2359304 | tf_op jit(solution)/shard_map/ppermute | solution.py:748
  247.7 25.2 %collective-permute-start.58 = (bf16[2,2,32,3072]{3,2,1,0:T(8,128)(2,1)}, bf16[2,2,32,3072]{3,2,1,0:T(8,128)(2,1)S(1)}, u32[]{:S(2)}, u32[]{:S(2)}) collective-permute-start(bf16[2,2,32,3072]{3,2,1,0:T(8,128)(2,1)} %get-tuple-element.293), channel_id=1, source_target_pairs={{0,4},{1,5},{2,6},{3,7},{4,0},{5,1},{6,2},{7,3},{8,12},{9,13},{10,... | collective-permute-start | bytes 2359304 | tf_op jit(solution)/shard_map/ppermute | solution.py:748
  276.1 47.3 %collective-permute-start.64 = (bf16[1,4,128,768]{3,2,1,0:T(8,128)(2,1)}, bf16[1,4,128,768]{3,2,1,0:T(8,128)(2,1)}, u32[]{:S(2)}, u32[]{:S(2)}) collective-permute-start(bf16[1,4,128,768]{3,2,1,0:T(8,128)(2,1)} %pad_maximum_fusion.6), channel_id=1, source_target_pairs={{0,16},{1,17},{2,18},{3,19},{4,20},{5,21},{6,22},{7,23},{8,24},{9,... | collective-permute-start | bytes 2359304 | tf_op jit(solution)/shard_map/ppermute | solution.py:748
  279.6 24.9 %collective-permute-start.62 = (bf16[2,2,32,3072]{3,2,1,0:T(8,128)(2,1)S(1)}, bf16[2,2,32,3072]{3,2,1,0:T(8,128)(2,1)S(1)}, u32[]{:S(2)}, u32[]{:S(2)}) collective-permute-start(bf16[2,2,32,3072]{3,2,1,0:T(8,128)(2,1)S(1)} %copy-done.57), channel_id=1, source_target_pairs={{0,4},{1,5},{2,6},{3,7},{4,0},{5,1},{6,2},{7,3},{8,12},{9,13},{10,... | collective-permute-start | bytes 2359304 | tf_op jit(solution)/shard_map/ppermute | solution.py:748
  293.4 72.0 %collective-permute-start.77 = (bf16[1,2,32,3072]{3,2,1,0:T(8,128)(2,1)}, bf16[1,2,32,3072]{3,2,1,0:T(8,128)(2,1)}, u32[]{:S(2)}, u32[]{:S(2)}) collective-permute-start(bf16[1,2,32,3072]{3,2,1,0:T(8,128)(2,1)} %constant_dynamic-slice_fusion.6), channel_id=1, source_target_pairs={{0,16},{1,17},{2,18},{3,19},{4,20},{5,21},{6,22},{7,23},{8,24},{9,... | collective-permute-start | bytes 1179656 | tf_op jit(solution)/shard_map/ppermute | solution.py:748
  294.9 36.1 %collective-permute-start.61 = (bf16[4,8,48,384]{3,2,1,0:T(8,128)(2,1)}, bf16[4,8,48,384]{3,2,1,0:T(8,128)(2,1)}, u32[]{:S(2)}, u32[]{:S(2)}) collective-permute-start(bf16[4,8,48,384]{3,2,1,0:T(8,128)(2,1)} %pad_maximum_fusion.2), channel_id=1, source_target_pairs={{0,2},{1,3},{2,0},{3,1},{4,6},{5,7},{6,4},{7,5},{8,10},{9,11},{10,... | collective-permute-start | bytes 3538952 | tf_op jit(solution)/shard_map/ppermute | solution.py:748
  308.5 21.0 %collective-permute-start.63 = (bf16[2,2,32,3072]{3,2,1,0:T(8,128)(2,1)}, bf16[2,2,32,3072]{3,2,1,0:T(8,128)(2,1)}, u32[]{:S(2)}, u32[]{:S(2)}) collective-permute-start(bf16[2,2,32,3072]{3,2,1,0:T(8,128)(2,1)} %get-tuple-element.313), channel_id=1, source_target_pairs={{0,4},{1,5},{2,6},{3,7},{4,0},{5,1},{6,2},{7,3},{8,12},{9,13},{10,... | collective-permute-start | bytes 2359304 | tf_op jit(solution)/shard_map/ppermute | solution.py:748
  333.6 20.1 %collective-permute-start.66 = (bf16[1,2,32,3072]{3,2,1,0:T(8,128)(2,1)S(1)}, bf16[1,2,32,3072]{3,2,1,0:T(8,128)(2,1)S(1)}, u32[]{:S(2)}, u32[]{:S(2)}) collective-permute-start(bf16[1,2,32,3072]{3,2,1,0:T(8,128)(2,1)S(1)} %copy-done.25), channel_id=1, source_target_pairs={{0,16},{1,17},{2,18},{3,19},{4,20},{5,21},{6,22},{7,23},{8,24},{9,... | collective-permute-start | bytes 1179656 | tf_op jit(solution)/shard_map/ppermute | solution.py:748
  335.7 28.9 %collective-permute-start.65 = (bf16[4,2,2,48,384]{4,3,0,1,2:T(8,128)(2,1)S(1)}, bf16[4,2,2,48,384]{4,3,0,1,2:T(8,128)(2,1)S(1)}, u32[]{:S(2)}, u32[]{:S(2)}) collective-permute-start(bf16[4,2,2,48,384]{4,3,0,1,2:T(8,128)(2,1)S(1)} %bitcast.87), channel_id=1, source_target_pairs={{0,8},{1,9},{2,10},{3,11},{4,12},{5,13},{6,14},{7,15},{8,0},{9,1},... | collective-permute-start | bytes 1769480 | tf_op jit(solution)/shard_map/ppermute | solution.py:748
  337.5 37.4 %collective-permute-start.69 = (bf16[1,2,32,3072]{3,2,1,0:T(8,128)(2,1)S(1)}, bf16[1,2,32,3072]{3,2,1,0:T(8,128)(2,1)S(1)}, u32[]{:S(2)}, u32[]{:S(2)}) collective-permute-start(bf16[1,2,32,3072]{3,2,1,0:T(8,128)(2,1)S(1)} %constant_dynamic-slice_fusion.4), channel_id=1, source_target_pairs={{0,16},{1,17},{2,18},{3,19},{4,20},{5,21},{6,22},{7,23},{8,24},{9,... | collective-permute-start | bytes 1179656 | tf_op jit(solution)/shard_map/ppermute | solution.py:748
  353.9 27.9 %collective-permute-start.79 = (bf16[1,32,3072]{2,1,0:T(8,128)(2,1)S(1)}, bf16[1,32,3072]{2,1,0:T(8,128)(2,1)S(1)}, u32[]{:S(2)}, u32[]{:S(2)}) collective-permute-start(bf16[1,32,3072]{2,1,0:T(8,128)(2,1)S(1)} %get-tuple-element.386), channel_id=1, source_target_pairs={{0,8},{1,9},{2,10},{3,11},{4,12},{5,13},{6,14},{7,15},{8,0},{9,1},... | collective-permute-start | bytes 589832 | tf_op jit(solution)/shard_map/ppermute | solution.py:748
  366.5 17.0 %collective-permute-start.78 = (bf16[2,32,3072]{2,1,0:T(8,128)(2,1)S(1)}, bf16[2,32,3072]{2,1,0:T(8,128)(2,1)S(1)}, u32[]{:S(2)}, u32[]{:S(2)}) collective-permute-start(bf16[2,32,3072]{2,1,0:T(8,128)(2,1)S(1)} %fusion.14), channel_id=1, source_target_pairs={{0,8},{1,9},{2,10},{3,11},{4,12},{5,13},{6,14},{7,15},{8,0},{9,1},... | collective-permute-start | bytes 1179656 | tf_op jit(solution)/shard_map/ppermute | solution.py:748
  375.0 21.8 %collective-permute-start.80 = (bf16[3,128,768]{2,1,0:T(8,128)(2,1)S(1)}, bf16[3,128,768]{2,1,0:T(8,128)(2,1)S(1)}, u32[]{:S(2)}, u32[]{:S(2)}) collective-permute-start(bf16[3,128,768]{2,1,0:T(8,128)(2,1)S(1)} %pad_maximum_fusion.9), channel_id=1, source_target_pairs={{0,8},{1,9},{2,10},{3,11},{4,12},{5,13},{6,14},{7,15},{8,0},{9,1},... | collective-permute-start | bytes 1769480 | tf_op jit(solution)/shard_map/ppermute | solution.py:748
  (129 other events, 989.7 us)

commit v8 on v7

--- a/solution.py
+++ b/solution.py
@@ -8,6 +8,7 @@
 
 BLOCK = 128
 THIRDS = 3
+SMALL = 8
 EPS = 1e-06
 GELU_A = math.sqrt(2.0 / math.pi)
 GELU_B = 0.044715
@@ -329,7 +330,7 @@
     return [jnp.stack([result[group, :, third] for group, third in plan], axis=1) for plan in plans]
 
 
-def weight_part(picks, lefts, rights, rows, plans, many, tile):
+def weight_part(picks, lefts, rights, rows, plans, many, tile, micros=4):
     depth, width = rights[0].shape
     count, part = picks.shape[0], rows // THIRDS
     if part % 16:
@@ -345,7 +346,7 @@
         ),
         out_shape=[jax.ShapeDtypeStruct((many, len(plan), part, width), jnp.bfloat16) for plan in plans],
         compiler_params=pltpu.CompilerParams(vmem_limit_bytes=VMEM_BYTES),
-        cost_estimate=cost(4),
+        cost_estimate=cost(micros),
         name="weight_part",
     )(picks, *([lefts[0]] * count), *([lefts[1]] * count), *rights)
 
@@ -622,7 +623,9 @@
     )(core, normed, attended, rights, last)
 
 
-def enter_kernel(core, grads, mine, other, tokens, gain, grad_middle, grad_input, grad_gain, total):
+def enter_kernel(
+    core, grads, mine, other, tokens, gain, grad_middle, moe_parts, squares, normed, grad_logits, grad_input, small, total
+):
     step = pl.program_id(0)
     first, second = halves(core[0], mine[...], other[...])
     half = first.shape[1]
@@ -639,28 +642,35 @@
 
     @pl.when(step == pl.num_programs(0) - 1)
     def _():
-        turned, grad_gain[...] = norm_back(tokens[...].astype(jnp.float32), gain[...], total[...])
+        turned, gain_parts = norm_back(tokens[...].astype(jnp.float32), gain[...], total[...])
         grad_input[...] = grad_middle[...] + turned
-
-
-def enter(core, grads, mine, other, tokens, gain, grad_middle):
+        sums = [jnp.sum(part, axis=0, keepdims=True) for part in (moe_parts[...], gain_parts, squares[...])]
+        sums.append(jnp.zeros((SMALL - len(sums), gain.shape[1]), jnp.float32))
+        small[pl.ds(0, SMALL), :] = jnp.concatenate(sums)
+        small[pl.ds(SMALL, grad_logits.shape[1]), :] = dot_f32(grad_logits[...], normed[...], TN)
+
+
+def enter(core, grads, mine, other, tokens, gain, grad_middle, moe_parts, squares, normed, grad_logits):
     length, width = tokens.shape
-    count, half = grads.shape[0], mine.shape[2]
+    count, half, experts = grads.shape[0], mine.shape[2], grad_logits.shape[1]
     weight = pl.BlockSpec((None, width, half), lambda i, core: (i, 0, 0))
+    plain = [tokens, gain.reshape(1, -1), grad_middle, moe_parts, squares, normed, grad_logits]
+    shapes = [(length, width), (SMALL + experts, width)]
     return pl.pallas_call(
         enter_kernel,
         grid_spec=pltpu.PrefetchScalarGridSpec(
             num_scalar_prefetch=1,
             grid=(count,),
-            in_specs=[pl.BlockSpec((None, length, width), lambda i, core: (i, 0, 0)), weight, weight, whole((length, width)), whole((1, width)), whole((length, width))],
-            out_specs=[whole((length, width)), whole((8, width))],
+            in_specs=[pl.BlockSpec((None, length, width), lambda i, core: (i, 0, 0)), weight, weight]
+            + [whole(array.shape) for array in plain],
+            out_specs=[whole(shape) for shape in shapes],
             scratch_shapes=[pltpu.VMEM((length, width), jnp.float32)],
         ),
-        out_shape=[jax.ShapeDtypeStruct((length, width), jnp.float32), jax.ShapeDtypeStruct((8, width), jnp.float32)],
+        out_shape=[jax.ShapeDtypeStruct(shape, jnp.float32) for shape in shapes],
         compiler_params=pltpu.CompilerParams(vmem_limit_bytes=VMEM_BYTES),
         cost_estimate=cost(6),
         name="enter",
-    )(core, grads, mine, other, tokens, gain.reshape(1, -1), grad_middle)
+    )(core, grads, mine, other, *plain)
 
 
 BOUNDS = (12, 16, 23, 32, 46, 64, 91)
@@ -946,53 +956,35 @@
     )
     weights_away, got_d = lax.optimization_barrier((weights_away, got_d))
     got_e = swap(after(send_e, got_d), 1, 0)
-    keep_d, keep_e, keep_f = weight_part(
-        kept, rows_in, after(grad_pre, *weights_away), in_rows, in_plans, rest, inner // 2
-    )
     group_masks = bits(groups)[1:]
-    dp_masks = sorted(bits(copies), key=lambda mask: (mask != PAIR, mask))
+    dp_masks = bits(copies)
 
     def over_dp(total, mask, passed):
         axis = 1 + sorted([other for other in dp_masks if other not in passed], reverse=True).index(mask)
         bit = (here_dp // mask) % 2
         away_part = lax.dynamic_index_in_dim(total, 1 - bit, axis, keepdims=False)
         stay_part = lax.dynamic_index_in_dim(total, bit, axis, keepdims=False)
-        return swap(away_part, mask, 0), stay_part
+        return away_part, swap(away_part, mask, 0), stay_part
 
     weights_got = [swap(part, 0, 1) for part in weights_away]
     halves_sum = [
-        add(after(got, keep_d), stay).reshape(2, copies, in_rows, columns) for got, stay in zip(weights_got, (stay_1, stay_2))
+        add(got, stay).reshape(2, copies, in_rows, columns) for got, stay in zip(weights_got, (stay_1, stay_2))
     ]
     for mask in group_masks[:-1]:
         folded = [fold(part, (here_group // mask) % 2, 2) for part in halves_sum]
         halves_sum = [add(swap(away_part, 0, mask), stay_part) for away_part, stay_part in folded]
     folded = [fold(part, (here_group // group_masks[-1]) % 2, 2) for part in halves_sum]
     y_stay = jnp.concatenate([stay_part for _, stay_part in folded])
-    y_got = swap(jnp.concatenate([away_part for away_part, _ in folded]), 0, group_masks[-1])
-    away_d, stay_d = near_add(after(got_d, y_stay), keep_d)
+    y_away = jnp.concatenate([away_part for away_part, _ in folded])
+    y_got = swap(y_away, 0, group_masks[-1])
+    keep_d, keep_e, keep_f = weight_part(
+        kept, rows_in, after(grad_pre, y_away), in_rows, in_plans, rest, inner // 2, 40
+    )
+    away_d, stay_d = near_add(got_d, keep_d)
     far_d = far_trade(away_d)
-    grad_input, gain_attn_parts = enter(
-        core_index, after(grad_qkv_rows, away_d), mine, other, tokens, gain_attn, grad_middle
-    )
-
-    away_e, stay_e = near_add(after(got_e, gain_attn_parts), keep_e)
-    got_f = swap(after(send_f, away_e), 1, 0)
-    away_f, stay_f = near_add(after(got_f, away_e), keep_f)
-    grad_table = table_gradient(after(bands, away_e), position_bias_table.shape[1])
-    normed2, squares, gain_moe_parts = after((normed2, squares, gain_moe_parts), y_stay)
-    grad_router = jnp.einsum("td,te->de", normed2, grad_logits, preferred_element_type=f32)
-    small = [
-        jnp.sum(gain_moe_parts, axis=0),
-        jnp.sum(gain_attn_parts, axis=0),
-        grad_router,
-        grad_table,
-        jnp.sum(squares),
-    ]
-    sizes = [value.size for value in small]
-    flat = jnp.concatenate([value.reshape(-1) for value in small])
-    flat = jnp.pad(flat, (0, -sum(sizes) % 1024)).reshape(-1, 128)
+    away_e, stay_e = near_add(after(got_e, away_d), keep_e)
     done_c = finish(after(far_c, away_e), stay_c)
-    total = add(after(y_got, away_f, far_c, grad_table), y_stay)
+    total = add(after(y_got, away_e, far_c), y_stay)
     total = total.reshape((4,) + (2,) * len(dp_masks) + (-1, columns))
 
 
@@ -1000,18 +992,39 @@
     small_trades += [(0, mask) for mask in group_masks[1:]]
     passed_masks = []
     for mask in dp_masks:
-        got, stay = over_dp(total, mask, passed_masks)
+        gone, got, stay = over_dp(total, mask, passed_masks)
         passed_masks.append(mask)
-        flat_got = swap(after(flat, stay), *small_trades.pop(0))
-        if mask == PAIR:
-            far_e, far_f = far_trade(after(away_e, stay)), far_trade(after(away_f, stay))
+        if len(passed_masks) == 1:
+            grad_input, small = enter(
+                core_index,
+                after(grad_qkv_rows, gone),
+                mine,
+                other,
+                tokens,
+                gain_attn,
+                grad_middle,
+                gain_moe_parts,
+                squares,
+                normed2,
+                grad_logits,
+            )
+            grad_table = table_gradient(after(bands, gone), position_bias_table.shape[1])
+            flat = lax.dynamic_update_slice(small, grad_table.reshape(1, -1), (3, 0))
+        for _ in range((0, 2, 1)[min(len(passed_masks), 3) - 1]):
+            flat = flat + swap(after(flat, gone), *small_trades.pop(0))
+        if len(passed_masks) == 1:
+            far_e = far_trade(after(away_e, gone))
+            got = after(got, far_d)
+            got_f = swap(after(send_f, gone), 1, 0)
+            done_e = finish(far_e, stay_e)
+        elif mask == PAIR:
             got = after(got, far_e)
-            done_e = finish(far_e, stay_e)
         elif len(passed_masks) == len(dp_masks):
-            got = after(got, far_f)
+            away_f, stay_f = near_add(after(got_f, stay), keep_f)
+            far_f = far_trade(away_f)
+            got = after(got, away_f)
             done_f = finish(far_f, stay_f)
         total = add(got, stay)
-        flat = flat + flat_got
         if mask == PAIR:
             done_d = finish(after(far_d, total), stay_d)
             in_first = swap(done_d, PAIR, 0)
@@ -1021,6 +1034,8 @@
     for mask in reversed(group_masks):
         bit = (here_group // mask) % 2
         other_part = swap(total, 0, mask)
+        if mask == group_masks[-1]:
+            other_part = after(other_part, out_theirs, in_first)
         total = jnp.concatenate([jnp.where(bit == 0, total, other_part), jnp.where(bit == 0, other_part, total)], axis=1)
         flat = flat + swap(flat, *small_trades.pop(0))
         total, flat = lax.optimization_barrier((total, flat))
@@ -1030,11 +1045,9 @@
     total = jnp.concatenate([jnp.where(core == 0, total, other_part), jnp.where(core == 0, other_part, total)], axis=2)
     weights_done = total.astype(f32)
     grad_qkv, grad_out_weight = weights_done[:3], weights_done[3]
-    flat = flat.reshape(-1)
-    starts = [sum(sizes[:place]) for place in range(len(sizes))]
-    grad_gain_moe, grad_gain_attn, grad_router, grad_table, square_total = [
-        flat[start : start + value.size].reshape(value.shape) for start, value in zip(starts, small)
-    ]
+    grad_gain_moe, grad_gain_attn, square_total = flat[0], flat[1], jnp.sum(flat[2])
+    grad_table = flat[3, : grad_table.size].reshape(grad_table.shape)
+    grad_router = flat[SMALL:].T
 
     out_mine, in_mine = done_c[1:], jnp.concatenate([done_e[1:], done_f])
 

time: 410 us -> 412 us (level)
  waiting for transfers between devices: 80.9 us -> 103 us
  local copies, waits for them, and re-layouts: 34.8 us -> 24.4 us
    ppermute x67, waiting for transfers between devices: 72 us -> 93.7 us  [swap(): return lax.ppermute(value, AXES, pairs)]
    unnamed x165 -> x146, local copies, waits for them, and re-layouts: 16.8 us -> 9.27 us
  transfers between devices with their start and end apart: 81 -> 81, of which waited for: 27 -> 28; matrix products, arithmetic and copies ran while one was open for 14% -> 11% of each run, Pallas kernels for 32% -> 32%
where the time goes in v8:
time: 412 us; the launch traced here: 408 us
  Pallas kernels  157 us (38%)
  waiting for transfers between devices  103 us (25%)
  starting transfers between devices  87.1 us (21%)
  other arithmetic  24.9 us (6%)
  local copies, waits for them, and re-layouts  24.4 us (6%)
  between operations  5.95 us (1%)
  matrix products  5.88 us (1%)
    ppermute x67, waiting for transfers between devices, swap(): return lax.ppermute(value, AXES, pairs)  93.7 us
    ppermute x67, starting transfers between devices, swap(): return lax.ppermute(value, AXES, pairs)  70 us
    pallas_call x4, Pallas kernels, weight_part(): pl.pallas_call(lambda *refs: weight_part_kernel(*refs, count=count, plans...  30.8 us
    pallas_call x2, Pallas kernels, expert_forward(): pl.pallas_call(lambda *refs: expert_forward_kernel(*refs, chunk=chunk, co...  27.5 us
    pallas_call x2, Pallas kernels, expert_backward(): pl.pallas_call(lambda *refs: expert_backward_kernel(*refs, chunk=chunk, c...  25.4 us
    ppermute x14, starting transfers between devices, gather_ring(): lax.ppermute(after(held, *due[step - 2:step - 1]) if step > 1 else held,...  17.1 us
    pallas_call x1, Pallas kernels, attention_forward(): pl.pallas_call(lambda *refs: attention_forward_kernel(*refs, heads=64, bl...  12.6 us
    pallas_call x1, Pallas kernels, attention_backward(): pl.pallas_call(lambda *refs: attention_backward_kernel(*refs, heads=64, b...  11.6 us
  transfers between devices with their start and end apart: 81, of which 28 were waited for; matrix products, arithmetic and copies ran while one was open for 11% of the time, Pallas kernels for 32%

profile of v8, /device:TPU:0, one launch (start us, length us, event | category | flops | bytes accessed | tf_op | source)
XLA Modules:
  0.0 407.9 jit_solution(12169089476034297215)
XLA Ops:
  1.7 3.1 collective-permute-start
  34.3 3.3 join.1.mine.refs_15_
  46.4 6.3 %project.1.refs_2_.refs_3_.refs_4_.refs_0_.refs_1_ = bf16[3,512,768]{2,1,0:T(8,128)(2,1)} custom-call(s32[1]{0:T(128)} %bitcast.2.core.refs_0_, bf16[512,768]{1,0:T(8,128)(2,1)} %fusion.6.rows.refs_1_, bf16[4,768,384]{2,1,0:T(8,128)(2,1)} %join.1.mine.refs_15_, bf16[4,768,384]{2,1,0:T(8,128)(2,1)} %copy-done), custom_call_target="tpu_custom_call" | custom-call | flops 1480000000 | tf_op jit(solution)/shard_map/project/pallas_call | solution.py:397
  54.9 12.6 %attention_forward.1 = (bf16[512,768]{1,0:T(8,128)(2,1)}, bf16[12,512,512]{2,1,0:T(8,128)(2,1)}) custom-call(f32[12]{0:T(128)} %slice_reduce_fusion.refs_0_, s32[1]{0:T(128)S(6)} %copy.86.refs_1_, bf16[3,512,768]{2,1,0:T(8,128)(2,1)} %project.1.refs_2_.refs_3_.refs_4_.refs_0_.refs_1_, bf16[3,512,768]{2,1,0:T(8,128)(2,1)} %project.1.refs_2_.refs_3_.refs_4_.refs_0_.refs_1_, ...), custom_call_target="tpu_custom_call" | custom-call | flops 4809999872 | tf_op jit(solution)/shard_map/attention_forward/pallas_call | solution.py:215
  67.6 5.9 %route.1 = (f32[512,768]{1,0:T(8,128)}, bf16[512,768]{1,0:T(8,128)(2,1)}, f32[512,2]{1,0:T(8,128)}, bf16[160,768]{1,0:T(8,128)(2,1)}, bf16[160,768]{1,0:T(8,128)...) custom-call(s32[1]{0:T(128)} %bitcast.2.core.refs_0_, ...), custom_call_target="tpu_custom_call" | custom-call | flops 2220000000 | tf_op jit(solution)/shard_map/route/pallas_call | solution.py:448
  79.8 3.8 collective-permute-done.18.refs_4_
  84.9 4.0 collective-permute-done.20.refs_2_
  91.2 13.7 %expert_forward.2 = (bf16[3072,640]{1,0:T(8,128)(2,1)}, bf16[640,3072]{1,0:T(8,128)(2,1)}, bf16[768,640]{1,0:T(8,128)(2,1)}, bf16[160,768]{1,0:T(8,128)(2,1)}, b...) custom-call(s32[1]{0:T(128)} %bitcast.4.refs_0_, ...), custom_call_target="tpu_custom_call" | custom-call | flops 4809999872 | tf_op jit(solution)/shard_map/expert_forward/pallas_call | solution.py:79
  105.8 4.2 %collective-permute-start.27 = (bf16[160,768]{1,0:T(8,128)(2,1)S(1)}, bf16[160,768]{1,0:T(8,128)(2,1)S(1)}, u32[]{:S(2)}, u32[]{:S(2)}) collective-permute-start(bf16[160,768]{1,0:T(8,128)(2,1)S(1)} %copy-done.67), channel_id=1, source_target_pairs={{0,2},{1,3},{2,0},{3,1},{4,6},{5,7},{6,4},{7,5},{8,10},{9,11},{10,... | collective-permute-start | bytes 737288 | tf_op jit(solution)/shard_map/ppermute | solution.py:758
  112.6 13.8 %expert_forward.3 = (bf16[3072,640]{1,0:T(8,128)(2,1)}, bf16[640,3072]{1,0:T(8,128)(2,1)}, bf16[768,640]{1,0:T(8,128)(2,1)}, bf16[160,768]{1,0:T(8,128)(2,1)}, b...) custom-call(s32[1]{0:T(128)} %bitcast.4.refs_0_, bf16[640,768]{1,0:T(8,128)(2,1)} %copy-done.10, ...), custom_call_target="tpu_custom_call" | custom-call | flops 4809999872 | tf_op jit(solution)/shard_map/expert_forward/pallas_call | solution.py:79
  135.4 5.6 %collective-permute-done.26 = f32[8,128]{1,0:T(8,128)S(1)} collective-permute-done((f32[8,128]{1,0:T(8,128)S(1)}, f32[8,128]{1,0:T(8,128)S(1)}, u32[]{:S(2)}, u32[]{:S(2)}) %collective-permute-start.26) | collective-permute-done | bytes 4128 | tf_op jit(solution)/shard_map/ppermute | solution.py:758
  144.0 8.5 %combine.1 = (bf16[512,768]{1,0:T(8,128)(2,1)}, f32[512,768]{1,0:T(8,128)}, bf16[512,8]{1,0:T(8,128)(2,1)}, f32[8,768]{1,0:T(8,128)}, bf16[160,768]{1,0:T(8,128)...) custom-call(s32[512,2]{1,0:T(8,128)} %multiply_add_fusion.refs_0_.re, ...), custom_call_target="tpu_custom_call" | custom-call | flops 2960000000 | tf_op jit(solution)/shard_map/combine/pallas_call | solution.py:504
  153.9 3.3 collective-permute-start.38
  164.2 6.2 %collective-permute-done.39.refs_4_ = bf16[160,768]{1,0:T(8,128)(2,1)S(1)} collective-permute-done((bf16[160,768]{1,0:T(8,128)(2,1)}, bf16[160,768]{1,0:T(8,128)(2,1)S(1)}, u32[]{:S(2)}, u32[]{:S(2)}) %collective-permute-start.39) | collective-permute-done | bytes 245792 | tf_op jit(solution)/shard_map/ppermute | solution.py:758
  171.1 12.5 %expert_backward.2 = (bf16[640,3072]{1,0:T(8,128)(2,1)}, bf16[640,768]{1,0:T(8,128)(2,1)}, bf16[160,768]{1,0:T(8,128)(2,1)}, bf16[160,768]{1,0:T(8,128)(2,1)}, b...) custom-call(s32[1]{0:T(128)} %bitcast.4.refs_0_, bf16[160,768]{1,0:T(8,128)(2,1)} %get-tuple-element.214.refs_1_, ...), custom_call_target="tpu_custom_call" | custom-call | flops 4070000128 | tf_op jit(solution)/shard_map/expert_backward/pallas_call | solution.py:136
  187.3 7.8 %weight_part.4 = (bf16[2,2,128,768]{3,2,1,0:T(8,128)(2,1)}, bf16[2,2,128,768]{3,2,1,0:T(8,128)(2,1)}, bf16[2,2,128,768]{3,2,1,0:T(8,128)(2,1)}) custom-call(s32[4]{0:T(128)} %pad_add_fusion.1.refs_0_, bf16[3072,640]{1,0:T(8,128)(2,1)} %get-tuple-element.190.refs_1_.refs_2_.refs_3_.refs_4_, ...), custom_call_target="tpu_custom_call" | custom-call | flops 1480000000 | tf_op jit(solution)/shard_map/weight_part/pallas_call | solution.py:338
  199.3 12.9 %expert_backward.3 = (bf16[640,3072]{1,0:T(8,128)(2,1)}, bf16[640,768]{1,0:T(8,128)(2,1)}, bf16[160,768]{1,0:T(8,128)(2,1)}, bf16[160,768]{1,0:T(8,128)(2,1)}, b...) custom-call(s32[1]{0:T(128)} %bitcast.4.refs_0_, bf16[640,768]{1,0:T(8,128)(2,1)} %copy-done.1, ...), custom_call_target="tpu_custom_call" | custom-call | flops 4070000128 | tf_op jit(solution)/shard_map/expert_backward/pallas_call | solution.py:136
  220.1 7.8 %weight_part.5 = (bf16[2,2,128,768]{3,2,1,0:T(8,128)(2,1)}, bf16[2,2,128,768]{3,2,1,0:T(8,128)(2,1)}, bf16[2,2,128,768]{3,2,1,0:T(8,128)(2,1)}) custom-call(s32[4]{0:T(128)} %pad_add_fusion.2.refs_0_, bf16[3072,640]{1,0:T(8,128)(2,1)} %get-tuple-element.190.refs_1_.refs_2_.refs_3_.refs_4_, ...), custom_call_target="tpu_custom_call" | custom-call | flops 1480000000 | tf_op jit(solution)/shard_map/weight_part/pallas_call | solution.py:338
  229.3 7.7 %weight_part.6 = (bf16[2,2,32,3072]{3,2,1,0:T(8,128)(2,1)}, bf16[2,2,32,3072]{3,2,1,0:T(8,128)(2,1)}, bf16[2,2,32,3072]{3,2,1,0:T(8,128)(2,1)}) custom-call(s32[4]{0:T(128)} %pad_add_fusion.1.refs_0_, bf16[768,640]{1,0:T(8,128)(2,1)} %get-tuple-element.220.refs_1_.refs_2_.refs_3_.refs_4_, ...), custom_call_target="tpu_custom_call" | custom-call | flops 1480000000 | tf_op jit(solution)/shard_map/weight_part/pallas_call | solution.py:338
  239.0 8.6 %collect.1 = (f32[512,768]{1,0:T(8,128)}, bf16[512,768]{1,0:T(8,128)(2,1)}, bf16[512,768]{1,0:T(8,128)(2,1)}, f32[8,768]{1,0:T(8,128)}) custom-call(s32[1]{0:T(128)} %bitcast.2.core.refs_0_, s32[512,2]{1,0:T(8,128)} %multiply_add_fusion.refs_0_.refs_1_, bf16[160,768]{1,0:T(8,128)(2,1)} %get-tuple-element.262.refs_2_, bf16[160,768]{1,0:T(8,128)(2,1)} %copy-done.54, ...), custom_call_target="tpu_custom_call" | custom-call | flops 2960000000 | tf_op jit(solution)/shard_map/collect/pallas_call | solution.py:555
  249.4 11.6 %attention_backward.1 = (bf16[3,512,768]{2,1,0:T(8,128)(2,1)}, f32[12,4,128,128]{3,2,1,0:T(8,128)}) custom-call(bf16[3,512,768]{2,1,0:T(8,128)(2,1)} %project.1.refs_2_.refs_3_.refs_4_.refs_0_.refs_1_, bf16[3,512,768]{2,1,0:T(8,128)(2,1)} %project.1.refs_2_.refs_3_.refs_4_.refs_0_.refs_1_, ...), custom_call_target="tpu_custom_call" | custom-call | flops 1480000000 | tf_op jit(solution)/shard_map/attention_backward/pallas_call | solution.py:281
  262.0 8.2 %outer_halves.1 = (bf16[2,768,384]{2,1,0:T(8,128)(2,1)}, bf16[2,768,384]{2,1,0:T(8,128)(2,1)}, bf16[2,768,384]{2,1,0:T(8,128)(2,1)}, bf16[2,768,384]{2,1,0:T(8,128)(2,1)}) custom-call(s32[1]{0:T(128)} %bitcast.2.core.refs_0_, bf16[512,768]{1,0:T(8,128)(2,1)} %fusion.6.rows.refs_1_, bf16[512,768]{1,0:T(8,128)(2,1)} %get-tuple-element.182.attended.refs_2_, ...), custom_call_target="tpu_custom_call" | custom-call | flops 740000000 | tf_op jit(solution)/shard_map/outer_halves/pallas_call | solution.py:605
  282.9 7.5 %weight_part.7 = (bf16[2,2,32,3072]{3,2,1,0:T(8,128)(2,1)}, bf16[2,2,32,3072]{3,2,1,0:T(8,128)(2,1)}, bf16[2,2,32,3072]{3,2,1,0:T(8,128)(2,1)}) custom-call(s32[4]{0:T(128)} %pad_add_fusion.2.refs_0_, bf16[768,640]{1,0:T(8,128)(2,1)} %get-tuple-element.220.refs_1_.refs_2_.refs_3_.refs_4_, ...), custom_call_target="tpu_custom_call" | custom-call | flops 14800000000 | tf_op jit(solution)/shard_map/weight_part/pallas_call | solution.py:338
  293.6 5.3 %collective-permute-done.62 = bf16[2,2,32,3072]{3,2,1,0:T(8,128)(2,1)S(1)} collective-permute-done((bf16[2,2,32,3072]{3,2,1,0:T(8,128)(2,1)}, bf16[2,2,32,3072]{3,2,1,0:T(8,128)(2,1)S(1)}, u32[]{:S(2)}, u32[]{:S(2)}) %collective-permute-start.62) | collective-permute-done | bytes 786464 | tf_op jit(solution)/shard_map/ppermute | solution.py:758
  299.9 23.8 %collective-permute-done.63 = bf16[1,4,128,768]{3,2,1,0:T(8,128)(2,1)} collective-permute-done((bf16[1,4,128,768]{3,2,1,0:T(8,128)(2,1)}, bf16[1,4,128,768]{3,2,1,0:T(8,128)(2,1)}, u32[]{:S(2)}, u32[]{:S(2)}) %collective-permute-start.63) | collective-permute-done | bytes 786464 | tf_op jit(solution)/shard_map/ppermute | solution.py:758
  329.2 5.3 %fusion.11 = f32[12,32]{1,0:T(8,128)S(1)} fusion(s32[4,128,128]{2,1,0:T(8,128)S(1)} %pad_add_fusion, f32[12,4,128,128]{3,2,1,0:T(8,128)S(1)} %copy-done.3), kind=kOutput, calls=%fused_computation.34 | convolution fusion | flops 304087040 | bytes 3409408 | tf_op jit(solution)/shard_map/hdxy,dxyb->hb/dot_general | solution.py:714
  334.5 8.5 %enter.1 = (f32[512,768]{1,0:T(8,128)}, f32[16,768]{1,0:T(8,128)}) custom-call(s32[1]{0:T(128)} %bitcast.2.core.refs_0_, bf16[3,512,768]{2,1,0:T(8,128)(2,1)} %get-tuple-element.316.refs_3_.grads, bf16[4,768,384]{2,1,0:T(8,128)(2,1)} %join.1.mine.refs_15_, bf16[4,768,384]{2,1,0:T(8,128)(2,1)} %copy-done, bf16[512,768]{1,0:T(8,128)(2,1)} %tokens.3, ...), custom_call_target="tpu_custom_call" | custom-call | flops 2220000000 | tf_op jit(solution)/shard_map/enter/pallas_call | solution.py:659
  354.3 4.8 %collective-permute-done.66 = bf16[4,2,48,384]{3,2,1,0:T(8,128)(2,1)S(1)} collective-permute-done((bf16[4,2,48,384]{3,2,1,0:T(8,128)(2,1)S(1)}, bf16[4,2,48,384]{3,2,1,0:T(8,128)(2,1)S(1)}, u32[]{:S(2)}, u32[]{:S(2)}) %collective-permute-start.66) | collective-permute-done | bytes 294944 | tf_op jit(solution)/shard_map/ppermute | solution.py:758
  365.4 4.0 collective-permute-done.68
  370.6 3.4 collective-permute-start.72
  373.9 14.6 %collective-permute-done.76 = f32[16,768]{1,0:T(8,128)S(1)} collective-permute-done((f32[16,768]{1,0:T(8,128)S(1)}, f32[16,768]{1,0:T(8,128)S(1)}, u32[]{:S(2)}, u32[]{:S(2)}) %collective-permute-start.76) | collective-permute-done | bytes 49184 | tf_op jit(solution)/shard_map/ppermute | solution.py:758
  389.3 6.7 %collective-permute-done.72 = bf16[2,32,3072]{2,1,0:T(8,128)(2,1)S(1)} collective-permute-done((bf16[2,32,3072]{2,1,0:T(8,128)(2,1)S(1)}, bf16[2,32,3072]{2,1,0:T(8,128)(2,1)S(1)}, u32[]{:S(2)}, u32[]{:S(2)}) %collective-permute-start.72) | collective-permute-done | bytes 393248 | tf_op jit(solution)/shard_map/ppermute | solution.py:758
  (394 shorter events, 147.0 us)
Async XLA Ops:
  77.0 27.9 %collective-permute-start.24 = (bf16[160,768]{1,0:T(8,128)(2,1)}, bf16[160,768]{1,0:T(8,128)(2,1)S(1)}, u32[]{:S(2)}, u32[]{:S(2)}) collective-permute-start(bf16[160,768]{1,0:T(8,128)(2,1)} %get-tuple-element.196), channel_id=1, source_target_pairs={{0,10},{1,11},{2,8},{3,9},{4,14},{5,15},{6,12},{7,13},{8,2},{9,3},... | collective-permute-start | bytes 737288 | tf_op jit(solution)/shard_map/ppermute | solution.py:758
  79.4 25.6 %collective-permute-start.23 = (bf16[160,768]{1,0:T(8,128)(2,1)}, bf16[160,768]{1,0:T(8,128)(2,1)S(1)}, u32[]{:S(2)}, u32[]{:S(2)}) collective-permute-start(bf16[160,768]{1,0:T(8,128)(2,1)} %get-tuple-element.194), channel_id=1, source_target_pairs={{0,8},{1,9},{2,10},{3,11},{4,12},{5,13},{6,14},{7,15},{8,0},{9,1},... | collective-permute-start | bytes 737288 | tf_op jit(solution)/shard_map/ppermute | solution.py:758
  83.6 21.4 %collective-permute-start.22 = (bf16[160,768]{1,0:T(8,128)(2,1)}, bf16[160,768]{1,0:T(8,128)(2,1)S(1)}, u32[]{:S(2)}, u32[]{:S(2)}) collective-permute-start(bf16[160,768]{1,0:T(8,128)(2,1)} %get-tuple-element.192), channel_id=1, source_target_pairs={{0,2},{1,3},{2,0},{3,1},{4,6},{5,7},{6,4},{7,5},{8,10},{9,11},{10,... | collective-permute-start | bytes 737288 | tf_op jit(solution)/shard_map/ppermute | solution.py:758
  88.9 16.0 %collective-permute-start.19 = (f32[8,128]{1,0:T(8,128)S(1)}, f32[8,128]{1,0:T(8,128)S(1)}, u32[]{:S(2)}, u32[]{:S(2)}) collective-permute-start(f32[8,128]{1,0:T(8,128)S(1)} %add.546), channel_id=1, source_target_pairs={{0,8},{1,9},{2,10},{3,11},{4,12},{5,13},{6,14},{7,15},{8,0},{9,1},... | collective-permute-start | bytes 12296 | tf_op jit(solution)/shard_map/ppermute | solution.py:758
  105.8 20.5 %collective-permute-start.27 = (bf16[160,768]{1,0:T(8,128)(2,1)S(1)}, bf16[160,768]{1,0:T(8,128)(2,1)S(1)}, u32[]{:S(2)}, u32[]{:S(2)}) collective-permute-start(bf16[160,768]{1,0:T(8,128)(2,1)S(1)} %copy-done.67), channel_id=1, source_target_pairs={{0,2},{1,3},{2,0},{3,1},{4,6},{5,7},{6,4},{7,5},{8,10},{9,11},{10,... | collective-permute-start | bytes 737288 | tf_op jit(solution)/shard_map/ppermute | solution.py:758
  110.0 16.3 %collective-permute-start.28 = (bf16[160,768]{1,0:T(8,128)(2,1)S(1)}, bf16[160,768]{1,0:T(8,128)(2,1)S(1)}, u32[]{:S(2)}, u32[]{:S(2)}) collective-permute-start(bf16[160,768]{1,0:T(8,128)(2,1)S(1)} %copy-done.65), channel_id=1, source_target_pairs={{0,8},{1,9},{2,10},{3,11},{4,12},{5,13},{6,14},{7,15},{8,0},{9,1},... | collective-permute-start | bytes 737288 | tf_op jit(solution)/shard_map/ppermute | solution.py:758
  110.1 16.3 %collective-permute-start.29 = (bf16[160,768]{1,0:T(8,128)(2,1)S(1)}, bf16[160,768]{1,0:T(8,128)(2,1)S(1)}, u32[]{:S(2)}, u32[]{:S(2)}) collective-permute-start(bf16[160,768]{1,0:T(8,128)(2,1)S(1)} %copy-done.63), channel_id=1, source_target_pairs={{0,10},{1,11},{2,8},{3,9},{4,14},{5,15},{6,12},{7,13},{8,2},{9,3},... | collective-permute-start | bytes 737288 | tf_op jit(solution)/shard_map/ppermute | solution.py:758
  158.0 25.6 %collective-permute-start.42 = (bf16[160,768]{1,0:T(8,128)(2,1)}, bf16[160,768]{1,0:T(8,128)(2,1)S(1)}, u32[]{:S(2)}, u32[]{:S(2)}) collective-permute-start(bf16[160,768]{1,0:T(8,128)(2,1)} %get-tuple-element.230), channel_id=1, source_target_pairs={{0,10},{1,11},{2,8},{3,9},{4,14},{5,15},{6,12},{7,13},{8,2},{9,3},... | collective-permute-start | bytes 737288 | tf_op jit(solution)/shard_map/ppermute | solution.py:758
  160.1 23.6 %collective-permute-start.41 = (bf16[160,768]{1,0:T(8,128)(2,1)}, bf16[160,768]{1,0:T(8,128)(2,1)S(1)}, u32[]{:S(2)}, u32[]{:S(2)}) collective-permute-start(bf16[160,768]{1,0:T(8,128)(2,1)} %get-tuple-element.228), channel_id=1, source_target_pairs={{0,8},{1,9},{2,10},{3,11},{4,12},{5,13},{6,14},{7,15},{8,0},{9,1},... | collective-permute-start | bytes 737288 | tf_op jit(solution)/shard_map/ppermute | solution.py:758
  160.1 23.5 %collective-permute-start.40 = (bf16[160,768]{1,0:T(8,128)(2,1)}, bf16[160,768]{1,0:T(8,128)(2,1)S(1)}, u32[]{:S(2)}, u32[]{:S(2)}) collective-permute-start(bf16[160,768]{1,0:T(8,128)(2,1)} %get-tuple-element.226), channel_id=1, source_target_pairs={{0,2},{1,3},{2,0},{3,1},{4,6},{5,7},{6,4},{7,5},{8,10},{9,11},{10,... | collective-permute-start | bytes 737288 | tf_op jit(solution)/shard_map/ppermute | solution.py:758
  195.2 19.8 %collective-permute-start.48 = (bf16[2,2,128,768]{3,2,1,0:T(8,128)(2,1)}, bf16[2,2,128,768]{3,2,1,0:T(8,128)(2,1)S(1)}, u32[]{:S(2)}, u32[]{:S(2)}) collective-permute-start(bf16[2,2,128,768]{3,2,1,0:T(8,128)(2,1)} %get-tuple-element.243), channel_id=1, source_target_pairs={{0,4},{1,5},{2,6},{3,7},{4,0},{5,1},{6,2},{7,3},{8,12},{9,13},{10,... | collective-permute-start | bytes 2359304 | tf_op jit(solution)/shard_map/ppermute | solution.py:758
  195.7 16.4 %collective-permute-start.44 = (bf16[160,768]{1,0:T(8,128)(2,1)S(1)}, bf16[160,768]{1,0:T(8,128)(2,1)S(1)}, u32[]{:S(2)}, u32[]{:S(2)}) collective-permute-start(bf16[160,768]{1,0:T(8,128)(2,1)S(1)} %copy-done.60), channel_id=1, source_target_pairs={{0,2},{1,3},{2,0},{3,1},{4,6},{5,7},{6,4},{7,5},{8,10},{9,11},{10,... | collective-permute-start | bytes 737288 | tf_op jit(solution)/shard_map/ppermute | solution.py:758
  196.3 15.8 %collective-permute-start.45 = (bf16[160,768]{1,0:T(8,128)(2,1)S(1)}, bf16[160,768]{1,0:T(8,128)(2,1)S(1)}, u32[]{:S(2)}, u32[]{:S(2)}) collective-permute-start(bf16[160,768]{1,0:T(8,128)(2,1)S(1)} %copy-done.59), channel_id=1, source_target_pairs={{0,8},{1,9},{2,10},{3,11},{4,12},{5,13},{6,14},{7,15},{8,0},{9,1},... | collective-permute-start | bytes 737288 | tf_op jit(solution)/shard_map/ppermute | solution.py:758
  215.2 22.4 %collective-permute-start.52 = (bf16[160,768]{1,0:T(8,128)(2,1)}, bf16[160,768]{1,0:T(8,128)(2,1)S(1)}, u32[]{:S(2)}, u32[]{:S(2)}) collective-permute-start(bf16[160,768]{1,0:T(8,128)(2,1)} %collective-permute-done.49), channel_id=1, source_target_pairs={{0,2},{1,3},{2,0},{3,1},{4,6},{5,7},{6,4},{7,5},{8,10},{9,11},{10,... | collective-permute-start | bytes 737288 | tf_op jit(solution)/shard_map/ppermute | solution.py:758
  215.8 22.3 %collective-permute-start.53 = (bf16[160,768]{1,0:T(8,128)(2,1)}, bf16[160,768]{1,0:T(8,128)(2,1)S(1)}, u32[]{:S(2)}, u32[]{:S(2)}) collective-permute-start(bf16[160,768]{1,0:T(8,128)(2,1)} %collective-permute-done.50), channel_id=1, source_target_pairs={{0,8},{1,9},{2,10},{3,11},{4,12},{5,13},{6,14},{7,15},{8,0},{9,1},... | collective-permute-start | bytes 737288 | tf_op jit(solution)/shard_map/ppermute | solution.py:758
  217.8 20.4 %collective-permute-start.54 = (bf16[160,768]{1,0:T(8,128)(2,1)}, bf16[160,768]{1,0:T(8,128)(2,1)S(1)}, u32[]{:S(2)}, u32[]{:S(2)}) collective-permute-start(bf16[160,768]{1,0:T(8,128)(2,1)} %collective-permute-done.51), channel_id=1, source_target_pairs={{0,10},{1,11},{2,8},{3,9},{4,14},{5,15},{6,12},{7,13},{8,2},{9,3},... | collective-permute-start | bytes 737288 | tf_op jit(solution)/shard_map/ppermute | solution.py:758
  218.6 30.5 %collective-permute-start.55 = (bf16[2,2,128,768]{3,2,1,0:T(8,128)(2,1)}, bf16[2,2,128,768]{3,2,1,0:T(8,128)(2,1)S(1)}, u32[]{:S(2)}, u32[]{:S(2)}) collective-permute-start(bf16[2,2,128,768]{3,2,1,0:T(8,128)(2,1)} %get-tuple-element.273), channel_id=1, source_target_pairs={{0,4},{1,5},{2,6},{3,7},{4,0},{5,1},{6,2},{7,3},{8,12},{9,13},{10,... | collective-permute-start | bytes 2359304 | tf_op jit(solution)/shard_map/ppermute | solution.py:758
  237.0 24.0 %collective-permute-start.57 = (bf16[1,2,128,768]{3,2,1,0:T(8,128)(2,1)S(1)}, bf16[1,2,128,768]{3,2,1,0:T(8,128)(2,1)S(1)}, u32[]{:S(2)}, u32[]{:S(2)}) collective-permute-start(bf16[1,2,128,768]{3,2,1,0:T(8,128)(2,1)S(1)} %constant_dynamic-slice_fusion.7), channel_id=1, source_target_pairs={{0,16},{1,17},{2,18},{3,19},{4,20},{5,21},{6,22},{7,23},{8,24},{9,... | collective-permute-start | bytes 1179656 | tf_op jit(solution)/shard_map/ppermute | solution.py:758
  237.6 23.4 %collective-permute-start.56 = (bf16[2,2,128,768]{3,2,1,0:T(8,128)(2,1)S(1)}, bf16[2,2,128,768]{3,2,1,0:T(8,128)(2,1)S(1)}, u32[]{:S(2)}, u32[]{:S(2)}) collective-permute-start(bf16[2,2,128,768]{3,2,1,0:T(8,128)(2,1)S(1)} %copy-done.49), channel_id=1, source_target_pairs={{0,4},{1,5},{2,6},{3,7},{4,0},{5,1},{6,2},{7,3},{8,12},{9,13},{10,... | collective-permute-start | bytes 2359304 | tf_op jit(solution)/shard_map/ppermute | solution.py:758
  247.6 25.1 %collective-permute-start.58 = (bf16[2,2,32,3072]{3,2,1,0:T(8,128)(2,1)S(1)}, bf16[2,2,32,3072]{3,2,1,0:T(8,128)(2,1)S(1)}, u32[]{:S(2)}, u32[]{:S(2)}) collective-permute-start(bf16[2,2,32,3072]{3,2,1,0:T(8,128)(2,1)S(1)} %copy-done.50), channel_id=1, source_target_pairs={{0,4},{1,5},{2,6},{3,7},{4,0},{5,1},{6,2},{7,3},{8,12},{9,13},{10,... | collective-permute-start | bytes 2359304 | tf_op jit(solution)/shard_map/ppermute | solution.py:758
  276.7 46.9 %collective-permute-start.63 = (bf16[1,4,128,768]{3,2,1,0:T(8,128)(2,1)}, bf16[1,4,128,768]{3,2,1,0:T(8,128)(2,1)}, u32[]{:S(2)}, u32[]{:S(2)}) collective-permute-start(bf16[1,4,128,768]{3,2,1,0:T(8,128)(2,1)} %pad_maximum_fusion.5), channel_id=1, source_target_pairs={{0,16},{1,17},{2,18},{3,19},{4,20},{5,21},{6,22},{7,23},{8,24},{9,... | collective-permute-start | bytes 2359304 | tf_op jit(solution)/shard_map/ppermute | solution.py:758
  279.4 19.5 %collective-permute-start.62 = (bf16[2,2,32,3072]{3,2,1,0:T(8,128)(2,1)}, bf16[2,2,32,3072]{3,2,1,0:T(8,128)(2,1)S(1)}, u32[]{:S(2)}, u32[]{:S(2)}) collective-permute-start(bf16[2,2,32,3072]{3,2,1,0:T(8,128)(2,1)} %get-tuple-element.295), channel_id=1, source_target_pairs={{0,4},{1,5},{2,6},{3,7},{4,0},{5,1},{6,2},{7,3},{8,12},{9,13},{10,... | collective-permute-start | bytes 2359304 | tf_op jit(solution)/shard_map/ppermute | solution.py:758
  282.2 42.8 %collective-permute-start.61 = (bf16[4,8,48,384]{3,2,1,0:T(8,128)(2,1)S(1)}, bf16[4,8,48,384]{3,2,1,0:T(8,128)(2,1)S(1)}, u32[]{:S(2)}, u32[]{:S(2)}) collective-permute-start(bf16[4,8,48,384]{3,2,1,0:T(8,128)(2,1)S(1)} %pad_maximum_fusion.2), channel_id=1, source_target_pairs={{0,2},{1,3},{2,0},{3,1},{4,6},{5,7},{6,4},{7,5},{8,10},{9,11},{10,... | collective-permute-start | bytes 3538952 | tf_op jit(solution)/shard_map/ppermute | solution.py:758
  292.6 51.8 %collective-permute-start.65 = (bf16[1,2,32,3072]{3,2,1,0:T(8,128)(2,1)}, bf16[1,2,32,3072]{3,2,1,0:T(8,128)(2,1)}, u32[]{:S(2)}, u32[]{:S(2)}) collective-permute-start(bf16[1,2,32,3072]{3,2,1,0:T(8,128)(2,1)} %constant_dynamic-slice_fusion.4), channel_id=1, source_target_pairs={{0,16},{1,17},{2,18},{3,19},{4,20},{5,21},{6,22},{7,23},{8,24},{9,... | collective-permute-start | bytes 1179656 | tf_op jit(solution)/shard_map/ppermute | solution.py:758
  326.2 18.1 %collective-permute-start.64 = (bf16[4,2,2,48,384]{4,3,2,1,0:T(8,128)(2,1)}, bf16[4,2,2,48,384]{4,3,2,1,0:T(8,128)(2,1)}, u32[]{:S(2)}, u32[]{:S(2)}) collective-permute-start(bf16[4,2,2,48,384]{4,3,2,1,0:T(8,128)(2,1)} %dynamic-slice_bitcast_fusion), channel_id=1, source_target_pairs={{0,4},{1,5},{2,6},{3,7},{4,0},{5,1},{6,2},{7,3},{8,12},{9,13},{10,... | collective-permute-start | bytes 1769480 | tf_op jit(solution)/shard_map/ppermute | solution.py:758
  327.7 20.3 %collective-permute-start.67 = (bf16[1,2,32,3072]{3,2,1,0:T(8,128)(2,1)}, bf16[1,2,32,3072]{3,2,1,0:T(8,128)(2,1)}, u32[]{:S(2)}, u32[]{:S(2)}) collective-permute-start(bf16[1,2,32,3072]{3,2,1,0:T(8,128)(2,1)} %constant_dynamic-slice_fusion.3), channel_id=1, source_target_pairs={{0,16},{1,17},{2,18},{3,19},{4,20},{5,21},{6,22},{7,23},{8,24},{9,... | collective-permute-start | bytes 1179656 | tf_op jit(solution)/shard_map/ppermute | solution.py:758
  327.7 33.5 %collective-permute-start.69 = (bf16[2,2,32,3072]{3,2,1,0:T(8,128)(2,1)}, bf16[2,2,32,3072]{3,2,1,0:T(8,128)(2,1)}, u32[]{:S(2)}, u32[]{:S(2)}) collective-permute-start(bf16[2,2,32,3072]{3,2,1,0:T(8,128)(2,1)} %get-tuple-element.307), channel_id=1, source_target_pairs={{0,4},{1,5},{2,6},{3,7},{4,0},{5,1},{6,2},{7,3},{8,12},{9,13},{10,... | collective-permute-start | bytes 2359304 | tf_op jit(solution)/shard_map/ppermute | solution.py:758
  350.9 38.5 %collective-permute-start.80 = (bf16[1,32,3072]{2,1,0:T(8,128)(2,1)S(1)}, bf16[1,32,3072]{2,1,0:T(8,128)(2,1)S(1)}, u32[]{:S(2)}, u32[]{:S(2)}) collective-permute-start(bf16[1,32,3072]{2,1,0:T(8,128)(2,1)S(1)} %get-tuple-element.351), channel_id=1, source_target_pairs={{0,8},{1,9},{2,10},{3,11},{4,12},{5,13},{6,14},{7,15},{8,0},{9,1},... | collective-permute-start | bytes 589832 | tf_op jit(solution)/shard_map/ppermute | solution.py:758
  363.2 34.7 %collective-permute-start.71 = (bf16[3,128,768]{2,1,0:T(8,128)(2,1)S(1)}, bf16[3,128,768]{2,1,0:T(8,128)(2,1)S(1)}, u32[]{:S(2)}, u32[]{:S(2)}) collective-permute-start(bf16[3,128,768]{2,1,0:T(8,128)(2,1)S(1)} %copy-done.19), channel_id=1, source_target_pairs={{0,8},{1,9},{2,10},{3,11},{4,12},{5,13},{6,14},{7,15},{8,0},{9,1},... | collective-permute-start | bytes 1769480 | tf_op jit(solution)/shard_map/ppermute | solution.py:758
  365.3 23.9 %collective-permute-start.79 = (bf16[1,2,32,3072]{3,2,1,0:T(8,128)(2,1)S(1)}, bf16[1,2,32,3072]{3,2,1,0:T(8,128)(2,1)S(1)}, u32[]{:S(2)}, u32[]{:S(2)}) collective-permute-start(bf16[1,2,32,3072]{3,2,1,0:T(8,128)(2,1)S(1)} %constant_dynamic-slice_fusion.2), channel_id=1, source_target_pairs={{0,16},{1,17},{2,18},{3,19},{4,20},{5,21},{6,22},{7,23},{8,24},{9,... | collective-permute-start | bytes 1179656 | tf_op jit(solution)/shard_map/ppermute | solution.py:758
  369.4 19.1 %collective-permute-start.76 = (f32[16,768]{1,0:T(8,128)S(1)}, f32[16,768]{1,0:T(8,128)S(1)}, u32[]{:S(2)}, u32[]{:S(2)}) collective-permute-start(f32[16,768]{1,0:T(8,128)S(1)} %add.626), channel_id=1, source_target_pairs={{0,16},{1,17},{2,18},{3,19},{4,20},{5,21},{6,22},{7,23},{8,24},{9,... | collective-permute-start | bytes 147464 | tf_op jit(solution)/shard_map/ppermute | solution.py:758
  370.6 25.5 %collective-permute-start.72 = (bf16[2,32,3072]{2,1,0:T(8,128)(2,1)S(1)}, bf16[2,32,3072]{2,1,0:T(8,128)(2,1)S(1)}, u32[]{:S(2)}, u32[]{:S(2)}) collective-permute-start(bf16[2,32,3072]{2,1,0:T(8,128)(2,1)S(1)} %fusion.16), channel_id=1, source_target_pairs={{0,8},{1,9},{2,10},{3,11},{4,12},{5,13},{6,14},{7,15},{8,0},{9,1},... | collective-permute-start | bytes 1179656 | tf_op jit(solution)/shard_map/ppermute | solution.py:758
  (122 other events, 948.8 us)

commit v9 on v8

--- a/solution.py
+++ b/solution.py
@@ -981,14 +981,14 @@
         kept, rows_in, after(grad_pre, y_away), in_rows, in_plans, rest, inner // 2, 40
     )
     away_d, stay_d = near_add(got_d, keep_d)
-    far_d = far_trade(away_d)
+    far_d = far_trade(after(away_d, far_c))
     away_e, stay_e = near_add(after(got_e, away_d), keep_e)
     done_c = finish(after(far_c, away_e), stay_c)
-    total = add(after(y_got, away_e, far_c), y_stay)
+    total = add(after(y_got, away_e), y_stay)
     total = total.reshape((4,) + (2,) * len(dp_masks) + (-1, columns))
 
 
-    small_trades = [(0, 1), (0, group_masks[0])] + [(mask, 0) for mask in dp_masks if mask != PAIR] + [(PAIR, 0)]
+    small_trades = [(0, 1), (0, group_masks[0])] + [(mask, 0) for mask in reversed(dp_masks) if mask != PAIR] + [(PAIR, 0)]
     small_trades += [(0, mask) for mask in group_masks[1:]]
     passed_masks = []
     for mask in dp_masks:
@@ -1013,16 +1013,16 @@
         for _ in range((0, 2, 1)[min(len(passed_masks), 3) - 1]):
             flat = flat + swap(after(flat, gone), *small_trades.pop(0))
         if len(passed_masks) == 1:
-            far_e = far_trade(after(away_e, gone))
+            far_e = far_trade(after(away_e, small))
+            got_f = swap(after(send_f, gone), 1, 0)
+        elif mask == PAIR:
             got = after(got, far_d)
-            got_f = swap(after(send_f, gone), 1, 0)
-            done_e = finish(far_e, stay_e)
-        elif mask == PAIR:
-            got = after(got, far_e)
         elif len(passed_masks) == len(dp_masks):
             away_f, stay_f = near_add(after(got_f, stay), keep_f)
             far_f = far_trade(away_f)
-            got = after(got, away_f)
+            far_e = after(far_e, gone)
+            done_e = finish(far_e, stay_e)
+            got = after(got, away_f, in_first, far_e)
             done_f = finish(far_f, stay_f)
         total = add(got, stay)
         if mask == PAIR:

time: 412 us -> 415 us (level)
    unnamed x146 -> x150, local copies, waits for them, and re-layouts: 9.27 us -> 9.28 us
  transfers between devices with their start and end apart: 81 -> 81, of which waited for: 28 -> 29; matrix products, arithmetic and copies ran while one was open for 11% -> 10% of each run, Pallas kernels for 32% -> 32%
where the time goes in v9:
time: 415 us; the launch traced here: 411 us
  Pallas kernels  157 us (38%)
  waiting for transfers between devices  103 us (25%)
  starting transfers between devices  88.6 us (21%)
  local copies, waits for them, and re-layouts  26.1 us (6%)
  other arithmetic  23.8 us (6%)
  between operations  5.96 us (1%)
  matrix products  5.88 us (1%)
    ppermute x67, waiting for transfers between devices, swap(): return lax.ppermute(value, AXES, pairs)  94 us
    ppermute x67, starting transfers between devices, swap(): return lax.ppermute(value, AXES, pairs)  71.5 us
    pallas_call x4, Pallas kernels, weight_part(): pl.pallas_call(lambda *refs: weight_part_kernel(*refs, count=count, plans...  30.8 us
    pallas_call x2, Pallas kernels, expert_forward(): pl.pallas_call(lambda *refs: expert_forward_kernel(*refs, chunk=chunk, co...  27.4 us
    pallas_call x2, Pallas kernels, expert_backward(): pl.pallas_call(lambda *refs: expert_backward_kernel(*refs, chunk=chunk, c...  25.2 us
    ppermute x14, starting transfers between devices, gather_ring(): lax.ppermute(after(held, *due[step - 2:step - 1]) if step > 1 else held,...  17.1 us
    pallas_call x1, Pallas kernels, attention_forward(): pl.pallas_call(lambda *refs: attention_forward_kernel(*refs, heads=64, bl...  12.7 us
    pallas_call x1, Pallas kernels, attention_backward(): pl.pallas_call(lambda *refs: attention_backward_kernel(*refs, heads=64, b...  11.6 us
  transfers between devices with their start and end apart: 81, of which 29 were waited for; matrix products, arithmetic and copies ran while one was open for 10% of the time, Pallas kernels for 32%

profile of v9, /device:TPU:0, one launch (start us, length us, event | category | flops | bytes accessed | tf_op | source)
XLA Modules:
  0.0 410.8 jit_solution(12129300202329867558)
XLA Ops:
  34.3 3.3 join.1.mine.refs_15_
  46.4 6.4 %project.1.refs_2_.refs_3_.refs_4_.refs_0_.refs_1_ = bf16[3,512,768]{2,1,0:T(8,128)(2,1)} custom-call(s32[1]{0:T(128)} %bitcast.2.core.refs_0_, bf16[512,768]{1,0:T(8,128)(2,1)} %fusion.6.rows.refs_1_, bf16[4,768,384]{2,1,0:T(8,128)(2,1)} %join.1.mine.refs_15_, bf16[4,768,384]{2,1,0:T(8,128)(2,1)} %copy-done), custom_call_target="tpu_custom_call" | custom-call | flops 1480000000 | tf_op jit(solution)/shard_map/project/pallas_call | solution.py:397
  55.0 12.7 %attention_forward.1 = (bf16[512,768]{1,0:T(8,128)(2,1)}, bf16[12,512,512]{2,1,0:T(8,128)(2,1)}) custom-call(f32[12]{0:T(128)} %slice_reduce_fusion.refs_0_, s32[1]{0:T(128)S(6)} %copy.86.refs_1_, bf16[3,512,768]{2,1,0:T(8,128)(2,1)} %project.1.refs_2_.refs_3_.refs_4_.refs_0_.refs_1_, bf16[3,512,768]{2,1,0:T(8,128)(2,1)} %project.1.refs_2_.refs_3_.refs_4_.refs_0_.refs_1_, ...), custom_call_target="tpu_custom_call" | custom-call | flops 4809999872 | tf_op jit(solution)/shard_map/attention_forward/pallas_call | solution.py:215
  67.7 5.9 %route.1 = (f32[512,768]{1,0:T(8,128)}, bf16[512,768]{1,0:T(8,128)(2,1)}, f32[512,2]{1,0:T(8,128)}, bf16[160,768]{1,0:T(8,128)(2,1)}, bf16[160,768]{1,0:T(8,128)...) custom-call(s32[1]{0:T(128)} %bitcast.2.core.refs_0_, ...), custom_call_target="tpu_custom_call" | custom-call | flops 2220000000 | tf_op jit(solution)/shard_map/route/pallas_call | solution.py:448
  79.9 3.8 collective-permute-done.18.refs_4_
  85.0 4.0 collective-permute-done.20.refs_2_
  91.3 13.7 %expert_forward.2 = (bf16[3072,640]{1,0:T(8,128)(2,1)}, bf16[640,3072]{1,0:T(8,128)(2,1)}, bf16[768,640]{1,0:T(8,128)(2,1)}, bf16[160,768]{1,0:T(8,128)(2,1)}, b...) custom-call(s32[1]{0:T(128)} %bitcast.4.refs_0_, ...), custom_call_target="tpu_custom_call" | custom-call | flops 4809999872 | tf_op jit(solution)/shard_map/expert_forward/pallas_call | solution.py:79
  105.9 4.2 %collective-permute-start.27 = (bf16[160,768]{1,0:T(8,128)(2,1)S(1)}, bf16[160,768]{1,0:T(8,128)(2,1)S(1)}, u32[]{:S(2)}, u32[]{:S(2)}) collective-permute-start(bf16[160,768]{1,0:T(8,128)(2,1)S(1)} %copy-done.69), channel_id=1, source_target_pairs={{0,2},{1,3},{2,0},{3,1},{4,6},{5,7},{6,4},{7,5},{8,10},{9,11},{10,... | collective-permute-start | bytes 737288 | tf_op jit(solution)/shard_map/ppermute | solution.py:758
  112.7 13.8 %expert_forward.3 = (bf16[3072,640]{1,0:T(8,128)(2,1)}, bf16[640,3072]{1,0:T(8,128)(2,1)}, bf16[768,640]{1,0:T(8,128)(2,1)}, bf16[160,768]{1,0:T(8,128)(2,1)}, b...) custom-call(s32[1]{0:T(128)} %bitcast.4.refs_0_, bf16[640,768]{1,0:T(8,128)(2,1)} %copy-done.12, ...), custom_call_target="tpu_custom_call" | custom-call | flops 4809999872 | tf_op jit(solution)/shard_map/expert_forward/pallas_call | solution.py:79
  135.5 5.6 %collective-permute-done.26 = f32[8,128]{1,0:T(8,128)S(1)} collective-permute-done((f32[8,128]{1,0:T(8,128)S(1)}, f32[8,128]{1,0:T(8,128)S(1)}, u32[]{:S(2)}, u32[]{:S(2)}) %collective-permute-start.26) | collective-permute-done | bytes 4128 | tf_op jit(solution)/shard_map/ppermute | solution.py:758
  144.1 8.5 %combine.1 = (bf16[512,768]{1,0:T(8,128)(2,1)}, f32[512,768]{1,0:T(8,128)}, bf16[512,8]{1,0:T(8,128)(2,1)}, f32[8,768]{1,0:T(8,128)}, bf16[160,768]{1,0:T(8,128)...) custom-call(s32[512,2]{1,0:T(8,128)} %multiply_add_fusion.refs_0_.re, ...), custom_call_target="tpu_custom_call" | custom-call | flops 2960000000 | tf_op jit(solution)/shard_map/combine/pallas_call | solution.py:504
  154.0 3.3 collective-permute-start.38
  164.4 6.2 %collective-permute-done.39.refs_4_ = bf16[160,768]{1,0:T(8,128)(2,1)S(1)} collective-permute-done((bf16[160,768]{1,0:T(8,128)(2,1)}, bf16[160,768]{1,0:T(8,128)(2,1)S(1)}, u32[]{:S(2)}, u32[]{:S(2)}) %collective-permute-start.39) | collective-permute-done | bytes 245792 | tf_op jit(solution)/shard_map/ppermute | solution.py:758
  171.2 12.5 %expert_backward.2 = (bf16[640,3072]{1,0:T(8,128)(2,1)}, bf16[640,768]{1,0:T(8,128)(2,1)}, bf16[160,768]{1,0:T(8,128)(2,1)}, bf16[160,768]{1,0:T(8,128)(2,1)}, b...) custom-call(s32[1]{0:T(128)} %bitcast.4.refs_0_, bf16[160,768]{1,0:T(8,128)(2,1)} %get-tuple-element.215.refs_1_, ...), custom_call_target="tpu_custom_call" | custom-call | flops 4070000128 | tf_op jit(solution)/shard_map/expert_backward/pallas_call | solution.py:136
  187.4 7.8 %weight_part.4 = (bf16[2,2,128,768]{3,2,1,0:T(8,128)(2,1)}, bf16[2,2,128,768]{3,2,1,0:T(8,128)(2,1)}, bf16[2,2,128,768]{3,2,1,0:T(8,128)(2,1)}) custom-call(s32[4]{0:T(128)} %pad_add_fusion.1.refs_0_, bf16[3072,640]{1,0:T(8,128)(2,1)} %get-tuple-element.191.refs_1_.refs_2_.refs_3_.refs_4_, ...), custom_call_target="tpu_custom_call" | custom-call | flops 1480000000 | tf_op jit(solution)/shard_map/weight_part/pallas_call | solution.py:338
  199.3 12.7 %expert_backward.3 = (bf16[640,3072]{1,0:T(8,128)(2,1)}, bf16[640,768]{1,0:T(8,128)(2,1)}, bf16[160,768]{1,0:T(8,128)(2,1)}, bf16[160,768]{1,0:T(8,128)(2,1)}, b...) custom-call(s32[1]{0:T(128)} %bitcast.4.refs_0_, bf16[640,768]{1,0:T(8,128)(2,1)} %copy-done.1, ...), custom_call_target="tpu_custom_call" | custom-call | flops 4070000128 | tf_op jit(solution)/shard_map/expert_backward/pallas_call | solution.py:136
  220.1 7.8 %weight_part.5 = (bf16[2,2,128,768]{3,2,1,0:T(8,128)(2,1)}, bf16[2,2,128,768]{3,2,1,0:T(8,128)(2,1)}, bf16[2,2,128,768]{3,2,1,0:T(8,128)(2,1)}) custom-call(s32[4]{0:T(128)} %pad_add_fusion.2.refs_0_, bf16[3072,640]{1,0:T(8,128)(2,1)} %get-tuple-element.191.refs_1_.refs_2_.refs_3_.refs_4_, ...), custom_call_target="tpu_custom_call" | custom-call | flops 1480000000 | tf_op jit(solution)/shard_map/weight_part/pallas_call | solution.py:338
  229.3 7.7 %weight_part.6 = (bf16[2,2,32,3072]{3,2,1,0:T(8,128)(2,1)}, bf16[2,2,32,3072]{3,2,1,0:T(8,128)(2,1)}, bf16[2,2,32,3072]{3,2,1,0:T(8,128)(2,1)}) custom-call(s32[4]{0:T(128)} %pad_add_fusion.1.refs_0_, bf16[768,640]{1,0:T(8,128)(2,1)} %get-tuple-element.221.refs_1_.refs_2_.refs_3_.refs_4_, ...), custom_call_target="tpu_custom_call" | custom-call | flops 1480000000 | tf_op jit(solution)/shard_map/weight_part/pallas_call | solution.py:338
  239.0 8.6 %collect.1 = (f32[512,768]{1,0:T(8,128)}, bf16[512,768]{1,0:T(8,128)(2,1)}, bf16[512,768]{1,0:T(8,128)(2,1)}, f32[8,768]{1,0:T(8,128)}) custom-call(s32[1]{0:T(128)} %bitcast.2.core.refs_0_, s32[512,2]{1,0:T(8,128)} %multiply_add_fusion.refs_0_.refs_1_, bf16[160,768]{1,0:T(8,128)(2,1)} %get-tuple-element.263.refs_2_, bf16[160,768]{1,0:T(8,128)(2,1)} %copy-done.56, ...), custom_call_target="tpu_custom_call" | custom-call | flops 2960000000 | tf_op jit(solution)/shard_map/collect/pallas_call | solution.py:555
  250.1 11.6 %attention_backward.1 = (bf16[3,512,768]{2,1,0:T(8,128)(2,1)}, f32[12,4,128,128]{3,2,1,0:T(8,128)}) custom-call(bf16[3,512,768]{2,1,0:T(8,128)(2,1)} %project.1.refs_2_.refs_3_.refs_4_.refs_0_.refs_1_, bf16[3,512,768]{2,1,0:T(8,128)(2,1)} %project.1.refs_2_.refs_3_.refs_4_.refs_0_.refs_1_, ...), custom_call_target="tpu_custom_call" | custom-call | flops 1480000000 | tf_op jit(solution)/shard_map/attention_backward/pallas_call | solution.py:281
  262.7 8.4 %outer_halves.1 = (bf16[2,768,384]{2,1,0:T(8,128)(2,1)}, bf16[2,768,384]{2,1,0:T(8,128)(2,1)}, bf16[2,768,384]{2,1,0:T(8,128)(2,1)}, bf16[2,768,384]{2,1,0:T(8,128)(2,1)}) custom-call(s32[1]{0:T(128)} %bitcast.2.core.refs_0_, bf16[512,768]{1,0:T(8,128)(2,1)} %fusion.6.rows.refs_1_, bf16[512,768]{1,0:T(8,128)(2,1)} %get-tuple-element.183.attended.refs_2_, ...), custom_call_target="tpu_custom_call" | custom-call | flops 740000000 | tf_op jit(solution)/shard_map/outer_halves/pallas_call | solution.py:605
  283.5 7.5 %weight_part.7 = (bf16[2,2,32,3072]{3,2,1,0:T(8,128)(2,1)}, bf16[2,2,32,3072]{3,2,1,0:T(8,128)(2,1)}, bf16[2,2,32,3072]{3,2,1,0:T(8,128)(2,1)}) custom-call(s32[4]{0:T(128)} %pad_add_fusion.2.refs_0_, bf16[768,640]{1,0:T(8,128)(2,1)} %get-tuple-element.221.refs_1_.refs_2_.refs_3_.refs_4_, ...), custom_call_target="tpu_custom_call" | custom-call | flops 14800000000 | tf_op jit(solution)/shard_map/weight_part/pallas_call | solution.py:338
  293.2 6.2 %collective-permute-done.62 = bf16[2,2,32,3072]{3,2,1,0:T(8,128)(2,1)S(1)} collective-permute-done((bf16[2,2,32,3072]{3,2,1,0:T(8,128)(2,1)}, bf16[2,2,32,3072]{3,2,1,0:T(8,128)(2,1)S(1)}, u32[]{:S(2)}, u32[]{:S(2)}) %collective-permute-start.62) | collective-permute-done | bytes 786464 | tf_op jit(solution)/shard_map/ppermute | solution.py:758
  299.5 14.7 %collective-permute-done.65 = bf16[1,4,128,768]{3,2,1,0:T(8,128)(2,1)} collective-permute-done((bf16[1,4,128,768]{3,2,1,0:T(8,128)(2,1)}, bf16[1,4,128,768]{3,2,1,0:T(8,128)(2,1)}, u32[]{:S(2)}, u32[]{:S(2)}) %collective-permute-start.65) | collective-permute-done | bytes 786464 | tf_op jit(solution)/shard_map/ppermute | solution.py:758
  319.8 8.7 %enter.1 = (f32[512,768]{1,0:T(8,128)}, f32[16,768]{1,0:T(8,128)}) custom-call(s32[1]{0:T(128)} %bitcast.2.core.refs_0_, bf16[3,512,768]{2,1,0:T(8,128)(2,1)} %get-tuple-element.311.refs_3_.grads, bf16[4,768,384]{2,1,0:T(8,128)(2,1)} %join.1.mine.refs_15_, bf16[4,768,384]{2,1,0:T(8,128)(2,1)} %copy-done, bf16[512,768]{1,0:T(8,128)(2,1)} %tokens.3, ...), custom_call_target="tpu_custom_call" | custom-call | flops 2220000000 | tf_op jit(solution)/shard_map/enter/pallas_call | solution.py:659
  328.6 5.3 %fusion.11 = f32[12,32]{1,0:T(8,128)S(1)} fusion(s32[4,128,128]{2,1,0:T(8,128)S(1)} %pad_add_fusion, f32[12,4,128,128]{3,2,1,0:T(8,128)S(1)} %copy-done.3), kind=kOutput, calls=%fused_computation.34 | convolution fusion | flops 304087040 | bytes 3409408 | tf_op jit(solution)/shard_map/hdxy,dxyb->hb/dot_general | solution.py:714
  336.6 4.1 %collective-permute-start.64 = (bf16[4,2,48,384]{3,2,1,0:T(8,128)(2,1)S(1)}, bf16[4,2,48,384]{3,2,1,0:T(8,128)(2,1)S(1)}, u32[]{:S(2)}, u32[]{:S(2)}) collective-permute-start(bf16[4,2,48,384]{3,2,1,0:T(8,128)(2,1)S(1)} %dynamic-slice_bitcast_fusion.5), channel_id=1, source_target_pairs={{0,8},{1,9},{2,10},{3,11},{4,12},{5,13},{6,14},{7,15},{8,0},{9,1},... | collective-permute-start | bytes 884744 | tf_op jit(solution)/shard_map/ppermute | solution.py:758
  342.9 3.3 collective-permute-done.74
  355.1 11.6 %collective-permute-done.70 = bf16[1,2,32,3072]{3,2,1,0:T(8,128)(2,1)S(1)} collective-permute-done((bf16[1,2,32,3072]{3,2,1,0:T(8,128)(2,1)S(1)}, bf16[1,2,32,3072]{3,2,1,0:T(8,128)(2,1)S(1)}, u32[]{:S(2)}, u32[]{:S(2)}) %collective-permute-start.70) | collective-permute-done | bytes 393248 | tf_op jit(solution)/shard_map/ppermute | solution.py:758
  369.8 11.7 %collective-permute-done.75 = f32[16,768]{1,0:T(8,128)S(1)} collective-permute-done((f32[16,768]{1,0:T(8,128)S(1)}, f32[16,768]{1,0:T(8,128)S(1)}, u32[]{:S(2)}, u32[]{:S(2)}) %collective-permute-start.75) | collective-permute-done | bytes 49184 | tf_op jit(solution)/shard_map/ppermute | solution.py:758
  385.7 4.2 %collective-permute-done.79 = bf16[1,2,32,3072]{3,2,1,0:T(8,128)(2,1)S(1)} collective-permute-done((bf16[1,2,32,3072]{3,2,1,0:T(8,128)(2,1)S(1)}, bf16[1,2,32,3072]{3,2,1,0:T(8,128)(2,1)S(1)}, u32[]{:S(2)}, u32[]{:S(2)}) %collective-permute-start.79) | collective-permute-done | bytes 393248 | tf_op jit(solution)/shard_map/ppermute | solution.py:758
  390.0 8.8 %collective-permute-done.80 = bf16[1,32,3072]{2,1,0:T(8,128)(2,1)S(1)} collective-permute-done((bf16[1,32,3072]{2,1,0:T(8,128)(2,1)S(1)}, bf16[1,32,3072]{2,1,0:T(8,128)(2,1)S(1)}, u32[]{:S(2)}, u32[]{:S(2)}) %collective-permute-start.80) | collective-permute-done | bytes 196640 | tf_op jit(solution)/shard_map/ppermute | solution.py:758
  (398 shorter events, 150.4 us)
Async XLA Ops:
  77.1 27.9 %collective-permute-start.24 = (bf16[160,768]{1,0:T(8,128)(2,1)}, bf16[160,768]{1,0:T(8,128)(2,1)S(1)}, u32[]{:S(2)}, u32[]{:S(2)}) collective-permute-start(bf16[160,768]{1,0:T(8,128)(2,1)} %get-tuple-element.197), channel_id=1, source_target_pairs={{0,10},{1,11},{2,8},{3,9},{4,14},{5,15},{6,12},{7,13},{8,2},{9,3},... | collective-permute-start | bytes 737288 | tf_op jit(solution)/shard_map/ppermute | solution.py:758
  79.5 25.6 %collective-permute-start.23 = (bf16[160,768]{1,0:T(8,128)(2,1)}, bf16[160,768]{1,0:T(8,128)(2,1)S(1)}, u32[]{:S(2)}, u32[]{:S(2)}) collective-permute-start(bf16[160,768]{1,0:T(8,128)(2,1)} %get-tuple-element.195), channel_id=1, source_target_pairs={{0,8},{1,9},{2,10},{3,11},{4,12},{5,13},{6,14},{7,15},{8,0},{9,1},... | collective-permute-start | bytes 737288 | tf_op jit(solution)/shard_map/ppermute | solution.py:758
  83.7 21.4 %collective-permute-start.22 = (bf16[160,768]{1,0:T(8,128)(2,1)}, bf16[160,768]{1,0:T(8,128)(2,1)S(1)}, u32[]{:S(2)}, u32[]{:S(2)}) collective-permute-start(bf16[160,768]{1,0:T(8,128)(2,1)} %get-tuple-element.193), channel_id=1, source_target_pairs={{0,2},{1,3},{2,0},{3,1},{4,6},{5,7},{6,4},{7,5},{8,10},{9,11},{10,... | collective-permute-start | bytes 737288 | tf_op jit(solution)/shard_map/ppermute | solution.py:758
  89.0 16.0 %collective-permute-start.19 = (f32[8,128]{1,0:T(8,128)S(1)}, f32[8,128]{1,0:T(8,128)S(1)}, u32[]{:S(2)}, u32[]{:S(2)}) collective-permute-start(f32[8,128]{1,0:T(8,128)S(1)} %add.546), channel_id=1, source_target_pairs={{0,8},{1,9},{2,10},{3,11},{4,12},{5,13},{6,14},{7,15},{8,0},{9,1},... | collective-permute-start | bytes 12296 | tf_op jit(solution)/shard_map/ppermute | solution.py:758
  105.9 20.6 %collective-permute-start.27 = (bf16[160,768]{1,0:T(8,128)(2,1)S(1)}, bf16[160,768]{1,0:T(8,128)(2,1)S(1)}, u32[]{:S(2)}, u32[]{:S(2)}) collective-permute-start(bf16[160,768]{1,0:T(8,128)(2,1)S(1)} %copy-done.69), channel_id=1, source_target_pairs={{0,2},{1,3},{2,0},{3,1},{4,6},{5,7},{6,4},{7,5},{8,10},{9,11},{10,... | collective-permute-start | bytes 737288 | tf_op jit(solution)/shard_map/ppermute | solution.py:758
  110.1 16.4 %collective-permute-start.28 = (bf16[160,768]{1,0:T(8,128)(2,1)S(1)}, bf16[160,768]{1,0:T(8,128)(2,1)S(1)}, u32[]{:S(2)}, u32[]{:S(2)}) collective-permute-start(bf16[160,768]{1,0:T(8,128)(2,1)S(1)} %copy-done.67), channel_id=1, source_target_pairs={{0,8},{1,9},{2,10},{3,11},{4,12},{5,13},{6,14},{7,15},{8,0},{9,1},... | collective-permute-start | bytes 737288 | tf_op jit(solution)/shard_map/ppermute | solution.py:758
  110.2 16.3 %collective-permute-start.29 = (bf16[160,768]{1,0:T(8,128)(2,1)S(1)}, bf16[160,768]{1,0:T(8,128)(2,1)S(1)}, u32[]{:S(2)}, u32[]{:S(2)}) collective-permute-start(bf16[160,768]{1,0:T(8,128)(2,1)S(1)} %copy-done.65), channel_id=1, source_target_pairs={{0,10},{1,11},{2,8},{3,9},{4,14},{5,15},{6,12},{7,13},{8,2},{9,3},... | collective-permute-start | bytes 737288 | tf_op jit(solution)/shard_map/ppermute | solution.py:758
  158.1 25.6 %collective-permute-start.42 = (bf16[160,768]{1,0:T(8,128)(2,1)}, bf16[160,768]{1,0:T(8,128)(2,1)S(1)}, u32[]{:S(2)}, u32[]{:S(2)}) collective-permute-start(bf16[160,768]{1,0:T(8,128)(2,1)} %get-tuple-element.231), channel_id=1, source_target_pairs={{0,10},{1,11},{2,8},{3,9},{4,14},{5,15},{6,12},{7,13},{8,2},{9,3},... | collective-permute-start | bytes 737288 | tf_op jit(solution)/shard_map/ppermute | solution.py:758
  160.2 23.5 %collective-permute-start.41 = (bf16[160,768]{1,0:T(8,128)(2,1)}, bf16[160,768]{1,0:T(8,128)(2,1)S(1)}, u32[]{:S(2)}, u32[]{:S(2)}) collective-permute-start(bf16[160,768]{1,0:T(8,128)(2,1)} %get-tuple-element.229), channel_id=1, source_target_pairs={{0,8},{1,9},{2,10},{3,11},{4,12},{5,13},{6,14},{7,15},{8,0},{9,1},... | collective-permute-start | bytes 737288 | tf_op jit(solution)/shard_map/ppermute | solution.py:758
  160.2 23.5 %collective-permute-start.40 = (bf16[160,768]{1,0:T(8,128)(2,1)}, bf16[160,768]{1,0:T(8,128)(2,1)S(1)}, u32[]{:S(2)}, u32[]{:S(2)}) collective-permute-start(bf16[160,768]{1,0:T(8,128)(2,1)} %get-tuple-element.227), channel_id=1, source_target_pairs={{0,2},{1,3},{2,0},{3,1},{4,6},{5,7},{6,4},{7,5},{8,10},{9,11},{10,... | collective-permute-start | bytes 737288 | tf_op jit(solution)/shard_map/ppermute | solution.py:758
  195.2 19.8 %collective-permute-start.48 = (bf16[2,2,128,768]{3,2,1,0:T(8,128)(2,1)}, bf16[2,2,128,768]{3,2,1,0:T(8,128)(2,1)S(1)}, u32[]{:S(2)}, u32[]{:S(2)}) collective-permute-start(bf16[2,2,128,768]{3,2,1,0:T(8,128)(2,1)} %get-tuple-element.244), channel_id=1, source_target_pairs={{0,4},{1,5},{2,6},{3,7},{4,0},{5,1},{6,2},{7,3},{8,12},{9,13},{10,... | collective-permute-start | bytes 2359304 | tf_op jit(solution)/shard_map/ppermute | solution.py:758
  195.8 16.3 %collective-permute-start.44 = (bf16[160,768]{1,0:T(8,128)(2,1)S(1)}, bf16[160,768]{1,0:T(8,128)(2,1)S(1)}, u32[]{:S(2)}, u32[]{:S(2)}) collective-permute-start(bf16[160,768]{1,0:T(8,128)(2,1)S(1)} %copy-done.62), channel_id=1, source_target_pairs={{0,2},{1,3},{2,0},{3,1},{4,6},{5,7},{6,4},{7,5},{8,10},{9,11},{10,... | collective-permute-start | bytes 737288 | tf_op jit(solution)/shard_map/ppermute | solution.py:758
  215.1 22.4 %collective-permute-start.52 = (bf16[160,768]{1,0:T(8,128)(2,1)}, bf16[160,768]{1,0:T(8,128)(2,1)S(1)}, u32[]{:S(2)}, u32[]{:S(2)}) collective-permute-start(bf16[160,768]{1,0:T(8,128)(2,1)} %collective-permute-done.49), channel_id=1, source_target_pairs={{0,2},{1,3},{2,0},{3,1},{4,6},{5,7},{6,4},{7,5},{8,10},{9,11},{10,... | collective-permute-start | bytes 737288 | tf_op jit(solution)/shard_map/ppermute | solution.py:758
  215.8 22.4 %collective-permute-start.53 = (bf16[160,768]{1,0:T(8,128)(2,1)}, bf16[160,768]{1,0:T(8,128)(2,1)S(1)}, u32[]{:S(2)}, u32[]{:S(2)}) collective-permute-start(bf16[160,768]{1,0:T(8,128)(2,1)} %collective-permute-done.50), channel_id=1, source_target_pairs={{0,8},{1,9},{2,10},{3,11},{4,12},{5,13},{6,14},{7,15},{8,0},{9,1},... | collective-permute-start | bytes 737288 | tf_op jit(solution)/shard_map/ppermute | solution.py:758
  217.8 20.4 %collective-permute-start.54 = (bf16[160,768]{1,0:T(8,128)(2,1)}, bf16[160,768]{1,0:T(8,128)(2,1)S(1)}, u32[]{:S(2)}, u32[]{:S(2)}) collective-permute-start(bf16[160,768]{1,0:T(8,128)(2,1)} %collective-permute-done.51), channel_id=1, source_target_pairs={{0,10},{1,11},{2,8},{3,9},{4,14},{5,15},{6,12},{7,13},{8,2},{9,3},... | collective-permute-start | bytes 737288 | tf_op jit(solution)/shard_map/ppermute | solution.py:758
  218.6 30.5 %collective-permute-start.55 = (bf16[2,2,128,768]{3,2,1,0:T(8,128)(2,1)}, bf16[2,2,128,768]{3,2,1,0:T(8,128)(2,1)S(1)}, u32[]{:S(2)}, u32[]{:S(2)}) collective-permute-start(bf16[2,2,128,768]{3,2,1,0:T(8,128)(2,1)} %get-tuple-element.274), channel_id=1, source_target_pairs={{0,4},{1,5},{2,6},{3,7},{4,0},{5,1},{6,2},{7,3},{8,12},{9,13},{10,... | collective-permute-start | bytes 2359304 | tf_op jit(solution)/shard_map/ppermute | solution.py:758
  236.9 24.7 %collective-permute-start.57 = (bf16[1,2,128,768]{3,2,1,0:T(8,128)(2,1)S(1)}, bf16[1,2,128,768]{3,2,1,0:T(8,128)(2,1)S(1)}, u32[]{:S(2)}, u32[]{:S(2)}) collective-permute-start(bf16[1,2,128,768]{3,2,1,0:T(8,128)(2,1)S(1)} %constant_dynamic-slice_fusion.7), channel_id=1, source_target_pairs={{0,16},{1,17},{2,18},{3,19},{4,20},{5,21},{6,22},{7,23},{8,24},{9,... | collective-permute-start | bytes 1179656 | tf_op jit(solution)/shard_map/ppermute | solution.py:758
  237.5 24.2 %collective-permute-start.56 = (bf16[2,2,128,768]{3,2,1,0:T(8,128)(2,1)S(1)}, bf16[2,2,128,768]{3,2,1,0:T(8,128)(2,1)S(1)}, u32[]{:S(2)}, u32[]{:S(2)}) collective-permute-start(bf16[2,2,128,768]{3,2,1,0:T(8,128)(2,1)S(1)} %copy-done.51), channel_id=1, source_target_pairs={{0,4},{1,5},{2,6},{3,7},{4,0},{5,1},{6,2},{7,3},{8,12},{9,13},{10,... | collective-permute-start | bytes 2359304 | tf_op jit(solution)/shard_map/ppermute | solution.py:758
  247.6 25.0 %collective-permute-start.58 = (bf16[2,2,32,3072]{3,2,1,0:T(8,128)(2,1)S(1)}, bf16[2,2,32,3072]{3,2,1,0:T(8,128)(2,1)S(1)}, u32[]{:S(2)}, u32[]{:S(2)}) collective-permute-start(bf16[2,2,32,3072]{3,2,1,0:T(8,128)(2,1)S(1)} %copy-done.52), channel_id=1, source_target_pairs={{0,4},{1,5},{2,6},{3,7},{4,0},{5,1},{6,2},{7,3},{8,12},{9,13},{10,... | collective-permute-start | bytes 2359304 | tf_op jit(solution)/shard_map/ppermute | solution.py:758
  276.7 37.5 %collective-permute-start.65 = (bf16[1,4,128,768]{3,2,1,0:T(8,128)(2,1)}, bf16[1,4,128,768]{3,2,1,0:T(8,128)(2,1)}, u32[]{:S(2)}, u32[]{:S(2)}) collective-permute-start(bf16[1,4,128,768]{3,2,1,0:T(8,128)(2,1)} %pad_maximum_fusion.5), channel_id=1, source_target_pairs={{0,16},{1,17},{2,18},{3,19},{4,20},{5,21},{6,22},{7,23},{8,24},{9,... | collective-permute-start | bytes 2359304 | tf_op jit(solution)/shard_map/ppermute | solution.py:758
  280.1 19.4 %collective-permute-start.62 = (bf16[2,2,32,3072]{3,2,1,0:T(8,128)(2,1)}, bf16[2,2,32,3072]{3,2,1,0:T(8,128)(2,1)S(1)}, u32[]{:S(2)}, u32[]{:S(2)}) collective-permute-start(bf16[2,2,32,3072]{3,2,1,0:T(8,128)(2,1)} %get-tuple-element.296), channel_id=1, source_target_pairs={{0,4},{1,5},{2,6},{3,7},{4,0},{5,1},{6,2},{7,3},{8,12},{9,13},{10,... | collective-permute-start | bytes 2359304 | tf_op jit(solution)/shard_map/ppermute | solution.py:758
  282.8 32.4 %collective-permute-start.61 = (bf16[4,8,48,384]{3,2,1,0:T(8,128)(2,1)S(1)}, bf16[4,8,48,384]{3,2,1,0:T(8,128)(2,1)S(1)}, u32[]{:S(2)}, u32[]{:S(2)}) collective-permute-start(bf16[4,8,48,384]{3,2,1,0:T(8,128)(2,1)S(1)} %pad_maximum_fusion.2), channel_id=1, source_target_pairs={{0,2},{1,3},{2,0},{3,1},{4,6},{5,7},{6,4},{7,5},{8,10},{9,11},{10,... | collective-permute-start | bytes 3538952 | tf_op jit(solution)/shard_map/ppermute | solution.py:758
  314.2 32.0 %collective-permute-start.66 = (bf16[1,2,32,3072]{3,2,1,0:T(8,128)(2,1)}, bf16[1,2,32,3072]{3,2,1,0:T(8,128)(2,1)}, u32[]{:S(2)}, u32[]{:S(2)}) collective-permute-start(bf16[1,2,32,3072]{3,2,1,0:T(8,128)(2,1)} %constant_dynamic-slice_fusion.4), channel_id=1, source_target_pairs={{0,16},{1,17},{2,18},{3,19},{4,20},{5,21},{6,22},{7,23},{8,24},{9,... | collective-permute-start | bytes 1179656 | tf_op jit(solution)/shard_map/ppermute | solution.py:758
  316.4 18.9 %collective-permute-start.63 = (bf16[4,2,2,48,384]{4,3,2,1,0:T(8,128)(2,1)}, bf16[4,2,2,48,384]{4,3,2,1,0:T(8,128)(2,1)}, u32[]{:S(2)}, u32[]{:S(2)}) collective-permute-start(bf16[4,2,2,48,384]{4,3,2,1,0:T(8,128)(2,1)} %dynamic-slice_bitcast_fusion), channel_id=1, source_target_pairs={{0,4},{1,5},{2,6},{3,7},{4,0},{5,1},{6,2},{7,3},{8,12},{9,13},{10,... | collective-permute-start | bytes 1769480 | tf_op jit(solution)/shard_map/ppermute | solution.py:758
  318.3 31.3 %collective-permute-start.68 = (bf16[2,2,32,3072]{3,2,1,0:T(8,128)(2,1)}, bf16[2,2,32,3072]{3,2,1,0:T(8,128)(2,1)}, u32[]{:S(2)}, u32[]{:S(2)}) collective-permute-start(bf16[2,2,32,3072]{3,2,1,0:T(8,128)(2,1)} %get-tuple-element.307), channel_id=1, source_target_pairs={{0,4},{1,5},{2,6},{3,7},{4,0},{5,1},{6,2},{7,3},{8,12},{9,13},{10,... | collective-permute-start | bytes 2359304 | tf_op jit(solution)/shard_map/ppermute | solution.py:758
  342.8 23.9 %collective-permute-start.70 = (bf16[1,2,32,3072]{3,2,1,0:T(8,128)(2,1)S(1)}, bf16[1,2,32,3072]{3,2,1,0:T(8,128)(2,1)S(1)}, u32[]{:S(2)}, u32[]{:S(2)}) collective-permute-start(bf16[1,2,32,3072]{3,2,1,0:T(8,128)(2,1)S(1)} %copy-done.21), channel_id=1, source_target_pairs={{0,16},{1,17},{2,18},{3,19},{4,20},{5,21},{6,22},{7,23},{8,24},{9,... | collective-permute-start | bytes 1179656 | tf_op jit(solution)/shard_map/ppermute | solution.py:758
  348.4 36.0 %collective-permute-start.67 = (bf16[4,48,384]{2,1,0:T(8,128)(2,1)S(1)}, bf16[4,48,384]{2,1,0:T(8,128)(2,1)S(1)}, u32[]{:S(2)}, u32[]{:S(2)}) collective-permute-start(bf16[4,48,384]{2,1,0:T(8,128)(2,1)S(1)} %get-tuple-element.356), channel_id=1, source_target_pairs={{0,16},{1,17},{2,18},{3,19},{4,20},{5,21},{6,22},{7,23},{8,24},{9,... | collective-permute-start | bytes 442376 | tf_op jit(solution)/shard_map/ppermute | solution.py:758
  350.6 33.7 %collective-permute-start.69 = (bf16[2,32,3072]{2,1,0:T(8,128)(2,1)S(1)}, bf16[2,32,3072]{2,1,0:T(8,128)(2,1)S(1)}, u32[]{:S(2)}, u32[]{:S(2)}) collective-permute-start(bf16[2,32,3072]{2,1,0:T(8,128)(2,1)S(1)} %fusion.15), channel_id=1, source_target_pairs={{0,8},{1,9},{2,10},{3,11},{4,12},{5,13},{6,14},{7,15},{8,0},{9,1},... | collective-permute-start | bytes 1179656 | tf_op jit(solution)/shard_map/ppermute | solution.py:758
  366.7 34.0 %collective-permute-start.72 = (bf16[3,128,768]{2,1,0:T(8,128)(2,1)S(1)}, bf16[3,128,768]{2,1,0:T(8,128)(2,1)S(1)}, u32[]{:S(2)}, u32[]{:S(2)}) collective-permute-start(bf16[3,128,768]{2,1,0:T(8,128)(2,1)S(1)} %pad_maximum_fusion.6), channel_id=1, source_target_pairs={{0,8},{1,9},{2,10},{3,11},{4,12},{5,13},{6,14},{7,15},{8,0},{9,1},... | collective-permute-start | bytes 1769480 | tf_op jit(solution)/shard_map/ppermute | solution.py:758
  369.2 20.8 %collective-permute-start.79 = (bf16[1,2,32,3072]{3,2,1,0:T(8,128)(2,1)S(1)}, bf16[1,2,32,3072]{3,2,1,0:T(8,128)(2,1)S(1)}, u32[]{:S(2)}, u32[]{:S(2)}) collective-permute-start(bf16[1,2,32,3072]{3,2,1,0:T(8,128)(2,1)S(1)} %constant_dynamic-slice_fusion.2), channel_id=1, source_target_pairs={{0,16},{1,17},{2,18},{3,19},{4,20},{5,21},{6,22},{7,23},{8,24},{9,... | collective-permute-start | bytes 1179656 | tf_op jit(solution)/shard_map/ppermute | solution.py:758
  381.5 17.3 %collective-permute-start.80 = (bf16[1,32,3072]{2,1,0:T(8,128)(2,1)S(1)}, bf16[1,32,3072]{2,1,0:T(8,128)(2,1)S(1)}, u32[]{:S(2)}, u32[]{:S(2)}) collective-permute-start(bf16[1,32,3072]{2,1,0:T(8,128)(2,1)S(1)} %get-tuple-element.353), channel_id=1, source_target_pairs={{0,8},{1,9},{2,10},{3,11},{4,12},{5,13},{6,14},{7,15},{8,0},{9,1},... | collective-permute-start | bytes 589832 | tf_op jit(solution)/shard_map/ppermute | solution.py:758
  384.4 16.3 %collective-permute-start.71 = (bf16[4,48,384]{2,1,0:T(8,128)(2,1)S(1)}, bf16[4,48,384]{2,1,0:T(8,128)(2,1)S(1)}, u32[]{:S(2)}, u32[]{:S(2)}) collective-permute-start(bf16[4,48,384]{2,1,0:T(8,128)(2,1)S(1)} %add_convert_fusion.14), channel_id=1, source_target_pairs={{0,2},{1,3},{2,0},{3,1},{4,6},{5,7},{6,4},{7,5},{8,10},{9,11},{10,... | collective-permute-start | bytes 442376 | tf_op jit(solution)/shard_map/ppermute | solution.py:758
  (124 other events, 1007.4 us)

commit v10 on v9

--- a/solution.py
+++ b/solution.py
@@ -1013,16 +1013,15 @@
         for _ in range((0, 2, 1)[min(len(passed_masks), 3) - 1]):
             flat = flat + swap(after(flat, gone), *small_trades.pop(0))
         if len(passed_masks) == 1:
-            far_e = far_trade(after(away_e, small))
+            far_e = far_trade(after(away_e, gone))
             got_f = swap(after(send_f, gone), 1, 0)
         elif mask == PAIR:
-            got = after(got, far_d)
+            got = after(got, far_d, far_e)
+            done_e = finish(far_e, stay_e)
         elif len(passed_masks) == len(dp_masks):
             away_f, stay_f = near_add(after(got_f, stay), keep_f)
-            far_f = far_trade(away_f)
-            far_e = after(far_e, gone)
-            done_e = finish(far_e, stay_e)
-            got = after(got, away_f, in_first, far_e)
+            far_f = far_trade(after(away_f, got))
+            got = after(got, away_f, in_first)
             done_f = finish(far_f, stay_f)
         total = add(got, stay)
         if mask == PAIR:
@@ -1034,12 +1033,10 @@
     for mask in reversed(group_masks):
         bit = (here_group // mask) % 2
         other_part = swap(total, 0, mask)
-        if mask == group_masks[-1]:
-            other_part = after(other_part, out_theirs, in_first)
         total = jnp.concatenate([jnp.where(bit == 0, total, other_part), jnp.where(bit == 0, other_part, total)], axis=1)
         flat = flat + swap(flat, *small_trades.pop(0))
         total, flat = lax.optimization_barrier((total, flat))
-    other_part = swap(total, 0, 1)
+    other_part = after(swap(total, 0, 1), out_theirs)
     for trade in small_trades:
         flat = flat + swap(flat, *trade)
     total = jnp.concatenate([jnp.where(core == 0, total, other_part), jnp.where(core == 0, other_part, total)], axis=2)

time: 415 us -> 419 us (level)
  transfers between devices with their start and end apart: 81 -> 81, of which waited for: 29 -> 30; matrix products, arithmetic and copies ran while one was open for 10% -> 11% of each run, Pallas kernels for 32% -> 32%
where the time goes in v10:
time: 419 us; the launch traced here: 414 us
  Pallas kernels  157 us (37%)
  waiting for transfers between devices  106 us (25%)
  starting transfers between devices  89.6 us (21%)
  local copies, waits for them, and re-layouts  25.3 us (6%)
  other arithmetic  24.5 us (6%)
  between operations  5.99 us (1%)
  matrix products  5.88 us (1%)
    ppermute x67, waiting for transfers between devices, swap(): return lax.ppermute(value, AXES, pairs)  96.9 us
    ppermute x67, starting transfers between devices, swap(): return lax.ppermute(value, AXES, pairs)  72.5 us
    pallas_call x4, Pallas kernels, weight_part(): pl.pallas_call(lambda *refs: weight_part_kernel(*refs, count=count, plans...  30.8 us
    pallas_call x2, Pallas kernels, expert_forward(): pl.pallas_call(lambda *refs: expert_forward_kernel(*refs, chunk=chunk, co...  27.5 us
    pallas_call x2, Pallas kernels, expert_backward(): pl.pallas_call(lambda *refs: expert_backward_kernel(*refs, chunk=chunk, c...  25.4 us
    ppermute x14, starting transfers between devices, gather_ring(): lax.ppermute(after(held, *due[step - 2:step - 1]) if step > 1 else held,...  17.1 us
    pallas_call x1, Pallas kernels, attention_forward(): pl.pallas_call(lambda *refs: attention_forward_kernel(*refs, heads=64, bl...  12.7 us
    pallas_call x1, Pallas kernels, attention_backward(): pl.pallas_call(lambda *refs: attention_backward_kernel(*refs, heads=64, b...  11.6 us
  transfers between devices with their start and end apart: 81, of which 30 were waited for; matrix products, arithmetic and copies ran while one was open for 11% of the time, Pallas kernels for 32%

profile of v10, /device:TPU:0, one launch (start us, length us, event | category | flops | bytes accessed | tf_op | source)
XLA Modules:
  0.0 414.1 jit_solution(4389386887258276373)
XLA Ops:
  34.3 3.3 join.1.mine.refs_15_
  46.4 6.4 %project.1.refs_2_.refs_3_.refs_4_.refs_0_.refs_1_ = bf16[3,512,768]{2,1,0:T(8,128)(2,1)} custom-call(s32[1]{0:T(128)} %bitcast.2.core.refs_0_, bf16[512,768]{1,0:T(8,128)(2,1)} %fusion.6.rows.refs_1_, bf16[4,768,384]{2,1,0:T(8,128)(2,1)} %join.1.mine.refs_15_, bf16[4,768,384]{2,1,0:T(8,128)(2,1)} %copy-done), custom_call_target="tpu_custom_call" | custom-call | flops 1480000000 | tf_op jit(solution)/shard_map/project/pallas_call | solution.py:397
  55.0 12.7 %attention_forward.1 = (bf16[512,768]{1,0:T(8,128)(2,1)}, bf16[12,512,512]{2,1,0:T(8,128)(2,1)}) custom-call(f32[12]{0:T(128)} %slice_reduce_fusion.refs_0_, s32[1]{0:T(128)S(6)} %copy.86.refs_1_, bf16[3,512,768]{2,1,0:T(8,128)(2,1)} %project.1.refs_2_.refs_3_.refs_4_.refs_0_.refs_1_, bf16[3,512,768]{2,1,0:T(8,128)(2,1)} %project.1.refs_2_.refs_3_.refs_4_.refs_0_.refs_1_, ...), custom_call_target="tpu_custom_call" | custom-call | flops 4809999872 | tf_op jit(solution)/shard_map/attention_forward/pallas_call | solution.py:215
  67.6 5.9 %route.1 = (f32[512,768]{1,0:T(8,128)}, bf16[512,768]{1,0:T(8,128)(2,1)}, f32[512,2]{1,0:T(8,128)}, bf16[160,768]{1,0:T(8,128)(2,1)}, bf16[160,768]{1,0:T(8,128)...) custom-call(s32[1]{0:T(128)} %bitcast.2.core.refs_0_, ...), custom_call_target="tpu_custom_call" | custom-call | flops 2220000000 | tf_op jit(solution)/shard_map/route/pallas_call | solution.py:448
  79.9 3.8 collective-permute-done.18.refs_4_
  84.9 4.0 collective-permute-done.20.refs_2_
  91.2 13.7 %expert_forward.2 = (bf16[3072,640]{1,0:T(8,128)(2,1)}, bf16[640,3072]{1,0:T(8,128)(2,1)}, bf16[768,640]{1,0:T(8,128)(2,1)}, bf16[160,768]{1,0:T(8,128)(2,1)}, b...) custom-call(s32[1]{0:T(128)} %bitcast.4.refs_0_, ...), custom_call_target="tpu_custom_call" | custom-call | flops 4809999872 | tf_op jit(solution)/shard_map/expert_forward/pallas_call | solution.py:79
  105.9 4.2 %collective-permute-start.27 = (bf16[160,768]{1,0:T(8,128)(2,1)S(1)}, bf16[160,768]{1,0:T(8,128)(2,1)S(1)}, u32[]{:S(2)}, u32[]{:S(2)}) collective-permute-start(bf16[160,768]{1,0:T(8,128)(2,1)S(1)} %copy-done.69), channel_id=1, source_target_pairs={{0,2},{1,3},{2,0},{3,1},{4,6},{5,7},{6,4},{7,5},{8,10},{9,11},{10,... | collective-permute-start | bytes 737288 | tf_op jit(solution)/shard_map/ppermute | solution.py:758
  112.6 13.8 %expert_forward.3 = (bf16[3072,640]{1,0:T(8,128)(2,1)}, bf16[640,3072]{1,0:T(8,128)(2,1)}, bf16[768,640]{1,0:T(8,128)(2,1)}, bf16[160,768]{1,0:T(8,128)(2,1)}, b...) custom-call(s32[1]{0:T(128)} %bitcast.4.refs_0_, bf16[640,768]{1,0:T(8,128)(2,1)} %copy-done.11, ...), custom_call_target="tpu_custom_call" | custom-call | flops 4809999872 | tf_op jit(solution)/shard_map/expert_forward/pallas_call | solution.py:79
  135.4 5.6 %collective-permute-done.26 = f32[8,128]{1,0:T(8,128)S(1)} collective-permute-done((f32[8,128]{1,0:T(8,128)S(1)}, f32[8,128]{1,0:T(8,128)S(1)}, u32[]{:S(2)}, u32[]{:S(2)}) %collective-permute-start.26) | collective-permute-done | bytes 4128 | tf_op jit(solution)/shard_map/ppermute | solution.py:758
  144.0 8.5 %combine.1 = (bf16[512,768]{1,0:T(8,128)(2,1)}, f32[512,768]{1,0:T(8,128)}, bf16[512,8]{1,0:T(8,128)(2,1)}, f32[8,768]{1,0:T(8,128)}, bf16[160,768]{1,0:T(8,128)...) custom-call(s32[512,2]{1,0:T(8,128)} %multiply_add_fusion.refs_0_.re, ...), custom_call_target="tpu_custom_call" | custom-call | flops 2960000000 | tf_op jit(solution)/shard_map/combine/pallas_call | solution.py:504
  154.0 3.2 collective-permute-start.38
  164.3 6.2 %collective-permute-done.39.refs_4_ = bf16[160,768]{1,0:T(8,128)(2,1)S(1)} collective-permute-done((bf16[160,768]{1,0:T(8,128)(2,1)}, bf16[160,768]{1,0:T(8,128)(2,1)S(1)}, u32[]{:S(2)}, u32[]{:S(2)}) %collective-permute-start.39) | collective-permute-done | bytes 245792 | tf_op jit(solution)/shard_map/ppermute | solution.py:758
  171.2 12.5 %expert_backward.2 = (bf16[640,3072]{1,0:T(8,128)(2,1)}, bf16[640,768]{1,0:T(8,128)(2,1)}, bf16[160,768]{1,0:T(8,128)(2,1)}, bf16[160,768]{1,0:T(8,128)(2,1)}, b...) custom-call(s32[1]{0:T(128)} %bitcast.4.refs_0_, bf16[160,768]{1,0:T(8,128)(2,1)} %get-tuple-element.215.refs_1_, ...), custom_call_target="tpu_custom_call" | custom-call | flops 4070000128 | tf_op jit(solution)/shard_map/expert_backward/pallas_call | solution.py:136
  187.3 7.8 %weight_part.4 = (bf16[2,2,128,768]{3,2,1,0:T(8,128)(2,1)}, bf16[2,2,128,768]{3,2,1,0:T(8,128)(2,1)}, bf16[2,2,128,768]{3,2,1,0:T(8,128)(2,1)}) custom-call(s32[4]{0:T(128)} %pad_add_fusion.1.refs_0_, bf16[3072,640]{1,0:T(8,128)(2,1)} %get-tuple-element.191.refs_1_.refs_2_.refs_3_.refs_4_, ...), custom_call_target="tpu_custom_call" | custom-call | flops 1480000000 | tf_op jit(solution)/shard_map/weight_part/pallas_call | solution.py:338
  199.3 12.9 %expert_backward.3 = (bf16[640,3072]{1,0:T(8,128)(2,1)}, bf16[640,768]{1,0:T(8,128)(2,1)}, bf16[160,768]{1,0:T(8,128)(2,1)}, bf16[160,768]{1,0:T(8,128)(2,1)}, b...) custom-call(s32[1]{0:T(128)} %bitcast.4.refs_0_, bf16[640,768]{1,0:T(8,128)(2,1)} %copy-done.1, ...), custom_call_target="tpu_custom_call" | custom-call | flops 4070000128 | tf_op jit(solution)/shard_map/expert_backward/pallas_call | solution.py:136
  220.2 7.8 %weight_part.5 = (bf16[2,2,128,768]{3,2,1,0:T(8,128)(2,1)}, bf16[2,2,128,768]{3,2,1,0:T(8,128)(2,1)}, bf16[2,2,128,768]{3,2,1,0:T(8,128)(2,1)}) custom-call(s32[4]{0:T(128)} %pad_add_fusion.2.refs_0_, bf16[3072,640]{1,0:T(8,128)(2,1)} %get-tuple-element.191.refs_1_.refs_2_.refs_3_.refs_4_, ...), custom_call_target="tpu_custom_call" | custom-call | flops 1480000000 | tf_op jit(solution)/shard_map/weight_part/pallas_call | solution.py:338
  229.4 7.7 %weight_part.6 = (bf16[2,2,32,3072]{3,2,1,0:T(8,128)(2,1)}, bf16[2,2,32,3072]{3,2,1,0:T(8,128)(2,1)}, bf16[2,2,32,3072]{3,2,1,0:T(8,128)(2,1)}) custom-call(s32[4]{0:T(128)} %pad_add_fusion.1.refs_0_, bf16[768,640]{1,0:T(8,128)(2,1)} %get-tuple-element.221.refs_1_.refs_2_.refs_3_.refs_4_, ...), custom_call_target="tpu_custom_call" | custom-call | flops 1480000000 | tf_op jit(solution)/shard_map/weight_part/pallas_call | solution.py:338
  239.0 8.6 %collect.1 = (f32[512,768]{1,0:T(8,128)}, bf16[512,768]{1,0:T(8,128)(2,1)}, bf16[512,768]{1,0:T(8,128)(2,1)}, f32[8,768]{1,0:T(8,128)}) custom-call(s32[1]{0:T(128)} %bitcast.2.core.refs_0_, s32[512,2]{1,0:T(8,128)} %multiply_add_fusion.refs_0_.refs_1_, bf16[160,768]{1,0:T(8,128)(2,1)} %get-tuple-element.263.refs_2_, bf16[160,768]{1,0:T(8,128)(2,1)} %copy-done.56, ...), custom_call_target="tpu_custom_call" | custom-call | flops 2960000000 | tf_op jit(solution)/shard_map/collect/pallas_call | solution.py:555
  249.5 11.6 %attention_backward.1 = (bf16[3,512,768]{2,1,0:T(8,128)(2,1)}, f32[12,4,128,128]{3,2,1,0:T(8,128)}) custom-call(bf16[3,512,768]{2,1,0:T(8,128)(2,1)} %project.1.refs_2_.refs_3_.refs_4_.refs_0_.refs_1_, bf16[3,512,768]{2,1,0:T(8,128)(2,1)} %project.1.refs_2_.refs_3_.refs_4_.refs_0_.refs_1_, ...), custom_call_target="tpu_custom_call" | custom-call | flops 1480000000 | tf_op jit(solution)/shard_map/attention_backward/pallas_call | solution.py:281
  262.1 8.2 %outer_halves.1 = (bf16[2,768,384]{2,1,0:T(8,128)(2,1)}, bf16[2,768,384]{2,1,0:T(8,128)(2,1)}, bf16[2,768,384]{2,1,0:T(8,128)(2,1)}, bf16[2,768,384]{2,1,0:T(8,128)(2,1)}) custom-call(s32[1]{0:T(128)} %bitcast.2.core.refs_0_, bf16[512,768]{1,0:T(8,128)(2,1)} %fusion.6.rows.refs_1_, bf16[512,768]{1,0:T(8,128)(2,1)} %get-tuple-element.183.attended.refs_2_, ...), custom_call_target="tpu_custom_call" | custom-call | flops 740000000 | tf_op jit(solution)/shard_map/outer_halves/pallas_call | solution.py:605
  283.7 7.5 %weight_part.7 = (bf16[2,2,32,3072]{3,2,1,0:T(8,128)(2,1)}, bf16[2,2,32,3072]{3,2,1,0:T(8,128)(2,1)}, bf16[2,2,32,3072]{3,2,1,0:T(8,128)(2,1)}) custom-call(s32[4]{0:T(128)} %pad_add_fusion.2.refs_0_, bf16[768,640]{1,0:T(8,128)(2,1)} %get-tuple-element.221.refs_1_.refs_2_.refs_3_.refs_4_, ...), custom_call_target="tpu_custom_call" | custom-call | flops 14800000000 | tf_op jit(solution)/shard_map/weight_part/pallas_call | solution.py:338
  293.4 6.3 %collective-permute-done.62 = bf16[2,2,32,3072]{3,2,1,0:T(8,128)(2,1)S(1)} collective-permute-done((bf16[2,2,32,3072]{3,2,1,0:T(8,128)(2,1)}, bf16[2,2,32,3072]{3,2,1,0:T(8,128)(2,1)S(1)}, u32[]{:S(2)}, u32[]{:S(2)}) %collective-permute-start.62) | collective-permute-done | bytes 786464 | tf_op jit(solution)/shard_map/ppermute | solution.py:758
  299.6 14.7 %collective-permute-done.65 = bf16[1,4,128,768]{3,2,1,0:T(8,128)(2,1)} collective-permute-done((bf16[1,4,128,768]{3,2,1,0:T(8,128)(2,1)}, bf16[1,4,128,768]{3,2,1,0:T(8,128)(2,1)}, u32[]{:S(2)}, u32[]{:S(2)}) %collective-permute-start.65) | collective-permute-done | bytes 786464 | tf_op jit(solution)/shard_map/ppermute | solution.py:758
  322.1 5.3 %fusion.11 = f32[12,32]{1,0:T(8,128)S(1)} fusion(s32[4,128,128]{2,1,0:T(8,128)S(1)} %pad_add_fusion, f32[12,4,128,128]{3,2,1,0:T(8,128)S(1)} %copy-done.3), kind=kOutput, calls=%fused_computation.34 | convolution fusion | flops 304087040 | bytes 3409408 | tf_op jit(solution)/shard_map/hdxy,dxyb->hb/dot_general | solution.py:714
  327.4 8.5 %enter.1 = (f32[512,768]{1,0:T(8,128)}, f32[16,768]{1,0:T(8,128)}) custom-call(s32[1]{0:T(128)} %bitcast.2.core.refs_0_, bf16[3,512,768]{2,1,0:T(8,128)(2,1)} %get-tuple-element.313.refs_3_.grads, bf16[4,768,384]{2,1,0:T(8,128)(2,1)} %join.1.mine.refs_15_, bf16[4,768,384]{2,1,0:T(8,128)(2,1)} %copy-done, bf16[512,768]{1,0:T(8,128)(2,1)} %tokens.3, ...), custom_call_target="tpu_custom_call" | custom-call | flops 2220000000 | tf_op jit(solution)/shard_map/enter/pallas_call | solution.py:659
  343.1 8.0 %collective-permute-done.67 = bf16[1,2,32,3072]{3,2,1,0:T(8,128)(2,1)} collective-permute-done((bf16[1,2,32,3072]{3,2,1,0:T(8,128)(2,1)}, bf16[1,2,32,3072]{3,2,1,0:T(8,128)(2,1)}, u32[]{:S(2)}, u32[]{:S(2)}) %collective-permute-start.67) | collective-permute-done | bytes 393248 | tf_op jit(solution)/shard_map/ppermute | solution.py:758
  352.3 5.0 %collective-permute-done.64 = bf16[4,2,48,384]{3,2,1,0:T(8,128)(2,1)S(1)} collective-permute-done((bf16[4,2,48,384]{3,2,1,0:T(8,128)(2,1)S(1)}, bf16[4,2,48,384]{3,2,1,0:T(8,128)(2,1)S(1)}, u32[]{:S(2)}, u32[]{:S(2)}) %collective-permute-start.64) | collective-permute-done | bytes 294944 | tf_op jit(solution)/shard_map/ppermute | solution.py:758
  365.0 6.0 %collective-permute-done.74 = f32[16,768]{1,0:T(8,128)S(1)} collective-permute-done((f32[16,768]{1,0:T(8,128)S(1)}, f32[16,768]{1,0:T(8,128)S(1)}, u32[]{:S(2)}, u32[]{:S(2)}) %collective-permute-start.74) | collective-permute-done | bytes 49184 | tf_op jit(solution)/shard_map/ppermute | solution.py:758
  371.0 3.4 collective-permute-start.79
  383.4 7.7 %collective-permute-done.79 = bf16[1,2,32,3072]{3,2,1,0:T(8,128)(2,1)S(1)} collective-permute-done((bf16[1,2,32,3072]{3,2,1,0:T(8,128)(2,1)S(1)}, bf16[1,2,32,3072]{3,2,1,0:T(8,128)(2,1)S(1)}, u32[]{:S(2)}, u32[]{:S(2)}) %collective-permute-start.79) | collective-permute-done | bytes 393248 | tf_op jit(solution)/shard_map/ppermute | solution.py:758
  395.5 11.0 %collective-permute-done.76 = f32[16,768]{1,0:T(8,128)S(1)} collective-permute-done((f32[16,768]{1,0:T(8,128)S(1)}, f32[16,768]{1,0:T(8,128)S(1)}, u32[]{:S(2)}, u32[]{:S(2)}) %collective-permute-start.76) | collective-permute-done | bytes 49184 | tf_op jit(solution)/shard_map/ppermute | solution.py:758
  (398 shorter events, 156.5 us)
Async XLA Ops:
  77.1 27.9 %collective-permute-start.24 = (bf16[160,768]{1,0:T(8,128)(2,1)}, bf16[160,768]{1,0:T(8,128)(2,1)S(1)}, u32[]{:S(2)}, u32[]{:S(2)}) collective-permute-start(bf16[160,768]{1,0:T(8,128)(2,1)} %get-tuple-element.197), channel_id=1, source_target_pairs={{0,10},{1,11},{2,8},{3,9},{4,14},{5,15},{6,12},{7,13},{8,2},{9,3},... | collective-permute-start | bytes 737288 | tf_op jit(solution)/shard_map/ppermute | solution.py:758
  79.4 25.6 %collective-permute-start.23 = (bf16[160,768]{1,0:T(8,128)(2,1)}, bf16[160,768]{1,0:T(8,128)(2,1)S(1)}, u32[]{:S(2)}, u32[]{:S(2)}) collective-permute-start(bf16[160,768]{1,0:T(8,128)(2,1)} %get-tuple-element.195), channel_id=1, source_target_pairs={{0,8},{1,9},{2,10},{3,11},{4,12},{5,13},{6,14},{7,15},{8,0},{9,1},... | collective-permute-start | bytes 737288 | tf_op jit(solution)/shard_map/ppermute | solution.py:758
  83.6 21.4 %collective-permute-start.22 = (bf16[160,768]{1,0:T(8,128)(2,1)}, bf16[160,768]{1,0:T(8,128)(2,1)S(1)}, u32[]{:S(2)}, u32[]{:S(2)}) collective-permute-start(bf16[160,768]{1,0:T(8,128)(2,1)} %get-tuple-element.193), channel_id=1, source_target_pairs={{0,2},{1,3},{2,0},{3,1},{4,6},{5,7},{6,4},{7,5},{8,10},{9,11},{10,... | collective-permute-start | bytes 737288 | tf_op jit(solution)/shard_map/ppermute | solution.py:758
  89.0 16.0 %collective-permute-start.19 = (f32[8,128]{1,0:T(8,128)S(1)}, f32[8,128]{1,0:T(8,128)S(1)}, u32[]{:S(2)}, u32[]{:S(2)}) collective-permute-start(f32[8,128]{1,0:T(8,128)S(1)} %add.546), channel_id=1, source_target_pairs={{0,8},{1,9},{2,10},{3,11},{4,12},{5,13},{6,14},{7,15},{8,0},{9,1},... | collective-permute-start | bytes 12296 | tf_op jit(solution)/shard_map/ppermute | solution.py:758
  105.9 20.6 %collective-permute-start.27 = (bf16[160,768]{1,0:T(8,128)(2,1)S(1)}, bf16[160,768]{1,0:T(8,128)(2,1)S(1)}, u32[]{:S(2)}, u32[]{:S(2)}) collective-permute-start(bf16[160,768]{1,0:T(8,128)(2,1)S(1)} %copy-done.69), channel_id=1, source_target_pairs={{0,2},{1,3},{2,0},{3,1},{4,6},{5,7},{6,4},{7,5},{8,10},{9,11},{10,... | collective-permute-start | bytes 737288 | tf_op jit(solution)/shard_map/ppermute | solution.py:758
  110.1 16.4 %collective-permute-start.28 = (bf16[160,768]{1,0:T(8,128)(2,1)S(1)}, bf16[160,768]{1,0:T(8,128)(2,1)S(1)}, u32[]{:S(2)}, u32[]{:S(2)}) collective-permute-start(bf16[160,768]{1,0:T(8,128)(2,1)S(1)} %copy-done.67), channel_id=1, source_target_pairs={{0,8},{1,9},{2,10},{3,11},{4,12},{5,13},{6,14},{7,15},{8,0},{9,1},... | collective-permute-start | bytes 737288 | tf_op jit(solution)/shard_map/ppermute | solution.py:758
  110.1 16.3 %collective-permute-start.29 = (bf16[160,768]{1,0:T(8,128)(2,1)S(1)}, bf16[160,768]{1,0:T(8,128)(2,1)S(1)}, u32[]{:S(2)}, u32[]{:S(2)}) collective-permute-start(bf16[160,768]{1,0:T(8,128)(2,1)S(1)} %copy-done.65), channel_id=1, source_target_pairs={{0,10},{1,11},{2,8},{3,9},{4,14},{5,15},{6,12},{7,13},{8,2},{9,3},... | collective-permute-start | bytes 737288 | tf_op jit(solution)/shard_map/ppermute | solution.py:758
  158.0 25.6 %collective-permute-start.42 = (bf16[160,768]{1,0:T(8,128)(2,1)}, bf16[160,768]{1,0:T(8,128)(2,1)S(1)}, u32[]{:S(2)}, u32[]{:S(2)}) collective-permute-start(bf16[160,768]{1,0:T(8,128)(2,1)} %get-tuple-element.231), channel_id=1, source_target_pairs={{0,10},{1,11},{2,8},{3,9},{4,14},{5,15},{6,12},{7,13},{8,2},{9,3},... | collective-permute-start | bytes 737288 | tf_op jit(solution)/shard_map/ppermute | solution.py:758
  160.1 23.5 %collective-permute-start.41 = (bf16[160,768]{1,0:T(8,128)(2,1)}, bf16[160,768]{1,0:T(8,128)(2,1)S(1)}, u32[]{:S(2)}, u32[]{:S(2)}) collective-permute-start(bf16[160,768]{1,0:T(8,128)(2,1)} %get-tuple-element.229), channel_id=1, source_target_pairs={{0,8},{1,9},{2,10},{3,11},{4,12},{5,13},{6,14},{7,15},{8,0},{9,1},... | collective-permute-start | bytes 737288 | tf_op jit(solution)/shard_map/ppermute | solution.py:758
  160.2 23.5 %collective-permute-start.40 = (bf16[160,768]{1,0:T(8,128)(2,1)}, bf16[160,768]{1,0:T(8,128)(2,1)S(1)}, u32[]{:S(2)}, u32[]{:S(2)}) collective-permute-start(bf16[160,768]{1,0:T(8,128)(2,1)} %get-tuple-element.227), channel_id=1, source_target_pairs={{0,2},{1,3},{2,0},{3,1},{4,6},{5,7},{6,4},{7,5},{8,10},{9,11},{10,... | collective-permute-start | bytes 737288 | tf_op jit(solution)/shard_map/ppermute | solution.py:758
  195.2 19.8 %collective-permute-start.48 = (bf16[2,2,128,768]{3,2,1,0:T(8,128)(2,1)}, bf16[2,2,128,768]{3,2,1,0:T(8,128)(2,1)S(1)}, u32[]{:S(2)}, u32[]{:S(2)}) collective-permute-start(bf16[2,2,128,768]{3,2,1,0:T(8,128)(2,1)} %get-tuple-element.244), channel_id=1, source_target_pairs={{0,4},{1,5},{2,6},{3,7},{4,0},{5,1},{6,2},{7,3},{8,12},{9,13},{10,... | collective-permute-start | bytes 2359304 | tf_op jit(solution)/shard_map/ppermute | solution.py:758
  195.7 16.5 %collective-permute-start.44 = (bf16[160,768]{1,0:T(8,128)(2,1)S(1)}, bf16[160,768]{1,0:T(8,128)(2,1)S(1)}, u32[]{:S(2)}, u32[]{:S(2)}) collective-permute-start(bf16[160,768]{1,0:T(8,128)(2,1)S(1)} %copy-done.62), channel_id=1, source_target_pairs={{0,2},{1,3},{2,0},{3,1},{4,6},{5,7},{6,4},{7,5},{8,10},{9,11},{10,... | collective-permute-start | bytes 737288 | tf_op jit(solution)/shard_map/ppermute | solution.py:758
  215.2 22.4 %collective-permute-start.52 = (bf16[160,768]{1,0:T(8,128)(2,1)}, bf16[160,768]{1,0:T(8,128)(2,1)S(1)}, u32[]{:S(2)}, u32[]{:S(2)}) collective-permute-start(bf16[160,768]{1,0:T(8,128)(2,1)} %collective-permute-done.49), channel_id=1, source_target_pairs={{0,2},{1,3},{2,0},{3,1},{4,6},{5,7},{6,4},{7,5},{8,10},{9,11},{10,... | collective-permute-start | bytes 737288 | tf_op jit(solution)/shard_map/ppermute | solution.py:758
  215.9 22.3 %collective-permute-start.53 = (bf16[160,768]{1,0:T(8,128)(2,1)}, bf16[160,768]{1,0:T(8,128)(2,1)S(1)}, u32[]{:S(2)}, u32[]{:S(2)}) collective-permute-start(bf16[160,768]{1,0:T(8,128)(2,1)} %collective-permute-done.50), channel_id=1, source_target_pairs={{0,8},{1,9},{2,10},{3,11},{4,12},{5,13},{6,14},{7,15},{8,0},{9,1},... | collective-permute-start | bytes 737288 | tf_op jit(solution)/shard_map/ppermute | solution.py:758
  217.8 20.4 %collective-permute-start.54 = (bf16[160,768]{1,0:T(8,128)(2,1)}, bf16[160,768]{1,0:T(8,128)(2,1)S(1)}, u32[]{:S(2)}, u32[]{:S(2)}) collective-permute-start(bf16[160,768]{1,0:T(8,128)(2,1)} %collective-permute-done.51), channel_id=1, source_target_pairs={{0,10},{1,11},{2,8},{3,9},{4,14},{5,15},{6,12},{7,13},{8,2},{9,3},... | collective-permute-start | bytes 737288 | tf_op jit(solution)/shard_map/ppermute | solution.py:758
  218.7 30.5 %collective-permute-start.55 = (bf16[2,2,128,768]{3,2,1,0:T(8,128)(2,1)}, bf16[2,2,128,768]{3,2,1,0:T(8,128)(2,1)S(1)}, u32[]{:S(2)}, u32[]{:S(2)}) collective-permute-start(bf16[2,2,128,768]{3,2,1,0:T(8,128)(2,1)} %get-tuple-element.274), channel_id=1, source_target_pairs={{0,4},{1,5},{2,6},{3,7},{4,0},{5,1},{6,2},{7,3},{8,12},{9,13},{10,... | collective-permute-start | bytes 2359304 | tf_op jit(solution)/shard_map/ppermute | solution.py:758
  237.1 24.0 %collective-permute-start.57 = (bf16[1,2,128,768]{3,2,1,0:T(8,128)(2,1)S(1)}, bf16[1,2,128,768]{3,2,1,0:T(8,128)(2,1)S(1)}, u32[]{:S(2)}, u32[]{:S(2)}) collective-permute-start(bf16[1,2,128,768]{3,2,1,0:T(8,128)(2,1)S(1)} %constant_dynamic-slice_fusion.7), channel_id=1, source_target_pairs={{0,16},{1,17},{2,18},{3,19},{4,20},{5,21},{6,22},{7,23},{8,24},{9,... | collective-permute-start | bytes 1179656 | tf_op jit(solution)/shard_map/ppermute | solution.py:758
  237.6 23.4 %collective-permute-start.56 = (bf16[2,2,128,768]{3,2,1,0:T(8,128)(2,1)S(1)}, bf16[2,2,128,768]{3,2,1,0:T(8,128)(2,1)S(1)}, u32[]{:S(2)}, u32[]{:S(2)}) collective-permute-start(bf16[2,2,128,768]{3,2,1,0:T(8,128)(2,1)S(1)} %copy-done.51), channel_id=1, source_target_pairs={{0,4},{1,5},{2,6},{3,7},{4,0},{5,1},{6,2},{7,3},{8,12},{9,13},{10,... | collective-permute-start | bytes 2359304 | tf_op jit(solution)/shard_map/ppermute | solution.py:758
  247.6 25.1 %collective-permute-start.58 = (bf16[2,2,32,3072]{3,2,1,0:T(8,128)(2,1)S(1)}, bf16[2,2,32,3072]{3,2,1,0:T(8,128)(2,1)S(1)}, u32[]{:S(2)}, u32[]{:S(2)}) collective-permute-start(bf16[2,2,32,3072]{3,2,1,0:T(8,128)(2,1)S(1)} %copy-done.52), channel_id=1, source_target_pairs={{0,4},{1,5},{2,6},{3,7},{4,0},{5,1},{6,2},{7,3},{8,12},{9,13},{10,... | collective-permute-start | bytes 2359304 | tf_op jit(solution)/shard_map/ppermute | solution.py:758
  276.8 37.5 %collective-permute-start.65 = (bf16[1,4,128,768]{3,2,1,0:T(8,128)(2,1)}, bf16[1,4,128,768]{3,2,1,0:T(8,128)(2,1)}, u32[]{:S(2)}, u32[]{:S(2)}) collective-permute-start(bf16[1,4,128,768]{3,2,1,0:T(8,128)(2,1)} %pad_maximum_fusion.5), channel_id=1, source_target_pairs={{0,16},{1,17},{2,18},{3,19},{4,20},{5,21},{6,22},{7,23},{8,24},{9,... | collective-permute-start | bytes 2359304 | tf_op jit(solution)/shard_map/ppermute | solution.py:758
  280.2 19.4 %collective-permute-start.62 = (bf16[2,2,32,3072]{3,2,1,0:T(8,128)(2,1)}, bf16[2,2,32,3072]{3,2,1,0:T(8,128)(2,1)S(1)}, u32[]{:S(2)}, u32[]{:S(2)}) collective-permute-start(bf16[2,2,32,3072]{3,2,1,0:T(8,128)(2,1)} %get-tuple-element.296), channel_id=1, source_target_pairs={{0,4},{1,5},{2,6},{3,7},{4,0},{5,1},{6,2},{7,3},{8,12},{9,13},{10,... | collective-permute-start | bytes 2359304 | tf_op jit(solution)/shard_map/ppermute | solution.py:758
  283.0 33.8 %collective-permute-start.61 = (bf16[4,8,48,384]{3,2,1,0:T(8,128)(2,1)S(1)}, bf16[4,8,48,384]{3,2,1,0:T(8,128)(2,1)S(1)}, u32[]{:S(2)}, u32[]{:S(2)}) collective-permute-start(bf16[4,8,48,384]{3,2,1,0:T(8,128)(2,1)S(1)} %pad_maximum_fusion.2), channel_id=1, source_target_pairs={{0,2},{1,3},{2,0},{3,1},{4,6},{5,7},{6,4},{7,5},{8,10},{9,11},{10,... | collective-permute-start | bytes 3538952 | tf_op jit(solution)/shard_map/ppermute | solution.py:758
  314.3 37.9 %collective-permute-start.66 = (bf16[1,2,32,3072]{3,2,1,0:T(8,128)(2,1)}, bf16[1,2,32,3072]{3,2,1,0:T(8,128)(2,1)}, u32[]{:S(2)}, u32[]{:S(2)}) collective-permute-start(bf16[1,2,32,3072]{3,2,1,0:T(8,128)(2,1)} %constant_dynamic-slice_fusion.4), channel_id=1, source_target_pairs={{0,16},{1,17},{2,18},{3,19},{4,20},{5,21},{6,22},{7,23},{8,24},{9,... | collective-permute-start | bytes 1179656 | tf_op jit(solution)/shard_map/ppermute | solution.py:758
  317.9 19.3 %collective-permute-start.63 = (bf16[4,2,2,48,384]{4,3,2,1,0:T(8,128)(2,1)}, bf16[4,2,2,48,384]{4,3,2,1,0:T(8,128)(2,1)}, u32[]{:S(2)}, u32[]{:S(2)}) collective-permute-start(bf16[4,2,2,48,384]{4,3,2,1,0:T(8,128)(2,1)} %dynamic-slice_bitcast_fusion), channel_id=1, source_target_pairs={{0,4},{1,5},{2,6},{3,7},{4,0},{5,1},{6,2},{7,3},{8,12},{9,13},{10,... | collective-permute-start | bytes 1769480 | tf_op jit(solution)/shard_map/ppermute | solution.py:758
  319.1 32.0 %collective-permute-start.67 = (bf16[1,2,32,3072]{3,2,1,0:T(8,128)(2,1)}, bf16[1,2,32,3072]{3,2,1,0:T(8,128)(2,1)}, u32[]{:S(2)}, u32[]{:S(2)}) collective-permute-start(bf16[1,2,32,3072]{3,2,1,0:T(8,128)(2,1)} %constant_dynamic-slice_fusion.3), channel_id=1, source_target_pairs={{0,16},{1,17},{2,18},{3,19},{4,20},{5,21},{6,22},{7,23},{8,24},{9,... | collective-permute-start | bytes 1179656 | tf_op jit(solution)/shard_map/ppermute | solution.py:758
  339.7 19.8 %collective-permute-start.69 = (bf16[2,2,32,3072]{3,2,1,0:T(8,128)(2,1)S(1)}, bf16[2,2,32,3072]{3,2,1,0:T(8,128)(2,1)S(1)}, u32[]{:S(2)}, u32[]{:S(2)}) collective-permute-start(bf16[2,2,32,3072]{3,2,1,0:T(8,128)(2,1)S(1)} %copy-done.50), channel_id=1, source_target_pairs={{0,4},{1,5},{2,6},{3,7},{4,0},{5,1},{6,2},{7,3},{8,12},{9,13},{10,... | collective-permute-start | bytes 2359304 | tf_op jit(solution)/shard_map/ppermute | solution.py:758
  341.2 16.0 %collective-permute-start.64 = (bf16[4,2,48,384]{3,2,1,0:T(8,128)(2,1)S(1)}, bf16[4,2,48,384]{3,2,1,0:T(8,128)(2,1)S(1)}, u32[]{:S(2)}, u32[]{:S(2)}) collective-permute-start(bf16[4,2,48,384]{3,2,1,0:T(8,128)(2,1)S(1)} %dynamic-slice_bitcast_fusion.5), channel_id=1, source_target_pairs={{0,8},{1,9},{2,10},{3,11},{4,12},{5,13},{6,14},{7,15},{8,0},{9,1},... | collective-permute-start | bytes 884744 | tf_op jit(solution)/shard_map/ppermute | solution.py:758
  360.6 17.1 %collective-permute-start.70 = (bf16[2,32,3072]{2,1,0:T(8,128)(2,1)S(1)}, bf16[2,32,3072]{2,1,0:T(8,128)(2,1)S(1)}, u32[]{:S(2)}, u32[]{:S(2)}) collective-permute-start(bf16[2,32,3072]{2,1,0:T(8,128)(2,1)S(1)} %fusion.15), channel_id=1, source_target_pairs={{0,8},{1,9},{2,10},{3,11},{4,12},{5,13},{6,14},{7,15},{8,0},{9,1},... | collective-permute-start | bytes 1179656 | tf_op jit(solution)/shard_map/ppermute | solution.py:758
  371.0 20.1 %collective-permute-start.79 = (bf16[1,2,32,3072]{3,2,1,0:T(8,128)(2,1)S(1)}, bf16[1,2,32,3072]{3,2,1,0:T(8,128)(2,1)S(1)}, u32[]{:S(2)}, u32[]{:S(2)}) collective-permute-start(bf16[1,2,32,3072]{3,2,1,0:T(8,128)(2,1)S(1)} %constant_dynamic-slice_fusion.2), channel_id=1, source_target_pairs={{0,16},{1,17},{2,18},{3,19},{4,20},{5,21},{6,22},{7,23},{8,24},{9,... | collective-permute-start | bytes 1179656 | tf_op jit(solution)/shard_map/ppermute | solution.py:758
  380.5 26.8 %collective-permute-start.78 = (bf16[3,128,768]{2,1,0:T(8,128)(2,1)}, bf16[3,128,768]{2,1,0:T(8,128)(2,1)S(1)}, u32[]{:S(2)}, u32[]{:S(2)}) collective-permute-start(bf16[3,128,768]{2,1,0:T(8,128)(2,1)} %pad_maximum_fusion.6), channel_id=1, source_target_pairs={{0,8},{1,9},{2,10},{3,11},{4,12},{5,13},{6,14},{7,15},{8,0},{9,1},... | collective-permute-start | bytes 1769480 | tf_op jit(solution)/shard_map/ppermute | solution.py:758
  383.2 23.4 %collective-permute-start.76 = (f32[16,768]{1,0:T(8,128)S(1)}, f32[16,768]{1,0:T(8,128)S(1)}, u32[]{:S(2)}, u32[]{:S(2)}) collective-permute-start(f32[16,768]{1,0:T(8,128)S(1)} %add.625), channel_id=1, source_target_pairs={{0,8},{1,9},{2,10},{3,11},{4,12},{5,13},{6,14},{7,15},{8,0},{9,1},... | collective-permute-start | bytes 147464 | tf_op jit(solution)/shard_map/ppermute | solution.py:758
  383.3 27.7 %collective-permute-start.77 = (bf16[4,96,384]{2,1,0:T(8,128)(2,1)S(1)}, bf16[4,96,384]{2,1,0:T(8,128)(2,1)S(1)}, u32[]{:S(2)}, u32[]{:S(2)}) collective-permute-start(bf16[4,96,384]{2,1,0:T(8,128)(2,1)S(1)} %pad_maximum_fusion.9), channel_id=1, source_target_pairs={{0,1},{1,0},{2,3},{3,2},{4,5},{5,4},{6,7},{7,6},{8,9},{9,8},{10,11... | collective-permute-start | bytes 884744 | tf_op jit(solution)/shard_map/ppermute | solution.py:758
  (124 other events, 1001.2 us)

commit v11 on v10

--- a/solution.py
+++ b/solution.py
@@ -988,7 +988,7 @@
     total = total.reshape((4,) + (2,) * len(dp_masks) + (-1, columns))
 
 
-    small_trades = [(0, 1), (0, group_masks[0])] + [(mask, 0) for mask in reversed(dp_masks) if mask != PAIR] + [(PAIR, 0)]
+    small_trades = [(0, 1), (0, group_masks[0])] + [(mask, 0) for mask in reversed(dp_masks)]
     small_trades += [(0, mask) for mask in group_masks[1:]]
     passed_masks = []
     for mask in dp_masks:
@@ -1014,7 +1014,9 @@
             flat = flat + swap(after(flat, gone), *small_trades.pop(0))
         if len(passed_masks) == 1:
             far_e = far_trade(after(away_e, gone))
-            got_f = swap(after(send_f, gone), 1, 0)
+            got_f = swap(after(send_f, got), 1, 0)
+            out_theirs = swap(after(jnp.concatenate([done_a, done_c[:1]]), gone), PAIR, 0)
+            got = after(got, out_theirs)
         elif mask == PAIR:
             got = after(got, far_d, far_e)
             done_e = finish(far_e, stay_e)
@@ -1027,7 +1029,6 @@
         if mask == PAIR:
             done_d = finish(after(far_d, total), stay_d)
             in_first = swap(done_d, PAIR, 0)
-            out_theirs = swap(after(jnp.concatenate([done_a, done_c[:1]]), total), PAIR, 0)
         flat = after(flat, total)
     in_theirs = jnp.concatenate([in_first, swap(done_e[:1], PAIR, 0)])
     for mask in reversed(group_masks):
@@ -1036,7 +1037,7 @@
         total = jnp.concatenate([jnp.where(bit == 0, total, other_part), jnp.where(bit == 0, other_part, total)], axis=1)
         flat = flat + swap(flat, *small_trades.pop(0))
         total, flat = lax.optimization_barrier((total, flat))
-    other_part = after(swap(total, 0, 1), out_theirs)
+    other_part = swap(total, 0, 1)
     for trade in small_trades:
         flat = flat + swap(flat, *trade)
     total = jnp.concatenate([jnp.where(core == 0, total, other_part), jnp.where(core == 0, other_part, total)], axis=2)

time: 419 us -> 415 us (level)
  starting transfers between devices: 89.6 us -> 85.1 us
    ppermute x67, starting transfers between devices: 72.5 us -> 68 us  [swap(): return lax.ppermute(value, AXES, pairs)]
    unnamed x150 -> x164, local copies, waits for them, and re-layouts: 9.38 us -> 10.3 us
  transfers between devices with their start and end apart: 81 -> 81, of which waited for: 30 -> 31; matrix products, arithmetic and copies ran while one was open for 11% -> 10% of each run, Pallas kernels for 32% -> 32%
where the time goes in v11:
time: 415 us; the launch traced here: 411 us
  Pallas kernels  157 us (38%)
  waiting for transfers between devices  106 us (26%)
  starting transfers between devices  85.1 us (21%)
  other arithmetic  26.1 us (6%)
  local copies, waits for them, and re-layouts  25 us (6%)
  between operations  5.99 us (1%)
  matrix products  5.88 us (1%)
    ppermute x67, waiting for transfers between devices, swap(): return lax.ppermute(value, AXES, pairs)  96.3 us
    ppermute x67, starting transfers between devices, swap(): return lax.ppermute(value, AXES, pairs)  68 us
    pallas_call x4, Pallas kernels, weight_part(): pl.pallas_call(lambda *refs: weight_part_kernel(*refs, count=count, plans...  30.8 us
    pallas_call x2, Pallas kernels, expert_forward(): pl.pallas_call(lambda *refs: expert_forward_kernel(*refs, chunk=chunk, co...  27.5 us
    pallas_call x2, Pallas kernels, expert_backward(): pl.pallas_call(lambda *refs: expert_backward_kernel(*refs, chunk=chunk, c...  25.3 us
    ppermute x14, starting transfers between devices, gather_ring(): lax.ppermute(after(held, *due[step - 2:step - 1]) if step > 1 else held,...  17.1 us
    pallas_call x1, Pallas kernels, attention_forward(): pl.pallas_call(lambda *refs: attention_forward_kernel(*refs, heads=64, bl...  12.7 us
    pallas_call x1, Pallas kernels, attention_backward(): pl.pallas_call(lambda *refs: attention_backward_kernel(*refs, heads=64, b...  11.5 us
  transfers between devices with their start and end apart: 81, of which 31 were waited for; matrix products, arithmetic and copies ran while one was open for 10% of the time, Pallas kernels for 32%

profile of v11, /device:TPU:0, one launch (start us, length us, event | category | flops | bytes accessed | tf_op | source)
XLA Modules:
  0.0 411.1 jit_solution(8466080630248762863)
XLA Ops:
  34.3 3.3 join.1.mine.refs_15_
  46.4 6.4 %project.1.refs_2_.refs_3_.refs_4_.refs_0_.refs_1_ = bf16[3,512,768]{2,1,0:T(8,128)(2,1)} custom-call(s32[1]{0:T(128)} %bitcast.2.core.refs_0_, bf16[512,768]{1,0:T(8,128)(2,1)} %fusion.6.rows.refs_1_, bf16[4,768,384]{2,1,0:T(8,128)(2,1)} %join.1.mine.refs_15_, bf16[4,768,384]{2,1,0:T(8,128)(2,1)} %copy-done), custom_call_target="tpu_custom_call" | custom-call | flops 1480000000 | tf_op jit(solution)/shard_map/project/pallas_call | solution.py:397
  55.0 12.7 %attention_forward.1 = (bf16[512,768]{1,0:T(8,128)(2,1)}, bf16[12,512,512]{2,1,0:T(8,128)(2,1)}) custom-call(f32[12]{0:T(128)} %slice_reduce_fusion.refs_0_, s32[1]{0:T(128)S(6)} %copy.86.refs_1_, bf16[3,512,768]{2,1,0:T(8,128)(2,1)} %project.1.refs_2_.refs_3_.refs_4_.refs_0_.refs_1_, bf16[3,512,768]{2,1,0:T(8,128)(2,1)} %project.1.refs_2_.refs_3_.refs_4_.refs_0_.refs_1_, ...), custom_call_target="tpu_custom_call" | custom-call | flops 4809999872 | tf_op jit(solution)/shard_map/attention_forward/pallas_call | solution.py:215
  67.7 5.9 %route.1 = (f32[512,768]{1,0:T(8,128)}, bf16[512,768]{1,0:T(8,128)(2,1)}, f32[512,2]{1,0:T(8,128)}, bf16[160,768]{1,0:T(8,128)(2,1)}, bf16[160,768]{1,0:T(8,128)...) custom-call(s32[1]{0:T(128)} %bitcast.2.core.refs_0_, ...), custom_call_target="tpu_custom_call" | custom-call | flops 2220000000 | tf_op jit(solution)/shard_map/route/pallas_call | solution.py:448
  79.9 3.8 collective-permute-done.18.refs_4_
  85.0 4.0 collective-permute-done.20.refs_2_
  91.3 13.7 %expert_forward.2 = (bf16[3072,640]{1,0:T(8,128)(2,1)}, bf16[640,3072]{1,0:T(8,128)(2,1)}, bf16[768,640]{1,0:T(8,128)(2,1)}, bf16[160,768]{1,0:T(8,128)(2,1)}, b...) custom-call(s32[1]{0:T(128)} %bitcast.4.refs_0_, ...), custom_call_target="tpu_custom_call" | custom-call | flops 4809999872 | tf_op jit(solution)/shard_map/expert_forward/pallas_call | solution.py:79
  105.9 4.2 %collective-permute-start.27 = (bf16[160,768]{1,0:T(8,128)(2,1)S(1)}, bf16[160,768]{1,0:T(8,128)(2,1)S(1)}, u32[]{:S(2)}, u32[]{:S(2)}) collective-permute-start(bf16[160,768]{1,0:T(8,128)(2,1)S(1)} %copy-done.76), channel_id=1, source_target_pairs={{0,2},{1,3},{2,0},{3,1},{4,6},{5,7},{6,4},{7,5},{8,10},{9,11},{10,... | collective-permute-start | bytes 737288 | tf_op jit(solution)/shard_map/ppermute | solution.py:758
  112.7 13.8 %expert_forward.3 = (bf16[3072,640]{1,0:T(8,128)(2,1)}, bf16[640,3072]{1,0:T(8,128)(2,1)}, bf16[768,640]{1,0:T(8,128)(2,1)}, bf16[160,768]{1,0:T(8,128)(2,1)}, b...) custom-call(s32[1]{0:T(128)} %bitcast.4.refs_0_, bf16[640,768]{1,0:T(8,128)(2,1)} %copy-done.15, ...), custom_call_target="tpu_custom_call" | custom-call | flops 4809999872 | tf_op jit(solution)/shard_map/expert_forward/pallas_call | solution.py:79
  135.5 5.6 %collective-permute-done.26 = f32[8,128]{1,0:T(8,128)S(1)} collective-permute-done((f32[8,128]{1,0:T(8,128)S(1)}, f32[8,128]{1,0:T(8,128)S(1)}, u32[]{:S(2)}, u32[]{:S(2)}) %collective-permute-start.26) | collective-permute-done | bytes 4128 | tf_op jit(solution)/shard_map/ppermute | solution.py:758
  144.1 8.5 %combine.1 = (bf16[512,768]{1,0:T(8,128)(2,1)}, f32[512,768]{1,0:T(8,128)}, bf16[512,8]{1,0:T(8,128)(2,1)}, f32[8,768]{1,0:T(8,128)}, bf16[160,768]{1,0:T(8,128)...) custom-call(s32[512,2]{1,0:T(8,128)} %copy-done.14, ...), custom_call_target="tpu_custom_call" | custom-call | flops 2960000000 | tf_op jit(solution)/shard_map/combine/pallas_call | solution.py:504
  164.4 6.2 %collective-permute-done.39.refs_4_ = bf16[160,768]{1,0:T(8,128)(2,1)S(1)} collective-permute-done((bf16[160,768]{1,0:T(8,128)(2,1)}, bf16[160,768]{1,0:T(8,128)(2,1)S(1)}, u32[]{:S(2)}, u32[]{:S(2)}) %collective-permute-start.39) | collective-permute-done | bytes 245792 | tf_op jit(solution)/shard_map/ppermute | solution.py:758
  171.2 12.5 %expert_backward.2 = (bf16[640,3072]{1,0:T(8,128)(2,1)}, bf16[640,768]{1,0:T(8,128)(2,1)}, bf16[160,768]{1,0:T(8,128)(2,1)}, bf16[160,768]{1,0:T(8,128)(2,1)}, b...) custom-call(s32[1]{0:T(128)} %bitcast.4.refs_0_, bf16[160,768]{1,0:T(8,128)(2,1)} %get-tuple-element.215.refs_1_, ...), custom_call_target="tpu_custom_call" | custom-call | flops 4070000128 | tf_op jit(solution)/shard_map/expert_backward/pallas_call | solution.py:136
  187.4 7.8 %weight_part.4 = (bf16[2,2,128,768]{3,2,1,0:T(8,128)(2,1)}, bf16[2,2,128,768]{3,2,1,0:T(8,128)(2,1)}, bf16[2,2,128,768]{3,2,1,0:T(8,128)(2,1)}) custom-call(s32[4]{0:T(128)} %pad_add_fusion.1.refs_0_, bf16[3072,640]{1,0:T(8,128)(2,1)} %get-tuple-element.191.refs_1_.refs_2_.refs_3_.refs_4_, ...), custom_call_target="tpu_custom_call" | custom-call | flops 1480000000 | tf_op jit(solution)/shard_map/weight_part/pallas_call | solution.py:338
  199.4 12.9 %expert_backward.3 = (bf16[640,3072]{1,0:T(8,128)(2,1)}, bf16[640,768]{1,0:T(8,128)(2,1)}, bf16[160,768]{1,0:T(8,128)(2,1)}, bf16[160,768]{1,0:T(8,128)(2,1)}, b...) custom-call(s32[1]{0:T(128)} %bitcast.4.refs_0_, bf16[640,768]{1,0:T(8,128)(2,1)} %copy-done.1, ...), custom_call_target="tpu_custom_call" | custom-call | flops 4070000128 | tf_op jit(solution)/shard_map/expert_backward/pallas_call | solution.py:136
  220.2 7.8 %weight_part.5 = (bf16[2,2,128,768]{3,2,1,0:T(8,128)(2,1)}, bf16[2,2,128,768]{3,2,1,0:T(8,128)(2,1)}, bf16[2,2,128,768]{3,2,1,0:T(8,128)(2,1)}) custom-call(s32[4]{0:T(128)} %pad_add_fusion.2.refs_0_, bf16[3072,640]{1,0:T(8,128)(2,1)} %get-tuple-element.191.refs_1_.refs_2_.refs_3_.refs_4_, ...), custom_call_target="tpu_custom_call" | custom-call | flops 1480000000 | tf_op jit(solution)/shard_map/weight_part/pallas_call | solution.py:338
  229.5 7.6 %weight_part.6 = (bf16[2,2,32,3072]{3,2,1,0:T(8,128)(2,1)}, bf16[2,2,32,3072]{3,2,1,0:T(8,128)(2,1)}, bf16[2,2,32,3072]{3,2,1,0:T(8,128)(2,1)}) custom-call(s32[4]{0:T(128)} %pad_add_fusion.1.refs_0_, bf16[768,640]{1,0:T(8,128)(2,1)} %get-tuple-element.221.refs_1_.refs_2_.refs_3_.refs_4_, ...), custom_call_target="tpu_custom_call" | custom-call | flops 1480000000 | tf_op jit(solution)/shard_map/weight_part/pallas_call | solution.py:338
  239.0 8.6 %collect.1 = (f32[512,768]{1,0:T(8,128)}, bf16[512,768]{1,0:T(8,128)(2,1)}, bf16[512,768]{1,0:T(8,128)(2,1)}, f32[8,768]{1,0:T(8,128)}) custom-call(s32[1]{0:T(128)} %bitcast.2.core.refs_0_, s32[512,2]{1,0:T(8,128)} %copy-done.14, bf16[160,768]{1,0:T(8,128)(2,1)} %get-tuple-element.263.refs_2_, bf16[160,768]{1,0:T(8,128)(2,1)} %copy-done.63, ...), custom_call_target="tpu_custom_call" | custom-call | flops 2960000000 | tf_op jit(solution)/shard_map/collect/pallas_call | solution.py:555
  249.5 11.5 %attention_backward.1 = (bf16[3,512,768]{2,1,0:T(8,128)(2,1)}, f32[12,4,128,128]{3,2,1,0:T(8,128)}) custom-call(bf16[3,512,768]{2,1,0:T(8,128)(2,1)} %project.1.refs_2_.refs_3_.refs_4_.refs_0_.refs_1_, bf16[3,512,768]{2,1,0:T(8,128)(2,1)} %project.1.refs_2_.refs_3_.refs_4_.refs_0_.refs_1_, ...), custom_call_target="tpu_custom_call" | custom-call | flops 1480000000 | tf_op jit(solution)/shard_map/attention_backward/pallas_call | solution.py:281
  262.0 8.2 %outer_halves.1 = (bf16[2,768,384]{2,1,0:T(8,128)(2,1)}, bf16[2,768,384]{2,1,0:T(8,128)(2,1)}, bf16[2,768,384]{2,1,0:T(8,128)(2,1)}, bf16[2,768,384]{2,1,0:T(8,128)(2,1)}) custom-call(s32[1]{0:T(128)} %bitcast.2.core.refs_0_, bf16[512,768]{1,0:T(8,128)(2,1)} %fusion.6.rows.refs_1_, bf16[512,768]{1,0:T(8,128)(2,1)} %get-tuple-element.183.attended.refs_2_, ...), custom_call_target="tpu_custom_call" | custom-call | flops 740000000 | tf_op jit(solution)/shard_map/outer_halves/pallas_call | solution.py:605
  283.7 7.5 %weight_part.7 = (bf16[2,2,32,3072]{3,2,1,0:T(8,128)(2,1)}, bf16[2,2,32,3072]{3,2,1,0:T(8,128)(2,1)}, bf16[2,2,32,3072]{3,2,1,0:T(8,128)(2,1)}) custom-call(s32[4]{0:T(128)} %pad_add_fusion.2.refs_0_, bf16[768,640]{1,0:T(8,128)(2,1)} %get-tuple-element.221.refs_1_.refs_2_.refs_3_.refs_4_, ...), custom_call_target="tpu_custom_call" | custom-call | flops 14800000000 | tf_op jit(solution)/shard_map/weight_part/pallas_call | solution.py:338
  293.7 3.5 collective-permute-done.62
  298.3 14.0 %collective-permute-done.64 = bf16[1,4,128,768]{3,2,1,0:T(8,128)(2,1)S(1)} collective-permute-done((bf16[1,4,128,768]{3,2,1,0:T(8,128)(2,1)S(1)}, bf16[1,4,128,768]{3,2,1,0:T(8,128)(2,1)S(1)}, u32[]{:S(2)}, u32[]{:S(2)}) %collective-permute-start.64) | collective-permute-done | bytes 786464 | tf_op jit(solution)/shard_map/ppermute | solution.py:758
  318.3 3.4 collective-permute-start.67
  321.9 5.3 %fusion.11 = f32[12,32]{1,0:T(8,128)S(1)} fusion(s32[4,128,128]{2,1,0:T(8,128)S(1)} %pad_add_fusion, f32[12,4,128,128]{3,2,1,0:T(8,128)S(1)} %copy-done.3), kind=kOutput, calls=%fused_computation.34 | convolution fusion | flops 304087040 | bytes 3409408 | tf_op jit(solution)/shard_map/hdxy,dxyb->hb/dot_general | solution.py:714
  327.1 8.5 %enter.1 = (f32[512,768]{1,0:T(8,128)}, f32[16,768]{1,0:T(8,128)}) custom-call(s32[1]{0:T(128)} %bitcast.2.core.refs_0_, bf16[3,512,768]{2,1,0:T(8,128)(2,1)} %get-tuple-element.317.refs_3_.grads, bf16[4,768,384]{2,1,0:T(8,128)(2,1)} %join.1.mine.refs_15_, bf16[4,768,384]{2,1,0:T(8,128)(2,1)} %copy-done, bf16[512,768]{1,0:T(8,128)(2,1)} %tokens.3, ...), custom_call_target="tpu_custom_call" | custom-call | flops 2220000000 | tf_op jit(solution)/shard_map/enter/pallas_call | solution.py:659
  337.2 4.5 %collective-permute-done.65 = bf16[3,128,768]{2,1,0:T(8,128)(2,1)} collective-permute-done((bf16[3,128,768]{2,1,0:T(8,128)(2,1)}, bf16[3,128,768]{2,1,0:T(8,128)(2,1)}, u32[]{:S(2)}, u32[]{:S(2)}) %collective-permute-start.65) | collective-permute-done | bytes 589856 | tf_op jit(solution)/shard_map/ppermute | solution.py:758
  343.0 13.1 %collective-permute-done.68 = bf16[1,2,32,3072]{3,2,1,0:T(8,128)(2,1)} collective-permute-done((bf16[1,2,32,3072]{3,2,1,0:T(8,128)(2,1)}, bf16[1,2,32,3072]{3,2,1,0:T(8,128)(2,1)}, u32[]{:S(2)}, u32[]{:S(2)}) %collective-permute-start.68) | collective-permute-done | bytes 393248 | tf_op jit(solution)/shard_map/ppermute | solution.py:758
  361.7 7.2 %collective-permute-done.66 = bf16[4,2,48,384]{3,2,1,0:T(8,128)(2,1)S(1)} collective-permute-done((bf16[4,2,48,384]{3,2,1,0:T(8,128)(2,1)S(1)}, bf16[4,2,48,384]{3,2,1,0:T(8,128)(2,1)S(1)}, u32[]{:S(2)}, u32[]{:S(2)}) %collective-permute-start.66) | collective-permute-done | bytes 294944 | tf_op jit(solution)/shard_map/ppermute | solution.py:758
  373.2 4.1 %collective-permute-done.75 = f32[16,768]{1,0:T(8,128)S(1)} collective-permute-done((f32[16,768]{1,0:T(8,128)S(1)}, f32[16,768]{1,0:T(8,128)S(1)}, u32[]{:S(2)}, u32[]{:S(2)}) %collective-permute-start.75) | collective-permute-done | bytes 49184 | tf_op jit(solution)/shard_map/ppermute | solution.py:758
  378.0 4.6 %collective-permute-done.71 = bf16[2,32,3072]{2,1,0:T(8,128)(2,1)S(1)} collective-permute-done((bf16[2,32,3072]{2,1,0:T(8,128)(2,1)S(1)}, bf16[2,32,3072]{2,1,0:T(8,128)(2,1)S(1)}, u32[]{:S(2)}, u32[]{:S(2)}) %collective-permute-start.71) | collective-permute-done | bytes 393248 | tf_op jit(solution)/shard_map/ppermute | solution.py:758
  394.6 11.3 %collective-permute-done.79 = bf16[1,2,32,3072]{3,2,1,0:T(8,128)(2,1)S(1)} collective-permute-done((bf16[1,2,32,3072]{3,2,1,0:T(8,128)(2,1)S(1)}, bf16[1,2,32,3072]{3,2,1,0:T(8,128)(2,1)S(1)}, u32[]{:S(2)}, u32[]{:S(2)}) %collective-permute-start.79) | collective-permute-done | bytes 393248 | tf_op jit(solution)/shard_map/ppermute | solution.py:758
  (412 shorter events, 153.1 us)
Async XLA Ops:
  77.1 27.9 %collective-permute-start.24 = (bf16[160,768]{1,0:T(8,128)(2,1)}, bf16[160,768]{1,0:T(8,128)(2,1)S(1)}, u32[]{:S(2)}, u32[]{:S(2)}) collective-permute-start(bf16[160,768]{1,0:T(8,128)(2,1)} %get-tuple-element.197), channel_id=1, source_target_pairs={{0,10},{1,11},{2,8},{3,9},{4,14},{5,15},{6,12},{7,13},{8,2},{9,3},... | collective-permute-start | bytes 737288 | tf_op jit(solution)/shard_map/ppermute | solution.py:758
  79.5 25.6 %collective-permute-start.23 = (bf16[160,768]{1,0:T(8,128)(2,1)}, bf16[160,768]{1,0:T(8,128)(2,1)S(1)}, u32[]{:S(2)}, u32[]{:S(2)}) collective-permute-start(bf16[160,768]{1,0:T(8,128)(2,1)} %get-tuple-element.195), channel_id=1, source_target_pairs={{0,8},{1,9},{2,10},{3,11},{4,12},{5,13},{6,14},{7,15},{8,0},{9,1},... | collective-permute-start | bytes 737288 | tf_op jit(solution)/shard_map/ppermute | solution.py:758
  83.7 21.4 %collective-permute-start.22 = (bf16[160,768]{1,0:T(8,128)(2,1)}, bf16[160,768]{1,0:T(8,128)(2,1)S(1)}, u32[]{:S(2)}, u32[]{:S(2)}) collective-permute-start(bf16[160,768]{1,0:T(8,128)(2,1)} %get-tuple-element.193), channel_id=1, source_target_pairs={{0,2},{1,3},{2,0},{3,1},{4,6},{5,7},{6,4},{7,5},{8,10},{9,11},{10,... | collective-permute-start | bytes 737288 | tf_op jit(solution)/shard_map/ppermute | solution.py:758
  89.0 16.0 %collective-permute-start.19 = (f32[8,128]{1,0:T(8,128)S(1)}, f32[8,128]{1,0:T(8,128)S(1)}, u32[]{:S(2)}, u32[]{:S(2)}) collective-permute-start(f32[8,128]{1,0:T(8,128)S(1)} %add.546), channel_id=1, source_target_pairs={{0,8},{1,9},{2,10},{3,11},{4,12},{5,13},{6,14},{7,15},{8,0},{9,1},... | collective-permute-start | bytes 12296 | tf_op jit(solution)/shard_map/ppermute | solution.py:758
  105.9 20.6 %collective-permute-start.27 = (bf16[160,768]{1,0:T(8,128)(2,1)S(1)}, bf16[160,768]{1,0:T(8,128)(2,1)S(1)}, u32[]{:S(2)}, u32[]{:S(2)}) collective-permute-start(bf16[160,768]{1,0:T(8,128)(2,1)S(1)} %copy-done.76), channel_id=1, source_target_pairs={{0,2},{1,3},{2,0},{3,1},{4,6},{5,7},{6,4},{7,5},{8,10},{9,11},{10,... | collective-permute-start | bytes 737288 | tf_op jit(solution)/shard_map/ppermute | solution.py:758
  110.1 16.4 %collective-permute-start.28 = (bf16[160,768]{1,0:T(8,128)(2,1)S(1)}, bf16[160,768]{1,0:T(8,128)(2,1)S(1)}, u32[]{:S(2)}, u32[]{:S(2)}) collective-permute-start(bf16[160,768]{1,0:T(8,128)(2,1)S(1)} %copy-done.74), channel_id=1, source_target_pairs={{0,8},{1,9},{2,10},{3,11},{4,12},{5,13},{6,14},{7,15},{8,0},{9,1},... | collective-permute-start | bytes 737288 | tf_op jit(solution)/shard_map/ppermute | solution.py:758
  110.2 16.3 %collective-permute-start.29 = (bf16[160,768]{1,0:T(8,128)(2,1)S(1)}, bf16[160,768]{1,0:T(8,128)(2,1)S(1)}, u32[]{:S(2)}, u32[]{:S(2)}) collective-permute-start(bf16[160,768]{1,0:T(8,128)(2,1)S(1)} %copy-done.72), channel_id=1, source_target_pairs={{0,10},{1,11},{2,8},{3,9},{4,14},{5,15},{6,12},{7,13},{8,2},{9,3},... | collective-permute-start | bytes 737288 | tf_op jit(solution)/shard_map/ppermute | solution.py:758
  127.2 15.1 %collective-permute-start.30 = (bf16[160,768]{1,0:T(8,128)(2,1)}, bf16[160,768]{1,0:T(8,128)(2,1)S(1)}, u32[]{:S(2)}, u32[]{:S(2)}) collective-permute-start(bf16[160,768]{1,0:T(8,128)(2,1)} %get-tuple-element.205), channel_id=1, source_target_pairs={{0,1},{1,0},{2,3},{3,2},{4,5},{5,4},{6,7},{7,6},{8,9},{9,8},{10,11... | collective-permute-start | bytes 737288 | tf_op jit(solution)/shard_map/ppermute | solution.py:758
  158.1 25.6 %collective-permute-start.42 = (bf16[160,768]{1,0:T(8,128)(2,1)}, bf16[160,768]{1,0:T(8,128)(2,1)S(1)}, u32[]{:S(2)}, u32[]{:S(2)}) collective-permute-start(bf16[160,768]{1,0:T(8,128)(2,1)} %get-tuple-element.231), channel_id=1, source_target_pairs={{0,10},{1,11},{2,8},{3,9},{4,14},{5,15},{6,12},{7,13},{8,2},{9,3},... | collective-permute-start | bytes 737288 | tf_op jit(solution)/shard_map/ppermute | solution.py:758
  160.2 23.5 %collective-permute-start.41 = (bf16[160,768]{1,0:T(8,128)(2,1)}, bf16[160,768]{1,0:T(8,128)(2,1)S(1)}, u32[]{:S(2)}, u32[]{:S(2)}) collective-permute-start(bf16[160,768]{1,0:T(8,128)(2,1)} %get-tuple-element.229), channel_id=1, source_target_pairs={{0,8},{1,9},{2,10},{3,11},{4,12},{5,13},{6,14},{7,15},{8,0},{9,1},... | collective-permute-start | bytes 737288 | tf_op jit(solution)/shard_map/ppermute | solution.py:758
  160.2 23.5 %collective-permute-start.40 = (bf16[160,768]{1,0:T(8,128)(2,1)}, bf16[160,768]{1,0:T(8,128)(2,1)S(1)}, u32[]{:S(2)}, u32[]{:S(2)}) collective-permute-start(bf16[160,768]{1,0:T(8,128)(2,1)} %get-tuple-element.227), channel_id=1, source_target_pairs={{0,2},{1,3},{2,0},{3,1},{4,6},{5,7},{6,4},{7,5},{8,10},{9,11},{10,... | collective-permute-start | bytes 737288 | tf_op jit(solution)/shard_map/ppermute | solution.py:758
  195.3 19.8 %collective-permute-start.48 = (bf16[2,2,128,768]{3,2,1,0:T(8,128)(2,1)}, bf16[2,2,128,768]{3,2,1,0:T(8,128)(2,1)S(1)}, u32[]{:S(2)}, u32[]{:S(2)}) collective-permute-start(bf16[2,2,128,768]{3,2,1,0:T(8,128)(2,1)} %get-tuple-element.244), channel_id=1, source_target_pairs={{0,4},{1,5},{2,6},{3,7},{4,0},{5,1},{6,2},{7,3},{8,12},{9,13},{10,... | collective-permute-start | bytes 2359304 | tf_op jit(solution)/shard_map/ppermute | solution.py:758
  195.8 16.4 %collective-permute-start.44 = (bf16[160,768]{1,0:T(8,128)(2,1)S(1)}, bf16[160,768]{1,0:T(8,128)(2,1)S(1)}, u32[]{:S(2)}, u32[]{:S(2)}) collective-permute-start(bf16[160,768]{1,0:T(8,128)(2,1)S(1)} %copy-done.69), channel_id=1, source_target_pairs={{0,2},{1,3},{2,0},{3,1},{4,6},{5,7},{6,4},{7,5},{8,10},{9,11},{10,... | collective-permute-start | bytes 737288 | tf_op jit(solution)/shard_map/ppermute | solution.py:758
  196.4 15.8 %collective-permute-start.45 = (bf16[160,768]{1,0:T(8,128)(2,1)S(1)}, bf16[160,768]{1,0:T(8,128)(2,1)S(1)}, u32[]{:S(2)}, u32[]{:S(2)}) collective-permute-start(bf16[160,768]{1,0:T(8,128)(2,1)S(1)} %copy-done.68), channel_id=1, source_target_pairs={{0,8},{1,9},{2,10},{3,11},{4,12},{5,13},{6,14},{7,15},{8,0},{9,1},... | collective-permute-start | bytes 737288 | tf_op jit(solution)/shard_map/ppermute | solution.py:758
  215.3 22.4 %collective-permute-start.52 = (bf16[160,768]{1,0:T(8,128)(2,1)}, bf16[160,768]{1,0:T(8,128)(2,1)S(1)}, u32[]{:S(2)}, u32[]{:S(2)}) collective-permute-start(bf16[160,768]{1,0:T(8,128)(2,1)} %collective-permute-done.49), channel_id=1, source_target_pairs={{0,2},{1,3},{2,0},{3,1},{4,6},{5,7},{6,4},{7,5},{8,10},{9,11},{10,... | collective-permute-start | bytes 737288 | tf_op jit(solution)/shard_map/ppermute | solution.py:758
  215.9 22.3 %collective-permute-start.53 = (bf16[160,768]{1,0:T(8,128)(2,1)}, bf16[160,768]{1,0:T(8,128)(2,1)S(1)}, u32[]{:S(2)}, u32[]{:S(2)}) collective-permute-start(bf16[160,768]{1,0:T(8,128)(2,1)} %collective-permute-done.50), channel_id=1, source_target_pairs={{0,8},{1,9},{2,10},{3,11},{4,12},{5,13},{6,14},{7,15},{8,0},{9,1},... | collective-permute-start | bytes 737288 | tf_op jit(solution)/shard_map/ppermute | solution.py:758
  217.9 20.4 %collective-permute-start.54 = (bf16[160,768]{1,0:T(8,128)(2,1)}, bf16[160,768]{1,0:T(8,128)(2,1)S(1)}, u32[]{:S(2)}, u32[]{:S(2)}) collective-permute-start(bf16[160,768]{1,0:T(8,128)(2,1)} %collective-permute-done.51), channel_id=1, source_target_pairs={{0,10},{1,11},{2,8},{3,9},{4,14},{5,15},{6,12},{7,13},{8,2},{9,3},... | collective-permute-start | bytes 737288 | tf_op jit(solution)/shard_map/ppermute | solution.py:758
  218.7 30.4 %collective-permute-start.55 = (bf16[2,2,128,768]{3,2,1,0:T(8,128)(2,1)S(1)}, bf16[2,2,128,768]{3,2,1,0:T(8,128)(2,1)S(1)}, u32[]{:S(2)}, u32[]{:S(2)}) collective-permute-start(bf16[2,2,128,768]{3,2,1,0:T(8,128)(2,1)S(1)} %copy-done.58), channel_id=1, source_target_pairs={{0,4},{1,5},{2,6},{3,7},{4,0},{5,1},{6,2},{7,3},{8,12},{9,13},{10,... | collective-permute-start | bytes 2359304 | tf_op jit(solution)/shard_map/ppermute | solution.py:758
  237.1 23.9 %collective-permute-start.57 = (bf16[1,2,128,768]{3,2,1,0:T(8,128)(2,1)S(1)}, bf16[1,2,128,768]{3,2,1,0:T(8,128)(2,1)S(1)}, u32[]{:S(2)}, u32[]{:S(2)}) collective-permute-start(bf16[1,2,128,768]{3,2,1,0:T(8,128)(2,1)S(1)} %constant_dynamic-slice_fusion.7), channel_id=1, source_target_pairs={{0,16},{1,17},{2,18},{3,19},{4,20},{5,21},{6,22},{7,23},{8,24},{9,... | collective-permute-start | bytes 1179656 | tf_op jit(solution)/shard_map/ppermute | solution.py:758
  237.6 23.4 %collective-permute-start.56 = (bf16[2,2,128,768]{3,2,1,0:T(8,128)(2,1)S(1)}, bf16[2,2,128,768]{3,2,1,0:T(8,128)(2,1)S(1)}, u32[]{:S(2)}, u32[]{:S(2)}) collective-permute-start(bf16[2,2,128,768]{3,2,1,0:T(8,128)(2,1)S(1)} %copy-done.57), channel_id=1, source_target_pairs={{0,4},{1,5},{2,6},{3,7},{4,0},{5,1},{6,2},{7,3},{8,12},{9,13},{10,... | collective-permute-start | bytes 2359304 | tf_op jit(solution)/shard_map/ppermute | solution.py:758
  247.6 25.3 %collective-permute-start.58 = (bf16[2,2,32,3072]{3,2,1,0:T(8,128)(2,1)S(1)}, bf16[2,2,32,3072]{3,2,1,0:T(8,128)(2,1)}, u32[]{:S(2)}, u32[]{:S(2)}) collective-permute-start(bf16[2,2,32,3072]{3,2,1,0:T(8,128)(2,1)S(1)} %copy-done.59), channel_id=1, source_target_pairs={{0,4},{1,5},{2,6},{3,7},{4,0},{5,1},{6,2},{7,3},{8,12},{9,13},{10,... | collective-permute-start | bytes 2359304 | tf_op jit(solution)/shard_map/ppermute | solution.py:758
  275.0 37.3 %collective-permute-start.64 = (bf16[1,4,128,768]{3,2,1,0:T(8,128)(2,1)S(1)}, bf16[1,4,128,768]{3,2,1,0:T(8,128)(2,1)S(1)}, u32[]{:S(2)}, u32[]{:S(2)}) collective-permute-start(bf16[1,4,128,768]{3,2,1,0:T(8,128)(2,1)S(1)} %pad_maximum_fusion.5), channel_id=1, source_target_pairs={{0,16},{1,17},{2,18},{3,19},{4,20},{5,21},{6,22},{7,23},{8,24},{9,... | collective-permute-start | bytes 2359304 | tf_op jit(solution)/shard_map/ppermute | solution.py:758
  277.7 19.4 %collective-permute-start.62 = (bf16[2,2,32,3072]{3,2,1,0:T(8,128)(2,1)}, bf16[2,2,32,3072]{3,2,1,0:T(8,128)(2,1)S(1)}, u32[]{:S(2)}, u32[]{:S(2)}) collective-permute-start(bf16[2,2,32,3072]{3,2,1,0:T(8,128)(2,1)} %get-tuple-element.296), channel_id=1, source_target_pairs={{0,4},{1,5},{2,6},{3,7},{4,0},{5,1},{6,2},{7,3},{8,12},{9,13},{10,... | collective-permute-start | bytes 2359304 | tf_op jit(solution)/shard_map/ppermute | solution.py:758
  283.0 30.4 %collective-permute-start.61 = (bf16[4,8,48,384]{3,2,1,0:T(8,128)(2,1)S(1)}, bf16[4,8,48,384]{3,2,1,0:T(8,128)(2,1)S(1)}, u32[]{:S(2)}, u32[]{:S(2)}) collective-permute-start(bf16[4,8,48,384]{3,2,1,0:T(8,128)(2,1)S(1)} %pad_maximum_fusion.2), channel_id=1, source_target_pairs={{0,2},{1,3},{2,0},{3,1},{4,6},{5,7},{6,4},{7,5},{8,10},{9,11},{10,... | collective-permute-start | bytes 3538952 | tf_op jit(solution)/shard_map/ppermute | solution.py:758
  315.8 21.4 %collective-permute-start.63 = (bf16[4,2,2,48,384]{4,3,2,1,0:T(8,128)(2,1)}, bf16[4,2,2,48,384]{4,3,2,1,0:T(8,128)(2,1)}, u32[]{:S(2)}, u32[]{:S(2)}) collective-permute-start(bf16[4,2,2,48,384]{4,3,2,1,0:T(8,128)(2,1)} %dynamic-slice_bitcast_fusion), channel_id=1, source_target_pairs={{0,4},{1,5},{2,6},{3,7},{4,0},{5,1},{6,2},{7,3},{8,12},{9,13},{10,... | collective-permute-start | bytes 1769480 | tf_op jit(solution)/shard_map/ppermute | solution.py:758
  316.3 25.4 %collective-permute-start.65 = (bf16[3,128,768]{2,1,0:T(8,128)(2,1)}, bf16[3,128,768]{2,1,0:T(8,128)(2,1)}, u32[]{:S(2)}, u32[]{:S(2)}) collective-permute-start(bf16[3,128,768]{2,1,0:T(8,128)(2,1)} %pad_maximum_fusion.6), channel_id=1, source_target_pairs={{0,8},{1,9},{2,10},{3,11},{4,12},{5,13},{6,14},{7,15},{8,0},{9,1},... | collective-permute-start | bytes 1769480 | tf_op jit(solution)/shard_map/ppermute | solution.py:758
  318.3 43.4 %collective-permute-start.67 = (bf16[1,2,32,3072]{3,2,1,0:T(8,128)(2,1)}, bf16[1,2,32,3072]{3,2,1,0:T(8,128)(2,1)}, u32[]{:S(2)}, u32[]{:S(2)}) collective-permute-start(bf16[1,2,32,3072]{3,2,1,0:T(8,128)(2,1)} %constant_dynamic-slice_fusion.4), channel_id=1, source_target_pairs={{0,16},{1,17},{2,18},{3,19},{4,20},{5,21},{6,22},{7,23},{8,24},{9,... | collective-permute-start | bytes 1179656 | tf_op jit(solution)/shard_map/ppermute | solution.py:758
  321.8 34.4 %collective-permute-start.68 = (bf16[1,2,32,3072]{3,2,1,0:T(8,128)(2,1)}, bf16[1,2,32,3072]{3,2,1,0:T(8,128)(2,1)}, u32[]{:S(2)}, u32[]{:S(2)}) collective-permute-start(bf16[1,2,32,3072]{3,2,1,0:T(8,128)(2,1)} %constant_dynamic-slice_fusion.3), channel_id=1, source_target_pairs={{0,16},{1,17},{2,18},{3,19},{4,20},{5,21},{6,22},{7,23},{8,24},{9,... | collective-permute-start | bytes 1179656 | tf_op jit(solution)/shard_map/ppermute | solution.py:758
  358.1 47.9 %collective-permute-start.80 = (bf16[1,32,3072]{2,1,0:T(8,128)(2,1)S(1)}, bf16[1,32,3072]{2,1,0:T(8,128)(2,1)S(1)}, u32[]{:S(2)}, u32[]{:S(2)}) collective-permute-start(bf16[1,32,3072]{2,1,0:T(8,128)(2,1)S(1)} %get-tuple-element.353), channel_id=1, source_target_pairs={{0,8},{1,9},{2,10},{3,11},{4,12},{5,13},{6,14},{7,15},{8,0},{9,1},... | collective-permute-start | bytes 589832 | tf_op jit(solution)/shard_map/ppermute | solution.py:758
  360.2 17.5 %collective-permute-start.70 = (bf16[2,2,32,3072]{3,2,1,0:T(8,128)(2,1)S(1)}, bf16[2,2,32,3072]{3,2,1,0:T(8,128)(2,1)S(1)}, u32[]{:S(2)}, u32[]{:S(2)}) collective-permute-start(bf16[2,2,32,3072]{3,2,1,0:T(8,128)(2,1)S(1)} %copy-done.56), channel_id=1, source_target_pairs={{0,4},{1,5},{2,6},{3,7},{4,0},{5,1},{6,2},{7,3},{8,12},{9,13},{10,... | collective-permute-start | bytes 2359304 | tf_op jit(solution)/shard_map/ppermute | solution.py:758
  391.0 14.9 %collective-permute-start.79 = (bf16[1,2,32,3072]{3,2,1,0:T(8,128)(2,1)S(1)}, bf16[1,2,32,3072]{3,2,1,0:T(8,128)(2,1)S(1)}, u32[]{:S(2)}, u32[]{:S(2)}) collective-permute-start(bf16[1,2,32,3072]{3,2,1,0:T(8,128)(2,1)S(1)} %constant_dynamic-slice_fusion), channel_id=1, source_target_pairs={{0,16},{1,17},{2,18},{3,19},{4,20},{5,21},{6,22},{7,23},{8,24},{9,... | collective-permute-start | bytes 1179656 | tf_op jit(solution)/shard_map/ppermute | solution.py:758
  391.7 16.2 %collective-permute-start.78 = (bf16[4,96,384]{2,1,0:T(8,128)(2,1)S(1)}, bf16[4,96,384]{2,1,0:T(8,128)(2,1)S(1)}, u32[]{:S(2)}, u32[]{:S(2)}) collective-permute-start(bf16[4,96,384]{2,1,0:T(8,128)(2,1)S(1)} %pad_maximum_fusion.9), channel_id=1, source_target_pairs={{0,1},{1,0},{2,3},{3,2},{4,5},{5,4},{6,7},{7,6},{8,9},{9,8},{10,11... | collective-permute-start | bytes 884744 | tf_op jit(solution)/shard_map/ppermute | solution.py:758
  (131 other events, 1077.3 us)
